TPU v7x, 32 devices: a whole 2x2x4 slice. The times are simulated.
32 devices in a mesh: space: 16 (over z, y, core), orb: 2 (over x).
Axes of the slice: x: 2, y: 2, z: 4, core: 2. Of those that a mesh axis runs over, the one named last changes fastest.
Arguments:
- hamiltonian: bfloat16 [128, 7, 256, 256], P('space'), may hold values from -0.125 to 0.125
- orbitals: bfloat16 [256, 32768], P('orb', 'space'), may hold values from -6 to 6
- adjacency: int32 [128, 6], P('space'), may hold values from 0 to 127, as said below
Outputs:
- basis: float32 [256, 32768], P('orb', 'space')
- factor: float32 [256, 256], replicated
Inputs may be any that keep to these rules, and one draw needn't show every extreme that they name: `adjacency`: with elements in blocks of 8 (block b holds elements b * 8 to b * 8 + 7), face 0 of an element in block b lies in block b - 1 and face 1 in block b + 1 (both modulo the number of blocks), faces 2 to 5 in block b; for each face, the elements of a block name every element of the target block exactly once.
All inputs are finite; a program needn't handle non-finite values.
Results may differ from a plain program's by a relative error of at most 0.0041.
Values may be sent and summed in bfloat16 or wider, within the bound.
No kernel may reach another device: no remote copies, remote signals or barrier semaphores. Data moves between devices by JAX's collectives and lax.ppermute only.
A program may use at most 64 MiB of HBM per device.

v0:
```python
import jax
import jax.numpy as jnp
from jax import lax
from jax.sharding import PartitionSpec as P

centre = 0.25
radius = 0.75


def with_halo(block, sides, width):
    for axis, dim in sides:
        count = lax.axis_size(axis)
        forward = [(i, i + 1) for i in range(count - 1)]
        forward.append((count - 1, 0))
        backward = [(target, source) for source, target in forward]
        low = lax.ppermute(
            lax.slice_in_dim(block, block.shape[dim] - width, None, axis=dim), axis, forward
        )
        high = lax.ppermute(lax.slice_in_dim(block, 0, width, axis=dim), axis, backward)
        block = jnp.concatenate([low, block, high], axis=dim)
    return block


def shards(hamiltonian, orbitals, adjacency):
    count = hamiltonian.shape[0]
    width = hamiltonian.shape[2]
    owned = orbitals.shape[0]
    total = count * lax.axis_size("space")
    first = lax.axis_index("space") * count
    located = (adjacency - first + count) % total

    def apply_ham(vec):
        padded = with_halo(vec, (("space", 1),), count * width)
        blocks = padded.reshape(owned, 3 * count, width)
        near = jnp.take(blocks, located.reshape(-1), axis=1).reshape(owned, count, 6, width)
        own_part = vec.reshape(owned, count, width)
        result = jnp.einsum(
            "oej,eij->oei", own_part, hamiltonian[:, 0], preferred_element_type=jnp.float32
        )
        result = result + jnp.einsum(
            "oefj,efij->oei", near, hamiltonian[:, 1:], preferred_element_type=jnp.float32
        )
        return result.reshape(owned, count * width)

    level_zero = orbitals.astype(jnp.float32)
    level_one = ((apply_ham(orbitals) - centre * level_zero) / radius).astype(jnp.bfloat16)
    one_wide = level_one.astype(jnp.float32)
    level_two = (2.0 * (apply_ham(level_one) - centre * one_wide) / radius - level_zero).astype(
        jnp.bfloat16
    )
    two_wide = level_two.astype(jnp.float32)
    filtered = 2.0 * (apply_ham(level_two) - centre * two_wide) / radius - one_wide
    columns = lax.all_gather(filtered, "orb", axis=0, tiled=True)
    partial_gram = jnp.dot(columns, columns.T, precision=lax.Precision.HIGHEST)
    gram = lax.psum(partial_gram, "space")
    lower = jnp.linalg.cholesky(gram)
    solved = lax.linalg.triangular_solve(lower, columns, left_side=True, lower=True)
    basis = lax.dynamic_slice_in_dim(solved, lax.axis_index("orb") * owned, owned, 0)
    return (basis, lower.T)


def solution(mesh):
    in_specs = (P("space", None, None, None), P("orb", "space"), P("space", None))
    out_specs = (P("orb", "space"), P())
    return jax.shard_map(shards, mesh=mesh, in_specs=in_specs, out_specs=out_specs, check_vma=False)
```

profile of v0, /device:TPU:0, one launch (start us, length us, event | category | flops | bytes accessed | tf_op | source)
XLA Modules:
  0.0 301.9 jit_solution(2157086342630050979)
XLA Ops:
  7.2 1.3 copy.30
  8.5 0.5 collective-permute-start
  9.0 5.1 %collective-permute-start.1 = (bf16[128,2048]{0,1:T(8,128)(2,1)S(1)}, bf16[128,2048]{0,1:T(8,128)(2,1)S(1)}, u32[]{:S(2)}, u32[]{:S(2)}) collective-permute-start(bf16[128,2048]{0,1:T(8,128)(2,1)S(1)} %copy.30), channel_id=1, source_target_pairs={{2,0},{4,2},{6,4},{8,6},{10,8},{12,10},{14,12},{16,14},{18,16},{20... | collective-permute-start | bytes 1572872 | tf_op jit(solution)/shard_map/ppermute | solution.py:19
  14.1 0.7 add_select_fusion
  14.8 0.1 reshape.69
  14.9 6.1 %collective-permute-done = bf16[128,2048]{0,1:T(8,128)(2,1)S(1)} collective-permute-done((bf16[128,2048]{0,1:T(8,128)(2,1)S(1)}, bf16[128,2048]{0,1:T(8,128)(2,1)S(1)}, u32[]{:S(2)}, u32[]{:S(2)}) %collective-permute-start) | collective-permute-done | bytes 524320 | tf_op jit(solution)/shard_map/ppermute | solution.py:16
  21.0 0.1 pad_maximum_fusion
  21.1 0.7 copy.33
  21.8 2.5 gather_fusion
  24.3 2.2 broadcast_select_fusion.2
  26.6 4.6 %fusion.6 = f32[128,8,256]{0,2,1:T(8,128)S(1)} fusion(bf16[128,8,6,256]{3,0,2,1:T(8,128)(2,1)S(1)} %bitcast.102, bf16[8,7,256,256]{3,2,1,0:T(8,128)(2,1)} %param.5), kind=kOutput, calls=%fused_computation.20 | convolution fusion | flops 805306368 | bytes 10485760 | tf_op jit(solution)/shard_map/oefj,efij->oei/dot_general | solution.py:40
  31.2 1.7 fusion.17
  32.9 0.3 copy.35
  33.2 0.2 fusion.20
  33.4 4.9 %collective-permute-start.2 = (bf16[128,2048]{1,0:T(8,128)(2,1)S(1)}, bf16[128,2048]{1,0:T(8,128)(2,1)S(1)}, u32[]{:S(2)}, u32[]{:S(2)}) collective-permute-start(bf16[128,2048]{1,0:T(8,128)(2,1)S(1)} %fusion.20), channel_id=1, source_target_pairs={{0,2},{2,4},{4,6},{6,8},{8,10},{10,12},{12,14},{14,16},{16,18},{18... | collective-permute-start | bytes 1572872 | tf_op jit(solution)/shard_map/ppermute | solution.py:16
  38.3 6.6 %collective-permute-done.2 = bf16[128,2048]{1,0:T(8,128)(2,1)S(1)} collective-permute-done((bf16[128,2048]{1,0:T(8,128)(2,1)S(1)}, bf16[128,2048]{1,0:T(8,128)(2,1)S(1)}, u32[]{:S(2)}, u32[]{:S(2)}) %collective-permute-start.2) | collective-permute-done | bytes 524320 | tf_op jit(solution)/shard_map/ppermute | solution.py:16
  44.9 0.1 collective-permute-done.3
  45.0 0.1 pad_maximum_fusion.1
  45.2 1.6 copy.37
  46.8 1.7 copy.38
  48.5 2.5 gather_fusion.1
  51.0 2.2 broadcast_select_fusion.1
  53.2 4.9 %fusion.9 = f32[8,128,256]{2,1,0:T(8,128)S(1)} fusion(bf16[128,8,6,256]{3,0,2,1:T(8,128)(2,1)S(1)} %bitcast.103, bf16[8,7,256,256]{3,2,1,0:T(8,128)(2,1)} %param.5), kind=kOutput, calls=%fused_computation.21 | convolution fusion | flops 805306368 | bytes 10485760 | tf_op jit(solution)/shard_map/oefj,efij->oei/dot_general | solution.py:40
  58.2 1.7 fusion.16
  59.9 1.3 copy.39
  61.2 1.6 copy.40
  62.7 0.2 fusion.21
  63.0 5.3 %collective-permute-start.4 = (bf16[128,2048]{1,0:T(8,128)(2,1)S(1)}, bf16[128,2048]{1,0:T(8,128)(2,1)S(1)}, u32[]{:S(2)}, u32[]{:S(2)}) collective-permute-start(bf16[128,2048]{1,0:T(8,128)(2,1)S(1)} %fusion.21), channel_id=1, source_target_pairs={{0,2},{2,4},{4,6},{6,8},{8,10},{10,12},{12,14},{14,16},{16,18},{18... | collective-permute-start | bytes 1572872 | tf_op jit(solution)/shard_map/ppermute | solution.py:16
  68.2 6.4 %collective-permute-done.4 = bf16[128,2048]{1,0:T(8,128)(2,1)S(1)} collective-permute-done((bf16[128,2048]{1,0:T(8,128)(2,1)S(1)}, bf16[128,2048]{1,0:T(8,128)(2,1)S(1)}, u32[]{:S(2)}, u32[]{:S(2)}) %collective-permute-start.4) | collective-permute-done | bytes 524320 | tf_op jit(solution)/shard_map/ppermute | solution.py:16
  74.7 0.3 collective-permute-done.5
  74.9 0.1 pad_maximum_fusion.2
  75.1 1.6 copy.42
  76.7 1.7 copy.43
  78.4 2.5 gather_fusion.2
  80.9 2.2 broadcast_select_fusion
  83.1 4.9 %fusion.12 = f32[8,128,256]{2,1,0:T(8,128)S(1)} fusion(bf16[128,8,6,256]{3,0,2,1:T(8,128)(2,1)S(1)} %bitcast.101, bf16[8,7,256,256]{3,2,1,0:T(8,128)(2,1)} %param.5), kind=kOutput, calls=%fused_computation.22 | convolution fusion | flops 805306368 | bytes 10485760 | tf_op jit(solution)/shard_map/oefj,efij->oei/dot_general | solution.py:40
  88.0 1.7 fusion.15
  89.8 0.3 copy.44
  90.1 0.3 copy.45
  90.4 1.2 convert_subtract_fusion
  91.7 0.2 all-reduce.3.cloned.1.call-start
  91.9 40.9 %all-gather.2.cloned.1.call-done = f32[256,2048]{1,0:T(8,128)} async-done(((f32[128,2048]{1,0:T(8,128)}), f32[256,2048]{1,0:T(8,128)}) %all-gather.2.cloned.1.call-update) | async-done | bytes 2097168 | tf_op jit(solution)/shard_map/all_gather | solution.py:53
  132.8 4.8 %fusion.49 = f32[256,256]{0,1:T(8,128)} fusion(f32[256,2048]{1,0:T(8,128)} %all-gather.2.cloned.1.call-done), kind=kOutput, calls=%fused_computation.86 | convolution fusion | flops 1610612736 | bytes 2359296 | tf_op jit(solution)/shard_map/dot_general | solution.py:54
  137.6 88.8 %all-reduce.3.cloned.1.call-done = f32[256,256]{0,1:T(8,128)} async-done(((f32[256,256]{0,1:T(8,128)}), f32[256,256]{0,1:T(8,128)}) %all-reduce.3.cloned.1.call-update) | async-done | bytes 262160 | tf_op jit(solution)/shard_map/psum | solution.py:55
  226.5 1.1 copy.47
  227.5 1.0 fusion.39
  228.5 11.7 %cholesky.50 = f32[128,128]{1,0:T(8,128)S(1)} custom-call(f32[128,128]{1,0:T(8,128)S(1)} %cholesky.118), custom_call_target="Cholesky" | custom-call | tf_op jit(solution)/shard_map/jit(cholesky)/cholesky | solution.py:56
  240.3 9.8 %custom-call.14 = f32[1,128,128]{1,2,0:T(8,128)S(1)} custom-call(f32[1,128,128]{2,1,0:T(8,128)S(1)} %get-tuple-element.32), custom_call_target="InvertDiagBlocksLowerTriangular" | custom-call | tf_op jit(solution)/shard_map/jit(cholesky)/cholesky | solution.py:56
  250.1 0.2 constant_dynamic-update-slice_fusion
  250.3 0.3 convolution_subtract_fusion.1
  250.6 11.8 %cholesky.105 = f32[128,128]{1,0:T(8,128)S(1)} custom-call(f32[128,128]{1,0:T(8,128)S(1)} %convolution_subtract_fusion.1), custom_call_target="Cholesky" | custom-call | tf_op jit(solution)/shard_map/jit(cholesky)/cholesky | solution.py:56
  262.5 0.6 compare_reduce_fusion
  264.4 0.7 fusion.41
  265.2 4.1 %while.1 = (s32[]{:T(128)}, f32[256,256]{1,0:T(8,128)S(1)}, s32[2,2]{1,0:T(2,128)S(1)}, f32[2,128,128]{2,1,0:T(8,128)S(1)}, s32[]{:T(128)}) while((s32[]{:T(128)}, f32[256,256]{1,0:T(8,128)S(1)}, s32[2,2]{1,0:T(2,128)S(1)}, f32[2,128,128]{2,1,0:T(8,128)S(1)}, s32[]{:T(128)}) %tuple.32), condition=%wide.while_cond, body=%wide.while_body.sunk | while | flops 2 | bytes 131181 | solution.py:57
  265.3 0.6 fusion.60
  265.8 1.4 bitcast_dynamic-update-slice_fusion.2
  267.3 0.6 fusion.60
  267.9 1.4 bitcast_dynamic-update-slice_fusion.2
  269.3 19.7 %custom-call.15 = f32[2,128,128]{1,2,0:T(8,128)S(1)} custom-call(f32[2,128,128]{2,1,0:T(8,128)S(1)} %get-tuple-element.10), custom_call_target="InvertDiagBlocksLowerTriangular" | custom-call | tf_op jit(solution)/shard_map/triangular_solve | solution.py:57
  289.0 1.1 fusion.25
  290.1 1.0 convolution_subtract_fusion
  291.1 1.1 fusion.43
  292.1 1.8 copy.48
  293.9 1.2 fusion.24
  (22 shorter events, 0.3 us)
Async XLA Ops:
  7.2 125.6 %all-gather.2.cloned.1.call-start = ((), (), s32[]{:S(2)}) async-start(), calls=%async_computation | async-start | bytes 3145728 | tf_op jit(solution)/shard_map/all_gather | solution.py:53
  8.5 12.5 %collective-permute-start = (bf16[128,2048]{0,1:T(8,128)(2,1)S(1)}, bf16[128,2048]{0,1:T(8,128)(2,1)S(1)}, u32[]{:S(2)}, u32[]{:S(2)}) collective-permute-start(bf16[128,2048]{0,1:T(8,128)(2,1)S(1)} %copy.30), channel_id=1, source_target_pairs={{0,2},{2,4},{4,6},{6,8},{8,10},{10,12},{12,14},{14,16},{16,18},{18... | collective-permute-start | bytes 1572872 | tf_op jit(solution)/shard_map/ppermute | solution.py:16
  9.0 12.0 %collective-permute-start.1 = (bf16[128,2048]{0,1:T(8,128)(2,1)S(1)}, bf16[128,2048]{0,1:T(8,128)(2,1)S(1)}, u32[]{:S(2)}, u32[]{:S(2)}) collective-permute-start(bf16[128,2048]{0,1:T(8,128)(2,1)S(1)} %copy.30), channel_id=1, source_target_pairs={{2,0},{4,2},{6,4},{8,6},{10,8},{12,10},{14,12},{16,14},{18,16},{20... | collective-permute-start | bytes 1572872 | tf_op jit(solution)/shard_map/ppermute | solution.py:19
  26.6 4.7 %copy-start.1 = (bf16[128,2048]{1,0:T(8,128)(2,1)S(1)}, bf16[128,2048]{1,0:T(8,128)(2,1)}, u32[]{:S(2)}) copy-start(bf16[128,2048]{1,0:T(8,128)(2,1)} %param.6) | copy-start | bytes 1572868
  33.4 11.5 %collective-permute-start.2 = (bf16[128,2048]{1,0:T(8,128)(2,1)S(1)}, bf16[128,2048]{1,0:T(8,128)(2,1)S(1)}, u32[]{:S(2)}, u32[]{:S(2)}) collective-permute-start(bf16[128,2048]{1,0:T(8,128)(2,1)S(1)} %fusion.20), channel_id=1, source_target_pairs={{0,2},{2,4},{4,6},{6,8},{8,10},{10,12},{12,14},{14,16},{16,18},{18... | collective-permute-start | bytes 1572872 | tf_op jit(solution)/shard_map/ppermute | solution.py:16
  38.3 6.7 %collective-permute-start.3 = (bf16[128,2048]{1,0:T(8,128)(2,1)S(1)}, bf16[128,2048]{1,0:T(8,128)(2,1)S(1)}, u32[]{:S(2)}, u32[]{:S(2)}) collective-permute-start(bf16[128,2048]{1,0:T(8,128)(2,1)S(1)} %fusion.20), channel_id=1, source_target_pairs={{2,0},{4,2},{6,4},{8,6},{10,8},{12,10},{14,12},{16,14},{18,16},{20... | collective-permute-start | bytes 1572872 | tf_op jit(solution)/shard_map/ppermute | solution.py:19
  63.0 11.7 %collective-permute-start.4 = (bf16[128,2048]{1,0:T(8,128)(2,1)S(1)}, bf16[128,2048]{1,0:T(8,128)(2,1)S(1)}, u32[]{:S(2)}, u32[]{:S(2)}) collective-permute-start(bf16[128,2048]{1,0:T(8,128)(2,1)S(1)} %fusion.21), channel_id=1, source_target_pairs={{0,2},{2,4},{4,6},{6,8},{8,10},{10,12},{12,14},{14,16},{16,18},{18... | collective-permute-start | bytes 1572872 | tf_op jit(solution)/shard_map/ppermute | solution.py:16
  68.2 6.7 %collective-permute-start.5 = (bf16[128,2048]{1,0:T(8,128)(2,1)S(1)}, bf16[128,2048]{1,0:T(8,128)(2,1)S(1)}, u32[]{:S(2)}, u32[]{:S(2)}) collective-permute-start(bf16[128,2048]{1,0:T(8,128)(2,1)S(1)} %fusion.21), channel_id=1, source_target_pairs={{2,0},{4,2},{6,4},{8,6},{10,8},{12,10},{14,12},{16,14},{18,16},{20... | collective-permute-start | bytes 1572872 | tf_op jit(solution)/shard_map/ppermute | solution.py:19
  91.7 134.8 %all-reduce.3.cloned.1.call-start = ((), (), s32[]{:S(2)}) async-start(), calls=%async_computation.1 | async-start | bytes 524288 | tf_op jit(solution)/shard_map/psum | solution.py:55
  137.6 151.4 %copy-start = (f32[256,2048]{1,0:T(8,128)S(1)}, f32[256,2048]{1,0:T(8,128)}, u32[]{:S(2)}) copy-start(f32[256,2048]{1,0:T(8,128)} %all-gather.2.cloned.1.call-done) | copy-start | bytes 6291460
Sparse Core Ops, SparseCore 0:
  91.8 40.9 all-gather.1
  137.7 88.6 all-reduce.2
where the time goes:
time: 303 us; the launch traced here: 302 us
  waiting for transfers between devices  149 us (49%)
  other arithmetic  66 us (22%)
  matrix products  28 us (9%)
  local copies, waits for them, and re-layouts  27 us (9%)
  starting transfers between devices  16 us (5%)
  between operations  15.6 us (5%)
    psum x1, waiting for transfers between devices, shards(): gram = lax.psum(partial_gram, 'space')  88.8 us
    all_gather x1, waiting for transfers between devices, shards(): columns = lax.all_gather(filtered, 'orb', axis=0, tiled=True)  40.9 us
    another operation x6, other arithmetic, shards(): lower = jnp.linalg.cholesky(gram)  34.1 us
    another operation x3, other arithmetic, shards(): lax.linalg.triangular_solve(lower, columns, left_side=True, lower=True)  20.8 us
    ppermute x3, waiting for transfers between devices, with_halo(): lax.ppermute(lax.slice_in_dim(block, block.shape[dim] - width, None, axis...  19.1 us
    dot_general x3, matrix products, apply_ham(): jnp.einsum('oefj,efij->oei', near, hamiltonian[:, 1:], preferred_element_...  14.5 us
    ppermute x3, starting transfers between devices, with_halo(): lax.ppermute(lax.slice_in_dim(block, block.shape[dim] - width, None, axis...  10.7 us
    gather x3, local copies, waits for them, and re-layouts, apply_ham(): jnp.take(blocks, located.reshape(-1), axis=1)  7.51 us
  transfers between devices with their start and end apart: 8, of which 7 were waited for; matrix products, arithmetic and copies ran while one was open for 0% of the time, Pallas kernels for 0%

commit v1 on v0

v1 whole, which is shorter than its diff:
```python
import functools

import jax
import jax.numpy as jnp
from jax import lax
from jax.experimental import pallas as pl
from jax.experimental.pallas import tpu as pltpu
from jax.sharding import PartitionSpec as P

centre = 0.25
radius = 0.75
SUB = 8


def vmem(count):
    return [pl.BlockSpec(memory_space=pltpu.VMEM)] * count


def dot_nt(a, b):
    return lax.dot_general(a, b, (((1,), (1,)), ((), ())), preferred_element_type=jnp.float32)


def dot_full(a, b, dims=((1,), (0,))):
    return lax.dot_general(
        a, b, (dims, ((), ())), precision=lax.Precision.HIGHEST, preferred_element_type=jnp.float32
    )


def split(a):
    high = a.astype(jnp.bfloat16)
    return high, (a - high.astype(jnp.float32)).astype(jnp.bfloat16)


def own_kernel(loc_ref, vec_ref, ham_ref, out_ref, buf, sems):
    count, _, width, _ = ham_ref.shape
    copies = []
    for e in range(count):
        copies.append(
            (
                pltpu.make_async_copy(ham_ref.at[e, 0:1], buf.at[e, 0:1], sems.at[e, 0]),
                pltpu.make_async_copy(ham_ref.at[e, 3:7], buf.at[e, 1:5], sems.at[e, 1]),
            )
        )
        for copy in copies[-1]:
            copy.start()
    for e in range(count):
        for copy in copies[e]:
            copy.wait()
        total = dot_nt(vec_ref[:, e * width : (e + 1) * width], buf[e, 0])
        for face in range(2, 6):
            start = pl.multiple_of(loc_ref[e, face] * width, width)
            total += dot_nt(vec_ref[:, pl.ds(start, width)], buf[e, face - 1])
        out_ref[:, e * width : (e + 1) * width] = total


def own_part(vec, hamiltonian, loc):
    count, _, width, _ = hamiltonian.shape
    owned = vec.shape[0]
    return pl.pallas_call(
        own_kernel,
        out_shape=jax.ShapeDtypeStruct(vec.shape, jnp.float32),
        in_specs=[pl.BlockSpec(memory_space=pltpu.SMEM)]
        + vmem(1)
        + [pl.BlockSpec(memory_space=pl.ANY)],
        out_specs=pl.BlockSpec(memory_space=pltpu.VMEM),
        scratch_shapes=[
            pltpu.VMEM((count, 5, width, width), jnp.bfloat16),
            pltpu.SemaphoreType.DMA((count, 2)),
        ],
        compiler_params=pltpu.CompilerParams(vmem_limit_bytes=24 << 20),
        cost_estimate=pl.CostEstimate(
            flops=2 * owned * count * width * width * 5,
            bytes_accessed=count * 5 * width * width * 2,
            transcendentals=0,
        ),
    )(loc, vec, hamiltonian)


def halo_kernel(level, loc_ref, low_ref, high_ref, acc_ref, vec_ref, prior_ref, ham_ref, *rest):
    outs, (buf, sems) = rest[:-2], rest[-2:]
    count, _, width, _ = ham_ref.shape
    copies = []
    for e in range(count):
        copies.append(pltpu.make_async_copy(ham_ref.at[e, 1:3], buf.at[e], sems.at[e]))
        copies[-1].start()
    for e in range(count):
        copies[e].wait()
        here = slice(e * width, (e + 1) * width)
        total = acc_ref[:, here]
        for face, ref in enumerate((low_ref, high_ref)):
            start = pl.multiple_of(loc_ref[e, face] * width, width)
            total += dot_nt(ref[:, pl.ds(start, width)], buf[e, face])
        shifted = (total - centre * vec_ref[:, here].astype(jnp.float32)) * (1.0 / radius)
        if level > 1:
            shifted = 2.0 * shifted - prior_ref[:, here].astype(jnp.float32)
        for out in outs:
            out[:, here] = shifted.astype(out.dtype)


def halo_part(level, low, high, acc, vec, prior, hamiltonian, loc):
    count, _, width, _ = hamiltonian.shape
    owned = vec.shape[0]
    kinds = [jnp.bfloat16] if level < 3 else [jnp.float32, jnp.bfloat16]
    out = pl.pallas_call(
        functools.partial(halo_kernel, level),
        out_shape=[jax.ShapeDtypeStruct(vec.shape, kind) for kind in kinds],
        in_specs=[pl.BlockSpec(memory_space=pltpu.SMEM)]
        + vmem(5)
        + [pl.BlockSpec(memory_space=pl.ANY)],
        out_specs=vmem(len(kinds)),
        scratch_shapes=[
            pltpu.VMEM((count, 2, width, width), jnp.bfloat16),
            pltpu.SemaphoreType.DMA((count,)),
        ],
        compiler_params=pltpu.CompilerParams(vmem_limit_bytes=24 << 20),
        cost_estimate=pl.CostEstimate(
            flops=2 * owned * count * width * width * 2,
            bytes_accessed=count * 2 * width * width * 2,
            transcendentals=0,
        ),
    )(loc, low, high, acc, vec, prior, hamiltonian)
    return out


def gram_kernel(place_ref, own_ref, other_ref, out_ref):
    def fill(first, second):
        out_ref[0] = dot_nt(first[...], first[...])
        out_ref[1] = dot_nt(first[...], second[...])
        out_ref[2] = dot_nt(second[...], second[...])

    @pl.when(place_ref[0] == 0)
    def _():
        fill(own_ref, other_ref)

    @pl.when(place_ref[0] != 0)
    def _():
        fill(other_ref, own_ref)


def factor_block(rows, right):
    strips = len(rows)
    shape = rows[0].shape
    sub = lax.broadcasted_iota(jnp.int32, shape, 0)
    upper, inverse = [], []
    for k in range(strips):
        strip, beside = rows[k], right[k]
        lanes = [jnp.broadcast_to(strip[:, k * SUB + j : k * SUB + j + 1], shape) for j in range(SUB)]
        entry = [
            [jnp.broadcast_to(lanes[j][i : i + 1, :], shape) if j <= i else None for j in range(SUB)]
            for i in range(SUB)
        ]
        low = [[None] * SUB for _ in range(SUB)]
        root = []
        for j in range(SUB):
            root.append(lax.rsqrt(entry[j][j]))
            for i in range(j + 1, SUB):
                low[i][j] = entry[i][j] * root[j]
            for i in range(j + 1, SUB):
                for t in range(j + 1, i + 1):
                    entry[i][t] = entry[i][t] - low[i][j] * low[t][j]
        inv = [[None] * SUB for _ in range(SUB)]
        for i in range(SUB):
            inv[i][i] = root[i]
            for j in range(i):
                total = low[i][j] * inv[j][j]
                for t in range(j + 1, i):
                    total = total + low[i][t] * inv[t][j]
                inv[i][j] = -root[i] * total

        def solve(source):
            wide = [jnp.broadcast_to(source[i : i + 1, :], shape) for i in range(SUB)]
            solved = []
            for i in range(SUB):
                total = inv[i][0] * wide[0]
                for j in range(1, i + 1):
                    total = total + inv[i][j] * wide[j]
                solved.append(total)
            back = []
            for i in range(SUB):
                total = inv[i][i] * solved[i]
                for j in range(i + 1, SUB):
                    total = total + inv[j][i] * solved[j]
                back.append(total)
            packed = solved[0]
            for i in range(1, SUB):
                packed = jnp.where(sub == i, solved[i], packed)
            return packed, back

        row_packed, row_back = solve(strip)
        inv_packed, inv_back = solve(beside)
        upper.append(row_packed)
        inverse.append(inv_packed)
        for r in range(k + 1, strips):
            for i in range(SUB):
                column = jnp.broadcast_to(rows[r][:, k * SUB + i : k * SUB + i + 1], shape)
                rows_r = row_back[i] * column
                right_r = inv_back[i] * column
                total = rows_r if i == 0 else total + rows_r
                beyond = right_r if i == 0 else beyond + right_r
            rows[r] = rows[r] - total
            right[r] = right[r] - beyond
    return upper, inverse


def factor_kernel(gram_ref, upper_ref, inv_ref, work, right):
    half = gram_ref.shape[1]
    strips = half // SUB
    row = lax.broadcasted_iota(jnp.int32, (half, half), 0)
    col = lax.broadcasted_iota(jnp.int32, (half, half), 1)

    def one(at):
        rows = [work[SUB * s : SUB * (s + 1), :] for s in range(strips)]
        eye = (row == col).astype(jnp.float32)
        beside = [eye[SUB * s : SUB * (s + 1), :] for s in range(strips)]
        upper, inverse = factor_block(rows, beside)
        for s in range(strips):
            work[SUB * s : SUB * (s + 1), :] = upper[s]
            right[SUB * s : SUB * (s + 1), :] = inverse[s]
        here = pl.ds(pl.multiple_of(at * half, half), half)
        upper_ref[here, here] = jnp.where(col >= row, work[...], 0.0)
        inv_ref[here, here] = jnp.where(col <= row, right[...], 0.0)

    work[...] = gram_ref[0]
    zero = jnp.zeros((half, half), jnp.float32)

    def body(at, carry):
        one(at)

        @pl.when(at == 0)
        def _():
            across = dot_full(inv_ref[0:half, 0:half], gram_ref[1])
            upper_ref[0:half, half:] = across
            work[...] = gram_ref[2] - dot_full(across, across, ((0,), (0,)))

        return carry

    lax.fori_loop(0, 2, body, 0)
    upper_ref[half:, 0:half] = zero
    inv_ref[0:half, half:] = zero
    between = dot_full(upper_ref[0:half, half:], inv_ref[0:half, 0:half], ((0,), (0,)))
    inv_ref[half:, 0:half] = -dot_full(inv_ref[half:, half:], between)


def factorize(gram):
    half = gram.shape[1]
    return pl.pallas_call(
        factor_kernel,
        out_shape=[jax.ShapeDtypeStruct((2 * half, 2 * half), jnp.float32)] * 2,
        in_specs=vmem(1),
        out_specs=vmem(2),
        scratch_shapes=[pltpu.VMEM((half, half), jnp.float32)] * 2,
        compiler_params=pltpu.CompilerParams(vmem_limit_bytes=24 << 20),
    )(gram)


def basis_kernel(place_ref, inv_ref, own_ref, other_ref, out_ref):
    half = own_ref.shape[0]
    place = place_ref[0]
    rows = pl.ds(pl.multiple_of(place * half, half), half)
    away = pl.ds(pl.multiple_of((1 - place) * half, half), half)
    near_high, near_low = split(inv_ref[rows, rows])
    far_high, far_low = split(inv_ref[rows, away])
    total = own_ref.shape[1]
    step = 512 if total % 512 == 0 else total
    for at in range(0, total, step):
        high, low = split(own_ref[:, at : at + step])
        other = other_ref[:, at : at + step]
        out_ref[:, at : at + step] = (
            jnp.dot(near_high, high, preferred_element_type=jnp.float32)
            + jnp.dot(near_high, low, preferred_element_type=jnp.float32)
            + jnp.dot(near_low, high, preferred_element_type=jnp.float32)
            + jnp.dot(far_high, other, preferred_element_type=jnp.float32)
            + jnp.dot(far_low, other, preferred_element_type=jnp.float32)
        )


def shards(hamiltonian, orbitals, adjacency):
    count = hamiltonian.shape[0]
    owned = orbitals.shape[0]
    blocks = lax.axis_size("space")
    groups = lax.axis_size("orb")
    half = owned * groups // 2
    loc = adjacency % count
    forward = [(i, (i + 1) % blocks) for i in range(blocks)]
    backward = [(target, source) for source, target in forward]

    def apply_level(level, vec, prior):
        low = lax.ppermute(vec, "space", forward)
        high = lax.ppermute(vec, "space", backward)
        acc = own_part(vec, hamiltonian, loc)
        return halo_part(level, low, high, acc, vec, prior, hamiltonian, loc)

    (level_one,) = apply_level(1, orbitals, orbitals)
    (level_two,) = apply_level(2, level_one, orbitals)
    filtered, narrow = apply_level(3, level_two, level_one)

    place = lax.axis_index("orb").astype(jnp.int32).reshape(1)
    if groups == 2:
        other = lax.ppermute(narrow, "orb", [(0, 1), (1, 0)])
        gram = pl.pallas_call(
            gram_kernel,
            out_shape=jax.ShapeDtypeStruct((3, half, half), jnp.float32),
            in_specs=[pl.BlockSpec(memory_space=pltpu.SMEM)] + vmem(2),
            out_specs=pl.BlockSpec(memory_space=pltpu.VMEM),
            compiler_params=pltpu.CompilerParams(vmem_limit_bytes=24 << 20),
        )(place, narrow, other)
    else:
        columns = lax.all_gather(narrow, "orb", axis=0, tiled=True)
        whole = dot_nt(columns, columns)
        gram = jnp.stack([whole[:half, :half], whole[:half, half:], whole[half:, half:]])
    step = 1
    while step < blocks:
        gram = gram + lax.ppermute(gram, "space", [(i, i ^ step) for i in range(blocks)])
        step *= 2
    upper, inverse = factorize(gram)
    if groups == 2:
        basis = pl.pallas_call(
            basis_kernel,
            out_shape=jax.ShapeDtypeStruct(filtered.shape, jnp.float32),
            in_specs=[pl.BlockSpec(memory_space=pltpu.SMEM)] + vmem(3),
            out_specs=pl.BlockSpec(memory_space=pltpu.VMEM),
            compiler_params=pltpu.CompilerParams(vmem_limit_bytes=24 << 20),
        )(place, inverse, filtered, other)
    else:
        mine = lax.dynamic_slice_in_dim(inverse, place[0] * owned, owned, 0)
        near = lax.dynamic_slice_in_dim(mine, place[0] * owned, owned, 1)
        rest = filtered - narrow.astype(jnp.float32)
        basis = dot_full(mine, columns.astype(jnp.float32)) + dot_full(near, rest)
    return (basis, upper)


def solution(mesh):
    in_specs = (P("space", None, None, None), P("orb", "space"), P("space", None))
    out_specs = (P("orb", "space"), P())
    return jax.shard_map(shards, mesh=mesh, in_specs=in_specs, out_specs=out_specs, check_vma=False)
```

time: 303 us -> 104 us (0.34)
  waiting for transfers between devices: 149 us -> 30.5 us
  other arithmetic: 66 us -> 0.79 us
  Pallas kernels: 0 us -> 42.1 us
  matrix products: 28 us -> 0 us
  local copies, waits for them, and re-layouts: 27 us -> 4.14 us
  between operations: 15.6 us -> 0.74 us
  starting transfers between devices: 16 us -> 25.4 us
    psum x1 -> x0, waiting for transfers between devices: 88.8 us -> none  [shards(): gram = lax.psum(partial_gram, 'space')]
    another operation x9 -> x0, other arithmetic: 54.9 us -> none  [the longest x6 34.1 us: shards(): lower = jnp.linalg.cholesky(gram)]
    pallas_call x0 -> x9, Pallas kernels: none -> 42.1 us  [the longest x3 19.1 us: own_part(): pl.pallas_call(own_kernel, out_shape=jax.ShapeDtypeStruct(vec.shape, jnp....]
    all_gather x1 -> x0, waiting for transfers between devices: 40.9 us -> none  [shards(): columns = lax.all_gather(filtered, 'orb', axis=0, tiled=True)]
    dot_general x7 -> x0, matrix products: 24.4 us -> none  [the longest x3 14.5 us: apply_ham(): jnp.einsum('oefj,efij->oei', near, hamiltonian[:, 1:], preferred_element_...]
    ppermute x6 -> x11, waiting for transfers between devices: 19.5 us -> 30.5 us  [the longest x4 21 us: shards(): lax.ppermute(gram, 'space', [(i, i ^ step) for i in range(blocks)])]
    ppermute x6 -> x11, starting transfers between devices: 15.8 us -> 25.4 us  [the longest x3 9.59 us: apply_level(): high = lax.ppermute(vec, 'space', backward)]
    gather x3 -> x0, local copies, waits for them, and re-layouts: 7.51 us -> none  [apply_ham(): jnp.take(blocks, located.reshape(-1), axis=1)]
  transfers between devices with their start and end apart: 8 -> 11, of which waited for: 7 -> 7; matrix products, arithmetic and copies ran while one was open for 0% -> 1% of each run, Pallas kernels for 0% -> 18%
where the time goes in v1:
time: 104 us
  Pallas kernels  42.1 us (40%)
  waiting for transfers between devices  30.5 us (29%)
  starting transfers between devices  25.4 us (24%)
  local copies, waits for them, and re-layouts  4.14 us (4%)
    ppermute x4, waiting for transfers between devices, shards(): lax.ppermute(gram, 'space', [(i, i ^ step) for i in range(blocks)])  21 us
    pallas_call x3, Pallas kernels, own_part(): pl.pallas_call(own_kernel, out_shape=jax.ShapeDtypeStruct(vec.shape, jnp....  19.1 us
    pallas_call x1, Pallas kernels, factorize(): pl.pallas_call(factor_kernel, out_shape=[jax.ShapeDtypeStruct((2 * half,...  11 us
    ppermute x3, starting transfers between devices, apply_level(): high = lax.ppermute(vec, 'space', backward)  9.59 us
    pallas_call x3, Pallas kernels, halo_part(): pl.pallas_call(functools.partial(halo_kernel, level), out_shape=[jax.Shap...  9.48 us
    ppermute x4, starting transfers between devices, shards(): lax.ppermute(gram, 'space', [(i, i ^ step) for i in range(blocks)])  8.85 us
    ppermute x1, waiting for transfers between devices, shards(): other = lax.ppermute(narrow, 'orb', [(0, 1), (1, 0)])  8.37 us
    ppermute x3, starting transfers between devices, apply_level(): low = lax.ppermute(vec, 'space', forward)  5.03 us
  transfers between devices with their start and end apart: 11, of which 7 were waited for; matrix products, arithmetic and copies ran while one was open for 1% of the time, Pallas kernels for 18%

profile of v1, /device:TPU:0, one launch (start us, length us, event | category | flops | bytes accessed | tf_op | source)
XLA Modules:
  0.0 103.6 jit_solution(7361380067451078554)
XLA Ops:
  0.6 0.5 collective-permute-start
  1.1 5.1 %collective-permute-start.1 = (bf16[128,2048]{1,0:T(8,128)(2,1)}, bf16[128,2048]{1,0:T(8,128)(2,1)S(1)}, u32[]{:S(2)}, u32[]{:S(2)}) collective-permute-start(bf16[128,2048]{1,0:T(8,128)(2,1)} %prior_ref.3), channel_id=1, source_target_pairs={{2,0},{4,2},{6,4},{8,6},{10,8},{12,10},{14,12},{16,14},{18,16},{20... | collective-permute-start | bytes 1572872 | tf_op jit(solution)/shard_map/ppermute | solution.py:289
  6.2 0.7 add_select_fusion.loc_ref
  6.9 0.0 copy-start
  6.9 3.1 %copy-done = bf16[8,7,256,256]{3,2,1,0:T(8,128)(2,1)S(1)} copy-done((bf16[8,7,256,256]{3,2,1,0:T(8,128)(2,1)S(1)}, bf16[8,7,256,256]{3,2,1,0:T(8,128)(2,1)}, u32[]{:S(2)}) %copy-start) | copy-done | bytes 7340056
  10.0 0.0 copy-start.1
  10.0 1.0 %copy-done.1 = bf16[128,2048]{1,0:T(8,128)(2,1)S(1)} copy-done((bf16[128,2048]{1,0:T(8,128)(2,1)S(1)}, bf16[128,2048]{1,0:T(8,128)(2,1)}, u32[]{:S(2)}) %copy-start.1) | copy-done | bytes 524312
  11.0 0.0 slice-start
  11.0 6.4 %shard_map.50.acc_ref = f32[128,2048]{1,0:T(8,128)S(1)} custom-call(s32[8,6]{1,0:T(8,128)S(1)} %add_select_fusion.loc_ref, bf16[128,2048]{1,0:T(8,128)(2,1)S(1)} %copy-done.1, bf16[8,7,256,256]{3,2,1,0:T(8,128)(2,1)S(1)} %copy-done), custom_call_target="tpu_custom_call" | custom-call | flops 671088640 | bytes 5242880 | tf_op jit(solution)/shard_map/pallas_call | solution.py:59
  17.4 0.0 slice-start.1
  17.4 0.0 collective-permute-done.low_ref
  17.4 0.0 collective-permute-done.1.high_ref
  17.4 3.1 %shard_map.51.vec_ref.prior_ref = bf16[128,2048]{1,0:T(8,128)(2,1)S(1)} custom-call(s32[8,6]{1,0:T(8,128)S(1)} %add_select_fusion.loc_ref, bf16[128,2048]{1,0:T(8,128)(2,1)S(1)} %collective-permute-done.low_ref, bf16[128,2048]{1,0:T(8,128)(2,1)S(1)} %collective-permute-done.1.high_ref, f32[128,2048]{1,0:T(8,128)S(1)} %shard_map.50.acc_ref, ...), custom_call_target="tpu_custom_call" | custom-call | flops 268435456 | bytes 2097152 | tf_op jit(solution)/shard_map/pallas_call | solution.py:104
  20.6 0.8 collective-permute-start.2
  21.4 3.7 %collective-permute-start.3 = (bf16[128,2048]{1,0:T(8,128)(2,1)S(1)}, bf16[128,2048]{1,0:T(8,128)(2,1)S(1)}, u32[]{:S(2)}, u32[]{:S(2)}) collective-permute-start(bf16[128,2048]{1,0:T(8,128)(2,1)S(1)} %shard_map.51.vec_ref.prior_ref), channel_id=1, source_target_pairs={{2,0},{4,2},{6,4},{8,6},{10,8},{12,10},{14,12},{16,14},{18,16},{20... | collective-permute-start | bytes 1572872 | tf_op jit(solution)/shard_map/ppermute | solution.py:289
  25.1 0.0 slice-done
  25.1 0.0 slice-done.1
  25.1 6.4 %shard_map.52.acc_ref = f32[128,2048]{1,0:T(8,128)S(1)} custom-call(s32[8,6]{1,0:T(8,128)S(1)} %add_select_fusion.loc_ref, bf16[128,2048]{1,0:T(8,128)(2,1)S(1)} %shard_map.51.vec_ref.prior_ref, bf16[8,7,256,256]{3,2,1,0:T(8,128)(2,1)S(1)} %bitcast.2), custom_call_target="tpu_custom_call" | custom-call | flops 671088640 | bytes 5242880 | tf_op jit(solution)/shard_map/pallas_call | solution.py:59
  31.5 0.6 collective-permute-done.2.low_ref
  32.0 0.0 collective-permute-done.3.high_ref
  32.0 3.2 %shard_map.53.vec_ref = bf16[128,2048]{1,0:T(8,128)(2,1)S(1)} custom-call(s32[8,6]{1,0:T(8,128)S(1)} %add_select_fusion.loc_ref, bf16[128,2048]{1,0:T(8,128)(2,1)S(1)} %collective-permute-done.2.low_ref, bf16[128,2048]{1,0:T(8,128)(2,1)S(1)} %collective-permute-done.3.high_ref, f32[128,2048]{1,0:T(8,128)S(1)} %shard_map.52.acc_ref, ...), custom_call_target="tpu_custom_call" | custom-call | flops 268435456 | bytes 2097152 | tf_op jit(solution)/shard_map/pallas_call | solution.py:104
  35.2 3.7 %collective-permute-start.4 = (bf16[128,2048]{1,0:T(8,128)(2,1)S(1)}, bf16[128,2048]{1,0:T(8,128)(2,1)S(1)}, u32[]{:S(2)}, u32[]{:S(2)}) collective-permute-start(bf16[128,2048]{1,0:T(8,128)(2,1)S(1)} %shard_map.53.vec_ref), channel_id=1, source_target_pairs={{0,2},{2,4},{4,6},{6,8},{8,10},{10,12},{12,14},{14,16},{16,18},{18... | collective-permute-start | bytes 1572872 | tf_op jit(solution)/shard_map/ppermute | solution.py:288
  38.9 0.9 collective-permute-start.5
  39.8 6.4 %shard_map.54.acc_ref = f32[128,2048]{1,0:T(8,128)S(1)} custom-call(s32[8,6]{1,0:T(8,128)S(1)} %add_select_fusion.loc_ref, bf16[128,2048]{1,0:T(8,128)(2,1)S(1)} %shard_map.53.vec_ref, bf16[8,7,256,256]{3,2,1,0:T(8,128)(2,1)S(1)} %bitcast.2), custom_call_target="tpu_custom_call" | custom-call | flops 671088640 | bytes 5242880 | tf_op jit(solution)/shard_map/pallas_call | solution.py:59
  46.2 0.5 collective-permute-done.4.low_ref
  46.7 0.0 collective-permute-done.5.high_ref
  46.7 3.2 %shard_map.55 = (f32[128,2048]{1,0:T(8,128)S(1)}, bf16[128,2048]{1,0:T(8,128)(2,1)S(1)}) custom-call(s32[8,6]{1,0:T(8,128)S(1)} %add_select_fusion.loc_ref, bf16[128,2048]{1,0:T(8,128)(2,1)S(1)} %collective-permute-done.4.low_ref, bf16[128,2048]{1,0:T(8,128)(2,1)S(1)} %collective-permute-done.5.high_ref, f32[128,2048]{1,0:T(8,128)S(1)} %shard_map.54.acc_ref, ...), custom_call_target="tpu_custom_call" | custom-call | flops 268435456 | bytes 2097152 | tf_op jit(solution)/shard_map/pallas_call | solution.py:104
  49.9 1.9 %collective-permute-start.6 = (bf16[128,2048]{1,0:T(8,128)(2,1)S(1)}, bf16[128,2048]{1,0:T(8,128)(2,1)S(1)}, u32[]{:S(2)}, u32[]{:S(2)}) collective-permute-start(bf16[128,2048]{1,0:T(8,128)(2,1)S(1)} %get-tuple-element.6.own_ref), channel_id=1, source_target_pairs={{0,1},{1,0},{2,3},{3,2},{4,5},{5,4},{6,7},{7,6},{8,9},{9,8},{10,11... | collective-permute-start | bytes 1572872 | tf_op jit(solution)/shard_map/ppermute | solution.py:299
  51.8 8.4 %collective-permute-done.6.other_ref = bf16[128,2048]{1,0:T(8,128)(2,1)S(1)} collective-permute-done((bf16[128,2048]{1,0:T(8,128)(2,1)S(1)}, bf16[128,2048]{1,0:T(8,128)(2,1)S(1)}, u32[]{:S(2)}, u32[]{:S(2)}) %collective-permute-start.6) | collective-permute-done | bytes 524320 | tf_op jit(solution)/shard_map/ppermute | solution.py:299
  60.2 0.8 shard_map.56
  60.9 4.4 %collective-permute-start.7 = (f32[3,128,128]{2,1,0:T(8,128)S(1)}, f32[3,128,128]{2,1,0:T(8,128)S(1)}, u32[]{:S(2)}, u32[]{:S(2)}) collective-permute-start(f32[3,128,128]{2,1,0:T(8,128)S(1)} %shard_map.56), channel_id=1, source_target_pairs={{0,2},{2,0},{4,6},{6,4},{8,10},{10,8},{12,14},{14,12},{16,18},{18,... | collective-permute-start | bytes 589832 | tf_op jit(solution)/shard_map/ppermute | solution.py:313
  65.4 1.1 %collective-permute-done.7 = f32[3,128,128]{2,1,0:T(8,128)S(1)} collective-permute-done((f32[3,128,128]{2,1,0:T(8,128)S(1)}, f32[3,128,128]{2,1,0:T(8,128)S(1)}, u32[]{:S(2)}, u32[]{:S(2)}) %collective-permute-start.7) | collective-permute-done | bytes 196640 | tf_op jit(solution)/shard_map/ppermute | solution.py:313
  66.5 1.3 %collective-permute-start.8 = (f32[3,128,128]{2,1,0:T(8,128)S(1)}, f32[3,128,128]{2,1,0:T(8,128)S(1)}, u32[]{:S(2)}, u32[]{:S(2)}) collective-permute-start(f32[3,128,128]{2,1,0:T(8,128)S(1)} %add.19), channel_id=1, source_target_pairs={{0,4},{2,6},{4,0},{6,2},{8,12},{10,14},{12,8},{14,10},{16,20},{18,... | collective-permute-start | bytes 589832 | tf_op jit(solution)/shard_map/ppermute | solution.py:313
  67.8 5.9 %collective-permute-done.8 = f32[3,128,128]{2,1,0:T(8,128)S(1)} collective-permute-done((f32[3,128,128]{2,1,0:T(8,128)S(1)}, f32[3,128,128]{2,1,0:T(8,128)S(1)}, u32[]{:S(2)}, u32[]{:S(2)}) %collective-permute-start.8) | collective-permute-done | bytes 196640 | tf_op jit(solution)/shard_map/ppermute | solution.py:313
  73.7 0.9 collective-permute-start.9
  74.6 5.5 %collective-permute-done.9 = f32[3,128,128]{2,1,0:T(8,128)S(1)} collective-permute-done((f32[3,128,128]{2,1,0:T(8,128)S(1)}, f32[3,128,128]{2,1,0:T(8,128)S(1)}, u32[]{:S(2)}, u32[]{:S(2)}) %collective-permute-start.9) | collective-permute-done | bytes 196640 | tf_op jit(solution)/shard_map/ppermute | solution.py:313
  80.2 2.2 %collective-permute-start.10 = (f32[3,128,128]{2,1,0:T(8,128)S(1)}, f32[3,128,128]{2,1,0:T(8,128)S(1)}, u32[]{:S(2)}, u32[]{:S(2)}) collective-permute-start(f32[3,128,128]{2,1,0:T(8,128)S(1)} %add.21), channel_id=1, source_target_pairs={{0,16},{2,18},{4,20},{6,22},{8,24},{10,26},{12,28},{14,30},{16,0},... | collective-permute-start | bytes 589832 | tf_op jit(solution)/shard_map/ppermute | solution.py:313
  82.4 8.5 %collective-permute-done.10 = f32[3,128,128]{2,1,0:T(8,128)S(1)} collective-permute-done((f32[3,128,128]{2,1,0:T(8,128)S(1)}, f32[3,128,128]{2,1,0:T(8,128)S(1)}, u32[]{:S(2)}, u32[]{:S(2)}) %collective-permute-start.10) | collective-permute-done | bytes 196640 | tf_op jit(solution)/shard_map/ppermute | solution.py:313
  90.8 11.0 %shard_map.57 = (f32[256,256]{1,0:T(8,128)}, f32[256,256]{1,0:T(8,128)S(1)}) custom-call(f32[3,128,128]{2,1,0:T(8,128)S(1)} %add.22.gram_ref), custom_call_target="tpu_custom_call" | custom-call | tf_op jit(solution)/shard_map/pallas_call | solution.py:246
  101.8 1.8 %shard_map.58 = f32[128,2048]{1,0:T(8,128)} custom-call(s32[1]{0:T(128)} %bitcast.place_ref, f32[256,256]{1,0:T(8,128)S(1)} %get-tuple-element.7.inv_ref, f32[128,2048]{1,0:T(8,128)S(1)} %get-tuple-element.8.own_ref, bf16[128,2048]{1,0:T(8,128)(2,1)S(1)} %collective-permute-done.6.other_ref), custom_call_target="tpu_custom_call" | custom-call | tf_op jit(solution)/shard_map/pallas_call | solution.py:317
  (5 shorter events, 0.1 us)
Async XLA Ops:
  0.6 16.8 %collective-permute-start = (bf16[128,2048]{1,0:T(8,128)(2,1)}, bf16[128,2048]{1,0:T(8,128)(2,1)S(1)}, u32[]{:S(2)}, u32[]{:S(2)}) collective-permute-start(bf16[128,2048]{1,0:T(8,128)(2,1)} %prior_ref.3), channel_id=1, source_target_pairs={{0,2},{2,4},{4,6},{6,8},{8,10},{10,12},{12,14},{14,16},{16,18},{18... | collective-permute-start | bytes 1572872 | tf_op jit(solution)/shard_map/ppermute | solution.py:288
  1.1 16.3 %collective-permute-start.1 = (bf16[128,2048]{1,0:T(8,128)(2,1)}, bf16[128,2048]{1,0:T(8,128)(2,1)S(1)}, u32[]{:S(2)}, u32[]{:S(2)}) collective-permute-start(bf16[128,2048]{1,0:T(8,128)(2,1)} %prior_ref.3), channel_id=1, source_target_pairs={{2,0},{4,2},{6,4},{8,6},{10,8},{12,10},{14,12},{16,14},{18,16},{20... | collective-permute-start | bytes 1572872 | tf_op jit(solution)/shard_map/ppermute | solution.py:289
  6.9 3.1 %copy-start = (bf16[8,7,256,256]{3,2,1,0:T(8,128)(2,1)S(1)}, bf16[8,7,256,256]{3,2,1,0:T(8,128)(2,1)}, u32[]{:S(2)}) copy-start(bf16[8,7,256,256]{3,2,1,0:T(8,128)(2,1)} %ham_ref.11) | copy-start | bytes 22020100
  10.0 1.0 %copy-start.1 = (bf16[128,2048]{1,0:T(8,128)(2,1)S(1)}, bf16[128,2048]{1,0:T(8,128)(2,1)}, u32[]{:S(2)}) copy-start(bf16[128,2048]{1,0:T(8,128)(2,1)} %prior_ref.3) | copy-start | bytes 1572868
  11.0 14.1 %slice-start = ((s8[7340032]{0:T(1024)(128)(4,1)}), s8[4194304]{0:T(1024)(128)(4,1)S(1)}, s32[]{:S(2)}) async-start(s8[7340032]{0:T(1024)(128)(4,1)} %bitcast.1), calls=%async_computation | async-start | bytes 8388608
  17.4 7.7 %slice-start.1 = ((s8[7340032]{0:T(1024)(128)(4,1)}), s8[3145728]{0:T(1024)(128)(4,1)S(1)}, s32[]{:S(2)}) async-start(s8[7340032]{0:T(1024)(128)(4,1)} %bitcast.1), calls=%async_computation.1 | async-start | bytes 6291456
  20.6 11.5 %collective-permute-start.2 = (bf16[128,2048]{1,0:T(8,128)(2,1)S(1)}, bf16[128,2048]{1,0:T(8,128)(2,1)S(1)}, u32[]{:S(2)}, u32[]{:S(2)}) collective-permute-start(bf16[128,2048]{1,0:T(8,128)(2,1)S(1)} %shard_map.51.vec_ref.prior_ref), channel_id=1, source_target_pairs={{0,2},{2,4},{4,6},{6,8},{8,10},{10,12},{12,14},{14,16},{16,18},{18... | collective-permute-start | bytes 1572872 | tf_op jit(solution)/shard_map/ppermute | solution.py:288
  21.4 10.6 %collective-permute-start.3 = (bf16[128,2048]{1,0:T(8,128)(2,1)S(1)}, bf16[128,2048]{1,0:T(8,128)(2,1)S(1)}, u32[]{:S(2)}, u32[]{:S(2)}) collective-permute-start(bf16[128,2048]{1,0:T(8,128)(2,1)S(1)} %shard_map.51.vec_ref.prior_ref), channel_id=1, source_target_pairs={{2,0},{4,2},{6,4},{8,6},{10,8},{12,10},{14,12},{16,14},{18,16},{20... | collective-permute-start | bytes 1572872 | tf_op jit(solution)/shard_map/ppermute | solution.py:289
  35.2 11.5 %collective-permute-start.4 = (bf16[128,2048]{1,0:T(8,128)(2,1)S(1)}, bf16[128,2048]{1,0:T(8,128)(2,1)S(1)}, u32[]{:S(2)}, u32[]{:S(2)}) collective-permute-start(bf16[128,2048]{1,0:T(8,128)(2,1)S(1)} %shard_map.53.vec_ref), channel_id=1, source_target_pairs={{0,2},{2,4},{4,6},{6,8},{8,10},{10,12},{12,14},{14,16},{16,18},{18... | collective-permute-start | bytes 1572872 | tf_op jit(solution)/shard_map/ppermute | solution.py:288
  38.9 7.8 %collective-permute-start.5 = (bf16[128,2048]{1,0:T(8,128)(2,1)S(1)}, bf16[128,2048]{1,0:T(8,128)(2,1)S(1)}, u32[]{:S(2)}, u32[]{:S(2)}) collective-permute-start(bf16[128,2048]{1,0:T(8,128)(2,1)S(1)} %shard_map.53.vec_ref), channel_id=1, source_target_pairs={{2,0},{4,2},{6,4},{8,6},{10,8},{12,10},{14,12},{16,14},{18,16},{20... | collective-permute-start | bytes 1572872 | tf_op jit(solution)/shard_map/ppermute | solution.py:289
  49.9 10.3 %collective-permute-start.6 = (bf16[128,2048]{1,0:T(8,128)(2,1)S(1)}, bf16[128,2048]{1,0:T(8,128)(2,1)S(1)}, u32[]{:S(2)}, u32[]{:S(2)}) collective-permute-start(bf16[128,2048]{1,0:T(8,128)(2,1)S(1)} %get-tuple-element.6.own_ref), channel_id=1, source_target_pairs={{0,1},{1,0},{2,3},{3,2},{4,5},{5,4},{6,7},{7,6},{8,9},{9,8},{10,11... | collective-permute-start | bytes 1572872 | tf_op jit(solution)/shard_map/ppermute | solution.py:299
  60.9 5.5 %collective-permute-start.7 = (f32[3,128,128]{2,1,0:T(8,128)S(1)}, f32[3,128,128]{2,1,0:T(8,128)S(1)}, u32[]{:S(2)}, u32[]{:S(2)}) collective-permute-start(f32[3,128,128]{2,1,0:T(8,128)S(1)} %shard_map.56), channel_id=1, source_target_pairs={{0,2},{2,0},{4,6},{6,4},{8,10},{10,8},{12,14},{14,12},{16,18},{18,... | collective-permute-start | bytes 589832 | tf_op jit(solution)/shard_map/ppermute | solution.py:313
  66.5 7.2 %collective-permute-start.8 = (f32[3,128,128]{2,1,0:T(8,128)S(1)}, f32[3,128,128]{2,1,0:T(8,128)S(1)}, u32[]{:S(2)}, u32[]{:S(2)}) collective-permute-start(f32[3,128,128]{2,1,0:T(8,128)S(1)} %add.19), channel_id=1, source_target_pairs={{0,4},{2,6},{4,0},{6,2},{8,12},{10,14},{12,8},{14,10},{16,20},{18,... | collective-permute-start | bytes 589832 | tf_op jit(solution)/shard_map/ppermute | solution.py:313
  73.7 6.4 %collective-permute-start.9 = (f32[3,128,128]{2,1,0:T(8,128)S(1)}, f32[3,128,128]{2,1,0:T(8,128)S(1)}, u32[]{:S(2)}, u32[]{:S(2)}) collective-permute-start(f32[3,128,128]{2,1,0:T(8,128)S(1)} %add.20), channel_id=1, source_target_pairs={{0,8},{2,10},{4,12},{6,14},{8,0},{10,2},{12,4},{14,6},{16,24},{18,... | collective-permute-start | bytes 589832 | tf_op jit(solution)/shard_map/ppermute | solution.py:313
  80.2 10.6 %collective-permute-start.10 = (f32[3,128,128]{2,1,0:T(8,128)S(1)}, f32[3,128,128]{2,1,0:T(8,128)S(1)}, u32[]{:S(2)}, u32[]{:S(2)}) collective-permute-start(f32[3,128,128]{2,1,0:T(8,128)S(1)} %add.21), channel_id=1, source_target_pairs={{0,16},{2,18},{4,20},{6,22},{8,24},{10,26},{12,28},{14,30},{16,0},... | collective-permute-start | bytes 589832 | tf_op jit(solution)/shard_map/ppermute | solution.py:313

commit v2 on v1

--- a/solution.py
+++ b/solution.py
@@ -31,65 +31,82 @@
     return high, (a - high.astype(jnp.float32)).astype(jnp.bfloat16)
 
 
-def own_kernel(loc_ref, vec_ref, ham_ref, out_ref, buf, sems):
-    count, _, width, _ = ham_ref.shape
-    copies = []
+def turn_kernel(loc_ref, vec_ref, ham_ref, turned_ref, *outs):
+    count, faces, width, _ = ham_ref.shape
+    rows = outs[0].shape[0]
     for e in range(count):
-        copies.append(
-            (
-                pltpu.make_async_copy(ham_ref.at[e, 0:1], buf.at[e, 0:1], sems.at[e, 0]),
-                pltpu.make_async_copy(ham_ref.at[e, 3:7], buf.at[e, 1:5], sems.at[e, 1]),
+        here = slice(e * width, (e + 1) * width)
+        total = None
+        for face in range(faces):
+            turned = ham_ref[e, face].T
+            turned_ref[e, face] = turned
+            if face == 1 or face == 2:
+                continue
+            at = here if face == 0 else pl.ds(pl.multiple_of(loc_ref[e, face - 1] * width, width), width)
+            part = jnp.dot(vec_ref[:, at], turned, preferred_element_type=jnp.float32)
+            total = part if total is None else total + part
+        for piece, out in enumerate(outs):
+            out[:, here] = total[piece * rows : (piece + 1) * rows]
+
+
+def turn_part(vec, hamiltonian, loc, chunks):
+    count, faces, width, _ = hamiltonian.shape
+    owned = vec.shape[0]
+    share = jax.ShapeDtypeStruct((owned // chunks, vec.shape[1]), jnp.float32)
+    return pl.pallas_call(
+        turn_kernel,
+        out_shape=[jax.ShapeDtypeStruct(hamiltonian.shape, hamiltonian.dtype)] + [share] * chunks,
+        in_specs=[pl.BlockSpec(memory_space=pltpu.SMEM)] + vmem(2),
+        out_specs=vmem(1 + chunks),
+        compiler_params=pltpu.CompilerParams(vmem_limit_bytes=32 << 20),
+        cost_estimate=pl.CostEstimate(
+            flops=2 * owned * count * width * width * 5,
+            bytes_accessed=count * faces * width * width * 4,
+            transcendentals=0,
+        ),
+    )(loc, vec, hamiltonian)
+
+
+def own_kernel(loc_ref, vec_ref, turned_ref, out_ref):
+    count, _, width, _ = turned_ref.shape
+    for e in range(count):
+        here = slice(e * width, (e + 1) * width)
+        total = jnp.dot(vec_ref[:, here], turned_ref[e, 0], preferred_element_type=jnp.float32)
+        for face in range(2, 6):
+            at = pl.ds(pl.multiple_of(loc_ref[e, face] * width, width), width)
+            total += jnp.dot(
+                vec_ref[:, at], turned_ref[e, face + 1], preferred_element_type=jnp.float32
             )
-        )
-        for copy in copies[-1]:
-            copy.start()
-    for e in range(count):
-        for copy in copies[e]:
-            copy.wait()
-        total = dot_nt(vec_ref[:, e * width : (e + 1) * width], buf[e, 0])
-        for face in range(2, 6):
-            start = pl.multiple_of(loc_ref[e, face] * width, width)
-            total += dot_nt(vec_ref[:, pl.ds(start, width)], buf[e, face - 1])
-        out_ref[:, e * width : (e + 1) * width] = total
-
-
-def own_part(vec, hamiltonian, loc):
-    count, _, width, _ = hamiltonian.shape
+        out_ref[:, here] = total
+
+
+def own_part(vec, turned, loc):
+    count, _, width, _ = turned.shape
     owned = vec.shape[0]
     return pl.pallas_call(
         own_kernel,
         out_shape=jax.ShapeDtypeStruct(vec.shape, jnp.float32),
-        in_specs=[pl.BlockSpec(memory_space=pltpu.SMEM)]
-        + vmem(1)
-        + [pl.BlockSpec(memory_space=pl.ANY)],
+        in_specs=[pl.BlockSpec(memory_space=pltpu.SMEM)] + vmem(2),
         out_specs=pl.BlockSpec(memory_space=pltpu.VMEM),
-        scratch_shapes=[
-            pltpu.VMEM((count, 5, width, width), jnp.bfloat16),
-            pltpu.SemaphoreType.DMA((count, 2)),
-        ],
         compiler_params=pltpu.CompilerParams(vmem_limit_bytes=24 << 20),
         cost_estimate=pl.CostEstimate(
             flops=2 * owned * count * width * width * 5,
             bytes_accessed=count * 5 * width * width * 2,
             transcendentals=0,
         ),
-    )(loc, vec, hamiltonian)
-
-
-def halo_kernel(level, loc_ref, low_ref, high_ref, acc_ref, vec_ref, prior_ref, ham_ref, *rest):
-    outs, (buf, sems) = rest[:-2], rest[-2:]
-    count, _, width, _ = ham_ref.shape
-    copies = []
+    )(loc, vec, turned)
+
+
+def halo_kernel(level, loc_ref, low_ref, high_ref, acc_ref, vec_ref, prior_ref, turned_ref, *outs):
+    count, _, width, _ = turned_ref.shape
     for e in range(count):
-        copies.append(pltpu.make_async_copy(ham_ref.at[e, 1:3], buf.at[e], sems.at[e]))
-        copies[-1].start()
-    for e in range(count):
-        copies[e].wait()
         here = slice(e * width, (e + 1) * width)
         total = acc_ref[:, here]
         for face, ref in enumerate((low_ref, high_ref)):
-            start = pl.multiple_of(loc_ref[e, face] * width, width)
-            total += dot_nt(ref[:, pl.ds(start, width)], buf[e, face])
+            at = pl.ds(pl.multiple_of(loc_ref[e, face] * width, width), width)
+            total += jnp.dot(
+                ref[:, at], turned_ref[e, face + 1], preferred_element_type=jnp.float32
+            )
         shifted = (total - centre * vec_ref[:, here].astype(jnp.float32)) * (1.0 / radius)
         if level > 1:
             shifted = 2.0 * shifted - prior_ref[:, here].astype(jnp.float32)
@@ -97,44 +114,45 @@
             out[:, here] = shifted.astype(out.dtype)
 
 
-def halo_part(level, low, high, acc, vec, prior, hamiltonian, loc):
-    count, _, width, _ = hamiltonian.shape
+def halo_part(level, low, high, acc, vec, prior, turned, loc):
+    count, _, width, _ = turned.shape
     owned = vec.shape[0]
     kinds = [jnp.bfloat16] if level < 3 else [jnp.float32, jnp.bfloat16]
-    out = pl.pallas_call(
+    return pl.pallas_call(
         functools.partial(halo_kernel, level),
         out_shape=[jax.ShapeDtypeStruct(vec.shape, kind) for kind in kinds],
-        in_specs=[pl.BlockSpec(memory_space=pltpu.SMEM)]
-        + vmem(5)
-        + [pl.BlockSpec(memory_space=pl.ANY)],
+        in_specs=[pl.BlockSpec(memory_space=pltpu.SMEM)] + vmem(6),
         out_specs=vmem(len(kinds)),
-        scratch_shapes=[
-            pltpu.VMEM((count, 2, width, width), jnp.bfloat16),
-            pltpu.SemaphoreType.DMA((count,)),
-        ],
         compiler_params=pltpu.CompilerParams(vmem_limit_bytes=24 << 20),
         cost_estimate=pl.CostEstimate(
             flops=2 * owned * count * width * width * 2,
             bytes_accessed=count * 2 * width * width * 2,
             transcendentals=0,
         ),
-    )(loc, low, high, acc, vec, prior, hamiltonian)
-    return out
-
-
-def gram_kernel(place_ref, own_ref, other_ref, out_ref):
+    )(loc, low, high, acc, vec, prior, turned)
+
+
+def gram_kernel(chunks, place_ref, *refs):
+    own_refs, other_refs, out_ref, columns = refs[:chunks], refs[chunks:-2], refs[-2], refs[-1]
+    share = own_refs[0].shape[0]
+    half = share * chunks
+
     def fill(first, second):
-        out_ref[0] = dot_nt(first[...], first[...])
-        out_ref[1] = dot_nt(first[...], second[...])
-        out_ref[2] = dot_nt(second[...], second[...])
+        for piece in range(chunks):
+            columns[piece * share : (piece + 1) * share, :] = first[piece][...]
+            columns[half + piece * share : half + (piece + 1) * share, :] = second[piece][...]
 
     @pl.when(place_ref[0] == 0)
     def _():
-        fill(own_ref, other_ref)
+        fill(own_refs, other_refs)
 
     @pl.when(place_ref[0] != 0)
     def _():
-        fill(other_ref, own_ref)
+        fill(other_refs, own_refs)
+
+    out_ref[0] = dot_nt(columns[:half, :], columns[:half, :])
+    out_ref[1] = dot_nt(columns[:half, :], columns[half:, :])
+    out_ref[2] = dot_nt(columns[half:, :], columns[half:, :])
 
 
 def factor_block(rows, right):
@@ -253,19 +271,20 @@
     )(gram)
 
 
-def basis_kernel(place_ref, inv_ref, own_ref, other_ref, out_ref):
-    half = own_ref.shape[0]
+def basis_kernel(chunks, place_ref, inv_ref, *refs):
+    own_refs, other_refs, out_ref = refs[:chunks], refs[chunks:-1], refs[-1]
+    half, total = out_ref.shape
     place = place_ref[0]
     rows = pl.ds(pl.multiple_of(place * half, half), half)
     away = pl.ds(pl.multiple_of((1 - place) * half, half), half)
     near_high, near_low = split(inv_ref[rows, rows])
     far_high, far_low = split(inv_ref[rows, away])
-    total = own_ref.shape[1]
     step = 512 if total % 512 == 0 else total
     for at in range(0, total, step):
-        high, low = split(own_ref[:, at : at + step])
-        other = other_ref[:, at : at + step]
-        out_ref[:, at : at + step] = (
+        here = slice(at, at + step)
+        high, low = split(jnp.concatenate([ref[:, here] for ref in own_refs], axis=0))
+        other = jnp.concatenate([ref[:, here] for ref in other_refs], axis=0)
+        out_ref[:, here] = (
             jnp.dot(near_high, high, preferred_element_type=jnp.float32)
             + jnp.dot(near_high, low, preferred_element_type=jnp.float32)
             + jnp.dot(near_low, high, preferred_element_type=jnp.float32)
@@ -280,32 +299,46 @@
     blocks = lax.axis_size("space")
     groups = lax.axis_size("orb")
     half = owned * groups // 2
+    chunks = 2
+    share = owned // chunks
     loc = adjacency % count
     forward = [(i, (i + 1) % blocks) for i in range(blocks)]
     backward = [(target, source) for source, target in forward]
-
-    def apply_level(level, vec, prior):
-        low = lax.ppermute(vec, "space", forward)
-        high = lax.ppermute(vec, "space", backward)
-        acc = own_part(vec, hamiltonian, loc)
-        return halo_part(level, low, high, acc, vec, prior, hamiltonian, loc)
-
-    (level_one,) = apply_level(1, orbitals, orbitals)
-    (level_two,) = apply_level(2, level_one, orbitals)
-    filtered, narrow = apply_level(3, level_two, level_one)
+    smem = [pl.BlockSpec(memory_space=pltpu.SMEM)]
+
+    def halo(vec):
+        return lax.ppermute(vec, "space", forward), lax.ppermute(vec, "space", backward)
+
+    zero = [orbitals[piece * share : (piece + 1) * share] for piece in range(chunks)]
+    sides = [halo(vec) for vec in zero]
+    turned, *accs = turn_part(orbitals, hamiltonian, loc, chunks)
+    one, two, filtered, narrow = [], [], [], []
+    for piece in range(chunks):
+        one += halo_part(1, *sides[piece], accs[piece], zero[piece], zero[piece], turned, loc)
+    for piece in range(chunks):
+        side = halo(one[piece])
+        acc = own_part(one[piece], turned, loc)
+        two += halo_part(2, *side, acc, one[piece], zero[piece], turned, loc)
+    for piece in range(chunks):
+        side = halo(two[piece])
+        acc = own_part(two[piece], turned, loc)
+        wide, short = halo_part(3, *side, acc, two[piece], one[piece], turned, loc)
+        filtered.append(wide)
+        narrow.append(short)
 
     place = lax.axis_index("orb").astype(jnp.int32).reshape(1)
     if groups == 2:
-        other = lax.ppermute(narrow, "orb", [(0, 1), (1, 0)])
+        other = [lax.ppermute(piece, "orb", [(0, 1), (1, 0)]) for piece in narrow]
         gram = pl.pallas_call(
-            gram_kernel,
+            functools.partial(gram_kernel, chunks),
             out_shape=jax.ShapeDtypeStruct((3, half, half), jnp.float32),
-            in_specs=[pl.BlockSpec(memory_space=pltpu.SMEM)] + vmem(2),
+            in_specs=smem + vmem(2 * chunks),
             out_specs=pl.BlockSpec(memory_space=pltpu.VMEM),
+            scratch_shapes=[pltpu.VMEM((2 * half, orbitals.shape[1]), jnp.bfloat16)],
             compiler_params=pltpu.CompilerParams(vmem_limit_bytes=24 << 20),
-        )(place, narrow, other)
+        )(place, *narrow, *other)
     else:
-        columns = lax.all_gather(narrow, "orb", axis=0, tiled=True)
+        columns = lax.all_gather(jnp.concatenate(narrow), "orb", axis=0, tiled=True)
         whole = dot_nt(columns, columns)
         gram = jnp.stack([whole[:half, :half], whole[:half, half:], whole[half:, half:]])
     step = 1
@@ -315,16 +348,16 @@
     upper, inverse = factorize(gram)
     if groups == 2:
         basis = pl.pallas_call(
-            basis_kernel,
-            out_shape=jax.ShapeDtypeStruct(filtered.shape, jnp.float32),
-            in_specs=[pl.BlockSpec(memory_space=pltpu.SMEM)] + vmem(3),
+            functools.partial(basis_kernel, chunks),
+            out_shape=jax.ShapeDtypeStruct(orbitals.shape, jnp.float32),
+            in_specs=smem + vmem(1 + 2 * chunks),
             out_specs=pl.BlockSpec(memory_space=pltpu.VMEM),
             compiler_params=pltpu.CompilerParams(vmem_limit_bytes=24 << 20),
-        )(place, inverse, filtered, other)
+        )(place, inverse, *filtered, *other)
     else:
         mine = lax.dynamic_slice_in_dim(inverse, place[0] * owned, owned, 0)
         near = lax.dynamic_slice_in_dim(mine, place[0] * owned, owned, 1)
-        rest = filtered - narrow.astype(jnp.float32)
+        rest = jnp.concatenate(filtered) - jnp.concatenate(narrow).astype(jnp.float32)
         basis = dot_full(mine, columns.astype(jnp.float32)) + dot_full(near, rest)
     return (basis, upper)
 

time: 104 us -> 98.7 us (0.949)
  Pallas kernels: 42.1 us -> 29.6 us
  starting transfers between devices: 25.4 us -> 30.4 us
  waiting for transfers between devices: 30.5 us -> 31.7 us
  local copies, waits for them, and re-layouts: 4.14 us -> 5.2 us
    ppermute x7 -> x14, starting transfers between devices: 16.5 us -> 30.1 us  [the longest x6 27.2 us: halo(): lax.ppermute(vec, 'space', backward)]
    pallas_call x3 -> x4, Pallas kernels: 19.1 us -> 6.52 us  [own_part(): pl.pallas_call(own_kernel, out_shape=jax.ShapeDtypeStruct(vec.shape, jnp....]
    ppermute x4, starting transfers between devices: 8.85 us -> 0.28 us  [shards(): lax.ppermute(gram, 'space', [(i, i ^ step) for i in range(blocks)])]
    ppermute x4, waiting for transfers between devices: 21 us -> 24.8 us  [shards(): lax.ppermute(gram, 'space', [(i, i ^ step) for i in range(blocks)])]
    pallas_call x2 -> x3, Pallas kernels: 2.56 us -> 5.37 us  [the longest x1 2.74 us: turn_part(): pl.pallas_call(turn_kernel, out_shape=[jax.ShapeDtypeStruct(hamiltonian.s...]
    pallas_call x3 -> x6, Pallas kernels: 9.48 us -> 6.68 us  [halo_part(): pl.pallas_call(functools.partial(halo_kernel, level), out_shape=[jax.Shap...]
    ppermute x7 -> x14, waiting for transfers between devices: 9.49 us -> 6.91 us  [the longest x2 6.88 us: shards(): other = [lax.ppermute(piece, 'orb', [(0, 1), (1, 0)]) for piece in narrow]]
    slice x0 -> x1, local copies, waits for them, and re-layouts: none -> 1.07 us  [shards(): orbitals[piece * share:(piece + 1) * share]]
  transfers between devices with their start and end apart: 11 -> 18, of which waited for: 7 -> 6; matrix products, arithmetic and copies ran while one was open for 1% -> 1% of each run, Pallas kernels for 18% -> 16%
where the time goes in v2:
time: 98.7 us; the launch traced here: 98.5 us
  waiting for transfers between devices  31.7 us (32%)
  starting transfers between devices  30.4 us (31%)
  Pallas kernels  29.6 us (30%)
  local copies, waits for them, and re-layouts  5.2 us (5%)
    ppermute x6, starting transfers between devices, halo(): lax.ppermute(vec, 'space', backward)  27.2 us
    ppermute x4, waiting for transfers between devices, shards(): lax.ppermute(gram, 'space', [(i, i ^ step) for i in range(blocks)])  24.8 us
    pallas_call x1, Pallas kernels, factorize(): pl.pallas_call(factor_kernel, out_shape=[jax.ShapeDtypeStruct((2 * half,...  11 us
    ppermute x2, waiting for transfers between devices, shards(): other = [lax.ppermute(piece, 'orb', [(0, 1), (1, 0)]) for piece in narrow]  6.88 us
    pallas_call x6, Pallas kernels, halo_part(): pl.pallas_call(functools.partial(halo_kernel, level), out_shape=[jax.Shap...  6.68 us
    pallas_call x4, Pallas kernels, own_part(): pl.pallas_call(own_kernel, out_shape=jax.ShapeDtypeStruct(vec.shape, jnp....  6.52 us
    unnamed x4, local copies, waits for them, and re-layouts  4.12 us
    pallas_call x1, Pallas kernels, turn_part(): pl.pallas_call(turn_kernel, out_shape=[jax.ShapeDtypeStruct(hamiltonian.s...  2.74 us
  transfers between devices with their start and end apart: 18, of which 6 were waited for; matrix products, arithmetic and copies ran while one was open for 1% of the time, Pallas kernels for 16%

profile of v2, /device:TPU:0, one launch (start us, length us, event | category | flops | bytes accessed | tf_op | source)
XLA Modules:
  0.0 98.5 jit_solution(38236926232895347)
XLA Ops:
  0.6 1.1 %fusion.1 = (bf16[64,2048]{1,0:T(8,128)(2,1)S(1)}, bf16[64,2048]{1,0:T(8,128)(2,1)S(1)}) fusion(bf16[128,2048]{1,0:T(8,128)(2,1)} %vec_ref.1), kind=kLoop, calls=%fused_computation.4 | loop fusion | bytes 1048576 | tf_op jit(solution)/shard_map/slice | solution.py:312
  1.7 0.5 collective-permute-start
  2.2 5.1 %collective-permute-start.1 = (bf16[64,2048]{1,0:T(8,128)(2,1)S(1)}, bf16[64,2048]{1,0:T(8,128)(2,1)S(1)}, u32[]{:S(2)}, u32[]{:S(2)}) collective-permute-start(bf16[64,2048]{1,0:T(8,128)(2,1)S(1)} %get-tuple-element.21.vec_ref.prior_ref), channel_id=1, source_target_pairs={{2,0},{4,2},{6,4},{8,6},{10,8},{12,10},{14,12},{16,14},{18,16},{20... | collective-permute-start | bytes 786440 | tf_op jit(solution)/shard_map/ppermute | solution.py:310
  7.3 0.0 collective-permute-start.6
  7.3 4.4 %collective-permute-start.7 = (bf16[64,2048]{1,0:T(8,128)(2,1)S(1)}, bf16[64,2048]{1,0:T(8,128)(2,1)S(1)}, u32[]{:S(2)}, u32[]{:S(2)}) collective-permute-start(bf16[64,2048]{1,0:T(8,128)(2,1)S(1)} %get-tuple-element.20.vec_ref.prior_ref), channel_id=1, source_target_pairs={{2,0},{4,2},{6,4},{8,6},{10,8},{12,10},{14,12},{16,14},{18,16},{20... | collective-permute-start | bytes 786440 | tf_op jit(solution)/shard_map/ppermute | solution.py:310
  11.7 0.7 add_select_fusion.loc_ref
  12.4 0.0 copy-start
  12.4 3.1 %copy-done = bf16[8,7,256,256]{3,2,1,0:T(8,128)(2,1)S(1)} copy-done((bf16[8,7,256,256]{3,2,1,0:T(8,128)(2,1)S(1)}, bf16[8,7,256,256]{3,2,1,0:T(8,128)(2,1)}, u32[]{:S(2)}) %copy-start) | copy-done | bytes 7340056
  15.5 0.0 copy-start.1
  15.5 1.0 %copy-done.1 = bf16[128,2048]{1,0:T(8,128)(2,1)S(1)} copy-done((bf16[128,2048]{1,0:T(8,128)(2,1)S(1)}, bf16[128,2048]{1,0:T(8,128)(2,1)}, u32[]{:S(2)}) %copy-start.1) | copy-done | bytes 524312
  16.5 2.7 %shard_map.50 = (bf16[8,7,256,256]{3,2,1,0:T(8,128)(2,1)S(1)}, f32[64,2048]{1,0:T(8,128)S(1)}, f32[64,2048]{1,0:T(8,128)S(1)}) custom-call(s32[8,6]{1,0:T(8,128)S(1)} %add_select_fusion.loc_ref, bf16[128,2048]{1,0:T(8,128)(2,1)S(1)} %copy-done.1, bf16[8,7,256,256]{3,2,1,0:T(8,128)(2,1)S(1)} %copy-done), custom_call_target="tpu_custom_call" | custom-call | flops 671088640 | bytes 14680064 | tf_op jit(solution)/shard_map/pallas_call | solution.py:56
  19.3 0.0 collective-permute-done.low_ref
  19.3 0.0 collective-permute-done.1.high_ref
  19.3 1.1 %shard_map.51.vec_ref.prior_ref = bf16[64,2048]{1,0:T(8,128)(2,1)S(1)} custom-call(s32[8,6]{1,0:T(8,128)S(1)} %add_select_fusion.loc_ref, bf16[64,2048]{1,0:T(8,128)(2,1)S(1)} %collective-permute-done.low_ref, bf16[64,2048]{1,0:T(8,128)(2,1)S(1)} %collective-permute-done.1.high_ref, f32[64,2048]{1,0:T(8,128)S(1)} %get-tuple-element.11.acc_ref, ...), custom_call_target="tpu_custom_call" | custom-call | flops 134217728 | bytes 2097152 | tf_op jit(solution)/shard_map/pallas_call | solution.py:121
  20.4 0.1 collective-permute-start.2
  20.5 4.4 %collective-permute-start.3 = (bf16[64,2048]{1,0:T(8,128)(2,1)S(1)}, bf16[64,2048]{1,0:T(8,128)(2,1)S(1)}, u32[]{:S(2)}, u32[]{:S(2)}) collective-permute-start(bf16[64,2048]{1,0:T(8,128)(2,1)S(1)} %shard_map.51.vec_ref.prior_ref), channel_id=1, source_target_pairs={{2,0},{4,2},{6,4},{8,6},{10,8},{12,10},{14,12},{16,14},{18,16},{20... | collective-permute-start | bytes 786440 | tf_op jit(solution)/shard_map/ppermute | solution.py:310
  24.9 0.0 collective-permute-done.6.low_ref
  24.9 0.0 collective-permute-done.7.high_ref
  24.9 1.1 %shard_map.56.vec_ref.prior_ref = bf16[64,2048]{1,0:T(8,128)(2,1)S(1)} custom-call(s32[8,6]{1,0:T(8,128)S(1)} %add_select_fusion.loc_ref, bf16[64,2048]{1,0:T(8,128)(2,1)S(1)} %collective-permute-done.6.low_ref, bf16[64,2048]{1,0:T(8,128)(2,1)S(1)} %collective-permute-done.7.high_ref, f32[64,2048]{1,0:T(8,128)S(1)} %get-tuple-element.14.acc_ref, ...), custom_call_target="tpu_custom_call" | custom-call | flops 134217728 | bytes 2097152 | tf_op jit(solution)/shard_map/pallas_call | solution.py:121
  26.0 0.1 collective-permute-start.8
  26.1 4.4 %collective-permute-start.9 = (bf16[64,2048]{1,0:T(8,128)(2,1)S(1)}, bf16[64,2048]{1,0:T(8,128)(2,1)S(1)}, u32[]{:S(2)}, u32[]{:S(2)}) collective-permute-start(bf16[64,2048]{1,0:T(8,128)(2,1)S(1)} %shard_map.56.vec_ref.prior_ref), channel_id=1, source_target_pairs={{2,0},{4,2},{6,4},{8,6},{10,8},{12,10},{14,12},{16,14},{18,16},{20... | collective-permute-start | bytes 786440 | tf_op jit(solution)/shard_map/ppermute | solution.py:310
  30.5 1.6 %shard_map.52.acc_ref = f32[64,2048]{1,0:T(8,128)S(1)} custom-call(s32[8,6]{1,0:T(8,128)S(1)} %add_select_fusion.loc_ref, bf16[64,2048]{1,0:T(8,128)(2,1)S(1)} %shard_map.51.vec_ref.prior_ref, bf16[8,7,256,256]{3,2,1,0:T(8,128)(2,1)S(1)} %get-tuple-element.12.turned_ref), custom_call_target="tpu_custom_call" | custom-call | flops 335544320 | bytes 5242880 | tf_op jit(solution)/shard_map/pallas_call | solution.py:86
  32.1 1.6 %shard_map.57.acc_ref = f32[64,2048]{1,0:T(8,128)S(1)} custom-call(s32[8,6]{1,0:T(8,128)S(1)} %add_select_fusion.loc_ref, bf16[64,2048]{1,0:T(8,128)(2,1)S(1)} %shard_map.56.vec_ref.prior_ref, bf16[8,7,256,256]{3,2,1,0:T(8,128)(2,1)S(1)} %get-tuple-element.12.turned_ref), custom_call_target="tpu_custom_call" | custom-call | flops 335544320 | bytes 5242880 | tf_op jit(solution)/shard_map/pallas_call | solution.py:86
  33.8 0.0 collective-permute-done.2.low_ref
  33.8 0.0 collective-permute-done.3.high_ref
  33.8 1.1 %shard_map.53.vec_ref = bf16[64,2048]{1,0:T(8,128)(2,1)S(1)} custom-call(s32[8,6]{1,0:T(8,128)S(1)} %add_select_fusion.loc_ref, bf16[64,2048]{1,0:T(8,128)(2,1)S(1)} %collective-permute-done.2.low_ref, bf16[64,2048]{1,0:T(8,128)(2,1)S(1)} %collective-permute-done.3.high_ref, f32[64,2048]{1,0:T(8,128)S(1)} %shard_map.52.acc_ref, ...), custom_call_target="tpu_custom_call" | custom-call | flops 134217728 | bytes 2097152 | tf_op jit(solution)/shard_map/pallas_call | solution.py:121
  34.9 0.1 collective-permute-start.4
  35.0 4.4 %collective-permute-start.5 = (bf16[64,2048]{1,0:T(8,128)(2,1)S(1)}, bf16[64,2048]{1,0:T(8,128)(2,1)S(1)}, u32[]{:S(2)}, u32[]{:S(2)}) collective-permute-start(bf16[64,2048]{1,0:T(8,128)(2,1)S(1)} %shard_map.53.vec_ref), channel_id=1, source_target_pairs={{2,0},{4,2},{6,4},{8,6},{10,8},{12,10},{14,12},{16,14},{18,16},{20... | collective-permute-start | bytes 786440 | tf_op jit(solution)/shard_map/ppermute | solution.py:310
  39.4 0.0 collective-permute-done.8.low_ref
  39.4 0.0 collective-permute-done.9.high_ref
  39.4 1.1 %shard_map.58.vec_ref = bf16[64,2048]{1,0:T(8,128)(2,1)S(1)} custom-call(s32[8,6]{1,0:T(8,128)S(1)} %add_select_fusion.loc_ref, bf16[64,2048]{1,0:T(8,128)(2,1)S(1)} %collective-permute-done.8.low_ref, bf16[64,2048]{1,0:T(8,128)(2,1)S(1)} %collective-permute-done.9.high_ref, f32[64,2048]{1,0:T(8,128)S(1)} %shard_map.57.acc_ref, ...), custom_call_target="tpu_custom_call" | custom-call | flops 134217728 | bytes 2097152 | tf_op jit(solution)/shard_map/pallas_call | solution.py:121
  40.6 0.1 collective-permute-start.10
  40.6 4.4 %collective-permute-start.11 = (bf16[64,2048]{1,0:T(8,128)(2,1)S(1)}, bf16[64,2048]{1,0:T(8,128)(2,1)S(1)}, u32[]{:S(2)}, u32[]{:S(2)}) collective-permute-start(bf16[64,2048]{1,0:T(8,128)(2,1)S(1)} %shard_map.58.vec_ref), channel_id=1, source_target_pairs={{2,0},{4,2},{6,4},{8,6},{10,8},{12,10},{14,12},{16,14},{18,16},{20... | collective-permute-start | bytes 786440 | tf_op jit(solution)/shard_map/ppermute | solution.py:310
  45.1 1.6 %shard_map.54.acc_ref = f32[64,2048]{1,0:T(8,128)S(1)} custom-call(s32[8,6]{1,0:T(8,128)S(1)} %add_select_fusion.loc_ref, bf16[64,2048]{1,0:T(8,128)(2,1)S(1)} %shard_map.53.vec_ref, bf16[8,7,256,256]{3,2,1,0:T(8,128)(2,1)S(1)} %get-tuple-element.12.turned_ref), custom_call_target="tpu_custom_call" | custom-call | flops 335544320 | bytes 5242880 | tf_op jit(solution)/shard_map/pallas_call | solution.py:86
  46.7 1.6 %shard_map.59.acc_ref = f32[64,2048]{1,0:T(8,128)S(1)} custom-call(s32[8,6]{1,0:T(8,128)S(1)} %add_select_fusion.loc_ref, bf16[64,2048]{1,0:T(8,128)(2,1)S(1)} %shard_map.58.vec_ref, bf16[8,7,256,256]{3,2,1,0:T(8,128)(2,1)S(1)} %get-tuple-element.12.turned_ref), custom_call_target="tpu_custom_call" | custom-call | flops 335544320 | bytes 5242880 | tf_op jit(solution)/shard_map/pallas_call | solution.py:86
  48.3 0.0 collective-permute-done.4.low_ref
  48.3 0.0 collective-permute-done.5.high_ref
  48.3 1.1 %shard_map.55 = (f32[64,2048]{1,0:T(8,128)S(1)}, bf16[64,2048]{1,0:T(8,128)(2,1)S(1)}) custom-call(s32[8,6]{1,0:T(8,128)S(1)} %add_select_fusion.loc_ref, bf16[64,2048]{1,0:T(8,128)(2,1)S(1)} %collective-permute-done.4.low_ref, bf16[64,2048]{1,0:T(8,128)(2,1)S(1)} %collective-permute-done.5.high_ref, f32[64,2048]{1,0:T(8,128)S(1)} %shard_map.54.acc_ref, ...), custom_call_target="tpu_custom_call" | custom-call | flops 134217728 | bytes 2097152 | tf_op jit(solution)/shard_map/pallas_call | solution.py:121
  49.5 1.9 %collective-permute-start.12 = (bf16[64,2048]{1,0:T(8,128)(2,1)S(1)}, bf16[64,2048]{1,0:T(8,128)(2,1)S(1)}, u32[]{:S(2)}, u32[]{:S(2)}) collective-permute-start(bf16[64,2048]{1,0:T(8,128)(2,1)S(1)} %get-tuple-element.13.refs_0_), channel_id=1, source_target_pairs={{0,1},{1,0},{2,3},{3,2},{4,5},{5,4},{6,7},{7,6},{8,9},{9,8},{10,11... | collective-permute-start | bytes 786440 | tf_op jit(solution)/shard_map/ppermute | solution.py:331
  51.4 0.0 collective-permute-done.10.low_ref
  51.4 0.0 collective-permute-done.11.high_ref
  51.4 1.1 %shard_map.60 = (f32[64,2048]{1,0:T(8,128)S(1)}, bf16[64,2048]{1,0:T(8,128)(2,1)S(1)}) custom-call(s32[8,6]{1,0:T(8,128)S(1)} %add_select_fusion.loc_ref, bf16[64,2048]{1,0:T(8,128)(2,1)S(1)} %collective-permute-done.10.low_ref, bf16[64,2048]{1,0:T(8,128)(2,1)S(1)} %collective-permute-done.11.high_ref, f32[64,2048]{1,0:T(8,128)S(1)} %shard_map.59.acc_ref, ...), custom_call_target="tpu_custom_call" | custom-call | flops 134217728 | bytes 2097152 | tf_op jit(solution)/shard_map/pallas_call | solution.py:121
  52.6 0.2 collective-permute-start.13
  52.8 4.1 %collective-permute-done.12.refs_2_ = bf16[64,2048]{1,0:T(8,128)(2,1)S(1)} collective-permute-done((bf16[64,2048]{1,0:T(8,128)(2,1)S(1)}, bf16[64,2048]{1,0:T(8,128)(2,1)S(1)}, u32[]{:S(2)}, u32[]{:S(2)}) %collective-permute-start.12) | collective-permute-done | bytes 262176 | tf_op jit(solution)/shard_map/ppermute | solution.py:331
  56.9 2.8 %collective-permute-done.13.refs_3_ = bf16[64,2048]{1,0:T(8,128)(2,1)S(1)} collective-permute-done((bf16[64,2048]{1,0:T(8,128)(2,1)S(1)}, bf16[64,2048]{1,0:T(8,128)(2,1)S(1)}, u32[]{:S(2)}, u32[]{:S(2)}) %collective-permute-start.13) | collective-permute-done | bytes 262176 | tf_op jit(solution)/shard_map/ppermute | solution.py:331
  59.7 0.8 shard_map.61
  60.5 0.1 collective-permute-start.14
  60.6 1.4 %collective-permute-done.14 = f32[3,128,128]{2,1,0:T(8,128)S(1)} collective-permute-done((f32[3,128,128]{2,1,0:T(8,128)S(1)}, f32[3,128,128]{2,1,0:T(8,128)S(1)}, u32[]{:S(2)}, u32[]{:S(2)}) %collective-permute-start.14) | collective-permute-done | bytes 196640 | tf_op jit(solution)/shard_map/ppermute | solution.py:346
  62.0 0.1 collective-permute-start.15
  62.1 6.9 %collective-permute-done.15 = f32[3,128,128]{2,1,0:T(8,128)S(1)} collective-permute-done((f32[3,128,128]{2,1,0:T(8,128)S(1)}, f32[3,128,128]{2,1,0:T(8,128)S(1)}, u32[]{:S(2)}, u32[]{:S(2)}) %collective-permute-start.15) | collective-permute-done | bytes 196640 | tf_op jit(solution)/shard_map/ppermute | solution.py:346
  69.1 0.1 collective-permute-start.16
  69.1 6.1 %collective-permute-done.16 = f32[3,128,128]{2,1,0:T(8,128)S(1)} collective-permute-done((f32[3,128,128]{2,1,0:T(8,128)S(1)}, f32[3,128,128]{2,1,0:T(8,128)S(1)}, u32[]{:S(2)}, u32[]{:S(2)}) %collective-permute-start.16) | collective-permute-done | bytes 196640 | tf_op jit(solution)/shard_map/ppermute | solution.py:346
  75.3 0.1 collective-permute-start.17
  75.3 10.3 %collective-permute-done.17 = f32[3,128,128]{2,1,0:T(8,128)S(1)} collective-permute-done((f32[3,128,128]{2,1,0:T(8,128)S(1)}, f32[3,128,128]{2,1,0:T(8,128)S(1)}, u32[]{:S(2)}, u32[]{:S(2)}) %collective-permute-start.17) | collective-permute-done | bytes 196640 | tf_op jit(solution)/shard_map/ppermute | solution.py:346
  85.7 11.0 %shard_map.62 = (f32[256,256]{1,0:T(8,128)}, f32[256,256]{1,0:T(8,128)S(1)}) custom-call(f32[3,128,128]{2,1,0:T(8,128)S(1)} %add.22.gram_ref), custom_call_target="tpu_custom_call" | custom-call | tf_op jit(solution)/shard_map/pallas_call | solution.py:264
  96.7 1.8 %shard_map.63 = f32[128,2048]{1,0:T(8,128)} custom-call(s32[1]{0:T(128)} %bitcast.place_ref, f32[256,256]{1,0:T(8,128)S(1)} %get-tuple-element.16.inv_ref, f32[64,2048]{1,0:T(8,128)S(1)} %get-tuple-element.17.refs_0_, f32[64,2048]{1,0:T(8,128)S(1)} %get-tuple-element.18.refs_1_, bf16[64,2048]{1,0:T(8,128)(2,1)S(1)} %collective-permute-done.12.refs_2_, ...), custom_call_target="tpu_custom_call" | custom-call | tf_op jit(solution)/shard_map/pallas_call | solution.py:350
  (4 shorter events, 0.1 us)
Async XLA Ops:
  1.7 17.6 %collective-permute-start = (bf16[64,2048]{1,0:T(8,128)(2,1)S(1)}, bf16[64,2048]{1,0:T(8,128)(2,1)S(1)}, u32[]{:S(2)}, u32[]{:S(2)}) collective-permute-start(bf16[64,2048]{1,0:T(8,128)(2,1)S(1)} %get-tuple-element.21.vec_ref.prior_ref), channel_id=1, source_target_pairs={{0,2},{2,4},{4,6},{6,8},{8,10},{10,12},{12,14},{14,16},{16,18},{18... | collective-permute-start | bytes 786440 | tf_op jit(solution)/shard_map/ppermute | solution.py:310
  2.2 17.1 %collective-permute-start.1 = (bf16[64,2048]{1,0:T(8,128)(2,1)S(1)}, bf16[64,2048]{1,0:T(8,128)(2,1)S(1)}, u32[]{:S(2)}, u32[]{:S(2)}) collective-permute-start(bf16[64,2048]{1,0:T(8,128)(2,1)S(1)} %get-tuple-element.21.vec_ref.prior_ref), channel_id=1, source_target_pairs={{2,0},{4,2},{6,4},{8,6},{10,8},{12,10},{14,12},{16,14},{18,16},{20... | collective-permute-start | bytes 786440 | tf_op jit(solution)/shard_map/ppermute | solution.py:310
  7.3 17.6 %collective-permute-start.6 = (bf16[64,2048]{1,0:T(8,128)(2,1)S(1)}, bf16[64,2048]{1,0:T(8,128)(2,1)S(1)}, u32[]{:S(2)}, u32[]{:S(2)}) collective-permute-start(bf16[64,2048]{1,0:T(8,128)(2,1)S(1)} %get-tuple-element.20.vec_ref.prior_ref), channel_id=1, source_target_pairs={{0,2},{2,4},{4,6},{6,8},{8,10},{10,12},{12,14},{14,16},{16,18},{18... | collective-permute-start | bytes 786440 | tf_op jit(solution)/shard_map/ppermute | solution.py:310
  7.3 17.6 %collective-permute-start.7 = (bf16[64,2048]{1,0:T(8,128)(2,1)S(1)}, bf16[64,2048]{1,0:T(8,128)(2,1)S(1)}, u32[]{:S(2)}, u32[]{:S(2)}) collective-permute-start(bf16[64,2048]{1,0:T(8,128)(2,1)S(1)} %get-tuple-element.20.vec_ref.prior_ref), channel_id=1, source_target_pairs={{2,0},{4,2},{6,4},{8,6},{10,8},{12,10},{14,12},{16,14},{18,16},{20... | collective-permute-start | bytes 786440 | tf_op jit(solution)/shard_map/ppermute | solution.py:310
  12.4 3.1 %copy-start = (bf16[8,7,256,256]{3,2,1,0:T(8,128)(2,1)S(1)}, bf16[8,7,256,256]{3,2,1,0:T(8,128)(2,1)}, u32[]{:S(2)}) copy-start(bf16[8,7,256,256]{3,2,1,0:T(8,128)(2,1)} %ham_ref.1) | copy-start | bytes 22020100
  15.5 1.0 %copy-start.1 = (bf16[128,2048]{1,0:T(8,128)(2,1)S(1)}, bf16[128,2048]{1,0:T(8,128)(2,1)}, u32[]{:S(2)}) copy-start(bf16[128,2048]{1,0:T(8,128)(2,1)} %vec_ref.1) | copy-start | bytes 1572868
  20.4 13.4 %collective-permute-start.2 = (bf16[64,2048]{1,0:T(8,128)(2,1)S(1)}, bf16[64,2048]{1,0:T(8,128)(2,1)S(1)}, u32[]{:S(2)}, u32[]{:S(2)}) collective-permute-start(bf16[64,2048]{1,0:T(8,128)(2,1)S(1)} %shard_map.51.vec_ref.prior_ref), channel_id=1, source_target_pairs={{0,2},{2,4},{4,6},{6,8},{8,10},{10,12},{12,14},{14,16},{16,18},{18... | collective-permute-start | bytes 786440 | tf_op jit(solution)/shard_map/ppermute | solution.py:310
  20.5 13.3 %collective-permute-start.3 = (bf16[64,2048]{1,0:T(8,128)(2,1)S(1)}, bf16[64,2048]{1,0:T(8,128)(2,1)S(1)}, u32[]{:S(2)}, u32[]{:S(2)}) collective-permute-start(bf16[64,2048]{1,0:T(8,128)(2,1)S(1)} %shard_map.51.vec_ref.prior_ref), channel_id=1, source_target_pairs={{2,0},{4,2},{6,4},{8,6},{10,8},{12,10},{14,12},{16,14},{18,16},{20... | collective-permute-start | bytes 786440 | tf_op jit(solution)/shard_map/ppermute | solution.py:310
  26.0 13.4 %collective-permute-start.8 = (bf16[64,2048]{1,0:T(8,128)(2,1)S(1)}, bf16[64,2048]{1,0:T(8,128)(2,1)S(1)}, u32[]{:S(2)}, u32[]{:S(2)}) collective-permute-start(bf16[64,2048]{1,0:T(8,128)(2,1)S(1)} %shard_map.56.vec_ref.prior_ref), channel_id=1, source_target_pairs={{0,2},{2,4},{4,6},{6,8},{8,10},{10,12},{12,14},{14,16},{16,18},{18... | collective-permute-start | bytes 786440 | tf_op jit(solution)/shard_map/ppermute | solution.py:310
  26.1 13.4 %collective-permute-start.9 = (bf16[64,2048]{1,0:T(8,128)(2,1)S(1)}, bf16[64,2048]{1,0:T(8,128)(2,1)S(1)}, u32[]{:S(2)}, u32[]{:S(2)}) collective-permute-start(bf16[64,2048]{1,0:T(8,128)(2,1)S(1)} %shard_map.56.vec_ref.prior_ref), channel_id=1, source_target_pairs={{2,0},{4,2},{6,4},{8,6},{10,8},{12,10},{14,12},{16,14},{18,16},{20... | collective-permute-start | bytes 786440 | tf_op jit(solution)/shard_map/ppermute | solution.py:310
  34.9 13.4 %collective-permute-start.4 = (bf16[64,2048]{1,0:T(8,128)(2,1)S(1)}, bf16[64,2048]{1,0:T(8,128)(2,1)S(1)}, u32[]{:S(2)}, u32[]{:S(2)}) collective-permute-start(bf16[64,2048]{1,0:T(8,128)(2,1)S(1)} %shard_map.53.vec_ref), channel_id=1, source_target_pairs={{0,2},{2,4},{4,6},{6,8},{8,10},{10,12},{12,14},{14,16},{16,18},{18... | collective-permute-start | bytes 786440 | tf_op jit(solution)/shard_map/ppermute | solution.py:310
  35.0 13.4 %collective-permute-start.5 = (bf16[64,2048]{1,0:T(8,128)(2,1)S(1)}, bf16[64,2048]{1,0:T(8,128)(2,1)S(1)}, u32[]{:S(2)}, u32[]{:S(2)}) collective-permute-start(bf16[64,2048]{1,0:T(8,128)(2,1)S(1)} %shard_map.53.vec_ref), channel_id=1, source_target_pairs={{2,0},{4,2},{6,4},{8,6},{10,8},{12,10},{14,12},{16,14},{18,16},{20... | collective-permute-start | bytes 786440 | tf_op jit(solution)/shard_map/ppermute | solution.py:310
  40.6 10.9 %collective-permute-start.10 = (bf16[64,2048]{1,0:T(8,128)(2,1)S(1)}, bf16[64,2048]{1,0:T(8,128)(2,1)S(1)}, u32[]{:S(2)}, u32[]{:S(2)}) collective-permute-start(bf16[64,2048]{1,0:T(8,128)(2,1)S(1)} %shard_map.58.vec_ref), channel_id=1, source_target_pairs={{0,2},{2,4},{4,6},{6,8},{8,10},{10,12},{12,14},{14,16},{16,18},{18... | collective-permute-start | bytes 786440 | tf_op jit(solution)/shard_map/ppermute | solution.py:310
  40.6 10.8 %collective-permute-start.11 = (bf16[64,2048]{1,0:T(8,128)(2,1)S(1)}, bf16[64,2048]{1,0:T(8,128)(2,1)S(1)}, u32[]{:S(2)}, u32[]{:S(2)}) collective-permute-start(bf16[64,2048]{1,0:T(8,128)(2,1)S(1)} %shard_map.58.vec_ref), channel_id=1, source_target_pairs={{2,0},{4,2},{6,4},{8,6},{10,8},{12,10},{14,12},{16,14},{18,16},{20... | collective-permute-start | bytes 786440 | tf_op jit(solution)/shard_map/ppermute | solution.py:310
  49.5 7.4 %collective-permute-start.12 = (bf16[64,2048]{1,0:T(8,128)(2,1)S(1)}, bf16[64,2048]{1,0:T(8,128)(2,1)S(1)}, u32[]{:S(2)}, u32[]{:S(2)}) collective-permute-start(bf16[64,2048]{1,0:T(8,128)(2,1)S(1)} %get-tuple-element.13.refs_0_), channel_id=1, source_target_pairs={{0,1},{1,0},{2,3},{3,2},{4,5},{5,4},{6,7},{7,6},{8,9},{9,8},{10,11... | collective-permute-start | bytes 786440 | tf_op jit(solution)/shard_map/ppermute | solution.py:331
  52.6 7.1 %collective-permute-start.13 = (bf16[64,2048]{1,0:T(8,128)(2,1)S(1)}, bf16[64,2048]{1,0:T(8,128)(2,1)S(1)}, u32[]{:S(2)}, u32[]{:S(2)}) collective-permute-start(bf16[64,2048]{1,0:T(8,128)(2,1)S(1)} %get-tuple-element.15.refs_1_), channel_id=1, source_target_pairs={{0,1},{1,0},{2,3},{3,2},{4,5},{5,4},{6,7},{7,6},{8,9},{9,8},{10,11... | collective-permute-start | bytes 786440 | tf_op jit(solution)/shard_map/ppermute | solution.py:331
  60.5 1.5 %collective-permute-start.14 = (f32[3,128,128]{2,1,0:T(8,128)S(1)}, f32[3,128,128]{2,1,0:T(8,128)S(1)}, u32[]{:S(2)}, u32[]{:S(2)}) collective-permute-start(f32[3,128,128]{2,1,0:T(8,128)S(1)} %shard_map.61), channel_id=1, source_target_pairs={{0,2},{2,0},{4,6},{6,4},{8,10},{10,8},{12,14},{14,12},{16,18},{18,... | collective-permute-start | bytes 589832 | tf_op jit(solution)/shard_map/ppermute | solution.py:346
  62.0 7.0 %collective-permute-start.15 = (f32[3,128,128]{2,1,0:T(8,128)S(1)}, f32[3,128,128]{2,1,0:T(8,128)S(1)}, u32[]{:S(2)}, u32[]{:S(2)}) collective-permute-start(f32[3,128,128]{2,1,0:T(8,128)S(1)} %add.19), channel_id=1, source_target_pairs={{0,4},{2,6},{4,0},{6,2},{8,12},{10,14},{12,8},{14,10},{16,20},{18,... | collective-permute-start | bytes 589832 | tf_op jit(solution)/shard_map/ppermute | solution.py:346
  69.1 6.2 %collective-permute-start.16 = (f32[3,128,128]{2,1,0:T(8,128)S(1)}, f32[3,128,128]{2,1,0:T(8,128)S(1)}, u32[]{:S(2)}, u32[]{:S(2)}) collective-permute-start(f32[3,128,128]{2,1,0:T(8,128)S(1)} %add.20), channel_id=1, source_target_pairs={{0,8},{2,10},{4,12},{6,14},{8,0},{10,2},{12,4},{14,6},{16,24},{18,... | collective-permute-start | bytes 589832 | tf_op jit(solution)/shard_map/ppermute | solution.py:346
  75.3 10.4 %collective-permute-start.17 = (f32[3,128,128]{2,1,0:T(8,128)S(1)}, f32[3,128,128]{2,1,0:T(8,128)S(1)}, u32[]{:S(2)}, u32[]{:S(2)}) collective-permute-start(f32[3,128,128]{2,1,0:T(8,128)S(1)} %add.21), channel_id=1, source_target_pairs={{0,16},{2,18},{4,20},{6,22},{8,24},{10,26},{12,28},{14,30},{16,0},... | collective-permute-start | bytes 589832 | tf_op jit(solution)/shard_map/ppermute | solution.py:346

commit v3 on v2

--- a/solution.py
+++ b/solution.py
@@ -31,9 +31,8 @@
     return high, (a - high.astype(jnp.float32)).astype(jnp.bfloat16)
 
 
-def turn_kernel(loc_ref, vec_ref, ham_ref, turned_ref, *outs):
+def turn_kernel(loc_ref, vec_ref, ham_ref, turned_ref, out_ref):
     count, faces, width, _ = ham_ref.shape
-    rows = outs[0].shape[0]
     for e in range(count):
         here = slice(e * width, (e + 1) * width)
         total = None
@@ -45,19 +44,20 @@
             at = here if face == 0 else pl.ds(pl.multiple_of(loc_ref[e, face - 1] * width, width), width)
             part = jnp.dot(vec_ref[:, at], turned, preferred_element_type=jnp.float32)
             total = part if total is None else total + part
-        for piece, out in enumerate(outs):
-            out[:, here] = total[piece * rows : (piece + 1) * rows]
-
-
-def turn_part(vec, hamiltonian, loc, chunks):
+        out_ref[:, here] = total
+
+
+def turn_part(vec, hamiltonian, loc):
     count, faces, width, _ = hamiltonian.shape
     owned = vec.shape[0]
-    share = jax.ShapeDtypeStruct((owned // chunks, vec.shape[1]), jnp.float32)
     return pl.pallas_call(
         turn_kernel,
-        out_shape=[jax.ShapeDtypeStruct(hamiltonian.shape, hamiltonian.dtype)] + [share] * chunks,
+        out_shape=[
+            jax.ShapeDtypeStruct(hamiltonian.shape, hamiltonian.dtype),
+            jax.ShapeDtypeStruct(vec.shape, jnp.float32),
+        ],
         in_specs=[pl.BlockSpec(memory_space=pltpu.SMEM)] + vmem(2),
-        out_specs=vmem(1 + chunks),
+        out_specs=vmem(2),
         compiler_params=pltpu.CompilerParams(vmem_limit_bytes=32 << 20),
         cost_estimate=pl.CostEstimate(
             flops=2 * owned * count * width * width * 5,
@@ -132,27 +132,21 @@
     )(loc, low, high, acc, vec, prior, turned)
 
 
-def gram_kernel(chunks, place_ref, *refs):
-    own_refs, other_refs, out_ref, columns = refs[:chunks], refs[chunks:-2], refs[-2], refs[-1]
-    share = own_refs[0].shape[0]
-    half = share * chunks
-
-    def fill(first, second):
-        for piece in range(chunks):
-            columns[piece * share : (piece + 1) * share, :] = first[piece][...]
-            columns[half + piece * share : half + (piece + 1) * share, :] = second[piece][...]
-
+def own_gram_kernel(own_ref, high_ref, out_ref):
+    high = high_ref[...]
+    low = (own_ref[...] - high.astype(jnp.float32)).astype(jnp.bfloat16)
+    mixed = dot_nt(high, low)
+    out_ref[...] = dot_nt(high, high) + (mixed + mixed.T)
+
+
+def cross_gram_kernel(place_ref, own_ref, other_ref, out_ref):
     @pl.when(place_ref[0] == 0)
     def _():
-        fill(own_refs, other_refs)
+        out_ref[...] = dot_nt(own_ref[...], other_ref[...])
 
     @pl.when(place_ref[0] != 0)
     def _():
-        fill(other_refs, own_refs)
-
-    out_ref[0] = dot_nt(columns[:half, :], columns[:half, :])
-    out_ref[1] = dot_nt(columns[:half, :], columns[half:, :])
-    out_ref[2] = dot_nt(columns[half:, :], columns[half:, :])
+        out_ref[...] = dot_nt(other_ref[...], own_ref[...])
 
 
 def factor_block(rows, right):
@@ -220,59 +214,84 @@
     return upper, inverse
 
 
-def factor_kernel(gram_ref, upper_ref, inv_ref, work, right):
-    half = gram_ref.shape[1]
+def factor_into(work, right, upper_ref, inv_ref):
+    half = work.shape[0]
     strips = half // SUB
     row = lax.broadcasted_iota(jnp.int32, (half, half), 0)
     col = lax.broadcasted_iota(jnp.int32, (half, half), 1)
-
-    def one(at):
-        rows = [work[SUB * s : SUB * (s + 1), :] for s in range(strips)]
-        eye = (row == col).astype(jnp.float32)
-        beside = [eye[SUB * s : SUB * (s + 1), :] for s in range(strips)]
-        upper, inverse = factor_block(rows, beside)
-        for s in range(strips):
-            work[SUB * s : SUB * (s + 1), :] = upper[s]
-            right[SUB * s : SUB * (s + 1), :] = inverse[s]
-        here = pl.ds(pl.multiple_of(at * half, half), half)
-        upper_ref[here, here] = jnp.where(col >= row, work[...], 0.0)
-        inv_ref[here, here] = jnp.where(col <= row, right[...], 0.0)
-
-    work[...] = gram_ref[0]
+    rows = [work[SUB * s : SUB * (s + 1), :] for s in range(strips)]
+    eye = (row == col).astype(jnp.float32)
+    beside = [eye[SUB * s : SUB * (s + 1), :] for s in range(strips)]
+    upper, inverse = factor_block(rows, beside)
+    for s in range(strips):
+        work[SUB * s : SUB * (s + 1), :] = upper[s]
+        right[SUB * s : SUB * (s + 1), :] = inverse[s]
+    upper_ref[...] = jnp.where(col >= row, work[...], 0.0)
+    inv_ref[...] = jnp.where(col <= row, right[...], 0.0)
+
+
+def first_kernel(place_ref, own_ref, other_ref, upper_ref, inv_ref, work, right):
+    @pl.when(place_ref[0] == 0)
+    def _():
+        work[...] = own_ref[...]
+
+    @pl.when(place_ref[0] != 0)
+    def _():
+        work[...] = other_ref[...]
+
+    factor_into(work, right, upper_ref, inv_ref)
+
+
+def second_kernel(place_ref, own_ref, other_ref, cross_ref, first_ref, first_inv_ref, upper_ref, inv_ref, work, right):
+    half = own_ref.shape[0]
+    across = dot_full(first_inv_ref[...], cross_ref[...])
+    update = dot_full(across, across, ((0,), (0,)))
+
+    @pl.when(place_ref[0] == 0)
+    def _():
+        work[...] = other_ref[...] - update
+
+    @pl.when(place_ref[0] != 0)
+    def _():
+        work[...] = own_ref[...] - update
+
     zero = jnp.zeros((half, half), jnp.float32)
-
-    def body(at, carry):
-        one(at)
-
-        @pl.when(at == 0)
-        def _():
-            across = dot_full(inv_ref[0:half, 0:half], gram_ref[1])
-            upper_ref[0:half, half:] = across
-            work[...] = gram_ref[2] - dot_full(across, across, ((0,), (0,)))
-
-        return carry
-
-    lax.fori_loop(0, 2, body, 0)
+    upper_ref[0:half, 0:half] = first_ref[...]
+    upper_ref[0:half, half:] = across
     upper_ref[half:, 0:half] = zero
+    inv_ref[0:half, 0:half] = first_inv_ref[...]
     inv_ref[0:half, half:] = zero
-    between = dot_full(upper_ref[0:half, half:], inv_ref[0:half, 0:half], ((0,), (0,)))
+    between = dot_full(across, first_inv_ref[...], ((0,), (0,)))
+    factor_into(work, right, upper_ref.at[half:, half:], inv_ref.at[half:, half:])
     inv_ref[half:, 0:half] = -dot_full(inv_ref[half:, half:], between)
 
 
-def factorize(gram):
-    half = gram.shape[1]
+def factorize(place, own, other, cross):
+    half = own.shape[0]
+    smem = [pl.BlockSpec(memory_space=pltpu.SMEM)]
+    tile = jax.ShapeDtypeStruct((half, half), jnp.float32)
+    scratch = [pltpu.VMEM((half, half), jnp.float32)] * 2
+    params = pltpu.CompilerParams(vmem_limit_bytes=24 << 20)
+    first, first_inv = pl.pallas_call(
+        first_kernel,
+        out_shape=[tile] * 2,
+        in_specs=smem + vmem(2),
+        out_specs=vmem(2),
+        scratch_shapes=scratch,
+        compiler_params=params,
+        cost_estimate=pl.CostEstimate(flops=2 * half**3, bytes_accessed=1 << 24, transcendentals=half),
+    )(place, own, other)
     return pl.pallas_call(
-        factor_kernel,
+        second_kernel,
         out_shape=[jax.ShapeDtypeStruct((2 * half, 2 * half), jnp.float32)] * 2,
-        in_specs=vmem(1),
+        in_specs=smem + vmem(5),
         out_specs=vmem(2),
-        scratch_shapes=[pltpu.VMEM((half, half), jnp.float32)] * 2,
-        compiler_params=pltpu.CompilerParams(vmem_limit_bytes=24 << 20),
-    )(gram)
-
-
-def basis_kernel(chunks, place_ref, inv_ref, *refs):
-    own_refs, other_refs, out_ref = refs[:chunks], refs[chunks:-1], refs[-1]
+        scratch_shapes=scratch,
+        compiler_params=params,
+    )(place, own, other, cross, first, first_inv)
+
+
+def basis_kernel(place_ref, inv_ref, own_ref, other_ref, out_ref):
     half, total = out_ref.shape
     place = place_ref[0]
     rows = pl.ds(pl.multiple_of(place * half, half), half)
@@ -282,8 +301,8 @@
     step = 512 if total % 512 == 0 else total
     for at in range(0, total, step):
         here = slice(at, at + step)
-        high, low = split(jnp.concatenate([ref[:, here] for ref in own_refs], axis=0))
-        other = jnp.concatenate([ref[:, here] for ref in other_refs], axis=0)
+        high, low = split(own_ref[:, here])
+        other = other_ref[:, here]
         out_ref[:, here] = (
             jnp.dot(near_high, high, preferred_element_type=jnp.float32)
             + jnp.dot(near_high, low, preferred_element_type=jnp.float32)
@@ -299,8 +318,6 @@
     blocks = lax.axis_size("space")
     groups = lax.axis_size("orb")
     half = owned * groups // 2
-    chunks = 2
-    share = owned // chunks
     loc = adjacency % count
     forward = [(i, (i + 1) % blocks) for i in range(blocks)]
     backward = [(target, source) for source, target in forward]
@@ -309,55 +326,62 @@
     def halo(vec):
         return lax.ppermute(vec, "space", forward), lax.ppermute(vec, "space", backward)
 
-    zero = [orbitals[piece * share : (piece + 1) * share] for piece in range(chunks)]
-    sides = [halo(vec) for vec in zero]
-    turned, *accs = turn_part(orbitals, hamiltonian, loc, chunks)
-    one, two, filtered, narrow = [], [], [], []
-    for piece in range(chunks):
-        one += halo_part(1, *sides[piece], accs[piece], zero[piece], zero[piece], turned, loc)
-    for piece in range(chunks):
-        side = halo(one[piece])
-        acc = own_part(one[piece], turned, loc)
-        two += halo_part(2, *side, acc, one[piece], zero[piece], turned, loc)
-    for piece in range(chunks):
-        side = halo(two[piece])
-        acc = own_part(two[piece], turned, loc)
-        wide, short = halo_part(3, *side, acc, two[piece], one[piece], turned, loc)
-        filtered.append(wide)
-        narrow.append(short)
+    side = halo(orbitals)
+    turned, acc = turn_part(orbitals, hamiltonian, loc)
+    (one,) = halo_part(1, *side, acc, orbitals, orbitals, turned, loc)
+    side = halo(one)
+    (two,) = halo_part(2, *side, own_part(one, turned, loc), one, orbitals, turned, loc)
+    side = halo(two)
+    filtered, narrow = halo_part(3, *side, own_part(two, turned, loc), two, one, turned, loc)
+
+    def summed(part):
+        step = 1
+        while step < blocks:
+            part = part + lax.ppermute(part, "space", [(i, i ^ step) for i in range(blocks)])
+            step *= 2
+        return part
 
     place = lax.axis_index("orb").astype(jnp.int32).reshape(1)
     if groups == 2:
-        other = [lax.ppermute(piece, "orb", [(0, 1), (1, 0)]) for piece in narrow]
-        gram = pl.pallas_call(
-            functools.partial(gram_kernel, chunks),
-            out_shape=jax.ShapeDtypeStruct((3, half, half), jnp.float32),
-            in_specs=smem + vmem(2 * chunks),
+        swap = [(0, 1), (1, 0)]
+        other = lax.ppermute(narrow, "orb", swap)
+        tile = jax.ShapeDtypeStruct((half, half), jnp.float32)
+        params = pltpu.CompilerParams(vmem_limit_bytes=24 << 20)
+        near = pl.pallas_call(
+            own_gram_kernel,
+            out_shape=tile,
+            in_specs=vmem(2),
             out_specs=pl.BlockSpec(memory_space=pltpu.VMEM),
-            scratch_shapes=[pltpu.VMEM((2 * half, orbitals.shape[1]), jnp.bfloat16)],
-            compiler_params=pltpu.CompilerParams(vmem_limit_bytes=24 << 20),
-        )(place, *narrow, *other)
+            compiler_params=params,
+        )(filtered, narrow)
+        near = summed(near)
+        far = lax.ppermute(near, "orb", swap)
+        cross = pl.pallas_call(
+            cross_gram_kernel,
+            out_shape=tile,
+            in_specs=smem + vmem(2),
+            out_specs=pl.BlockSpec(memory_space=pltpu.VMEM),
+            compiler_params=params,
+        )(place, narrow, other)
+        upper, inverse = factorize(place, near, far, summed(cross))
     else:
-        columns = lax.all_gather(jnp.concatenate(narrow), "orb", axis=0, tiled=True)
-        whole = dot_nt(columns, columns)
-        gram = jnp.stack([whole[:half, :half], whole[:half, half:], whole[half:, half:]])
-    step = 1
-    while step < blocks:
-        gram = gram + lax.ppermute(gram, "space", [(i, i ^ step) for i in range(blocks)])
-        step *= 2
-    upper, inverse = factorize(gram)
+        columns = lax.all_gather(narrow, "orb", axis=0, tiled=True)
+        whole = summed(dot_nt(columns, columns))
+        upper, inverse = factorize(
+            jnp.zeros_like(place), whole[:half, :half], whole[half:, half:], whole[:half, half:]
+        )
     if groups == 2:
         basis = pl.pallas_call(
-            functools.partial(basis_kernel, chunks),
+            basis_kernel,
             out_shape=jax.ShapeDtypeStruct(orbitals.shape, jnp.float32),
-            in_specs=smem + vmem(1 + 2 * chunks),
+            in_specs=smem + vmem(3),
             out_specs=pl.BlockSpec(memory_space=pltpu.VMEM),
             compiler_params=pltpu.CompilerParams(vmem_limit_bytes=24 << 20),
-        )(place, inverse, *filtered, *other)
+        )(place, inverse, filtered, other)
     else:
         mine = lax.dynamic_slice_in_dim(inverse, place[0] * owned, owned, 0)
         near = lax.dynamic_slice_in_dim(mine, place[0] * owned, owned, 1)
-        rest = jnp.concatenate(filtered) - jnp.concatenate(narrow).astype(jnp.float32)
+        rest = filtered - narrow.astype(jnp.float32)
         basis = dot_full(mine, columns.astype(jnp.float32)) + dot_full(near, rest)
     return (basis, upper)
 

time: 98.7 us -> 84.7 us (0.86)
  waiting for transfers between devices: 31.7 us -> 15.4 us
  starting transfers between devices: 30.4 us -> 40.4 us
  Pallas kernels: 29.6 us -> 23.1 us
  local copies, waits for them, and re-layouts: 5.2 us -> 4.13 us
    ppermute x6 -> x10, waiting for transfers between devices: 31.6 us -> 4.73 us  [the longest x8 3.83 us: summed(): lax.ppermute(part, 'space', [(i, i ^ step) for i in range(blocks)])]
    ppermute x6 -> x10, starting transfers between devices: 2.44 us -> 24.9 us  [the longest x8 21.4 us: summed(): lax.ppermute(part, 'space', [(i, i ^ step) for i in range(blocks)])]
    ppermute x6 -> x3, starting transfers between devices: 27.2 us -> 5.11 us  [halo(): lax.ppermute(vec, 'space', backward)]
    ppermute x6 -> x3, waiting for transfers between devices: 0.02 us -> 10 us  [halo(): lax.ppermute(vec, 'space', forward)]
    ppermute x6 -> x3, starting transfers between devices: 0.74 us -> 10.3 us  [halo(): lax.ppermute(vec, 'space', forward)]
    pallas_call x4 -> x2, Pallas kernels: 6.52 us -> 3 us  [own_part(): pl.pallas_call(own_kernel, out_shape=jax.ShapeDtypeStruct(vec.shape, jnp....]
    pallas_call x6 -> x3, Pallas kernels: 6.68 us -> 3.49 us  [halo_part(): pl.pallas_call(functools.partial(halo_kernel, level), out_shape=[jax.Shap...]
    slice x1 -> x0, local copies, waits for them, and re-layouts: 1.07 us -> none  [shards(): orbitals[piece * share:(piece + 1) * share]]
  transfers between devices with their start and end apart: 18 -> 16, of which waited for: 6 -> 7; matrix products, arithmetic and copies ran while one was open for 1% -> 1% of each run, Pallas kernels for 16% -> 13%
where the time goes in v3:
time: 84.7 us; the launch traced here: 84.5 us
  starting transfers between devices  40.4 us (48%)
  Pallas kernels  23.1 us (27%)
  waiting for transfers between devices  15.4 us (18%)
  local copies, waits for them, and re-layouts  4.13 us (5%)
    ppermute x8, starting transfers between devices, summed(): lax.ppermute(part, 'space', [(i, i ^ step) for i in range(blocks)])  21.4 us
    ppermute x3, starting transfers between devices, halo(): lax.ppermute(vec, 'space', forward)  10.3 us
    ppermute x3, waiting for transfers between devices, halo(): lax.ppermute(vec, 'space', forward)  10 us
    pallas_call x1, Pallas kernels, factorize(): pl.pallas_call(second_kernel, out_shape=[jax.ShapeDtypeStruct((2 * half,...  6.53 us
    ppermute x3, starting transfers between devices, halo(): lax.ppermute(vec, 'space', backward)  5.11 us
    pallas_call x1, Pallas kernels, factorize(): pl.pallas_call(first_kernel, out_shape=[tile] * 2, in_specs=smem + vmem(2...  4.68 us
    unnamed x6, local copies, waits for them, and re-layouts  4.13 us
    ppermute x8, waiting for transfers between devices, summed(): lax.ppermute(part, 'space', [(i, i ^ step) for i in range(blocks)])  3.83 us
  transfers between devices with their start and end apart: 16, of which 7 were waited for; matrix products, arithmetic and copies ran while one was open for 1% of the time, Pallas kernels for 13%

profile of v3, /device:TPU:0, one launch (start us, length us, event | category | flops | bytes accessed | tf_op | source)
XLA Modules:
  0.0 84.5 jit_solution(14984755082215919875)
XLA Ops:
  0.6 0.5 collective-permute-start
  1.1 5.1 %collective-permute-start.1 = (bf16[128,2048]{1,0:T(8,128)(2,1)}, bf16[128,2048]{1,0:T(8,128)(2,1)S(1)}, u32[]{:S(2)}, u32[]{:S(2)}) collective-permute-start(bf16[128,2048]{1,0:T(8,128)(2,1)} %prior_ref.3), channel_id=1, source_target_pairs={{2,0},{4,2},{6,4},{8,6},{10,8},{12,10},{14,12},{16,14},{18,16},{20... | collective-permute-start | bytes 1572872 | tf_op jit(solution)/shard_map/ppermute | solution.py:327
  6.2 0.7 add_select_fusion.loc_ref
  6.9 0.0 copy-start
  6.9 1.0 %copy-done = bf16[128,2048]{1,0:T(8,128)(2,1)S(1)} copy-done((bf16[128,2048]{1,0:T(8,128)(2,1)S(1)}, bf16[128,2048]{1,0:T(8,128)(2,1)}, u32[]{:S(2)}) %copy-start) | copy-done | bytes 524312
  7.9 0.0 copy-start.2
  7.9 3.1 %copy-done.2 = bf16[8,7,256,256]{3,2,1,0:T(8,128)(2,1)S(1)} copy-done((bf16[8,7,256,256]{3,2,1,0:T(8,128)(2,1)S(1)}, bf16[8,7,256,256]{3,2,1,0:T(8,128)(2,1)}, u32[]{:S(2)}) %copy-start.2) | copy-done | bytes 7340056
  11.0 0.0 copy-start.1
  11.0 2.7 %shard_map.50 = (bf16[8,7,256,256]{3,2,1,0:T(8,128)(2,1)S(1)}, f32[128,2048]{1,0:T(8,128)S(1)}) custom-call(s32[8,6]{1,0:T(8,128)S(1)} %add_select_fusion.loc_ref, bf16[128,2048]{1,0:T(8,128)(2,1)S(1)} %copy-done, bf16[8,7,256,256]{3,2,1,0:T(8,128)(2,1)S(1)} %copy-done.2), custom_call_target="tpu_custom_call" | custom-call | flops 671088640 | bytes 14680064 | tf_op jit(solution)/shard_map/pallas_call | solution.py:53
  13.8 0.0 collective-permute-done.low_ref
  13.8 0.0 collective-permute-done.1.high_ref
  13.8 0.0 copy-done.1
  13.8 1.1 %shard_map.51.vec_ref.prior_ref = bf16[128,2048]{1,0:T(8,128)(2,1)S(1)} custom-call(s32[8,6]{1,0:T(8,128)S(1)} %add_select_fusion.loc_ref, bf16[128,2048]{1,0:T(8,128)(2,1)S(1)} %collective-permute-done.low_ref, bf16[128,2048]{1,0:T(8,128)(2,1)S(1)} %collective-permute-done.1.high_ref, f32[128,2048]{1,0:T(8,128)S(1)} %get-tuple-element.10.acc_ref, ...), custom_call_target="tpu_custom_call" | custom-call | flops 268435456 | bytes 2097152 | tf_op jit(solution)/shard_map/pallas_call | solution.py:121
  14.9 4.4 %collective-permute-start.2 = (bf16[128,2048]{1,0:T(8,128)(2,1)S(1)}, bf16[128,2048]{1,0:T(8,128)(2,1)S(1)}, u32[]{:S(2)}, u32[]{:S(2)}) collective-permute-start(bf16[128,2048]{1,0:T(8,128)(2,1)S(1)} %shard_map.51.vec_ref.prior_ref), channel_id=1, source_target_pairs={{0,2},{2,4},{4,6},{6,8},{8,10},{10,12},{12,14},{14,16},{16,18},{18... | collective-permute-start | bytes 1572872 | tf_op jit(solution)/shard_map/ppermute | solution.py:327
  19.4 0.0 collective-permute-start.3
  19.4 1.5 %shard_map.52.acc_ref = f32[128,2048]{1,0:T(8,128)S(1)} custom-call(s32[8,6]{1,0:T(8,128)S(1)} %add_select_fusion.loc_ref, bf16[128,2048]{1,0:T(8,128)(2,1)S(1)} %shard_map.51.vec_ref.prior_ref, bf16[8,7,256,256]{3,2,1,0:T(8,128)(2,1)S(1)} %get-tuple-element.11.turned_ref), custom_call_target="tpu_custom_call" | custom-call | flops 671088640 | bytes 5242880 | tf_op jit(solution)/shard_map/pallas_call | solution.py:86
  20.9 5.5 %collective-permute-done.2.low_ref = bf16[128,2048]{1,0:T(8,128)(2,1)S(1)} collective-permute-done((bf16[128,2048]{1,0:T(8,128)(2,1)S(1)}, bf16[128,2048]{1,0:T(8,128)(2,1)S(1)}, u32[]{:S(2)}, u32[]{:S(2)}) %collective-permute-start.2) | collective-permute-done | bytes 524320 | tf_op jit(solution)/shard_map/ppermute | solution.py:327
  26.4 0.0 collective-permute-done.3.high_ref
  26.4 1.2 %shard_map.53.vec_ref = bf16[128,2048]{1,0:T(8,128)(2,1)S(1)} custom-call(s32[8,6]{1,0:T(8,128)S(1)} %add_select_fusion.loc_ref, bf16[128,2048]{1,0:T(8,128)(2,1)S(1)} %collective-permute-done.2.low_ref, bf16[128,2048]{1,0:T(8,128)(2,1)S(1)} %collective-permute-done.3.high_ref, f32[128,2048]{1,0:T(8,128)S(1)} %shard_map.52.acc_ref, ...), custom_call_target="tpu_custom_call" | custom-call | flops 268435456 | bytes 2097152 | tf_op jit(solution)/shard_map/pallas_call | solution.py:121
  27.6 5.4 %collective-permute-start.4 = (bf16[128,2048]{1,0:T(8,128)(2,1)S(1)}, bf16[128,2048]{1,0:T(8,128)(2,1)S(1)}, u32[]{:S(2)}, u32[]{:S(2)}) collective-permute-start(bf16[128,2048]{1,0:T(8,128)(2,1)S(1)} %shard_map.53.vec_ref), channel_id=1, source_target_pairs={{0,2},{2,4},{4,6},{6,8},{8,10},{10,12},{12,14},{14,16},{16,18},{18... | collective-permute-start | bytes 1572872 | tf_op jit(solution)/shard_map/ppermute | solution.py:327
  32.9 0.0 collective-permute-start.5
  33.0 1.5 %shard_map.54.acc_ref = f32[128,2048]{1,0:T(8,128)S(1)} custom-call(s32[8,6]{1,0:T(8,128)S(1)} %add_select_fusion.loc_ref, bf16[128,2048]{1,0:T(8,128)(2,1)S(1)} %shard_map.53.vec_ref, bf16[8,7,256,256]{3,2,1,0:T(8,128)(2,1)S(1)} %get-tuple-element.11.turned_ref), custom_call_target="tpu_custom_call" | custom-call | flops 671088640 | bytes 5242880 | tf_op jit(solution)/shard_map/pallas_call | solution.py:86
  34.5 4.6 %collective-permute-done.4.low_ref = bf16[128,2048]{1,0:T(8,128)(2,1)S(1)} collective-permute-done((bf16[128,2048]{1,0:T(8,128)(2,1)S(1)}, bf16[128,2048]{1,0:T(8,128)(2,1)S(1)}, u32[]{:S(2)}, u32[]{:S(2)}) %collective-permute-start.4) | collective-permute-done | bytes 524320 | tf_op jit(solution)/shard_map/ppermute | solution.py:327
  39.0 0.6 collective-permute-done.5.high_ref
  39.7 1.2 %shard_map.55 = (f32[128,2048]{1,0:T(8,128)S(1)}, bf16[128,2048]{1,0:T(8,128)(2,1)S(1)}) custom-call(s32[8,6]{1,0:T(8,128)S(1)} %add_select_fusion.loc_ref, bf16[128,2048]{1,0:T(8,128)(2,1)S(1)} %collective-permute-done.4.low_ref, bf16[128,2048]{1,0:T(8,128)(2,1)S(1)} %collective-permute-done.5.high_ref, f32[128,2048]{1,0:T(8,128)S(1)} %shard_map.54.acc_ref, ...), custom_call_target="tpu_custom_call" | custom-call | flops 268435456 | bytes 2097152 | tf_op jit(solution)/shard_map/pallas_call | solution.py:121
  40.8 1.9 %collective-permute-start.11 = (bf16[128,2048]{1,0:T(8,128)(2,1)S(1)}, bf16[128,2048]{1,0:T(8,128)(2,1)S(1)}, u32[]{:S(2)}, u32[]{:S(2)}) collective-permute-start(bf16[128,2048]{1,0:T(8,128)(2,1)S(1)} %get-tuple-element.13.high_ref.own_ref), channel_id=1, source_target_pairs={{0,1},{1,0},{2,3},{3,2},{4,5},{5,4},{6,7},{7,6},{8,9},{9,8},{10,11... | collective-permute-start | bytes 1572872 | tf_op jit(solution)/shard_map/ppermute | solution.py:347
  42.8 0.5 shard_map.56
  43.3 5.5 %collective-permute-start.6 = (f32[128,128]{1,0:T(8,128)S(1)}, f32[128,128]{1,0:T(8,128)S(1)}, u32[]{:S(2)}, u32[]{:S(2)}) collective-permute-start(f32[128,128]{1,0:T(8,128)S(1)} %shard_map.56), channel_id=1, source_target_pairs={{0,2},{2,0},{4,6},{6,4},{8,10},{10,8},{12,14},{14,12},{16,18},{18,... | collective-permute-start | bytes 196616 | tf_op jit(solution)/shard_map/ppermute | solution.py:340
  48.9 0.9 %collective-permute-done.6 = f32[128,128]{1,0:T(8,128)S(1)} collective-permute-done((f32[128,128]{1,0:T(8,128)S(1)}, f32[128,128]{1,0:T(8,128)S(1)}, u32[]{:S(2)}, u32[]{:S(2)}) %collective-permute-start.6) | collective-permute-done | bytes 65568 | tf_op jit(solution)/shard_map/ppermute | solution.py:340
  49.8 3.1 %collective-permute-start.7 = (f32[128,128]{1,0:T(8,128)S(1)}, f32[128,128]{1,0:T(8,128)S(1)}, u32[]{:S(2)}, u32[]{:S(2)}) collective-permute-start(f32[128,128]{1,0:T(8,128)S(1)} %add.31), channel_id=1, source_target_pairs={{0,4},{2,6},{4,0},{6,2},{8,12},{10,14},{12,8},{14,10},{16,20},{18,... | collective-permute-start | bytes 196616 | tf_op jit(solution)/shard_map/ppermute | solution.py:340
  52.8 0.0 collective-permute-done.11.other_ref
  52.8 0.3 shard_map.57
  53.2 2.8 %collective-permute-start.12 = (f32[128,128]{1,0:T(8,128)S(1)}, f32[128,128]{1,0:T(8,128)S(1)}, u32[]{:S(2)}, u32[]{:S(2)}) collective-permute-start(f32[128,128]{1,0:T(8,128)S(1)} %shard_map.57), channel_id=1, source_target_pairs={{0,2},{2,0},{4,6},{6,4},{8,10},{10,8},{12,14},{14,12},{16,18},{18,... | collective-permute-start | bytes 196616 | tf_op jit(solution)/shard_map/ppermute | solution.py:340
  55.9 0.0 collective-permute-done.7
  55.9 1.5 %collective-permute-start.8 = (f32[128,128]{1,0:T(8,128)S(1)}, f32[128,128]{1,0:T(8,128)S(1)}, u32[]{:S(2)}, u32[]{:S(2)}) collective-permute-start(f32[128,128]{1,0:T(8,128)S(1)} %add.32), channel_id=1, source_target_pairs={{0,8},{2,10},{4,12},{6,14},{8,0},{10,2},{12,4},{14,6},{16,24},{18,... | collective-permute-start | bytes 196616 | tf_op jit(solution)/shard_map/ppermute | solution.py:340
  57.4 0.0 collective-permute-done.12
  57.4 3.3 %collective-permute-start.13 = (f32[128,128]{1,0:T(8,128)S(1)}, f32[128,128]{1,0:T(8,128)S(1)}, u32[]{:S(2)}, u32[]{:S(2)}) collective-permute-start(f32[128,128]{1,0:T(8,128)S(1)} %add.35), channel_id=1, source_target_pairs={{0,4},{2,6},{4,0},{6,2},{8,12},{10,14},{12,8},{14,10},{16,20},{18,... | collective-permute-start | bytes 196616 | tf_op jit(solution)/shard_map/ppermute | solution.py:340
  60.8 0.0 collective-permute-done.8
  60.8 2.2 %collective-permute-start.9 = (f32[128,128]{1,0:T(8,128)S(1)}, f32[128,128]{1,0:T(8,128)S(1)}, u32[]{:S(2)}, u32[]{:S(2)}) collective-permute-start(f32[128,128]{1,0:T(8,128)S(1)} %add.33), channel_id=1, source_target_pairs={{0,16},{2,18},{4,20},{6,22},{8,24},{10,26},{12,28},{14,30},{16,0},... | collective-permute-start | bytes 196616 | tf_op jit(solution)/shard_map/ppermute | solution.py:340
  63.0 0.2 collective-permute-done.13
  63.2 1.2 %collective-permute-start.14 = (f32[128,128]{1,0:T(8,128)S(1)}, f32[128,128]{1,0:T(8,128)S(1)}, u32[]{:S(2)}, u32[]{:S(2)}) collective-permute-start(f32[128,128]{1,0:T(8,128)S(1)} %add.36), channel_id=1, source_target_pairs={{0,8},{2,10},{4,12},{6,14},{8,0},{10,2},{12,4},{14,6},{16,24},{18,... | collective-permute-start | bytes 196616 | tf_op jit(solution)/shard_map/ppermute | solution.py:340
  64.4 2.7 %collective-permute-done.9 = f32[128,128]{1,0:T(8,128)S(1)} collective-permute-done((f32[128,128]{1,0:T(8,128)S(1)}, f32[128,128]{1,0:T(8,128)S(1)}, u32[]{:S(2)}, u32[]{:S(2)}) %collective-permute-start.9) | collective-permute-done | bytes 65568 | tf_op jit(solution)/shard_map/ppermute | solution.py:340
  67.1 1.6 %collective-permute-start.10 = (f32[128,128]{1,0:T(8,128)S(1)}, f32[128,128]{1,0:T(8,128)S(1)}, u32[]{:S(2)}, u32[]{:S(2)}) collective-permute-start(f32[128,128]{1,0:T(8,128)S(1)} %add.34.own_ref), channel_id=1, source_target_pairs={{0,1},{1,0},{2,3},{3,2},{4,5},{5,4},{6,7},{7,6},{8,9},{9,8},{10,11... | collective-permute-start | bytes 196616 | tf_op jit(solution)/shard_map/ppermute | solution.py:358
  68.7 0.0 collective-permute-done.14
  68.7 1.9 %collective-permute-start.15 = (f32[128,128]{1,0:T(8,128)S(1)}, f32[128,128]{1,0:T(8,128)S(1)}, u32[]{:S(2)}, u32[]{:S(2)}) collective-permute-start(f32[128,128]{1,0:T(8,128)S(1)} %add.37), channel_id=1, source_target_pairs={{0,16},{2,18},{4,20},{6,22},{8,24},{10,26},{12,28},{14,30},{16,0},... | collective-permute-start | bytes 196616 | tf_op jit(solution)/shard_map/ppermute | solution.py:340
  70.5 0.9 %collective-permute-done.10.other_ref = f32[128,128]{1,0:T(8,128)S(1)} collective-permute-done((f32[128,128]{1,0:T(8,128)S(1)}, f32[128,128]{1,0:T(8,128)S(1)}, u32[]{:S(2)}, u32[]{:S(2)}) %collective-permute-start.10) | collective-permute-done | bytes 65568 | tf_op jit(solution)/shard_map/ppermute | solution.py:358
  71.4 4.7 %shard_map.58 = (f32[128,128]{1,0:T(8,128)S(1)}, f32[128,128]{1,0:T(8,128)S(1)}) custom-call(s32[1]{0:T(128)} %bitcast.place_ref, f32[128,128]{1,0:T(8,128)S(1)} %add.34.own_ref, f32[128,128]{1,0:T(8,128)S(1)} %collective-permute-done.10.other_ref), custom_call_target="tpu_custom_call" | custom-call | flops 4194304 | bytes 16777216 | tf_op jit(solution)/shard_map/pallas_call | solution.py:275
  76.1 0.0 collective-permute-done.15
  76.2 6.5 %shard_map.59 = (f32[256,256]{1,0:T(8,128)}, f32[256,256]{1,0:T(8,128)S(1)}) custom-call(s32[1]{0:T(128)} %bitcast.place_ref, f32[128,128]{1,0:T(8,128)S(1)} %add.34.own_ref, f32[128,128]{1,0:T(8,128)S(1)} %collective-permute-done.10.other_ref, f32[128,128]{1,0:T(8,128)S(1)} %add.38.cross_ref, f32[128,128]{1,0:T(8,128)S(1)} %get-tuple-element.14.first_ref, ...), custom_call_target="tpu_custom_call" | custom-call | tf_op jit(solution)/shard_map/pallas_call | solution.py:284
  82.7 1.8 %shard_map.60 = f32[128,2048]{1,0:T(8,128)} custom-call(s32[1]{0:T(128)} %bitcast.place_ref, f32[256,256]{1,0:T(8,128)S(1)} %get-tuple-element.16.inv_ref, f32[128,2048]{1,0:T(8,128)S(1)} %get-tuple-element.12.own_ref, bf16[128,2048]{1,0:T(8,128)(2,1)S(1)} %collective-permute-done.11.other_ref), custom_call_target="tpu_custom_call" | custom-call | tf_op jit(solution)/shard_map/pallas_call | solution.py:374
  (8 shorter events, 0.1 us)
Async XLA Ops:
  0.6 13.1 %collective-permute-start = (bf16[128,2048]{1,0:T(8,128)(2,1)}, bf16[128,2048]{1,0:T(8,128)(2,1)S(1)}, u32[]{:S(2)}, u32[]{:S(2)}) collective-permute-start(bf16[128,2048]{1,0:T(8,128)(2,1)} %prior_ref.3), channel_id=1, source_target_pairs={{0,2},{2,4},{4,6},{6,8},{8,10},{10,12},{12,14},{14,16},{16,18},{18... | collective-permute-start | bytes 1572872 | tf_op jit(solution)/shard_map/ppermute | solution.py:327
  1.1 12.6 %collective-permute-start.1 = (bf16[128,2048]{1,0:T(8,128)(2,1)}, bf16[128,2048]{1,0:T(8,128)(2,1)S(1)}, u32[]{:S(2)}, u32[]{:S(2)}) collective-permute-start(bf16[128,2048]{1,0:T(8,128)(2,1)} %prior_ref.3), channel_id=1, source_target_pairs={{2,0},{4,2},{6,4},{8,6},{10,8},{12,10},{14,12},{16,14},{18,16},{20... | collective-permute-start | bytes 1572872 | tf_op jit(solution)/shard_map/ppermute | solution.py:327
  6.9 1.0 %copy-start = (bf16[128,2048]{1,0:T(8,128)(2,1)S(1)}, bf16[128,2048]{1,0:T(8,128)(2,1)}, u32[]{:S(2)}) copy-start(bf16[128,2048]{1,0:T(8,128)(2,1)} %prior_ref.3) | copy-start | bytes 1572868
  7.9 3.1 %copy-start.2 = (bf16[8,7,256,256]{3,2,1,0:T(8,128)(2,1)S(1)}, bf16[8,7,256,256]{3,2,1,0:T(8,128)(2,1)}, u32[]{:S(2)}) copy-start(bf16[8,7,256,256]{3,2,1,0:T(8,128)(2,1)} %ham_ref.1) | copy-start | bytes 22020100
  11.0 2.8 %copy-start.1 = (bf16[128,2048]{1,0:T(8,128)(2,1)S(1)}, bf16[128,2048]{1,0:T(8,128)(2,1)}, u32[]{:S(2)}) copy-start(bf16[128,2048]{1,0:T(8,128)(2,1)} %prior_ref.3) | copy-start | bytes 1572868
  14.9 11.5 %collective-permute-start.2 = (bf16[128,2048]{1,0:T(8,128)(2,1)S(1)}, bf16[128,2048]{1,0:T(8,128)(2,1)S(1)}, u32[]{:S(2)}, u32[]{:S(2)}) collective-permute-start(bf16[128,2048]{1,0:T(8,128)(2,1)S(1)} %shard_map.51.vec_ref.prior_ref), channel_id=1, source_target_pairs={{0,2},{2,4},{4,6},{6,8},{8,10},{10,12},{12,14},{14,16},{16,18},{18... | collective-permute-start | bytes 1572872 | tf_op jit(solution)/shard_map/ppermute | solution.py:327
  19.4 7.0 %collective-permute-start.3 = (bf16[128,2048]{1,0:T(8,128)(2,1)S(1)}, bf16[128,2048]{1,0:T(8,128)(2,1)S(1)}, u32[]{:S(2)}, u32[]{:S(2)}) collective-permute-start(bf16[128,2048]{1,0:T(8,128)(2,1)S(1)} %shard_map.51.vec_ref.prior_ref), channel_id=1, source_target_pairs={{2,0},{4,2},{6,4},{8,6},{10,8},{12,10},{14,12},{16,14},{18,16},{20... | collective-permute-start | bytes 1572872 | tf_op jit(solution)/shard_map/ppermute | solution.py:327
  27.6 11.5 %collective-permute-start.4 = (bf16[128,2048]{1,0:T(8,128)(2,1)S(1)}, bf16[128,2048]{1,0:T(8,128)(2,1)S(1)}, u32[]{:S(2)}, u32[]{:S(2)}) collective-permute-start(bf16[128,2048]{1,0:T(8,128)(2,1)S(1)} %shard_map.53.vec_ref), channel_id=1, source_target_pairs={{0,2},{2,4},{4,6},{6,8},{8,10},{10,12},{12,14},{14,16},{16,18},{18... | collective-permute-start | bytes 1572872 | tf_op jit(solution)/shard_map/ppermute | solution.py:327
  32.9 6.7 %collective-permute-start.5 = (bf16[128,2048]{1,0:T(8,128)(2,1)S(1)}, bf16[128,2048]{1,0:T(8,128)(2,1)S(1)}, u32[]{:S(2)}, u32[]{:S(2)}) collective-permute-start(bf16[128,2048]{1,0:T(8,128)(2,1)S(1)} %shard_map.53.vec_ref), channel_id=1, source_target_pairs={{2,0},{4,2},{6,4},{8,6},{10,8},{12,10},{14,12},{16,14},{18,16},{20... | collective-permute-start | bytes 1572872 | tf_op jit(solution)/shard_map/ppermute | solution.py:327
  40.8 12.0 %collective-permute-start.11 = (bf16[128,2048]{1,0:T(8,128)(2,1)S(1)}, bf16[128,2048]{1,0:T(8,128)(2,1)S(1)}, u32[]{:S(2)}, u32[]{:S(2)}) collective-permute-start(bf16[128,2048]{1,0:T(8,128)(2,1)S(1)} %get-tuple-element.13.high_ref.own_ref), channel_id=1, source_target_pairs={{0,1},{1,0},{2,3},{3,2},{4,5},{5,4},{6,7},{7,6},{8,9},{9,8},{10,11... | collective-permute-start | bytes 1572872 | tf_op jit(solution)/shard_map/ppermute | solution.py:347
  43.3 6.5 %collective-permute-start.6 = (f32[128,128]{1,0:T(8,128)S(1)}, f32[128,128]{1,0:T(8,128)S(1)}, u32[]{:S(2)}, u32[]{:S(2)}) collective-permute-start(f32[128,128]{1,0:T(8,128)S(1)} %shard_map.56), channel_id=1, source_target_pairs={{0,2},{2,0},{4,6},{6,4},{8,10},{10,8},{12,14},{14,12},{16,18},{18,... | collective-permute-start | bytes 196616 | tf_op jit(solution)/shard_map/ppermute | solution.py:340
  49.8 6.1 %collective-permute-start.7 = (f32[128,128]{1,0:T(8,128)S(1)}, f32[128,128]{1,0:T(8,128)S(1)}, u32[]{:S(2)}, u32[]{:S(2)}) collective-permute-start(f32[128,128]{1,0:T(8,128)S(1)} %add.31), channel_id=1, source_target_pairs={{0,4},{2,6},{4,0},{6,2},{8,12},{10,14},{12,8},{14,10},{16,20},{18,... | collective-permute-start | bytes 196616 | tf_op jit(solution)/shard_map/ppermute | solution.py:340
  53.2 4.3 %collective-permute-start.12 = (f32[128,128]{1,0:T(8,128)S(1)}, f32[128,128]{1,0:T(8,128)S(1)}, u32[]{:S(2)}, u32[]{:S(2)}) collective-permute-start(f32[128,128]{1,0:T(8,128)S(1)} %shard_map.57), channel_id=1, source_target_pairs={{0,2},{2,0},{4,6},{6,4},{8,10},{10,8},{12,14},{14,12},{16,18},{18,... | collective-permute-start | bytes 196616 | tf_op jit(solution)/shard_map/ppermute | solution.py:340
  55.9 4.8 %collective-permute-start.8 = (f32[128,128]{1,0:T(8,128)S(1)}, f32[128,128]{1,0:T(8,128)S(1)}, u32[]{:S(2)}, u32[]{:S(2)}) collective-permute-start(f32[128,128]{1,0:T(8,128)S(1)} %add.32), channel_id=1, source_target_pairs={{0,8},{2,10},{4,12},{6,14},{8,0},{10,2},{12,4},{14,6},{16,24},{18,... | collective-permute-start | bytes 196616 | tf_op jit(solution)/shard_map/ppermute | solution.py:340
  57.4 5.8 %collective-permute-start.13 = (f32[128,128]{1,0:T(8,128)S(1)}, f32[128,128]{1,0:T(8,128)S(1)}, u32[]{:S(2)}, u32[]{:S(2)}) collective-permute-start(f32[128,128]{1,0:T(8,128)S(1)} %add.35), channel_id=1, source_target_pairs={{0,4},{2,6},{4,0},{6,2},{8,12},{10,14},{12,8},{14,10},{16,20},{18,... | collective-permute-start | bytes 196616 | tf_op jit(solution)/shard_map/ppermute | solution.py:340
  60.8 6.3 %collective-permute-start.9 = (f32[128,128]{1,0:T(8,128)S(1)}, f32[128,128]{1,0:T(8,128)S(1)}, u32[]{:S(2)}, u32[]{:S(2)}) collective-permute-start(f32[128,128]{1,0:T(8,128)S(1)} %add.33), channel_id=1, source_target_pairs={{0,16},{2,18},{4,20},{6,22},{8,24},{10,26},{12,28},{14,30},{16,0},... | collective-permute-start | bytes 196616 | tf_op jit(solution)/shard_map/ppermute | solution.py:340
  63.2 5.4 %collective-permute-start.14 = (f32[128,128]{1,0:T(8,128)S(1)}, f32[128,128]{1,0:T(8,128)S(1)}, u32[]{:S(2)}, u32[]{:S(2)}) collective-permute-start(f32[128,128]{1,0:T(8,128)S(1)} %add.36), channel_id=1, source_target_pairs={{0,8},{2,10},{4,12},{6,14},{8,0},{10,2},{12,4},{14,6},{16,24},{18,... | collective-permute-start | bytes 196616 | tf_op jit(solution)/shard_map/ppermute | solution.py:340
  67.1 4.3 %collective-permute-start.10 = (f32[128,128]{1,0:T(8,128)S(1)}, f32[128,128]{1,0:T(8,128)S(1)}, u32[]{:S(2)}, u32[]{:S(2)}) collective-permute-start(f32[128,128]{1,0:T(8,128)S(1)} %add.34.own_ref), channel_id=1, source_target_pairs={{0,1},{1,0},{2,3},{3,2},{4,5},{5,4},{6,7},{7,6},{8,9},{9,8},{10,11... | collective-permute-start | bytes 196616 | tf_op jit(solution)/shard_map/ppermute | solution.py:358
  68.7 7.5 %collective-permute-start.15 = (f32[128,128]{1,0:T(8,128)S(1)}, f32[128,128]{1,0:T(8,128)S(1)}, u32[]{:S(2)}, u32[]{:S(2)}) collective-permute-start(f32[128,128]{1,0:T(8,128)S(1)} %add.37), channel_id=1, source_target_pairs={{0,16},{2,18},{4,20},{6,22},{8,24},{10,26},{12,28},{14,30},{16,0},... | collective-permute-start | bytes 196616 | tf_op jit(solution)/shard_map/ppermute | solution.py:340

commit v4 on v3

--- a/solution.py
+++ b/solution.py
@@ -335,11 +335,10 @@
     filtered, narrow = halo_part(3, *side, own_part(two, turned, loc), two, one, turned, loc)
 
     def summed(part):
-        step = 1
-        while step < blocks:
-            part = part + lax.ppermute(part, "space", [(i, i ^ step) for i in range(blocks)])
-            step *= 2
-        return part
+        pieces = part.reshape(blocks, part.shape[0] // blocks, part.shape[1])
+        owned_sum = jnp.sum(lax.all_to_all(pieces, "space", 0, 0), axis=0)
+        spread = jnp.broadcast_to(owned_sum, pieces.shape)
+        return lax.all_to_all(spread, "space", 0, 0).reshape(part.shape)
 
     place = lax.axis_index("orb").astype(jnp.int32).reshape(1)
     if groups == 2:

time: 84.7 us -> 106 us (1.25)
  waiting for transfers between devices: 15.4 us -> 34.4 us
  local copies, waits for them, and re-layouts: 4.13 us -> 5.4 us
  Pallas kernels: 23.1 us -> 24.3 us
    all_to_all x0 -> x4, starting transfers between devices: none -> 22.7 us  [the longest x2 15.7 us: summed(): owned_sum = jnp.sum(lax.all_to_all(pieces, 'space', 0, 0), axis=0)]
    ppermute x8 -> x0, starting transfers between devices: 21.4 us -> none  [summed(): lax.ppermute(part, 'space', [(i, i ^ step) for i in range(blocks)])]
    all_to_all x0 -> x4, waiting for transfers between devices: none -> 19.6 us  [the longest x2 12.8 us: summed(): owned_sum = jnp.sum(lax.all_to_all(pieces, 'space', 0, 0), axis=0)]
    ppermute x8 -> x0, waiting for transfers between devices: 3.83 us -> none  [summed(): lax.ppermute(part, 'space', [(i, i ^ step) for i in range(blocks)])]
    ppermute x1, waiting for transfers between devices: 0.89 us -> 4.11 us  [shards(): far = lax.ppermute(near, 'orb', swap)]
    ppermute x1, starting transfers between devices: 1.55 us -> 0.22 us  [shards(): far = lax.ppermute(near, 'orb', swap)]
    broadcast_in_dim x0 -> x2, local copies, waits for them, and re-layouts: none -> 1.27 us  [summed(): spread = jnp.broadcast_to(owned_sum, pieces.shape)]
  transfers between devices with their start and end apart: 16 -> 12, of which waited for: 7 -> 7; matrix products, arithmetic and copies ran while one was open for 1% -> 1% of each run, Pallas kernels for 13% -> 12%
where the time goes in v4:
time: 106 us
  starting transfers between devices  40.3 us (38%)
  waiting for transfers between devices  34.4 us (32%)
  Pallas kernels  24.3 us (23%)
  local copies, waits for them, and re-layouts  5.4 us (5%)
    all_to_all x2, starting transfers between devices, summed(): owned_sum = jnp.sum(lax.all_to_all(pieces, 'space', 0, 0), axis=0)  15.7 us
    all_to_all x2, waiting for transfers between devices, summed(): owned_sum = jnp.sum(lax.all_to_all(pieces, 'space', 0, 0), axis=0)  12.8 us
    ppermute x3, starting transfers between devices, halo(): lax.ppermute(vec, 'space', forward)  10.4 us
    ppermute x3, waiting for transfers between devices, halo(): lax.ppermute(vec, 'space', forward)  10 us
    all_to_all x2, starting transfers between devices, summed(): return lax.all_to_all(spread, 'space', 0, 0).reshape(part.shape)  7.01 us
    all_to_all x2, waiting for transfers between devices, summed(): return lax.all_to_all(spread, 'space', 0, 0).reshape(part.shape)  6.84 us
    pallas_call x1, Pallas kernels, factorize(): pl.pallas_call(second_kernel, out_shape=[jax.ShapeDtypeStruct((2 * half,...  6.53 us
    ppermute x3, starting transfers between devices, halo(): lax.ppermute(vec, 'space', backward)  5.09 us
  transfers between devices with their start and end apart: 12, of which 7 were waited for; matrix products, arithmetic and copies ran while one was open for 1% of the time, Pallas kernels for 12%

profile of v4, /device:TPU:0, one launch (start us, length us, event | category | flops | bytes accessed | tf_op | source)
XLA Modules:
  0.0 105.9 jit_solution(7325142744667679809)
XLA Ops:
  0.6 0.5 collective-permute-start
  1.1 5.1 %collective-permute-start.1 = (bf16[128,2048]{1,0:T(8,128)(2,1)}, bf16[128,2048]{1,0:T(8,128)(2,1)S(1)}, u32[]{:S(2)}, u32[]{:S(2)}) collective-permute-start(bf16[128,2048]{1,0:T(8,128)(2,1)} %prior_ref.3), channel_id=1, source_target_pairs={{2,0},{4,2},{6,4},{8,6},{10,8},{12,10},{14,12},{16,14},{18,16},{20... | collective-permute-start | bytes 1572872 | tf_op jit(solution)/shard_map/ppermute | solution.py:327
  6.2 0.7 add_select_fusion.loc_ref
  6.9 0.0 copy-start
  6.9 1.0 copy-done
  7.9 0.0 copy-start.2
  7.9 3.1 %copy-done.2 = bf16[8,7,256,256]{3,2,1,0:T(8,128)(2,1)S(1)} copy-done((bf16[8,7,256,256]{3,2,1,0:T(8,128)(2,1)S(1)}, bf16[8,7,256,256]{3,2,1,0:T(8,128)(2,1)}, u32[]{:S(2)}) %copy-start.2) | copy-done | bytes 7340056
  11.0 0.0 copy-start.1
  11.0 2.7 %shard_map.50 = (bf16[8,7,256,256]{3,2,1,0:T(8,128)(2,1)S(1)}, f32[128,2048]{1,0:T(8,128)S(1)}) custom-call(s32[8,6]{1,0:T(8,128)S(1)} %add_select_fusion.loc_ref, bf16[128,2048]{1,0:T(8,128)(2,1)S(1)} %copy-done, bf16[8,7,256,256]{3,2,1,0:T(8,128)(2,1)S(1)} %copy-done.2), custom_call_target="tpu_custom_call" | custom-call | flops 671088640 | bytes 14680064 | tf_op jit(solution)/shard_map/pallas_call | solution.py:53
  13.8 0.0 collective-permute-done.low_ref
  13.8 0.0 collective-permute-done.1.high_ref
  13.8 0.0 copy-done.1
  13.8 1.1 %shard_map.51.vec_ref.prior_ref = bf16[128,2048]{1,0:T(8,128)(2,1)S(1)} custom-call(s32[8,6]{1,0:T(8,128)S(1)} %add_select_fusion.loc_ref, bf16[128,2048]{1,0:T(8,128)(2,1)S(1)} %collective-permute-done.low_ref, bf16[128,2048]{1,0:T(8,128)(2,1)S(1)} %collective-permute-done.1.high_ref, f32[128,2048]{1,0:T(8,128)S(1)} %get-tuple-element.10.acc_ref, ...), custom_call_target="tpu_custom_call" | custom-call | flops 268435456 | bytes 2097152 | tf_op jit(solution)/shard_map/pallas_call | solution.py:121
  14.9 4.5 %collective-permute-start.2 = (bf16[128,2048]{1,0:T(8,128)(2,1)S(1)}, bf16[128,2048]{1,0:T(8,128)(2,1)S(1)}, u32[]{:S(2)}, u32[]{:S(2)}) collective-permute-start(bf16[128,2048]{1,0:T(8,128)(2,1)S(1)} %shard_map.51.vec_ref.prior_ref), channel_id=1, source_target_pairs={{0,2},{2,4},{4,6},{6,8},{8,10},{10,12},{12,14},{14,16},{16,18},{18... | collective-permute-start | bytes 1572872 | tf_op jit(solution)/shard_map/ppermute | solution.py:327
  19.4 0.0 collective-permute-start.3
  19.4 1.5 %shard_map.52.acc_ref = f32[128,2048]{1,0:T(8,128)S(1)} custom-call(s32[8,6]{1,0:T(8,128)S(1)} %add_select_fusion.loc_ref, bf16[128,2048]{1,0:T(8,128)(2,1)S(1)} %shard_map.51.vec_ref.prior_ref, bf16[8,7,256,256]{3,2,1,0:T(8,128)(2,1)S(1)} %get-tuple-element.11.turned_ref), custom_call_target="tpu_custom_call" | custom-call | flops 671088640 | bytes 5242880 | tf_op jit(solution)/shard_map/pallas_call | solution.py:86
  20.9 5.5 %collective-permute-done.2.low_ref = bf16[128,2048]{1,0:T(8,128)(2,1)S(1)} collective-permute-done((bf16[128,2048]{1,0:T(8,128)(2,1)S(1)}, bf16[128,2048]{1,0:T(8,128)(2,1)S(1)}, u32[]{:S(2)}, u32[]{:S(2)}) %collective-permute-start.2) | collective-permute-done | bytes 524320 | tf_op jit(solution)/shard_map/ppermute | solution.py:327
  26.4 0.0 collective-permute-done.3.high_ref
  26.4 1.2 %shard_map.53.vec_ref = bf16[128,2048]{1,0:T(8,128)(2,1)S(1)} custom-call(s32[8,6]{1,0:T(8,128)S(1)} %add_select_fusion.loc_ref, bf16[128,2048]{1,0:T(8,128)(2,1)S(1)} %collective-permute-done.2.low_ref, bf16[128,2048]{1,0:T(8,128)(2,1)S(1)} %collective-permute-done.3.high_ref, f32[128,2048]{1,0:T(8,128)S(1)} %shard_map.52.acc_ref, ...), custom_call_target="tpu_custom_call" | custom-call | flops 268435456 | bytes 2097152 | tf_op jit(solution)/shard_map/pallas_call | solution.py:121
  27.5 5.4 %collective-permute-start.4 = (bf16[128,2048]{1,0:T(8,128)(2,1)S(1)}, bf16[128,2048]{1,0:T(8,128)(2,1)S(1)}, u32[]{:S(2)}, u32[]{:S(2)}) collective-permute-start(bf16[128,2048]{1,0:T(8,128)(2,1)S(1)} %shard_map.53.vec_ref), channel_id=1, source_target_pairs={{0,2},{2,4},{4,6},{6,8},{8,10},{10,12},{12,14},{14,16},{16,18},{18... | collective-permute-start | bytes 1572872 | tf_op jit(solution)/shard_map/ppermute | solution.py:327
  32.9 0.0 collective-permute-start.5
  32.9 1.5 %shard_map.54.acc_ref = f32[128,2048]{1,0:T(8,128)S(1)} custom-call(s32[8,6]{1,0:T(8,128)S(1)} %add_select_fusion.loc_ref, bf16[128,2048]{1,0:T(8,128)(2,1)S(1)} %shard_map.53.vec_ref, bf16[8,7,256,256]{3,2,1,0:T(8,128)(2,1)S(1)} %get-tuple-element.11.turned_ref), custom_call_target="tpu_custom_call" | custom-call | flops 671088640 | bytes 5242880 | tf_op jit(solution)/shard_map/pallas_call | solution.py:86
  34.4 4.6 %collective-permute-done.4.low_ref = bf16[128,2048]{1,0:T(8,128)(2,1)S(1)} collective-permute-done((bf16[128,2048]{1,0:T(8,128)(2,1)S(1)}, bf16[128,2048]{1,0:T(8,128)(2,1)S(1)}, u32[]{:S(2)}, u32[]{:S(2)}) %collective-permute-start.4) | collective-permute-done | bytes 524320 | tf_op jit(solution)/shard_map/ppermute | solution.py:327
  39.0 0.6 collective-permute-done.5.high_ref
  39.6 1.2 %shard_map.55 = (f32[128,2048]{1,0:T(8,128)S(1)}, bf16[128,2048]{1,0:T(8,128)(2,1)S(1)}) custom-call(s32[8,6]{1,0:T(8,128)S(1)} %add_select_fusion.loc_ref, bf16[128,2048]{1,0:T(8,128)(2,1)S(1)} %collective-permute-done.4.low_ref, bf16[128,2048]{1,0:T(8,128)(2,1)S(1)} %collective-permute-done.5.high_ref, f32[128,2048]{1,0:T(8,128)S(1)} %shard_map.54.acc_ref, ...), custom_call_target="tpu_custom_call" | custom-call | flops 268435456 | bytes 2097152 | tf_op jit(solution)/shard_map/pallas_call | solution.py:121
  40.8 1.9 %collective-permute-start.7 = (bf16[128,2048]{1,0:T(8,128)(2,1)S(1)}, bf16[128,2048]{1,0:T(8,128)(2,1)S(1)}, u32[]{:S(2)}, u32[]{:S(2)}) collective-permute-start(bf16[128,2048]{1,0:T(8,128)(2,1)S(1)} %get-tuple-element.13.high_ref.own_ref), channel_id=1, source_target_pairs={{0,1},{1,0},{2,3},{3,2},{4,5},{5,4},{6,7},{7,6},{8,9},{9,8},{10,11... | collective-permute-start | bytes 1572872 | tf_op jit(solution)/shard_map/ppermute | solution.py:346
  42.8 1.1 %shard_map.56 = f32[128,128]{1,0:T(8,128)} custom-call(f32[128,2048]{1,0:T(8,128)S(1)} %get-tuple-element.12.own_ref, bf16[128,2048]{1,0:T(8,128)(2,1)S(1)} %get-tuple-element.13.high_ref.own_ref), custom_call_target="tpu_custom_call" | custom-call | tf_op jit(solution)/shard_map/pallas_call | solution.py:349
  43.9 12.2 %all-to-all-start = ((f32[16,8,128]{2,1,0:T(8,128)}), f32[16,8,128]{2,1,0:T(8,128)S(1)}, u32[]{:S(2)}, u32[]{:S(2)}) async-start(f32[16,8,128]{2,1,0:T(8,128)} %bitcast.1), calls=%async_computation | async-start | bytes 131072 | tf_op jit(solution)/shard_map/all_to_all | solution.py:339
  56.1 0.0 collective-permute-done.7.other_ref
  56.1 0.9 shard_map.57
  57.0 5.9 %all-to-all-done = f32[16,8,128]{2,1,0:T(8,128)S(1)} async-done(((f32[16,8,128]{2,1,0:T(8,128)}), f32[16,8,128]{2,1,0:T(8,128)S(1)}, u32[]{:S(2)}, u32[]{:S(2)}) %all-to-all-start) | async-done | bytes 65568 | tf_op jit(solution)/shard_map/all_to_all | solution.py:339
  63.0 3.5 %all-to-all-start.2 = ((f32[16,8,128]{2,1,0:T(8,128)}), f32[16,8,128]{2,1,0:T(8,128)S(1)}, u32[]{:S(2)}, u32[]{:S(2)}) async-start(f32[16,8,128]{2,1,0:T(8,128)} %bitcast.3), calls=%async_computation.2 | async-start | bytes 131072 | tf_op jit(solution)/shard_map/all_to_all | solution.py:339
  66.5 6.8 %all-to-all-done.2 = f32[16,8,128]{2,1,0:T(8,128)S(1)} async-done(((f32[16,8,128]{2,1,0:T(8,128)}), f32[16,8,128]{2,1,0:T(8,128)S(1)}, u32[]{:S(2)}, u32[]{:S(2)}) %all-to-all-start.2) | async-done | bytes 65568 | tf_op jit(solution)/shard_map/all_to_all | solution.py:339
  73.4 0.6 broadcast_in_dim.6
  74.0 3.5 %all-to-all-start.1 = ((f32[16,8,128]{2,1,0:T(8,128)}), f32[16,8,128]{2,1,0:T(8,128)S(1)}, u32[]{:S(2)}, u32[]{:S(2)}) async-start(f32[16,8,128]{2,1,0:T(8,128)} %broadcast_in_dim.6), calls=%async_computation.1 | async-start | bytes 131072 | tf_op jit(solution)/shard_map/all_to_all | solution.py:341
  77.5 6.8 %all-to-all-done.1 = f32[16,8,128]{2,1,0:T(8,128)S(1)} async-done(((f32[16,8,128]{2,1,0:T(8,128)}), f32[16,8,128]{2,1,0:T(8,128)S(1)}, u32[]{:S(2)}, u32[]{:S(2)}) %all-to-all-start.1) | async-done | bytes 65568 | tf_op jit(solution)/shard_map/all_to_all | solution.py:341
  84.4 0.6 broadcast_in_dim.7
  85.0 3.5 %all-to-all-start.3 = ((f32[16,8,128]{2,1,0:T(8,128)}), f32[16,8,128]{2,1,0:T(8,128)S(1)}, u32[]{:S(2)}, u32[]{:S(2)}) async-start(f32[16,8,128]{2,1,0:T(8,128)} %broadcast_in_dim.7), calls=%async_computation.3 | async-start | bytes 131072 | tf_op jit(solution)/shard_map/all_to_all | solution.py:341
  88.5 0.2 collective-permute-start.6
  88.7 4.1 %collective-permute-done.6.other_ref = f32[128,128]{1,0:T(8,128)S(1)} collective-permute-done((f32[128,128]{1,0:T(8,128)S(1)}, f32[128,128]{1,0:T(8,128)S(1)}, u32[]{:S(2)}, u32[]{:S(2)}) %collective-permute-start.6) | collective-permute-done | bytes 65568 | tf_op jit(solution)/shard_map/ppermute | solution.py:357
  92.8 4.7 %shard_map.58 = (f32[128,128]{1,0:T(8,128)S(1)}, f32[128,128]{1,0:T(8,128)S(1)}) custom-call(s32[1]{0:T(128)} %bitcast.place_ref, f32[128,128]{1,0:T(8,128)S(1)} %bitcast.6, f32[128,128]{1,0:T(8,128)S(1)} %collective-permute-done.6.other_ref), custom_call_target="tpu_custom_call" | custom-call | flops 4194304 | bytes 16777216 | tf_op jit(solution)/shard_map/pallas_call | solution.py:275
  97.5 0.0 all-to-all-done.3
  97.5 6.5 %shard_map.59 = (f32[256,256]{1,0:T(8,128)}, f32[256,256]{1,0:T(8,128)S(1)}) custom-call(s32[1]{0:T(128)} %bitcast.place_ref, f32[128,128]{1,0:T(8,128)S(1)} %bitcast.7, f32[128,128]{1,0:T(8,128)S(1)} %collective-permute-done.6.other_ref, f32[128,128]{1,0:T(8,128)S(1)} %bitcast.8, f32[128,128]{1,0:T(8,128)S(1)} %get-tuple-element.14.first_ref, ...), custom_call_target="tpu_custom_call" | custom-call | tf_op jit(solution)/shard_map/pallas_call | solution.py:284
  104.1 1.8 %shard_map.60 = f32[128,2048]{1,0:T(8,128)} custom-call(s32[1]{0:T(128)} %bitcast.place_ref, f32[256,256]{1,0:T(8,128)S(1)} %get-tuple-element.16.inv_ref, f32[128,2048]{1,0:T(8,128)S(1)} %get-tuple-element.12.own_ref, bf16[128,2048]{1,0:T(8,128)(2,1)S(1)} %collective-permute-done.7.other_ref), custom_call_target="tpu_custom_call" | custom-call | tf_op jit(solution)/shard_map/pallas_call | solution.py:373
  (2 shorter events, 0.0 us)
Async XLA Ops:
  0.6 13.1 %collective-permute-start = (bf16[128,2048]{1,0:T(8,128)(2,1)}, bf16[128,2048]{1,0:T(8,128)(2,1)S(1)}, u32[]{:S(2)}, u32[]{:S(2)}) collective-permute-start(bf16[128,2048]{1,0:T(8,128)(2,1)} %prior_ref.3), channel_id=1, source_target_pairs={{0,2},{2,4},{4,6},{6,8},{8,10},{10,12},{12,14},{14,16},{16,18},{18... | collective-permute-start | bytes 1572872 | tf_op jit(solution)/shard_map/ppermute | solution.py:327
  1.1 12.6 %collective-permute-start.1 = (bf16[128,2048]{1,0:T(8,128)(2,1)}, bf16[128,2048]{1,0:T(8,128)(2,1)S(1)}, u32[]{:S(2)}, u32[]{:S(2)}) collective-permute-start(bf16[128,2048]{1,0:T(8,128)(2,1)} %prior_ref.3), channel_id=1, source_target_pairs={{2,0},{4,2},{6,4},{8,6},{10,8},{12,10},{14,12},{16,14},{18,16},{20... | collective-permute-start | bytes 1572872 | tf_op jit(solution)/shard_map/ppermute | solution.py:327
  6.9 1.0 copy-start
  7.9 3.1 %copy-start.2 = (bf16[8,7,256,256]{3,2,1,0:T(8,128)(2,1)S(1)}, bf16[8,7,256,256]{3,2,1,0:T(8,128)(2,1)}, u32[]{:S(2)}) copy-start(bf16[8,7,256,256]{3,2,1,0:T(8,128)(2,1)} %ham_ref.1) | copy-start | bytes 22020100
  11.0 2.8 %copy-start.1 = (bf16[128,2048]{1,0:T(8,128)(2,1)S(1)}, bf16[128,2048]{1,0:T(8,128)(2,1)}, u32[]{:S(2)}) copy-start(bf16[128,2048]{1,0:T(8,128)(2,1)} %prior_ref.3) | copy-start | bytes 1572868
  14.9 11.5 %collective-permute-start.2 = (bf16[128,2048]{1,0:T(8,128)(2,1)S(1)}, bf16[128,2048]{1,0:T(8,128)(2,1)S(1)}, u32[]{:S(2)}, u32[]{:S(2)}) collective-permute-start(bf16[128,2048]{1,0:T(8,128)(2,1)S(1)} %shard_map.51.vec_ref.prior_ref), channel_id=1, source_target_pairs={{0,2},{2,4},{4,6},{6,8},{8,10},{10,12},{12,14},{14,16},{16,18},{18... | collective-permute-start | bytes 1572872 | tf_op jit(solution)/shard_map/ppermute | solution.py:327
  19.4 7.0 %collective-permute-start.3 = (bf16[128,2048]{1,0:T(8,128)(2,1)S(1)}, bf16[128,2048]{1,0:T(8,128)(2,1)S(1)}, u32[]{:S(2)}, u32[]{:S(2)}) collective-permute-start(bf16[128,2048]{1,0:T(8,128)(2,1)S(1)} %shard_map.51.vec_ref.prior_ref), channel_id=1, source_target_pairs={{2,0},{4,2},{6,4},{8,6},{10,8},{12,10},{14,12},{16,14},{18,16},{20... | collective-permute-start | bytes 1572872 | tf_op jit(solution)/shard_map/ppermute | solution.py:327
  27.5 11.5 %collective-permute-start.4 = (bf16[128,2048]{1,0:T(8,128)(2,1)S(1)}, bf16[128,2048]{1,0:T(8,128)(2,1)S(1)}, u32[]{:S(2)}, u32[]{:S(2)}) collective-permute-start(bf16[128,2048]{1,0:T(8,128)(2,1)S(1)} %shard_map.53.vec_ref), channel_id=1, source_target_pairs={{0,2},{2,4},{4,6},{6,8},{8,10},{10,12},{12,14},{14,16},{16,18},{18... | collective-permute-start | bytes 1572872 | tf_op jit(solution)/shard_map/ppermute | solution.py:327
  32.9 6.7 %collective-permute-start.5 = (bf16[128,2048]{1,0:T(8,128)(2,1)S(1)}, bf16[128,2048]{1,0:T(8,128)(2,1)S(1)}, u32[]{:S(2)}, u32[]{:S(2)}) collective-permute-start(bf16[128,2048]{1,0:T(8,128)(2,1)S(1)} %shard_map.53.vec_ref), channel_id=1, source_target_pairs={{2,0},{4,2},{6,4},{8,6},{10,8},{12,10},{14,12},{16,14},{18,16},{20... | collective-permute-start | bytes 1572872 | tf_op jit(solution)/shard_map/ppermute | solution.py:327
  40.8 15.3 %collective-permute-start.7 = (bf16[128,2048]{1,0:T(8,128)(2,1)S(1)}, bf16[128,2048]{1,0:T(8,128)(2,1)S(1)}, u32[]{:S(2)}, u32[]{:S(2)}) collective-permute-start(bf16[128,2048]{1,0:T(8,128)(2,1)S(1)} %get-tuple-element.13.high_ref.own_ref), channel_id=1, source_target_pairs={{0,1},{1,0},{2,3},{3,2},{4,5},{5,4},{6,7},{7,6},{8,9},{9,8},{10,11... | collective-permute-start | bytes 1572872 | tf_op jit(solution)/shard_map/ppermute | solution.py:346
  43.9 19.1 %all-to-all-start = ((f32[16,8,128]{2,1,0:T(8,128)}), f32[16,8,128]{2,1,0:T(8,128)S(1)}, u32[]{:S(2)}, u32[]{:S(2)}) async-start(f32[16,8,128]{2,1,0:T(8,128)} %bitcast.1), calls=%async_computation | async-start | bytes 131072 | tf_op jit(solution)/shard_map/all_to_all | solution.py:339
  63.0 10.4 %all-to-all-start.2 = ((f32[16,8,128]{2,1,0:T(8,128)}), f32[16,8,128]{2,1,0:T(8,128)S(1)}, u32[]{:S(2)}, u32[]{:S(2)}) async-start(f32[16,8,128]{2,1,0:T(8,128)} %bitcast.3), calls=%async_computation.2 | async-start | bytes 131072 | tf_op jit(solution)/shard_map/all_to_all | solution.py:339
  74.0 10.4 %all-to-all-start.1 = ((f32[16,8,128]{2,1,0:T(8,128)}), f32[16,8,128]{2,1,0:T(8,128)S(1)}, u32[]{:S(2)}, u32[]{:S(2)}) async-start(f32[16,8,128]{2,1,0:T(8,128)} %broadcast_in_dim.6), calls=%async_computation.1 | async-start | bytes 131072 | tf_op jit(solution)/shard_map/all_to_all | solution.py:341
  85.0 12.5 %all-to-all-start.3 = ((f32[16,8,128]{2,1,0:T(8,128)}), f32[16,8,128]{2,1,0:T(8,128)S(1)}, u32[]{:S(2)}, u32[]{:S(2)}) async-start(f32[16,8,128]{2,1,0:T(8,128)} %broadcast_in_dim.7), calls=%async_computation.3 | async-start | bytes 131072 | tf_op jit(solution)/shard_map/all_to_all | solution.py:341
  88.5 4.3 %collective-permute-start.6 = (f32[128,128]{1,0:T(8,128)S(1)}, f32[128,128]{1,0:T(8,128)S(1)}, u32[]{:S(2)}, u32[]{:S(2)}) collective-permute-start(f32[128,128]{1,0:T(8,128)S(1)} %bitcast.5), channel_id=1, source_target_pairs={{0,1},{1,0},{2,3},{3,2},{4,5},{5,4},{6,7},{7,6},{8,9},{9,8},{10,11... | collective-permute-start | bytes 196616 | tf_op jit(solution)/shard_map/ppermute | solution.py:357

commit v5 on v3

--- a/solution.py
+++ b/solution.py
@@ -31,23 +31,26 @@
     return high, (a - high.astype(jnp.float32)).astype(jnp.bfloat16)
 
 
-def turn_kernel(loc_ref, vec_ref, ham_ref, turned_ref, out_ref):
+def turn_kernel(loc_ref, odd_ref, vec_ref, near_ref, ham_ref, turned_ref, out_ref):
     count, faces, width, _ = ham_ref.shape
+    odd = odd_ref[0]
     for e in range(count):
         here = slice(e * width, (e + 1) * width)
         total = None
         for face in range(faces):
-            turned = ham_ref[e, face].T
+            source = 2 - odd if face == 1 else 1 + odd if face == 2 else face
+            turned = ham_ref[e, source].T
             turned_ref[e, face] = turned
-            if face == 1 or face == 2:
+            if face == 2:
                 continue
             at = here if face == 0 else pl.ds(pl.multiple_of(loc_ref[e, face - 1] * width, width), width)
-            part = jnp.dot(vec_ref[:, at], turned, preferred_element_type=jnp.float32)
+            vec = near_ref if face == 1 else vec_ref
+            part = jnp.dot(vec[:, at], turned, preferred_element_type=jnp.float32)
             total = part if total is None else total + part
         out_ref[:, here] = total
 
 
-def turn_part(vec, hamiltonian, loc):
+def turn_part(vec, near, hamiltonian, loc, odd):
     count, faces, width, _ = hamiltonian.shape
     owned = vec.shape[0]
     return pl.pallas_call(
@@ -56,7 +59,7 @@
             jax.ShapeDtypeStruct(hamiltonian.shape, hamiltonian.dtype),
             jax.ShapeDtypeStruct(vec.shape, jnp.float32),
         ],
-        in_specs=[pl.BlockSpec(memory_space=pltpu.SMEM)] + vmem(2),
+        in_specs=[pl.BlockSpec(memory_space=pltpu.SMEM)] * 2 + vmem(3),
         out_specs=vmem(2),
         compiler_params=pltpu.CompilerParams(vmem_limit_bytes=32 << 20),
         cost_estimate=pl.CostEstimate(
@@ -64,49 +67,48 @@
             bytes_accessed=count * faces * width * width * 4,
             transcendentals=0,
         ),
-    )(loc, vec, hamiltonian)
-
-
-def own_kernel(loc_ref, vec_ref, turned_ref, out_ref):
+    )(loc, odd, vec, near, hamiltonian)
+
+
+def own_kernel(loc_ref, vec_ref, near_ref, turned_ref, out_ref):
     count, _, width, _ = turned_ref.shape
     for e in range(count):
         here = slice(e * width, (e + 1) * width)
         total = jnp.dot(vec_ref[:, here], turned_ref[e, 0], preferred_element_type=jnp.float32)
-        for face in range(2, 6):
+        for face in (2, 3, 4, 5, 0):
+            ref = near_ref if face == 0 else vec_ref
             at = pl.ds(pl.multiple_of(loc_ref[e, face] * width, width), width)
             total += jnp.dot(
-                vec_ref[:, at], turned_ref[e, face + 1], preferred_element_type=jnp.float32
+                ref[:, at], turned_ref[e, face + 1], preferred_element_type=jnp.float32
             )
         out_ref[:, here] = total
 
 
-def own_part(vec, turned, loc):
+def own_part(vec, near, turned, loc):
     count, _, width, _ = turned.shape
     owned = vec.shape[0]
     return pl.pallas_call(
         own_kernel,
         out_shape=jax.ShapeDtypeStruct(vec.shape, jnp.float32),
-        in_specs=[pl.BlockSpec(memory_space=pltpu.SMEM)] + vmem(2),
+        in_specs=[pl.BlockSpec(memory_space=pltpu.SMEM)] + vmem(3),
         out_specs=pl.BlockSpec(memory_space=pltpu.VMEM),
         compiler_params=pltpu.CompilerParams(vmem_limit_bytes=24 << 20),
         cost_estimate=pl.CostEstimate(
-            flops=2 * owned * count * width * width * 5,
-            bytes_accessed=count * 5 * width * width * 2,
+            flops=2 * owned * count * width * width * 6,
+            bytes_accessed=count * 6 * width * width * 2,
             transcendentals=0,
         ),
-    )(loc, vec, turned)
-
-
-def halo_kernel(level, loc_ref, low_ref, high_ref, acc_ref, vec_ref, prior_ref, turned_ref, *outs):
+    )(loc, vec, near, turned)
+
+
+def halo_kernel(level, loc_ref, far_ref, acc_ref, vec_ref, prior_ref, turned_ref, *outs):
     count, _, width, _ = turned_ref.shape
     for e in range(count):
         here = slice(e * width, (e + 1) * width)
-        total = acc_ref[:, here]
-        for face, ref in enumerate((low_ref, high_ref)):
-            at = pl.ds(pl.multiple_of(loc_ref[e, face] * width, width), width)
-            total += jnp.dot(
-                ref[:, at], turned_ref[e, face + 1], preferred_element_type=jnp.float32
-            )
+        at = pl.ds(pl.multiple_of(loc_ref[e, 1] * width, width), width)
+        total = acc_ref[:, here] + jnp.dot(
+            far_ref[:, at], turned_ref[e, 2], preferred_element_type=jnp.float32
+        )
         shifted = (total - centre * vec_ref[:, here].astype(jnp.float32)) * (1.0 / radius)
         if level > 1:
             shifted = 2.0 * shifted - prior_ref[:, here].astype(jnp.float32)
@@ -114,22 +116,22 @@
             out[:, here] = shifted.astype(out.dtype)
 
 
-def halo_part(level, low, high, acc, vec, prior, turned, loc):
+def halo_part(level, far, acc, vec, prior, turned, loc):
     count, _, width, _ = turned.shape
     owned = vec.shape[0]
     kinds = [jnp.bfloat16] if level < 3 else [jnp.float32, jnp.bfloat16]
     return pl.pallas_call(
         functools.partial(halo_kernel, level),
         out_shape=[jax.ShapeDtypeStruct(vec.shape, kind) for kind in kinds],
-        in_specs=[pl.BlockSpec(memory_space=pltpu.SMEM)] + vmem(6),
+        in_specs=[pl.BlockSpec(memory_space=pltpu.SMEM)] + vmem(5),
         out_specs=vmem(len(kinds)),
         compiler_params=pltpu.CompilerParams(vmem_limit_bytes=24 << 20),
         cost_estimate=pl.CostEstimate(
-            flops=2 * owned * count * width * width * 2,
-            bytes_accessed=count * 2 * width * width * 2,
+            flops=2 * owned * count * width * width,
+            bytes_accessed=count * width * width * 2,
             transcendentals=0,
         ),
-    )(loc, low, high, acc, vec, prior, turned)
+    )(loc, far, acc, vec, prior, turned)
 
 
 def own_gram_kernel(own_ref, high_ref, out_ref):
@@ -318,21 +320,25 @@
     blocks = lax.axis_size("space")
     groups = lax.axis_size("orb")
     half = owned * groups // 2
+    odd = lax.axis_index("space").astype(jnp.int32).reshape(1) % 2
     loc = adjacency % count
-    forward = [(i, (i + 1) % blocks) for i in range(blocks)]
-    backward = [(target, source) for source, target in forward]
+    swapped = jnp.concatenate([loc[:, 1:2], loc[:, 0:1], loc[:, 2:]], axis=1)
+    loc = jnp.where(odd[0] == 1, loc, swapped)
+    near_pairs = [(i, i ^ 1) for i in range(blocks)]
+    far_pairs = [(i, (i + 1 if i % 2 else i - 1) % blocks) for i in range(blocks)]
     smem = [pl.BlockSpec(memory_space=pltpu.SMEM)]
 
     def halo(vec):
-        return lax.ppermute(vec, "space", forward), lax.ppermute(vec, "space", backward)
-
-    side = halo(orbitals)
-    turned, acc = turn_part(orbitals, hamiltonian, loc)
-    (one,) = halo_part(1, *side, acc, orbitals, orbitals, turned, loc)
-    side = halo(one)
-    (two,) = halo_part(2, *side, own_part(one, turned, loc), one, orbitals, turned, loc)
-    side = halo(two)
-    filtered, narrow = halo_part(3, *side, own_part(two, turned, loc), two, one, turned, loc)
+        far = lax.ppermute(vec, "space", far_pairs)
+        return far, lax.ppermute(vec, "space", near_pairs)
+
+    far, near = halo(orbitals)
+    turned, acc = turn_part(orbitals, near, hamiltonian, loc, odd)
+    (one,) = halo_part(1, far, acc, orbitals, orbitals, turned, loc)
+    far, near = halo(one)
+    (two,) = halo_part(2, far, own_part(one, near, turned, loc), one, orbitals, turned, loc)
+    far, near = halo(two)
+    filtered, narrow = halo_part(3, far, own_part(two, near, turned, loc), two, one, turned, loc)
 
     def summed(part):
         step = 1

time: 84.7 us -> 88.5 us (1.045)
  waiting for transfers between devices: 15.4 us -> 25.1 us
  starting transfers between devices: 40.4 us -> 33.4 us
    ppermute x8, starting transfers between devices: 21.4 us -> 10.3 us  [summed(): lax.ppermute(part, 'space', [(i, i ^ step) for i in range(blocks)])]
    ppermute x1, waiting for transfers between devices: 0.01 us -> 5.25 us  [shards(): other = lax.ppermute(narrow, 'orb', swap)]
    ppermute x6, starting transfers between devices: 15.4 us -> 19.6 us  [the longest x3 15.2 us: halo(): far = lax.ppermute(vec, 'space', far_pairs)]
    ppermute x8, waiting for transfers between devices: 3.83 us -> 7.87 us  [summed(): lax.ppermute(part, 'space', [(i, i ^ step) for i in range(blocks)])]
  transfers between devices with their start and end apart: 16 -> 16, of which waited for: 7 -> 8; matrix products, arithmetic and copies ran while one was open for 1% -> 2% of each run, Pallas kernels for 13% -> 13%
where the time goes in v5:
time: 88.5 us; the launch traced here: 88.2 us
  starting transfers between devices  33.4 us (38%)
  waiting for transfers between devices  25.1 us (28%)
  Pallas kernels  23.1 us (26%)
  local copies, waits for them, and re-layouts  4.27 us (5%)
  other arithmetic  1.53 us (2%)
    ppermute x3, starting transfers between devices, halo(): far = lax.ppermute(vec, 'space', far_pairs)  15.2 us
    ppermute x3, waiting for transfers between devices, halo(): far = lax.ppermute(vec, 'space', far_pairs)  10.6 us
    ppermute x8, starting transfers between devices, summed(): lax.ppermute(part, 'space', [(i, i ^ step) for i in range(blocks)])  10.3 us
    ppermute x8, waiting for transfers between devices, summed(): lax.ppermute(part, 'space', [(i, i ^ step) for i in range(blocks)])  7.87 us
    pallas_call x1, Pallas kernels, factorize(): pl.pallas_call(second_kernel, out_shape=[jax.ShapeDtypeStruct((2 * half,...  6.53 us
    ppermute x1, waiting for transfers between devices, shards(): other = lax.ppermute(narrow, 'orb', swap)  5.25 us
    pallas_call x1, Pallas kernels, factorize(): pl.pallas_call(first_kernel, out_shape=[tile] * 2, in_specs=smem + vmem(2...  4.68 us
    ppermute x3, starting transfers between devices, halo(): return (far, lax.ppermute(vec, 'space', near_pairs))  4.39 us
  transfers between devices with their start and end apart: 16, of which 8 were waited for; matrix products, arithmetic and copies ran while one was open for 2% of the time, Pallas kernels for 13%

profile of v5, /device:TPU:0, one launch (start us, length us, event | category | flops | bytes accessed | tf_op | source)
XLA Modules:
  0.0 88.2 jit_solution(92800813194227785)
XLA Ops:
  0.6 0.5 collective-permute-start.1
  1.1 5.7 %collective-permute-start = (bf16[128,2048]{1,0:T(8,128)(2,1)}, bf16[128,2048]{1,0:T(8,128)(2,1)S(1)}, u32[]{:S(2)}, u32[]{:S(2)}) collective-permute-start(bf16[128,2048]{1,0:T(8,128)(2,1)} %prior_ref.3), channel_id=1, source_target_pairs={{0,30},{2,4},{4,2},{6,8},{8,6},{10,12},{12,10},{14,16},{16,14},{18... | collective-permute-start | bytes 1572872 | tf_op jit(solution)/shard_map/ppermute | solution.py:332
  6.8 0.7 add_select_fusion
  7.5 0.1 slice.11
  7.6 0.1 fusion.1
  7.7 0.8 add_select_fusion.1.loc_ref
  8.4 0.0 collective-permute-done.1.near_ref
  8.4 0.0 copy-start
  8.4 1.0 %copy-done = bf16[128,2048]{1,0:T(8,128)(2,1)S(1)} copy-done((bf16[128,2048]{1,0:T(8,128)(2,1)S(1)}, bf16[128,2048]{1,0:T(8,128)(2,1)}, u32[]{:S(2)}) %copy-start) | copy-done | bytes 524312
  9.5 0.0 copy-start.2
  9.5 3.1 %copy-done.2 = bf16[8,7,256,256]{3,2,1,0:T(8,128)(2,1)S(1)} copy-done((bf16[8,7,256,256]{3,2,1,0:T(8,128)(2,1)S(1)}, bf16[8,7,256,256]{3,2,1,0:T(8,128)(2,1)}, u32[]{:S(2)}) %copy-start.2) | copy-done | bytes 7340056
  12.6 0.0 copy-start.1
  12.6 2.8 %shard_map.50 = (bf16[8,7,256,256]{3,2,1,0:T(8,128)(2,1)S(1)}, f32[128,2048]{1,0:T(8,128)S(1)}) custom-call(s32[8,6]{1,0:T(8,128)S(1)} %add_select_fusion.1.loc_ref, s32[1]{0:T(128)S(6)} %select_n.21.odd_ref, bf16[128,2048]{1,0:T(8,128)(2,1)S(1)} %copy-done, bf16[128,2048]{1,0:T(8,128)(2,1)S(1)} %collective-permute-done.1.near_ref, ...), custom_call_target="tpu_custom_call" | custom-call | flops 671088640 | bytes 14680064 | tf_op jit(solution)/shard_map/pallas_call | solution.py:56
  15.4 0.0 collective-permute-done.far_ref
  15.4 0.0 copy-done.1
  15.4 1.0 %shard_map.51.vec_ref.prior_ref = bf16[128,2048]{1,0:T(8,128)(2,1)S(1)} custom-call(s32[8,6]{1,0:T(8,128)S(1)} %add_select_fusion.1.loc_ref, bf16[128,2048]{1,0:T(8,128)(2,1)S(1)} %collective-permute-done.far_ref, f32[128,2048]{1,0:T(8,128)S(1)} %get-tuple-element.10.acc_ref, bf16[128,2048]{1,0:T(8,128)(2,1)S(1)} %copy-done.1, ...), custom_call_target="tpu_custom_call" | custom-call | flops 134217728 | bytes 1048576 | tf_op jit(solution)/shard_map/pallas_call | solution.py:123
  16.4 1.2 %collective-permute-start.3 = (bf16[128,2048]{1,0:T(8,128)(2,1)S(1)}, bf16[128,2048]{1,0:T(8,128)(2,1)S(1)}, u32[]{:S(2)}, u32[]{:S(2)}) collective-permute-start(bf16[128,2048]{1,0:T(8,128)(2,1)S(1)} %shard_map.51.vec_ref.prior_ref), channel_id=1, source_target_pairs={{0,2},{2,0},{4,6},{6,4},{8,10},{10,8},{12,14},{14,12},{16,18},{18,... | collective-permute-start | bytes 1572872 | tf_op jit(solution)/shard_map/ppermute | solution.py:333
  17.6 4.8 %collective-permute-start.2 = (bf16[128,2048]{1,0:T(8,128)(2,1)S(1)}, bf16[128,2048]{1,0:T(8,128)(2,1)S(1)}, u32[]{:S(2)}, u32[]{:S(2)}) collective-permute-start(bf16[128,2048]{1,0:T(8,128)(2,1)S(1)} %shard_map.51.vec_ref.prior_ref), channel_id=1, source_target_pairs={{0,30},{2,4},{4,2},{6,8},{8,6},{10,12},{12,10},{14,16},{16,14},{18... | collective-permute-start | bytes 1572872 | tf_op jit(solution)/shard_map/ppermute | solution.py:332
  22.4 0.0 collective-permute-done.3.near_ref
  22.4 1.7 %shard_map.52.acc_ref = f32[128,2048]{1,0:T(8,128)S(1)} custom-call(s32[8,6]{1,0:T(8,128)S(1)} %add_select_fusion.1.loc_ref, bf16[128,2048]{1,0:T(8,128)(2,1)S(1)} %shard_map.51.vec_ref.prior_ref, bf16[128,2048]{1,0:T(8,128)(2,1)S(1)} %collective-permute-done.3.near_ref, bf16[8,7,256,256]{3,2,1,0:T(8,128)(2,1)S(1)} %get-tuple-element.11.turned_ref), custom_call_target="tpu_custom_call" | custom-call | flops 805306368 | bytes 6291456 | tf_op jit(solution)/shard_map/pallas_call | solution.py:90
  24.0 5.3 %collective-permute-done.2.far_ref = bf16[128,2048]{1,0:T(8,128)(2,1)S(1)} collective-permute-done((bf16[128,2048]{1,0:T(8,128)(2,1)S(1)}, bf16[128,2048]{1,0:T(8,128)(2,1)S(1)}, u32[]{:S(2)}, u32[]{:S(2)}) %collective-permute-start.2) | collective-permute-done | bytes 524320 | tf_op jit(solution)/shard_map/ppermute | solution.py:332
  29.3 1.1 %shard_map.53.vec_ref = bf16[128,2048]{1,0:T(8,128)(2,1)S(1)} custom-call(s32[8,6]{1,0:T(8,128)S(1)} %add_select_fusion.1.loc_ref, bf16[128,2048]{1,0:T(8,128)(2,1)S(1)} %collective-permute-done.2.far_ref, f32[128,2048]{1,0:T(8,128)S(1)} %shard_map.52.acc_ref, bf16[128,2048]{1,0:T(8,128)(2,1)S(1)} %shard_map.51.vec_ref.prior_ref, ...), custom_call_target="tpu_custom_call" | custom-call | flops 134217728 | bytes 1048576 | tf_op jit(solution)/shard_map/pallas_call | solution.py:123
  30.4 2.6 %collective-permute-start.5 = (bf16[128,2048]{1,0:T(8,128)(2,1)S(1)}, bf16[128,2048]{1,0:T(8,128)(2,1)S(1)}, u32[]{:S(2)}, u32[]{:S(2)}) collective-permute-start(bf16[128,2048]{1,0:T(8,128)(2,1)S(1)} %shard_map.53.vec_ref), channel_id=1, source_target_pairs={{0,2},{2,0},{4,6},{6,4},{8,10},{10,8},{12,14},{14,12},{16,18},{18,... | collective-permute-start | bytes 1572872 | tf_op jit(solution)/shard_map/ppermute | solution.py:333
  33.1 4.8 %collective-permute-start.4 = (bf16[128,2048]{1,0:T(8,128)(2,1)S(1)}, bf16[128,2048]{1,0:T(8,128)(2,1)S(1)}, u32[]{:S(2)}, u32[]{:S(2)}) collective-permute-start(bf16[128,2048]{1,0:T(8,128)(2,1)S(1)} %shard_map.53.vec_ref), channel_id=1, source_target_pairs={{0,30},{2,4},{4,2},{6,8},{8,6},{10,12},{12,10},{14,16},{16,14},{18... | collective-permute-start | bytes 1572872 | tf_op jit(solution)/shard_map/ppermute | solution.py:332
  37.8 0.0 collective-permute-done.5.near_ref
  37.8 1.7 %shard_map.54.acc_ref = f32[128,2048]{1,0:T(8,128)S(1)} custom-call(s32[8,6]{1,0:T(8,128)S(1)} %add_select_fusion.1.loc_ref, bf16[128,2048]{1,0:T(8,128)(2,1)S(1)} %shard_map.53.vec_ref, bf16[128,2048]{1,0:T(8,128)(2,1)S(1)} %collective-permute-done.5.near_ref, bf16[8,7,256,256]{3,2,1,0:T(8,128)(2,1)S(1)} %get-tuple-element.11.turned_ref), custom_call_target="tpu_custom_call" | custom-call | flops 805306368 | bytes 6291456 | tf_op jit(solution)/shard_map/pallas_call | solution.py:90
  39.5 5.3 %collective-permute-done.4.far_ref = bf16[128,2048]{1,0:T(8,128)(2,1)S(1)} collective-permute-done((bf16[128,2048]{1,0:T(8,128)(2,1)S(1)}, bf16[128,2048]{1,0:T(8,128)(2,1)S(1)}, u32[]{:S(2)}, u32[]{:S(2)}) %collective-permute-start.4) | collective-permute-done | bytes 524320 | tf_op jit(solution)/shard_map/ppermute | solution.py:332
  44.8 1.1 %shard_map.55 = (f32[128,2048]{1,0:T(8,128)S(1)}, bf16[128,2048]{1,0:T(8,128)(2,1)S(1)}) custom-call(s32[8,6]{1,0:T(8,128)S(1)} %add_select_fusion.1.loc_ref, bf16[128,2048]{1,0:T(8,128)(2,1)S(1)} %collective-permute-done.4.far_ref, f32[128,2048]{1,0:T(8,128)S(1)} %shard_map.54.acc_ref, bf16[128,2048]{1,0:T(8,128)(2,1)S(1)} %shard_map.53.vec_ref, ...), custom_call_target="tpu_custom_call" | custom-call | flops 134217728 | bytes 1048576 | tf_op jit(solution)/shard_map/pallas_call | solution.py:123
  45.9 1.8 %collective-permute-start.11 = (bf16[128,2048]{1,0:T(8,128)(2,1)S(1)}, bf16[128,2048]{1,0:T(8,128)(2,1)S(1)}, u32[]{:S(2)}, u32[]{:S(2)}) collective-permute-start(bf16[128,2048]{1,0:T(8,128)(2,1)S(1)} %get-tuple-element.13.high_ref.own_ref), channel_id=1, source_target_pairs={{0,1},{1,0},{2,3},{3,2},{4,5},{5,4},{6,7},{7,6},{8,9},{9,8},{10,11... | collective-permute-start | bytes 1572872 | tf_op jit(solution)/shard_map/ppermute | solution.py:353
  47.7 0.5 shard_map.56
  48.2 2.7 %collective-permute-start.6 = (f32[128,128]{1,0:T(8,128)S(1)}, f32[128,128]{1,0:T(8,128)S(1)}, u32[]{:S(2)}, u32[]{:S(2)}) collective-permute-start(f32[128,128]{1,0:T(8,128)S(1)} %shard_map.56), channel_id=1, source_target_pairs={{0,2},{2,0},{4,6},{6,4},{8,10},{10,8},{12,14},{14,12},{16,18},{18,... | collective-permute-start | bytes 196616 | tf_op jit(solution)/shard_map/ppermute | solution.py:346
  50.9 0.9 %collective-permute-done.6 = f32[128,128]{1,0:T(8,128)S(1)} collective-permute-done((f32[128,128]{1,0:T(8,128)S(1)}, f32[128,128]{1,0:T(8,128)S(1)}, u32[]{:S(2)}, u32[]{:S(2)}) %collective-permute-start.6) | collective-permute-done | bytes 65568 | tf_op jit(solution)/shard_map/ppermute | solution.py:346
  51.8 1.8 %collective-permute-start.7 = (f32[128,128]{1,0:T(8,128)S(1)}, f32[128,128]{1,0:T(8,128)S(1)}, u32[]{:S(2)}, u32[]{:S(2)}) collective-permute-start(f32[128,128]{1,0:T(8,128)S(1)} %add.38), channel_id=1, source_target_pairs={{0,4},{2,6},{4,0},{6,2},{8,12},{10,14},{12,8},{14,10},{16,20},{18,... | collective-permute-start | bytes 196616 | tf_op jit(solution)/shard_map/ppermute | solution.py:346
  53.6 5.3 %collective-permute-done.11.other_ref = bf16[128,2048]{1,0:T(8,128)(2,1)S(1)} collective-permute-done((bf16[128,2048]{1,0:T(8,128)(2,1)S(1)}, bf16[128,2048]{1,0:T(8,128)(2,1)S(1)}, u32[]{:S(2)}, u32[]{:S(2)}) %collective-permute-start.11) | collective-permute-done | bytes 524320 | tf_op jit(solution)/shard_map/ppermute | solution.py:353
  58.8 0.3 shard_map.57
  59.1 1.8 %collective-permute-start.12 = (f32[128,128]{1,0:T(8,128)S(1)}, f32[128,128]{1,0:T(8,128)S(1)}, u32[]{:S(2)}, u32[]{:S(2)}) collective-permute-start(f32[128,128]{1,0:T(8,128)S(1)} %shard_map.57), channel_id=1, source_target_pairs={{0,2},{2,0},{4,6},{6,4},{8,10},{10,8},{12,14},{14,12},{16,18},{18,... | collective-permute-start | bytes 196616 | tf_op jit(solution)/shard_map/ppermute | solution.py:346
  61.0 0.0 collective-permute-done.7
  61.0 0.1 collective-permute-start.8
  61.1 0.8 collective-permute-done.12
  61.9 0.1 collective-permute-start.13
  62.0 3.4 %collective-permute-done.8 = f32[128,128]{1,0:T(8,128)S(1)} collective-permute-done((f32[128,128]{1,0:T(8,128)S(1)}, f32[128,128]{1,0:T(8,128)S(1)}, u32[]{:S(2)}, u32[]{:S(2)}) %collective-permute-start.8) | collective-permute-done | bytes 65568 | tf_op jit(solution)/shard_map/ppermute | solution.py:346
  65.3 1.1 %collective-permute-start.9 = (f32[128,128]{1,0:T(8,128)S(1)}, f32[128,128]{1,0:T(8,128)S(1)}, u32[]{:S(2)}, u32[]{:S(2)}) collective-permute-start(f32[128,128]{1,0:T(8,128)S(1)} %add.40), channel_id=1, source_target_pairs={{0,16},{2,18},{4,20},{6,22},{8,24},{10,26},{12,28},{14,30},{16,0},... | collective-permute-start | bytes 196616 | tf_op jit(solution)/shard_map/ppermute | solution.py:346
  66.4 0.0 collective-permute-done.13
  66.4 1.6 %collective-permute-start.14 = (f32[128,128]{1,0:T(8,128)S(1)}, f32[128,128]{1,0:T(8,128)S(1)}, u32[]{:S(2)}, u32[]{:S(2)}) collective-permute-start(f32[128,128]{1,0:T(8,128)S(1)} %add.43), channel_id=1, source_target_pairs={{0,8},{2,10},{4,12},{6,14},{8,0},{10,2},{12,4},{14,6},{16,24},{18,... | collective-permute-start | bytes 196616 | tf_op jit(solution)/shard_map/ppermute | solution.py:346
  68.0 2.8 %collective-permute-done.9 = f32[128,128]{1,0:T(8,128)S(1)} collective-permute-done((f32[128,128]{1,0:T(8,128)S(1)}, f32[128,128]{1,0:T(8,128)S(1)}, u32[]{:S(2)}, u32[]{:S(2)}) %collective-permute-start.9) | collective-permute-done | bytes 65568 | tf_op jit(solution)/shard_map/ppermute | solution.py:346
  70.9 1.7 %collective-permute-start.10 = (f32[128,128]{1,0:T(8,128)S(1)}, f32[128,128]{1,0:T(8,128)S(1)}, u32[]{:S(2)}, u32[]{:S(2)}) collective-permute-start(f32[128,128]{1,0:T(8,128)S(1)} %add.41.own_ref), channel_id=1, source_target_pairs={{0,1},{1,0},{2,3},{3,2},{4,5},{5,4},{6,7},{7,6},{8,9},{9,8},{10,11... | collective-permute-start | bytes 196616 | tf_op jit(solution)/shard_map/ppermute | solution.py:364
  72.6 0.0 collective-permute-done.14
  72.6 1.2 %collective-permute-start.15 = (f32[128,128]{1,0:T(8,128)S(1)}, f32[128,128]{1,0:T(8,128)S(1)}, u32[]{:S(2)}, u32[]{:S(2)}) collective-permute-start(f32[128,128]{1,0:T(8,128)S(1)} %add.44), channel_id=1, source_target_pairs={{0,16},{2,18},{4,20},{6,22},{8,24},{10,26},{12,28},{14,30},{16,0},... | collective-permute-start | bytes 196616 | tf_op jit(solution)/shard_map/ppermute | solution.py:346
  73.8 1.4 %collective-permute-done.10.other_ref = f32[128,128]{1,0:T(8,128)S(1)} collective-permute-done((f32[128,128]{1,0:T(8,128)S(1)}, f32[128,128]{1,0:T(8,128)S(1)}, u32[]{:S(2)}, u32[]{:S(2)}) %collective-permute-start.10) | collective-permute-done | bytes 65568 | tf_op jit(solution)/shard_map/ppermute | solution.py:364
  75.2 4.7 %shard_map.58 = (f32[128,128]{1,0:T(8,128)S(1)}, f32[128,128]{1,0:T(8,128)S(1)}) custom-call(s32[1]{0:T(128)} %bitcast.place_ref, f32[128,128]{1,0:T(8,128)S(1)} %add.41.own_ref, f32[128,128]{1,0:T(8,128)S(1)} %collective-permute-done.10.other_ref), custom_call_target="tpu_custom_call" | custom-call | flops 4194304 | bytes 16777216 | tf_op jit(solution)/shard_map/pallas_call | solution.py:277
  79.9 0.0 collective-permute-done.15
  79.9 6.5 %shard_map.59 = (f32[256,256]{1,0:T(8,128)}, f32[256,256]{1,0:T(8,128)S(1)}) custom-call(s32[1]{0:T(128)} %bitcast.place_ref, f32[128,128]{1,0:T(8,128)S(1)} %add.41.own_ref, f32[128,128]{1,0:T(8,128)S(1)} %collective-permute-done.10.other_ref, f32[128,128]{1,0:T(8,128)S(1)} %add.45.cross_ref, f32[128,128]{1,0:T(8,128)S(1)} %get-tuple-element.14.first_ref, ...), custom_call_target="tpu_custom_call" | custom-call | tf_op jit(solution)/shard_map/pallas_call | solution.py:286
  86.4 1.8 %shard_map.60 = f32[128,2048]{1,0:T(8,128)} custom-call(s32[1]{0:T(128)} %bitcast.place_ref, f32[256,256]{1,0:T(8,128)S(1)} %get-tuple-element.16.inv_ref, f32[128,2048]{1,0:T(8,128)S(1)} %get-tuple-element.12.own_ref, bf16[128,2048]{1,0:T(8,128)(2,1)S(1)} %collective-permute-done.11.other_ref), custom_call_target="tpu_custom_call" | custom-call | tf_op jit(solution)/shard_map/pallas_call | solution.py:380
  (8 shorter events, 0.1 us)
Async XLA Ops:
  0.6 7.8 %collective-permute-start.1 = (bf16[128,2048]{1,0:T(8,128)(2,1)}, bf16[128,2048]{1,0:T(8,128)(2,1)S(1)}, u32[]{:S(2)}, u32[]{:S(2)}) collective-permute-start(bf16[128,2048]{1,0:T(8,128)(2,1)} %prior_ref.3), channel_id=1, source_target_pairs={{0,2},{2,0},{4,6},{6,4},{8,10},{10,8},{12,14},{14,12},{16,18},{18,... | collective-permute-start | bytes 1572872 | tf_op jit(solution)/shard_map/ppermute | solution.py:333
  1.1 14.2 %collective-permute-start = (bf16[128,2048]{1,0:T(8,128)(2,1)}, bf16[128,2048]{1,0:T(8,128)(2,1)S(1)}, u32[]{:S(2)}, u32[]{:S(2)}) collective-permute-start(bf16[128,2048]{1,0:T(8,128)(2,1)} %prior_ref.3), channel_id=1, source_target_pairs={{0,30},{2,4},{4,2},{6,8},{8,6},{10,12},{12,10},{14,16},{16,14},{18... | collective-permute-start | bytes 1572872 | tf_op jit(solution)/shard_map/ppermute | solution.py:332
  8.4 1.0 %copy-start = (bf16[128,2048]{1,0:T(8,128)(2,1)S(1)}, bf16[128,2048]{1,0:T(8,128)(2,1)}, u32[]{:S(2)}) copy-start(bf16[128,2048]{1,0:T(8,128)(2,1)} %prior_ref.3) | copy-start | bytes 1572868
  9.5 3.1 %copy-start.2 = (bf16[8,7,256,256]{3,2,1,0:T(8,128)(2,1)S(1)}, bf16[8,7,256,256]{3,2,1,0:T(8,128)(2,1)}, u32[]{:S(2)}) copy-start(bf16[8,7,256,256]{3,2,1,0:T(8,128)(2,1)} %ham_ref.1) | copy-start | bytes 22020100
  12.6 2.8 %copy-start.1 = (bf16[128,2048]{1,0:T(8,128)(2,1)S(1)}, bf16[128,2048]{1,0:T(8,128)(2,1)}, u32[]{:S(2)}) copy-start(bf16[128,2048]{1,0:T(8,128)(2,1)} %prior_ref.3) | copy-start | bytes 1572868
  16.4 6.0 %collective-permute-start.3 = (bf16[128,2048]{1,0:T(8,128)(2,1)S(1)}, bf16[128,2048]{1,0:T(8,128)(2,1)S(1)}, u32[]{:S(2)}, u32[]{:S(2)}) collective-permute-start(bf16[128,2048]{1,0:T(8,128)(2,1)S(1)} %shard_map.51.vec_ref.prior_ref), channel_id=1, source_target_pairs={{0,2},{2,0},{4,6},{6,4},{8,10},{10,8},{12,14},{14,12},{16,18},{18,... | collective-permute-start | bytes 1572872 | tf_op jit(solution)/shard_map/ppermute | solution.py:333
  17.6 11.7 %collective-permute-start.2 = (bf16[128,2048]{1,0:T(8,128)(2,1)S(1)}, bf16[128,2048]{1,0:T(8,128)(2,1)S(1)}, u32[]{:S(2)}, u32[]{:S(2)}) collective-permute-start(bf16[128,2048]{1,0:T(8,128)(2,1)S(1)} %shard_map.51.vec_ref.prior_ref), channel_id=1, source_target_pairs={{0,30},{2,4},{4,2},{6,8},{8,6},{10,12},{12,10},{14,16},{16,14},{18... | collective-permute-start | bytes 1572872 | tf_op jit(solution)/shard_map/ppermute | solution.py:332
  30.4 7.4 %collective-permute-start.5 = (bf16[128,2048]{1,0:T(8,128)(2,1)S(1)}, bf16[128,2048]{1,0:T(8,128)(2,1)S(1)}, u32[]{:S(2)}, u32[]{:S(2)}) collective-permute-start(bf16[128,2048]{1,0:T(8,128)(2,1)S(1)} %shard_map.53.vec_ref), channel_id=1, source_target_pairs={{0,2},{2,0},{4,6},{6,4},{8,10},{10,8},{12,14},{14,12},{16,18},{18,... | collective-permute-start | bytes 1572872 | tf_op jit(solution)/shard_map/ppermute | solution.py:333
  33.1 11.7 %collective-permute-start.4 = (bf16[128,2048]{1,0:T(8,128)(2,1)S(1)}, bf16[128,2048]{1,0:T(8,128)(2,1)S(1)}, u32[]{:S(2)}, u32[]{:S(2)}) collective-permute-start(bf16[128,2048]{1,0:T(8,128)(2,1)S(1)} %shard_map.53.vec_ref), channel_id=1, source_target_pairs={{0,30},{2,4},{4,2},{6,8},{8,6},{10,12},{12,10},{14,16},{16,14},{18... | collective-permute-start | bytes 1572872 | tf_op jit(solution)/shard_map/ppermute | solution.py:332
  45.9 12.9 %collective-permute-start.11 = (bf16[128,2048]{1,0:T(8,128)(2,1)S(1)}, bf16[128,2048]{1,0:T(8,128)(2,1)S(1)}, u32[]{:S(2)}, u32[]{:S(2)}) collective-permute-start(bf16[128,2048]{1,0:T(8,128)(2,1)S(1)} %get-tuple-element.13.high_ref.own_ref), channel_id=1, source_target_pairs={{0,1},{1,0},{2,3},{3,2},{4,5},{5,4},{6,7},{7,6},{8,9},{9,8},{10,11... | collective-permute-start | bytes 1572872 | tf_op jit(solution)/shard_map/ppermute | solution.py:353
  48.2 3.6 %collective-permute-start.6 = (f32[128,128]{1,0:T(8,128)S(1)}, f32[128,128]{1,0:T(8,128)S(1)}, u32[]{:S(2)}, u32[]{:S(2)}) collective-permute-start(f32[128,128]{1,0:T(8,128)S(1)} %shard_map.56), channel_id=1, source_target_pairs={{0,2},{2,0},{4,6},{6,4},{8,10},{10,8},{12,14},{14,12},{16,18},{18,... | collective-permute-start | bytes 196616 | tf_op jit(solution)/shard_map/ppermute | solution.py:346
  51.8 9.2 %collective-permute-start.7 = (f32[128,128]{1,0:T(8,128)S(1)}, f32[128,128]{1,0:T(8,128)S(1)}, u32[]{:S(2)}, u32[]{:S(2)}) collective-permute-start(f32[128,128]{1,0:T(8,128)S(1)} %add.38), channel_id=1, source_target_pairs={{0,4},{2,6},{4,0},{6,2},{8,12},{10,14},{12,8},{14,10},{16,20},{18,... | collective-permute-start | bytes 196616 | tf_op jit(solution)/shard_map/ppermute | solution.py:346
  59.1 2.7 %collective-permute-start.12 = (f32[128,128]{1,0:T(8,128)S(1)}, f32[128,128]{1,0:T(8,128)S(1)}, u32[]{:S(2)}, u32[]{:S(2)}) collective-permute-start(f32[128,128]{1,0:T(8,128)S(1)} %shard_map.57), channel_id=1, source_target_pairs={{0,2},{2,0},{4,6},{6,4},{8,10},{10,8},{12,14},{14,12},{16,18},{18,... | collective-permute-start | bytes 196616 | tf_op jit(solution)/shard_map/ppermute | solution.py:346
  61.0 4.3 %collective-permute-start.8 = (f32[128,128]{1,0:T(8,128)S(1)}, f32[128,128]{1,0:T(8,128)S(1)}, u32[]{:S(2)}, u32[]{:S(2)}) collective-permute-start(f32[128,128]{1,0:T(8,128)S(1)} %add.39), channel_id=1, source_target_pairs={{0,8},{2,10},{4,12},{6,14},{8,0},{10,2},{12,4},{14,6},{16,24},{18,... | collective-permute-start | bytes 196616 | tf_op jit(solution)/shard_map/ppermute | solution.py:346
  61.9 4.5 %collective-permute-start.13 = (f32[128,128]{1,0:T(8,128)S(1)}, f32[128,128]{1,0:T(8,128)S(1)}, u32[]{:S(2)}, u32[]{:S(2)}) collective-permute-start(f32[128,128]{1,0:T(8,128)S(1)} %add.42), channel_id=1, source_target_pairs={{0,4},{2,6},{4,0},{6,2},{8,12},{10,14},{12,8},{14,10},{16,20},{18,... | collective-permute-start | bytes 196616 | tf_op jit(solution)/shard_map/ppermute | solution.py:346
  65.3 5.5 %collective-permute-start.9 = (f32[128,128]{1,0:T(8,128)S(1)}, f32[128,128]{1,0:T(8,128)S(1)}, u32[]{:S(2)}, u32[]{:S(2)}) collective-permute-start(f32[128,128]{1,0:T(8,128)S(1)} %add.40), channel_id=1, source_target_pairs={{0,16},{2,18},{4,20},{6,22},{8,24},{10,26},{12,28},{14,30},{16,0},... | collective-permute-start | bytes 196616 | tf_op jit(solution)/shard_map/ppermute | solution.py:346
  66.4 6.2 %collective-permute-start.14 = (f32[128,128]{1,0:T(8,128)S(1)}, f32[128,128]{1,0:T(8,128)S(1)}, u32[]{:S(2)}, u32[]{:S(2)}) collective-permute-start(f32[128,128]{1,0:T(8,128)S(1)} %add.43), channel_id=1, source_target_pairs={{0,8},{2,10},{4,12},{6,14},{8,0},{10,2},{12,4},{14,6},{16,24},{18,... | collective-permute-start | bytes 196616 | tf_op jit(solution)/shard_map/ppermute | solution.py:346
  70.9 4.3 %collective-permute-start.10 = (f32[128,128]{1,0:T(8,128)S(1)}, f32[128,128]{1,0:T(8,128)S(1)}, u32[]{:S(2)}, u32[]{:S(2)}) collective-permute-start(f32[128,128]{1,0:T(8,128)S(1)} %add.41.own_ref), channel_id=1, source_target_pairs={{0,1},{1,0},{2,3},{3,2},{4,5},{5,4},{6,7},{7,6},{8,9},{9,8},{10,11... | collective-permute-start | bytes 196616 | tf_op jit(solution)/shard_map/ppermute | solution.py:364
  72.6 7.3 %collective-permute-start.15 = (f32[128,128]{1,0:T(8,128)S(1)}, f32[128,128]{1,0:T(8,128)S(1)}, u32[]{:S(2)}, u32[]{:S(2)}) collective-permute-start(f32[128,128]{1,0:T(8,128)S(1)} %add.44), channel_id=1, source_target_pairs={{0,16},{2,18},{4,20},{6,22},{8,24},{10,26},{12,28},{14,30},{16,0},... | collective-permute-start | bytes 196616 | tf_op jit(solution)/shard_map/ppermute | solution.py:346

commit v6 on v3

--- a/solution.py
+++ b/solution.py
@@ -31,13 +31,15 @@
     return high, (a - high.astype(jnp.float32)).astype(jnp.bfloat16)
 
 
-def turn_kernel(loc_ref, vec_ref, ham_ref, turned_ref, out_ref):
+def turn_kernel(loc_ref, odd_ref, vec_ref, ham_ref, turned_ref, out_ref):
     count, faces, width, _ = ham_ref.shape
+    odd = odd_ref[0]
     for e in range(count):
         here = slice(e * width, (e + 1) * width)
         total = None
         for face in range(faces):
-            turned = ham_ref[e, face].T
+            source = 2 - odd if face == 1 else 1 + odd if face == 2 else face
+            turned = ham_ref[e, source].T
             turned_ref[e, face] = turned
             if face == 1 or face == 2:
                 continue
@@ -47,7 +49,7 @@
         out_ref[:, here] = total
 
 
-def turn_part(vec, hamiltonian, loc):
+def turn_part(vec, hamiltonian, loc, odd):
     count, faces, width, _ = hamiltonian.shape
     owned = vec.shape[0]
     return pl.pallas_call(
@@ -56,7 +58,7 @@
             jax.ShapeDtypeStruct(hamiltonian.shape, hamiltonian.dtype),
             jax.ShapeDtypeStruct(vec.shape, jnp.float32),
         ],
-        in_specs=[pl.BlockSpec(memory_space=pltpu.SMEM)] + vmem(2),
+        in_specs=[pl.BlockSpec(memory_space=pltpu.SMEM)] * 2 + vmem(2),
         out_specs=vmem(2),
         compiler_params=pltpu.CompilerParams(vmem_limit_bytes=32 << 20),
         cost_estimate=pl.CostEstimate(
@@ -64,7 +66,7 @@
             bytes_accessed=count * faces * width * width * 4,
             transcendentals=0,
         ),
-    )(loc, vec, hamiltonian)
+    )(loc, odd, vec, hamiltonian)
 
 
 def own_kernel(loc_ref, vec_ref, turned_ref, out_ref):
@@ -97,12 +99,12 @@
     )(loc, vec, turned)
 
 
-def halo_kernel(level, loc_ref, low_ref, high_ref, acc_ref, vec_ref, prior_ref, turned_ref, *outs):
+def halo_kernel(level, loc_ref, near_ref, far_ref, acc_ref, vec_ref, prior_ref, turned_ref, *outs):
     count, _, width, _ = turned_ref.shape
     for e in range(count):
         here = slice(e * width, (e + 1) * width)
         total = acc_ref[:, here]
-        for face, ref in enumerate((low_ref, high_ref)):
+        for face, ref in enumerate((near_ref, far_ref)):
             at = pl.ds(pl.multiple_of(loc_ref[e, face] * width, width), width)
             total += jnp.dot(
                 ref[:, at], turned_ref[e, face + 1], preferred_element_type=jnp.float32
@@ -114,7 +116,7 @@
             out[:, here] = shifted.astype(out.dtype)
 
 
-def halo_part(level, low, high, acc, vec, prior, turned, loc):
+def halo_part(level, near, far, acc, vec, prior, turned, loc):
     count, _, width, _ = turned.shape
     owned = vec.shape[0]
     kinds = [jnp.bfloat16] if level < 3 else [jnp.float32, jnp.bfloat16]
@@ -129,7 +131,7 @@
             bytes_accessed=count * 2 * width * width * 2,
             transcendentals=0,
         ),
-    )(loc, low, high, acc, vec, prior, turned)
+    )(loc, near, far, acc, vec, prior, turned)
 
 
 def own_gram_kernel(own_ref, high_ref, out_ref):
@@ -318,16 +320,20 @@
     blocks = lax.axis_size("space")
     groups = lax.axis_size("orb")
     half = owned * groups // 2
+    odd = lax.axis_index("space").astype(jnp.int32).reshape(1) % 2
     loc = adjacency % count
-    forward = [(i, (i + 1) % blocks) for i in range(blocks)]
-    backward = [(target, source) for source, target in forward]
+    swapped = jnp.concatenate([loc[:, 1:2], loc[:, 0:1], loc[:, 2:]], axis=1)
+    loc = jnp.where(odd[0] == 1, loc, swapped)
+    near_pairs = [(i, i ^ 1) for i in range(blocks)]
+    far_pairs = [(i, (i + 1 if i % 2 else i - 1) % blocks) for i in range(blocks)]
     smem = [pl.BlockSpec(memory_space=pltpu.SMEM)]
 
     def halo(vec):
-        return lax.ppermute(vec, "space", forward), lax.ppermute(vec, "space", backward)
+        far = lax.ppermute(vec, "space", far_pairs)
+        return lax.ppermute(vec, "space", near_pairs), far
 
     side = halo(orbitals)
-    turned, acc = turn_part(orbitals, hamiltonian, loc)
+    turned, acc = turn_part(orbitals, hamiltonian, loc, odd)
     (one,) = halo_part(1, *side, acc, orbitals, orbitals, turned, loc)
     side = halo(one)
     (two,) = halo_part(2, *side, own_part(one, turned, loc), one, orbitals, turned, loc)

time: 84.7 us -> 84.2 us (level)
  starting transfers between devices: 40.4 us -> 36.9 us
  waiting for transfers between devices: 15.4 us -> 17.4 us
    ppermute x8, starting transfers between devices: 21.4 us -> 15.8 us  [summed(): lax.ppermute(part, 'space', [(i, i ^ step) for i in range(blocks)])]
    ppermute x8, waiting for transfers between devices: 3.83 us -> 7.18 us  [summed(): lax.ppermute(part, 'space', [(i, i ^ step) for i in range(blocks)])]
    ppermute x6, waiting for transfers between devices: 10.7 us -> 7.45 us  [the longest x3 7.44 us: halo(): far = lax.ppermute(vec, 'space', far_pairs)]
    ppermute x6, starting transfers between devices: 15.4 us -> 18 us  [the longest x3 11.9 us: halo(): far = lax.ppermute(vec, 'space', far_pairs)]
    ppermute x1, waiting for transfers between devices: 0.89 us -> 1.94 us  [shards(): far = lax.ppermute(near, 'orb', swap)]
  transfers between devices with their start and end apart: 16 -> 16, of which waited for: 7 -> 8; matrix products, arithmetic and copies ran while one was open for 1% -> 2% of each run, Pallas kernels for 13% -> 13%
where the time goes in v6:
time: 84.2 us; the launch traced here: 83.9 us
  starting transfers between devices  36.9 us (44%)
  Pallas kernels  23.1 us (27%)
  waiting for transfers between devices  17.4 us (21%)
  local copies, waits for them, and re-layouts  4.27 us (5%)
  other arithmetic  1.53 us (2%)
    ppermute x8, starting transfers between devices, summed(): lax.ppermute(part, 'space', [(i, i ^ step) for i in range(blocks)])  15.8 us
    ppermute x3, starting transfers between devices, halo(): far = lax.ppermute(vec, 'space', far_pairs)  11.9 us
    ppermute x3, waiting for transfers between devices, halo(): far = lax.ppermute(vec, 'space', far_pairs)  7.44 us
    ppermute x8, waiting for transfers between devices, summed(): lax.ppermute(part, 'space', [(i, i ^ step) for i in range(blocks)])  7.18 us
    pallas_call x1, Pallas kernels, factorize(): pl.pallas_call(second_kernel, out_shape=[jax.ShapeDtypeStruct((2 * half,...  6.53 us
    ppermute x3, starting transfers between devices, halo(): return (lax.ppermute(vec, 'space', near_pairs), far)  6.14 us
    pallas_call x1, Pallas kernels, factorize(): pl.pallas_call(first_kernel, out_shape=[tile] * 2, in_specs=smem + vmem(2...  4.68 us
    unnamed x6, local copies, waits for them, and re-layouts  4.13 us
  transfers between devices with their start and end apart: 16, of which 8 were waited for; matrix products, arithmetic and copies ran while one was open for 2% of the time, Pallas kernels for 13%

profile of v6, /device:TPU:0, one launch (start us, length us, event | category | flops | bytes accessed | tf_op | source)
XLA Modules:
  0.0 83.9 jit_solution(1320605880423066634)
XLA Ops:
  0.6 5.5 %collective-permute-start.1 = (bf16[128,2048]{1,0:T(8,128)(2,1)}, bf16[128,2048]{1,0:T(8,128)(2,1)S(1)}, u32[]{:S(2)}, u32[]{:S(2)}) collective-permute-start(bf16[128,2048]{1,0:T(8,128)(2,1)} %prior_ref.3), channel_id=1, source_target_pairs={{0,30},{2,4},{4,2},{6,8},{8,6},{10,12},{12,10},{14,16},{16,14},{18... | collective-permute-start | bytes 1572872 | tf_op jit(solution)/shard_map/ppermute | solution.py:332
  6.1 0.0 collective-permute-start
  6.1 0.7 add_select_fusion
  6.8 0.1 slice.11
  6.9 0.1 fusion.1
  7.0 0.8 add_select_fusion.1.loc_ref
  7.7 0.0 copy-start
  7.8 1.0 %copy-done = bf16[128,2048]{1,0:T(8,128)(2,1)S(1)} copy-done((bf16[128,2048]{1,0:T(8,128)(2,1)S(1)}, bf16[128,2048]{1,0:T(8,128)(2,1)}, u32[]{:S(2)}) %copy-start) | copy-done | bytes 524312
  8.8 0.0 copy-start.2
  8.8 3.1 %copy-done.2 = bf16[8,7,256,256]{3,2,1,0:T(8,128)(2,1)S(1)} copy-done((bf16[8,7,256,256]{3,2,1,0:T(8,128)(2,1)S(1)}, bf16[8,7,256,256]{3,2,1,0:T(8,128)(2,1)}, u32[]{:S(2)}) %copy-start.2) | copy-done | bytes 7340056
  11.9 0.0 copy-start.1
  11.9 2.7 %shard_map.50 = (bf16[8,7,256,256]{3,2,1,0:T(8,128)(2,1)S(1)}, f32[128,2048]{1,0:T(8,128)S(1)}) custom-call(s32[8,6]{1,0:T(8,128)S(1)} %add_select_fusion.1.loc_ref, s32[1]{0:T(128)S(6)} %select_n.21.odd_ref, bf16[128,2048]{1,0:T(8,128)(2,1)S(1)} %copy-done, bf16[8,7,256,256]{3,2,1,0:T(8,128)(2,1)S(1)} %copy-done.2), custom_call_target="tpu_custom_call" | custom-call | flops 671088640 | bytes 14680064 | tf_op jit(solution)/shard_map/pallas_call | solution.py:55
  14.6 0.0 collective-permute-done.1.far_ref
  14.6 0.0 collective-permute-done.near_ref
  14.6 0.0 copy-done.1
  14.6 1.1 %shard_map.51.vec_ref.prior_ref = bf16[128,2048]{1,0:T(8,128)(2,1)S(1)} custom-call(s32[8,6]{1,0:T(8,128)S(1)} %add_select_fusion.1.loc_ref, bf16[128,2048]{1,0:T(8,128)(2,1)S(1)} %collective-permute-done.near_ref, bf16[128,2048]{1,0:T(8,128)(2,1)S(1)} %collective-permute-done.1.far_ref, f32[128,2048]{1,0:T(8,128)S(1)} %get-tuple-element.10.acc_ref, ...), custom_call_target="tpu_custom_call" | custom-call | flops 268435456 | bytes 2097152 | tf_op jit(solution)/shard_map/pallas_call | solution.py:123
  15.8 3.2 %collective-permute-start.3 = (bf16[128,2048]{1,0:T(8,128)(2,1)S(1)}, bf16[128,2048]{1,0:T(8,128)(2,1)S(1)}, u32[]{:S(2)}, u32[]{:S(2)}) collective-permute-start(bf16[128,2048]{1,0:T(8,128)(2,1)S(1)} %shard_map.51.vec_ref.prior_ref), channel_id=1, source_target_pairs={{0,30},{2,4},{4,2},{6,8},{8,6},{10,12},{12,10},{14,16},{16,14},{18... | collective-permute-start | bytes 1572872 | tf_op jit(solution)/shard_map/ppermute | solution.py:332
  18.9 0.5 collective-permute-start.2
  19.4 1.5 %shard_map.52.acc_ref = f32[128,2048]{1,0:T(8,128)S(1)} custom-call(s32[8,6]{1,0:T(8,128)S(1)} %add_select_fusion.1.loc_ref, bf16[128,2048]{1,0:T(8,128)(2,1)S(1)} %shard_map.51.vec_ref.prior_ref, bf16[8,7,256,256]{3,2,1,0:T(8,128)(2,1)S(1)} %get-tuple-element.11.turned_ref), custom_call_target="tpu_custom_call" | custom-call | flops 671088640 | bytes 5242880 | tf_op jit(solution)/shard_map/pallas_call | solution.py:88
  20.9 6.3 %collective-permute-done.3.far_ref = bf16[128,2048]{1,0:T(8,128)(2,1)S(1)} collective-permute-done((bf16[128,2048]{1,0:T(8,128)(2,1)S(1)}, bf16[128,2048]{1,0:T(8,128)(2,1)S(1)}, u32[]{:S(2)}, u32[]{:S(2)}) %collective-permute-start.3) | collective-permute-done | bytes 524320 | tf_op jit(solution)/shard_map/ppermute | solution.py:332
  27.2 0.0 collective-permute-done.2.near_ref
  27.2 1.2 %shard_map.53.vec_ref = bf16[128,2048]{1,0:T(8,128)(2,1)S(1)} custom-call(s32[8,6]{1,0:T(8,128)S(1)} %add_select_fusion.1.loc_ref, bf16[128,2048]{1,0:T(8,128)(2,1)S(1)} %collective-permute-done.2.near_ref, bf16[128,2048]{1,0:T(8,128)(2,1)S(1)} %collective-permute-done.3.far_ref, f32[128,2048]{1,0:T(8,128)S(1)} %shard_map.52.acc_ref, ...), custom_call_target="tpu_custom_call" | custom-call | flops 268435456 | bytes 2097152 | tf_op jit(solution)/shard_map/pallas_call | solution.py:123
  28.4 3.2 %collective-permute-start.5 = (bf16[128,2048]{1,0:T(8,128)(2,1)S(1)}, bf16[128,2048]{1,0:T(8,128)(2,1)S(1)}, u32[]{:S(2)}, u32[]{:S(2)}) collective-permute-start(bf16[128,2048]{1,0:T(8,128)(2,1)S(1)} %shard_map.53.vec_ref), channel_id=1, source_target_pairs={{0,30},{2,4},{4,2},{6,8},{8,6},{10,12},{12,10},{14,16},{16,14},{18... | collective-permute-start | bytes 1572872 | tf_op jit(solution)/shard_map/ppermute | solution.py:332
  31.6 5.7 %collective-permute-start.4 = (bf16[128,2048]{1,0:T(8,128)(2,1)S(1)}, bf16[128,2048]{1,0:T(8,128)(2,1)S(1)}, u32[]{:S(2)}, u32[]{:S(2)}) collective-permute-start(bf16[128,2048]{1,0:T(8,128)(2,1)S(1)} %shard_map.53.vec_ref), channel_id=1, source_target_pairs={{0,2},{2,0},{4,6},{6,4},{8,10},{10,8},{12,14},{14,12},{16,18},{18,... | collective-permute-start | bytes 1572872 | tf_op jit(solution)/shard_map/ppermute | solution.py:333
  37.3 1.5 %shard_map.54.acc_ref = f32[128,2048]{1,0:T(8,128)S(1)} custom-call(s32[8,6]{1,0:T(8,128)S(1)} %add_select_fusion.1.loc_ref, bf16[128,2048]{1,0:T(8,128)(2,1)S(1)} %shard_map.53.vec_ref, bf16[8,7,256,256]{3,2,1,0:T(8,128)(2,1)S(1)} %get-tuple-element.11.turned_ref), custom_call_target="tpu_custom_call" | custom-call | flops 671088640 | bytes 5242880 | tf_op jit(solution)/shard_map/pallas_call | solution.py:88
  38.8 1.1 %collective-permute-done.5.far_ref = bf16[128,2048]{1,0:T(8,128)(2,1)S(1)} collective-permute-done((bf16[128,2048]{1,0:T(8,128)(2,1)S(1)}, bf16[128,2048]{1,0:T(8,128)(2,1)S(1)}, u32[]{:S(2)}, u32[]{:S(2)}) %collective-permute-start.5) | collective-permute-done | bytes 524320 | tf_op jit(solution)/shard_map/ppermute | solution.py:332
  39.9 0.0 collective-permute-done.4.near_ref
  39.9 1.2 %shard_map.55 = (f32[128,2048]{1,0:T(8,128)S(1)}, bf16[128,2048]{1,0:T(8,128)(2,1)S(1)}) custom-call(s32[8,6]{1,0:T(8,128)S(1)} %add_select_fusion.1.loc_ref, bf16[128,2048]{1,0:T(8,128)(2,1)S(1)} %collective-permute-done.4.near_ref, bf16[128,2048]{1,0:T(8,128)(2,1)S(1)} %collective-permute-done.5.far_ref, f32[128,2048]{1,0:T(8,128)S(1)} %shard_map.54.acc_ref, ...), custom_call_target="tpu_custom_call" | custom-call | flops 268435456 | bytes 2097152 | tf_op jit(solution)/shard_map/pallas_call | solution.py:123
  41.1 1.6 %collective-permute-start.11 = (bf16[128,2048]{1,0:T(8,128)(2,1)S(1)}, bf16[128,2048]{1,0:T(8,128)(2,1)S(1)}, u32[]{:S(2)}, u32[]{:S(2)}) collective-permute-start(bf16[128,2048]{1,0:T(8,128)(2,1)S(1)} %get-tuple-element.13.high_ref.own_ref), channel_id=1, source_target_pairs={{0,1},{1,0},{2,3},{3,2},{4,5},{5,4},{6,7},{7,6},{8,9},{9,8},{10,11... | collective-permute-start | bytes 1572872 | tf_op jit(solution)/shard_map/ppermute | solution.py:353
  42.7 0.5 shard_map.56
  43.2 5.4 %collective-permute-start.6 = (f32[128,128]{1,0:T(8,128)S(1)}, f32[128,128]{1,0:T(8,128)S(1)}, u32[]{:S(2)}, u32[]{:S(2)}) collective-permute-start(f32[128,128]{1,0:T(8,128)S(1)} %shard_map.56), channel_id=1, source_target_pairs={{0,2},{2,0},{4,6},{6,4},{8,10},{10,8},{12,14},{14,12},{16,18},{18,... | collective-permute-start | bytes 196616 | tf_op jit(solution)/shard_map/ppermute | solution.py:346
  48.6 0.9 %collective-permute-done.6 = f32[128,128]{1,0:T(8,128)S(1)} collective-permute-done((f32[128,128]{1,0:T(8,128)S(1)}, f32[128,128]{1,0:T(8,128)S(1)}, u32[]{:S(2)}, u32[]{:S(2)}) %collective-permute-start.6) | collective-permute-done | bytes 65568 | tf_op jit(solution)/shard_map/ppermute | solution.py:346
  49.5 0.9 %collective-permute-start.7 = (f32[128,128]{1,0:T(8,128)S(1)}, f32[128,128]{1,0:T(8,128)S(1)}, u32[]{:S(2)}, u32[]{:S(2)}) collective-permute-start(f32[128,128]{1,0:T(8,128)S(1)} %add.38), channel_id=1, source_target_pairs={{0,4},{2,6},{4,0},{6,2},{8,12},{10,14},{12,8},{14,10},{16,20},{18,... | collective-permute-start | bytes 196616 | tf_op jit(solution)/shard_map/ppermute | solution.py:346
  50.5 0.8 collective-permute-done.11.other_ref
  51.3 0.3 shard_map.57
  51.6 4.6 %collective-permute-start.12 = (f32[128,128]{1,0:T(8,128)S(1)}, f32[128,128]{1,0:T(8,128)S(1)}, u32[]{:S(2)}, u32[]{:S(2)}) collective-permute-start(f32[128,128]{1,0:T(8,128)S(1)} %shard_map.57), channel_id=1, source_target_pairs={{0,2},{2,0},{4,6},{6,4},{8,10},{10,8},{12,14},{14,12},{16,18},{18,... | collective-permute-start | bytes 196616 | tf_op jit(solution)/shard_map/ppermute | solution.py:346
  56.2 0.0 collective-permute-done.7
  56.2 0.6 collective-permute-start.8
  56.8 0.3 collective-permute-done.12
  57.1 1.3 %collective-permute-start.13 = (f32[128,128]{1,0:T(8,128)S(1)}, f32[128,128]{1,0:T(8,128)S(1)}, u32[]{:S(2)}, u32[]{:S(2)}) collective-permute-start(f32[128,128]{1,0:T(8,128)S(1)} %add.42), channel_id=1, source_target_pairs={{0,4},{2,6},{4,0},{6,2},{8,12},{10,14},{12,8},{14,10},{16,20},{18,... | collective-permute-start | bytes 196616 | tf_op jit(solution)/shard_map/ppermute | solution.py:346
  58.4 2.2 %collective-permute-done.8 = f32[128,128]{1,0:T(8,128)S(1)} collective-permute-done((f32[128,128]{1,0:T(8,128)S(1)}, f32[128,128]{1,0:T(8,128)S(1)}, u32[]{:S(2)}, u32[]{:S(2)}) %collective-permute-start.8) | collective-permute-done | bytes 65568 | tf_op jit(solution)/shard_map/ppermute | solution.py:346
  60.6 1.6 %collective-permute-start.9 = (f32[128,128]{1,0:T(8,128)S(1)}, f32[128,128]{1,0:T(8,128)S(1)}, u32[]{:S(2)}, u32[]{:S(2)}) collective-permute-start(f32[128,128]{1,0:T(8,128)S(1)} %add.40), channel_id=1, source_target_pairs={{0,16},{2,18},{4,20},{6,22},{8,24},{10,26},{12,28},{14,30},{16,0},... | collective-permute-start | bytes 196616 | tf_op jit(solution)/shard_map/ppermute | solution.py:346
  62.1 0.0 collective-permute-done.13
  62.1 0.6 collective-permute-start.14
  62.7 3.8 %collective-permute-done.9 = f32[128,128]{1,0:T(8,128)S(1)} collective-permute-done((f32[128,128]{1,0:T(8,128)S(1)}, f32[128,128]{1,0:T(8,128)S(1)}, u32[]{:S(2)}, u32[]{:S(2)}) %collective-permute-start.9) | collective-permute-done | bytes 65568 | tf_op jit(solution)/shard_map/ppermute | solution.py:346
  66.5 1.6 %collective-permute-start.10 = (f32[128,128]{1,0:T(8,128)S(1)}, f32[128,128]{1,0:T(8,128)S(1)}, u32[]{:S(2)}, u32[]{:S(2)}) collective-permute-start(f32[128,128]{1,0:T(8,128)S(1)} %add.41.own_ref), channel_id=1, source_target_pairs={{0,1},{1,0},{2,3},{3,2},{4,5},{5,4},{6,7},{7,6},{8,9},{9,8},{10,11... | collective-permute-start | bytes 196616 | tf_op jit(solution)/shard_map/ppermute | solution.py:364
  68.1 0.0 collective-permute-done.14
  68.1 0.8 collective-permute-start.15
  68.9 1.9 %collective-permute-done.10.other_ref = f32[128,128]{1,0:T(8,128)S(1)} collective-permute-done((f32[128,128]{1,0:T(8,128)S(1)}, f32[128,128]{1,0:T(8,128)S(1)}, u32[]{:S(2)}, u32[]{:S(2)}) %collective-permute-start.10) | collective-permute-done | bytes 65568 | tf_op jit(solution)/shard_map/ppermute | solution.py:364
  70.9 4.7 %shard_map.58 = (f32[128,128]{1,0:T(8,128)S(1)}, f32[128,128]{1,0:T(8,128)S(1)}) custom-call(s32[1]{0:T(128)} %bitcast.place_ref, f32[128,128]{1,0:T(8,128)S(1)} %add.41.own_ref, f32[128,128]{1,0:T(8,128)S(1)} %collective-permute-done.10.other_ref), custom_call_target="tpu_custom_call" | custom-call | flops 4194304 | bytes 16777216 | tf_op jit(solution)/shard_map/pallas_call | solution.py:277
  75.5 0.0 collective-permute-done.15
  75.6 6.5 %shard_map.59 = (f32[256,256]{1,0:T(8,128)}, f32[256,256]{1,0:T(8,128)S(1)}) custom-call(s32[1]{0:T(128)} %bitcast.place_ref, f32[128,128]{1,0:T(8,128)S(1)} %add.41.own_ref, f32[128,128]{1,0:T(8,128)S(1)} %collective-permute-done.10.other_ref, f32[128,128]{1,0:T(8,128)S(1)} %add.45.cross_ref, f32[128,128]{1,0:T(8,128)S(1)} %get-tuple-element.14.first_ref, ...), custom_call_target="tpu_custom_call" | custom-call | tf_op jit(solution)/shard_map/pallas_call | solution.py:286
  82.1 1.8 %shard_map.60 = f32[128,2048]{1,0:T(8,128)} custom-call(s32[1]{0:T(128)} %bitcast.place_ref, f32[256,256]{1,0:T(8,128)S(1)} %get-tuple-element.16.inv_ref, f32[128,2048]{1,0:T(8,128)S(1)} %get-tuple-element.12.own_ref, bf16[128,2048]{1,0:T(8,128)(2,1)S(1)} %collective-permute-done.11.other_ref), custom_call_target="tpu_custom_call" | custom-call | tf_op jit(solution)/shard_map/pallas_call | solution.py:380
  (8 shorter events, 0.1 us)
Async XLA Ops:
  0.6 14.0 %collective-permute-start.1 = (bf16[128,2048]{1,0:T(8,128)(2,1)}, bf16[128,2048]{1,0:T(8,128)(2,1)S(1)}, u32[]{:S(2)}, u32[]{:S(2)}) collective-permute-start(bf16[128,2048]{1,0:T(8,128)(2,1)} %prior_ref.3), channel_id=1, source_target_pairs={{0,30},{2,4},{4,2},{6,8},{8,6},{10,12},{12,10},{14,16},{16,14},{18... | collective-permute-start | bytes 1572872 | tf_op jit(solution)/shard_map/ppermute | solution.py:332
  6.1 8.5 %collective-permute-start = (bf16[128,2048]{1,0:T(8,128)(2,1)}, bf16[128,2048]{1,0:T(8,128)(2,1)S(1)}, u32[]{:S(2)}, u32[]{:S(2)}) collective-permute-start(bf16[128,2048]{1,0:T(8,128)(2,1)} %prior_ref.3), channel_id=1, source_target_pairs={{0,2},{2,0},{4,6},{6,4},{8,10},{10,8},{12,14},{14,12},{16,18},{18,... | collective-permute-start | bytes 1572872 | tf_op jit(solution)/shard_map/ppermute | solution.py:333
  7.7 1.0 %copy-start = (bf16[128,2048]{1,0:T(8,128)(2,1)S(1)}, bf16[128,2048]{1,0:T(8,128)(2,1)}, u32[]{:S(2)}) copy-start(bf16[128,2048]{1,0:T(8,128)(2,1)} %prior_ref.3) | copy-start | bytes 1572868
  8.8 3.1 %copy-start.2 = (bf16[8,7,256,256]{3,2,1,0:T(8,128)(2,1)S(1)}, bf16[8,7,256,256]{3,2,1,0:T(8,128)(2,1)}, u32[]{:S(2)}) copy-start(bf16[8,7,256,256]{3,2,1,0:T(8,128)(2,1)} %ham_ref.1) | copy-start | bytes 22020100
  11.9 2.8 %copy-start.1 = (bf16[128,2048]{1,0:T(8,128)(2,1)S(1)}, bf16[128,2048]{1,0:T(8,128)(2,1)}, u32[]{:S(2)}) copy-start(bf16[128,2048]{1,0:T(8,128)(2,1)} %prior_ref.3) | copy-start | bytes 1572868
  15.8 11.5 %collective-permute-start.3 = (bf16[128,2048]{1,0:T(8,128)(2,1)S(1)}, bf16[128,2048]{1,0:T(8,128)(2,1)S(1)}, u32[]{:S(2)}, u32[]{:S(2)}) collective-permute-start(bf16[128,2048]{1,0:T(8,128)(2,1)S(1)} %shard_map.51.vec_ref.prior_ref), channel_id=1, source_target_pairs={{0,30},{2,4},{4,2},{6,8},{8,6},{10,12},{12,10},{14,16},{16,14},{18... | collective-permute-start | bytes 1572872 | tf_op jit(solution)/shard_map/ppermute | solution.py:332
  18.9 8.3 %collective-permute-start.2 = (bf16[128,2048]{1,0:T(8,128)(2,1)S(1)}, bf16[128,2048]{1,0:T(8,128)(2,1)S(1)}, u32[]{:S(2)}, u32[]{:S(2)}) collective-permute-start(bf16[128,2048]{1,0:T(8,128)(2,1)S(1)} %shard_map.51.vec_ref.prior_ref), channel_id=1, source_target_pairs={{0,2},{2,0},{4,6},{6,4},{8,10},{10,8},{12,14},{14,12},{16,18},{18,... | collective-permute-start | bytes 1572872 | tf_op jit(solution)/shard_map/ppermute | solution.py:333
  28.4 11.5 %collective-permute-start.5 = (bf16[128,2048]{1,0:T(8,128)(2,1)S(1)}, bf16[128,2048]{1,0:T(8,128)(2,1)S(1)}, u32[]{:S(2)}, u32[]{:S(2)}) collective-permute-start(bf16[128,2048]{1,0:T(8,128)(2,1)S(1)} %shard_map.53.vec_ref), channel_id=1, source_target_pairs={{0,30},{2,4},{4,2},{6,8},{8,6},{10,12},{12,10},{14,16},{16,14},{18... | collective-permute-start | bytes 1572872 | tf_op jit(solution)/shard_map/ppermute | solution.py:332
  31.6 8.3 %collective-permute-start.4 = (bf16[128,2048]{1,0:T(8,128)(2,1)S(1)}, bf16[128,2048]{1,0:T(8,128)(2,1)S(1)}, u32[]{:S(2)}, u32[]{:S(2)}) collective-permute-start(bf16[128,2048]{1,0:T(8,128)(2,1)S(1)} %shard_map.53.vec_ref), channel_id=1, source_target_pairs={{0,2},{2,0},{4,6},{6,4},{8,10},{10,8},{12,14},{14,12},{16,18},{18,... | collective-permute-start | bytes 1572872 | tf_op jit(solution)/shard_map/ppermute | solution.py:333
  41.1 10.1 %collective-permute-start.11 = (bf16[128,2048]{1,0:T(8,128)(2,1)S(1)}, bf16[128,2048]{1,0:T(8,128)(2,1)S(1)}, u32[]{:S(2)}, u32[]{:S(2)}) collective-permute-start(bf16[128,2048]{1,0:T(8,128)(2,1)S(1)} %get-tuple-element.13.high_ref.own_ref), channel_id=1, source_target_pairs={{0,1},{1,0},{2,3},{3,2},{4,5},{5,4},{6,7},{7,6},{8,9},{9,8},{10,11... | collective-permute-start | bytes 1572872 | tf_op jit(solution)/shard_map/ppermute | solution.py:353
  43.2 6.3 %collective-permute-start.6 = (f32[128,128]{1,0:T(8,128)S(1)}, f32[128,128]{1,0:T(8,128)S(1)}, u32[]{:S(2)}, u32[]{:S(2)}) collective-permute-start(f32[128,128]{1,0:T(8,128)S(1)} %shard_map.56), channel_id=1, source_target_pairs={{0,2},{2,0},{4,6},{6,4},{8,10},{10,8},{12,14},{14,12},{16,18},{18,... | collective-permute-start | bytes 196616 | tf_op jit(solution)/shard_map/ppermute | solution.py:346
  49.5 6.7 %collective-permute-start.7 = (f32[128,128]{1,0:T(8,128)S(1)}, f32[128,128]{1,0:T(8,128)S(1)}, u32[]{:S(2)}, u32[]{:S(2)}) collective-permute-start(f32[128,128]{1,0:T(8,128)S(1)} %add.38), channel_id=1, source_target_pairs={{0,4},{2,6},{4,0},{6,2},{8,12},{10,14},{12,8},{14,10},{16,20},{18,... | collective-permute-start | bytes 196616 | tf_op jit(solution)/shard_map/ppermute | solution.py:346
  51.6 5.5 %collective-permute-start.12 = (f32[128,128]{1,0:T(8,128)S(1)}, f32[128,128]{1,0:T(8,128)S(1)}, u32[]{:S(2)}, u32[]{:S(2)}) collective-permute-start(f32[128,128]{1,0:T(8,128)S(1)} %shard_map.57), channel_id=1, source_target_pairs={{0,2},{2,0},{4,6},{6,4},{8,10},{10,8},{12,14},{14,12},{16,18},{18,... | collective-permute-start | bytes 196616 | tf_op jit(solution)/shard_map/ppermute | solution.py:346
  56.2 4.3 %collective-permute-start.8 = (f32[128,128]{1,0:T(8,128)S(1)}, f32[128,128]{1,0:T(8,128)S(1)}, u32[]{:S(2)}, u32[]{:S(2)}) collective-permute-start(f32[128,128]{1,0:T(8,128)S(1)} %add.39), channel_id=1, source_target_pairs={{0,8},{2,10},{4,12},{6,14},{8,0},{10,2},{12,4},{14,6},{16,24},{18,... | collective-permute-start | bytes 196616 | tf_op jit(solution)/shard_map/ppermute | solution.py:346
  57.1 5.0 %collective-permute-start.13 = (f32[128,128]{1,0:T(8,128)S(1)}, f32[128,128]{1,0:T(8,128)S(1)}, u32[]{:S(2)}, u32[]{:S(2)}) collective-permute-start(f32[128,128]{1,0:T(8,128)S(1)} %add.42), channel_id=1, source_target_pairs={{0,4},{2,6},{4,0},{6,2},{8,12},{10,14},{12,8},{14,10},{16,20},{18,... | collective-permute-start | bytes 196616 | tf_op jit(solution)/shard_map/ppermute | solution.py:346
  60.6 6.0 %collective-permute-start.9 = (f32[128,128]{1,0:T(8,128)S(1)}, f32[128,128]{1,0:T(8,128)S(1)}, u32[]{:S(2)}, u32[]{:S(2)}) collective-permute-start(f32[128,128]{1,0:T(8,128)S(1)} %add.40), channel_id=1, source_target_pairs={{0,16},{2,18},{4,20},{6,22},{8,24},{10,26},{12,28},{14,30},{16,0},... | collective-permute-start | bytes 196616 | tf_op jit(solution)/shard_map/ppermute | solution.py:346
  62.1 6.0 %collective-permute-start.14 = (f32[128,128]{1,0:T(8,128)S(1)}, f32[128,128]{1,0:T(8,128)S(1)}, u32[]{:S(2)}, u32[]{:S(2)}) collective-permute-start(f32[128,128]{1,0:T(8,128)S(1)} %add.43), channel_id=1, source_target_pairs={{0,8},{2,10},{4,12},{6,14},{8,0},{10,2},{12,4},{14,6},{16,24},{18,... | collective-permute-start | bytes 196616 | tf_op jit(solution)/shard_map/ppermute | solution.py:346
  66.5 4.3 %collective-permute-start.10 = (f32[128,128]{1,0:T(8,128)S(1)}, f32[128,128]{1,0:T(8,128)S(1)}, u32[]{:S(2)}, u32[]{:S(2)}) collective-permute-start(f32[128,128]{1,0:T(8,128)S(1)} %add.41.own_ref), channel_id=1, source_target_pairs={{0,1},{1,0},{2,3},{3,2},{4,5},{5,4},{6,7},{7,6},{8,9},{9,8},{10,11... | collective-permute-start | bytes 196616 | tf_op jit(solution)/shard_map/ppermute | solution.py:364
  68.1 7.5 %collective-permute-start.15 = (f32[128,128]{1,0:T(8,128)S(1)}, f32[128,128]{1,0:T(8,128)S(1)}, u32[]{:S(2)}, u32[]{:S(2)}) collective-permute-start(f32[128,128]{1,0:T(8,128)S(1)} %add.44), channel_id=1, source_target_pairs={{0,16},{2,18},{4,20},{6,22},{8,24},{10,26},{12,28},{14,30},{16,0},... | collective-permute-start | bytes 196616 | tf_op jit(solution)/shard_map/ppermute | solution.py:346

commit v7 on v6

--- a/solution.py
+++ b/solution.py
@@ -31,8 +31,9 @@
     return high, (a - high.astype(jnp.float32)).astype(jnp.bfloat16)
 
 
-def turn_kernel(loc_ref, odd_ref, vec_ref, ham_ref, turned_ref, out_ref):
+def turn_kernel(loc_ref, odd_ref, vec_ref, ham_ref, turned_ref, *outs):
     count, faces, width, _ = ham_ref.shape
+    share = outs[0].shape[0]
     odd = odd_ref[0]
     for e in range(count):
         here = slice(e * width, (e + 1) * width)
@@ -46,20 +47,21 @@
             at = here if face == 0 else pl.ds(pl.multiple_of(loc_ref[e, face - 1] * width, width), width)
             part = jnp.dot(vec_ref[:, at], turned, preferred_element_type=jnp.float32)
             total = part if total is None else total + part
-        out_ref[:, here] = total
-
-
-def turn_part(vec, hamiltonian, loc, odd):
+        for piece, out in enumerate(outs):
+            out[:, here] = total[piece * share : (piece + 1) * share]
+
+
+def turn_part(vec, hamiltonian, loc, odd, chunks):
     count, faces, width, _ = hamiltonian.shape
     owned = vec.shape[0]
     return pl.pallas_call(
         turn_kernel,
         out_shape=[
             jax.ShapeDtypeStruct(hamiltonian.shape, hamiltonian.dtype),
-            jax.ShapeDtypeStruct(vec.shape, jnp.float32),
+            *[jax.ShapeDtypeStruct((owned // chunks, vec.shape[1]), jnp.float32)] * chunks,
         ],
         in_specs=[pl.BlockSpec(memory_space=pltpu.SMEM)] * 2 + vmem(2),
-        out_specs=vmem(2),
+        out_specs=vmem(1 + chunks),
         compiler_params=pltpu.CompilerParams(vmem_limit_bytes=32 << 20),
         cost_estimate=pl.CostEstimate(
             flops=2 * owned * count * width * width * 5,
@@ -134,21 +136,28 @@
     )(loc, near, far, acc, vec, prior, turned)
 
 
-def own_gram_kernel(own_ref, high_ref, out_ref):
-    high = high_ref[...]
-    low = (own_ref[...] - high.astype(jnp.float32)).astype(jnp.bfloat16)
+def stacked(refs, here=slice(None)):
+    return jnp.concatenate([ref[:, here] for ref in refs], axis=0)
+
+
+def own_gram_kernel(chunks, *refs):
+    own_refs, high_refs, out_ref = refs[:chunks], refs[chunks:-1], refs[-1]
+    high = stacked(high_refs)
+    low = (stacked(own_refs) - high.astype(jnp.float32)).astype(jnp.bfloat16)
     mixed = dot_nt(high, low)
     out_ref[...] = dot_nt(high, high) + (mixed + mixed.T)
 
 
-def cross_gram_kernel(place_ref, own_ref, other_ref, out_ref):
+def cross_gram_kernel(chunks, place_ref, *refs):
+    own_refs, other_refs, out_ref = refs[:chunks], refs[chunks:-1], refs[-1]
+
     @pl.when(place_ref[0] == 0)
     def _():
-        out_ref[...] = dot_nt(own_ref[...], other_ref[...])
+        out_ref[...] = dot_nt(stacked(own_refs), stacked(other_refs))
 
     @pl.when(place_ref[0] != 0)
     def _():
-        out_ref[...] = dot_nt(other_ref[...], own_ref[...])
+        out_ref[...] = dot_nt(stacked(other_refs), stacked(own_refs))
 
 
 def factor_block(rows, right):
@@ -293,7 +302,8 @@
     )(place, own, other, cross, first, first_inv)
 
 
-def basis_kernel(place_ref, inv_ref, own_ref, other_ref, out_ref):
+def basis_kernel(chunks, place_ref, inv_ref, *refs):
+    own_refs, other_refs, out_ref = refs[:chunks], refs[chunks:-1], refs[-1]
     half, total = out_ref.shape
     place = place_ref[0]
     rows = pl.ds(pl.multiple_of(place * half, half), half)
@@ -303,8 +313,8 @@
     step = 512 if total % 512 == 0 else total
     for at in range(0, total, step):
         here = slice(at, at + step)
-        high, low = split(own_ref[:, here])
-        other = other_ref[:, here]
+        high, low = split(stacked(own_refs, here))
+        other = stacked(other_refs, here)
         out_ref[:, here] = (
             jnp.dot(near_high, high, preferred_element_type=jnp.float32)
             + jnp.dot(near_high, low, preferred_element_type=jnp.float32)
@@ -320,6 +330,8 @@
     blocks = lax.axis_size("space")
     groups = lax.axis_size("orb")
     half = owned * groups // 2
+    chunks = 2
+    share = owned // chunks
     odd = lax.axis_index("space").astype(jnp.int32).reshape(1) % 2
     loc = adjacency % count
     swapped = jnp.concatenate([loc[:, 1:2], loc[:, 0:1], loc[:, 2:]], axis=1)
@@ -328,17 +340,26 @@
     far_pairs = [(i, (i + 1 if i % 2 else i - 1) % blocks) for i in range(blocks)]
     smem = [pl.BlockSpec(memory_space=pltpu.SMEM)]
 
-    def halo(vec):
+    def level(number, vec, prior, turned):
         far = lax.ppermute(vec, "space", far_pairs)
-        return lax.ppermute(vec, "space", near_pairs), far
-
-    side = halo(orbitals)
-    turned, acc = turn_part(orbitals, hamiltonian, loc, odd)
-    (one,) = halo_part(1, *side, acc, orbitals, orbitals, turned, loc)
-    side = halo(one)
-    (two,) = halo_part(2, *side, own_part(one, turned, loc), one, orbitals, turned, loc)
-    side = halo(two)
-    filtered, narrow = halo_part(3, *side, own_part(two, turned, loc), two, one, turned, loc)
+        near = lax.ppermute(vec, "space", near_pairs)
+        acc = own_part(vec, turned, loc)
+        return halo_part(number, near, far, acc, vec, prior, turned, loc)
+
+    zero = [orbitals[piece * share : (piece + 1) * share] for piece in range(chunks)]
+    far = [lax.ppermute(vec, "space", far_pairs) for vec in zero]
+    near = [lax.ppermute(vec, "space", near_pairs) for vec in zero]
+    turned, *accs = turn_part(orbitals, hamiltonian, loc, odd, chunks)
+    one, two, filtered, narrow = [], [], [], []
+    for piece in range(chunks):
+        base = zero[piece]
+        one += halo_part(1, near[piece], far[piece], accs[piece], base, base, turned, loc)
+    for piece in range(chunks):
+        two += level(2, one[piece], zero[piece], turned)
+    for piece in range(chunks):
+        wide, short = level(3, two[piece], one[piece], turned)
+        filtered.append(wide)
+        narrow.append(short)
 
     def summed(part):
         step = 1
@@ -350,44 +371,44 @@
     place = lax.axis_index("orb").astype(jnp.int32).reshape(1)
     if groups == 2:
         swap = [(0, 1), (1, 0)]
-        other = lax.ppermute(narrow, "orb", swap)
+        other = [lax.ppermute(piece, "orb", swap) for piece in narrow]
         tile = jax.ShapeDtypeStruct((half, half), jnp.float32)
         params = pltpu.CompilerParams(vmem_limit_bytes=24 << 20)
         near = pl.pallas_call(
-            own_gram_kernel,
+            functools.partial(own_gram_kernel, chunks),
             out_shape=tile,
-            in_specs=vmem(2),
+            in_specs=vmem(2 * chunks),
             out_specs=pl.BlockSpec(memory_space=pltpu.VMEM),
             compiler_params=params,
-        )(filtered, narrow)
+        )(*filtered, *narrow)
         near = summed(near)
         far = lax.ppermute(near, "orb", swap)
         cross = pl.pallas_call(
-            cross_gram_kernel,
+            functools.partial(cross_gram_kernel, chunks),
             out_shape=tile,
-            in_specs=smem + vmem(2),
+            in_specs=smem + vmem(2 * chunks),
             out_specs=pl.BlockSpec(memory_space=pltpu.VMEM),
             compiler_params=params,
-        )(place, narrow, other)
+        )(place, *narrow, *other)
         upper, inverse = factorize(place, near, far, summed(cross))
     else:
-        columns = lax.all_gather(narrow, "orb", axis=0, tiled=True)
+        columns = lax.all_gather(jnp.concatenate(narrow), "orb", axis=0, tiled=True)
         whole = summed(dot_nt(columns, columns))
         upper, inverse = factorize(
             jnp.zeros_like(place), whole[:half, :half], whole[half:, half:], whole[:half, half:]
         )
     if groups == 2:
         basis = pl.pallas_call(
-            basis_kernel,
+            functools.partial(basis_kernel, chunks),
             out_shape=jax.ShapeDtypeStruct(orbitals.shape, jnp.float32),
-            in_specs=smem + vmem(3),
+            in_specs=smem + vmem(1 + 2 * chunks),
             out_specs=pl.BlockSpec(memory_space=pltpu.VMEM),
             compiler_params=pltpu.CompilerParams(vmem_limit_bytes=24 << 20),
-        )(place, inverse, filtered, other)
+        )(place, inverse, *filtered, *other)
     else:
         mine = lax.dynamic_slice_in_dim(inverse, place[0] * owned, owned, 0)
         near = lax.dynamic_slice_in_dim(mine, place[0] * owned, owned, 1)
-        rest = filtered - narrow.astype(jnp.float32)
+        rest = jnp.concatenate(filtered) - jnp.concatenate(narrow).astype(jnp.float32)
         basis = dot_full(mine, columns.astype(jnp.float32)) + dot_full(near, rest)
     return (basis, upper)
 

time: 84.2 us -> 85.1 us (1.011)
  starting transfers between devices: 36.9 us -> 29.1 us
  Pallas kernels: 23.1 us -> 29.7 us
  local copies, waits for them, and re-layouts: 4.27 us -> 5.34 us
  waiting for transfers between devices: 17.4 us -> 18.3 us
    ppermute x8, starting transfers between devices: 15.8 us -> 5.46 us  [summed(): lax.ppermute(part, 'space', [(i, i ^ step) for i in range(blocks)])]
    pallas_call x2 -> x4, Pallas kernels: 3 us -> 6.58 us  [own_part(): pl.pallas_call(own_kernel, out_shape=jax.ShapeDtypeStruct(vec.shape, jnp....]
    pallas_call x3 -> x6, Pallas kernels: 3.51 us -> 6.76 us  [halo_part(): pl.pallas_call(functools.partial(halo_kernel, level), out_shape=[jax.Shap...]
    ppermute x8, waiting for transfers between devices: 7.18 us -> 10.3 us  [summed(): lax.ppermute(part, 'space', [(i, i ^ step) for i in range(blocks)])]
    ppermute x7 -> x14, waiting for transfers between devices: 8.25 us -> 5.28 us  [the longest x2 5.25 us: shards(): other = [lax.ppermute(piece, 'orb', swap) for piece in narrow]]
    ppermute x7 -> x14, starting transfers between devices: 19.6 us -> 22.1 us  [the longest x4 10.9 us: level(): far = lax.ppermute(vec, 'space', far_pairs)]
    slice x0 -> x1, local copies, waits for them, and re-layouts: none -> 1.07 us  [shards(): orbitals[piece * share:(piece + 1) * share]]
    unnamed x6 -> x4, local copies, waits for them, and re-layouts: 4.13 us -> 4.12 us
  transfers between devices with their start and end apart: 16 -> 23, of which waited for: 8 -> 8; matrix products, arithmetic and copies ran while one was open for 2% -> 2% of each run, Pallas kernels for 13% -> 25%
where the time goes in v7:
time: 85.1 us; the launch traced here: 84.9 us
  Pallas kernels  29.7 us (35%)
  starting transfers between devices  29.1 us (34%)
  waiting for transfers between devices  18.3 us (22%)
  local copies, waits for them, and re-layouts  5.34 us (6%)
  other arithmetic  1.54 us (2%)
  between operations  0.88 us (1%)
    ppermute x4, starting transfers between devices, level(): far = lax.ppermute(vec, 'space', far_pairs)  10.9 us
    ppermute x8, waiting for transfers between devices, summed(): lax.ppermute(part, 'space', [(i, i ^ step) for i in range(blocks)])  10.3 us
    pallas_call x6, Pallas kernels, halo_part(): pl.pallas_call(functools.partial(halo_kernel, level), out_shape=[jax.Shap...  6.76 us
    pallas_call x4, Pallas kernels, own_part(): pl.pallas_call(own_kernel, out_shape=jax.ShapeDtypeStruct(vec.shape, jnp....  6.58 us
    pallas_call x1, Pallas kernels, factorize(): pl.pallas_call(second_kernel, out_shape=[jax.ShapeDtypeStruct((2 * half,...  6.35 us
    ppermute x2, starting transfers between devices, shards(): far = [lax.ppermute(vec, 'space', far_pairs) for vec in zero]  6.29 us
    ppermute x8, starting transfers between devices, summed(): lax.ppermute(part, 'space', [(i, i ^ step) for i in range(blocks)])  5.46 us
    ppermute x2, waiting for transfers between devices, shards(): other = [lax.ppermute(piece, 'orb', swap) for piece in narrow]  5.25 us
  transfers between devices with their start and end apart: 23, of which 8 were waited for; matrix products, arithmetic and copies ran while one was open for 2% of the time, Pallas kernels for 25%

profile of v7, /device:TPU:0, one launch (start us, length us, event | category | flops | bytes accessed | tf_op | source)
XLA Modules:
  0.0 84.9 jit_solution(473581296619787221)
XLA Ops:
  0.6 1.1 %fusion.1 = (bf16[64,2048]{1,0:T(8,128)(2,1)S(1)}, bf16[64,2048]{1,0:T(8,128)(2,1)S(1)}) fusion(bf16[128,2048]{1,0:T(8,128)(2,1)} %vec_ref.1), kind=kLoop, calls=%fused_computation.5 | loop fusion | bytes 1048576 | tf_op jit(solution)/shard_map/slice | solution.py:349
  1.7 0.5 collective-permute-start.6
  2.2 5.7 %collective-permute-start.7 = (bf16[64,2048]{1,0:T(8,128)(2,1)S(1)}, bf16[64,2048]{1,0:T(8,128)(2,1)S(1)}, u32[]{:S(2)}, u32[]{:S(2)}) collective-permute-start(bf16[64,2048]{1,0:T(8,128)(2,1)S(1)} %get-tuple-element.24.vec_ref.prior_ref), channel_id=1, source_target_pairs={{0,30},{2,4},{4,2},{6,8},{8,6},{10,12},{12,10},{14,16},{16,14},{18... | collective-permute-start | bytes 786440 | tf_op jit(solution)/shard_map/ppermute | solution.py:350
  7.9 0.0 collective-permute-start
  7.9 0.6 collective-permute-start.1
  8.5 0.7 add_select_fusion
  9.2 0.1 fusion.2
  9.3 0.1 slice.17
  9.3 0.8 add_select_fusion.1.loc_ref
  10.1 3.1 %copy-done = bf16[8,7,256,256]{3,2,1,0:T(8,128)(2,1)S(1)} copy-done((bf16[8,7,256,256]{3,2,1,0:T(8,128)(2,1)S(1)}, bf16[8,7,256,256]{3,2,1,0:T(8,128)(2,1)}, u32[]{:S(2)}) %copy-start) | copy-done | bytes 7340056
  13.2 1.0 %copy-done.1 = bf16[128,2048]{1,0:T(8,128)(2,1)S(1)} copy-done((bf16[128,2048]{1,0:T(8,128)(2,1)S(1)}, bf16[128,2048]{1,0:T(8,128)(2,1)}, u32[]{:S(2)}) %copy-start.1) | copy-done | bytes 524312
  14.2 2.7 %shard_map.50 = (bf16[8,7,256,256]{3,2,1,0:T(8,128)(2,1)S(1)}, f32[64,2048]{1,0:T(8,128)S(1)}, f32[64,2048]{1,0:T(8,128)S(1)}) custom-call(s32[8,6]{1,0:T(8,128)S(1)} %add_select_fusion.1.loc_ref, s32[1]{0:T(128)S(6)} %select_n.21.odd_ref, bf16[128,2048]{1,0:T(8,128)(2,1)S(1)} %copy-done.1, bf16[8,7,256,256]{3,2,1,0:T(8,128)(2,1)S(1)} %copy-done), custom_call_target="tpu_custom_call" | custom-call | flops 671088640 | bytes 14680064 | tf_op jit(solution)/shard_map/pallas_call | solution.py:57
  17.0 0.0 collective-permute-done.6.near_ref
  17.0 0.0 collective-permute-done.7.far_ref
  17.0 1.1 %shard_map.56.vec_ref.prior_ref = bf16[64,2048]{1,0:T(8,128)(2,1)S(1)} custom-call(s32[8,6]{1,0:T(8,128)S(1)} %add_select_fusion.1.loc_ref, bf16[64,2048]{1,0:T(8,128)(2,1)S(1)} %collective-permute-done.6.near_ref, bf16[64,2048]{1,0:T(8,128)(2,1)S(1)} %collective-permute-done.7.far_ref, f32[64,2048]{1,0:T(8,128)S(1)} %get-tuple-element.16.acc_ref, ...), custom_call_target="tpu_custom_call" | custom-call | flops 134217728 | bytes 2097152 | tf_op jit(solution)/shard_map/pallas_call | solution.py:125
  18.1 0.1 collective-permute-start.8
  18.2 3.9 %collective-permute-start.9 = (bf16[64,2048]{1,0:T(8,128)(2,1)S(1)}, bf16[64,2048]{1,0:T(8,128)(2,1)S(1)}, u32[]{:S(2)}, u32[]{:S(2)}) collective-permute-start(bf16[64,2048]{1,0:T(8,128)(2,1)S(1)} %shard_map.56.vec_ref.prior_ref), channel_id=1, source_target_pairs={{0,30},{2,4},{4,2},{6,8},{8,6},{10,12},{12,10},{14,16},{16,14},{18... | collective-permute-start | bytes 786440 | tf_op jit(solution)/shard_map/ppermute | solution.py:344
  22.1 0.0 collective-permute-done.1.far_ref
  22.1 1.1 %shard_map.51.vec_ref.prior_ref = bf16[64,2048]{1,0:T(8,128)(2,1)S(1)} custom-call(s32[8,6]{1,0:T(8,128)S(1)} %add_select_fusion.1.loc_ref, bf16[64,2048]{1,0:T(8,128)(2,1)S(1)} %collective-permute-done.near_ref, bf16[64,2048]{1,0:T(8,128)(2,1)S(1)} %collective-permute-done.1.far_ref, f32[64,2048]{1,0:T(8,128)S(1)} %get-tuple-element.13.acc_ref, ...), custom_call_target="tpu_custom_call" | custom-call | flops 134217728 | bytes 2097152 | tf_op jit(solution)/shard_map/pallas_call | solution.py:125
  23.2 0.1 collective-permute-start.2
  23.3 0.7 collective-permute-start.3
  24.0 1.6 %shard_map.57.acc_ref = f32[64,2048]{1,0:T(8,128)S(1)} custom-call(s32[8,6]{1,0:T(8,128)S(1)} %add_select_fusion.1.loc_ref, bf16[64,2048]{1,0:T(8,128)(2,1)S(1)} %shard_map.56.vec_ref.prior_ref, bf16[8,7,256,256]{3,2,1,0:T(8,128)(2,1)S(1)} %get-tuple-element.14.turned_ref), custom_call_target="tpu_custom_call" | custom-call | flops 335544320 | bytes 5242880 | tf_op jit(solution)/shard_map/pallas_call | solution.py:90
  25.6 1.6 %shard_map.52.acc_ref = f32[64,2048]{1,0:T(8,128)S(1)} custom-call(s32[8,6]{1,0:T(8,128)S(1)} %add_select_fusion.1.loc_ref, bf16[64,2048]{1,0:T(8,128)(2,1)S(1)} %shard_map.51.vec_ref.prior_ref, bf16[8,7,256,256]{3,2,1,0:T(8,128)(2,1)S(1)} %get-tuple-element.14.turned_ref), custom_call_target="tpu_custom_call" | custom-call | flops 335544320 | bytes 5242880 | tf_op jit(solution)/shard_map/pallas_call | solution.py:90
  27.3 0.0 collective-permute-done.8.near_ref
  27.3 0.0 collective-permute-done.9.far_ref
  27.3 1.1 %shard_map.58.vec_ref = bf16[64,2048]{1,0:T(8,128)(2,1)S(1)} custom-call(s32[8,6]{1,0:T(8,128)S(1)} %add_select_fusion.1.loc_ref, bf16[64,2048]{1,0:T(8,128)(2,1)S(1)} %collective-permute-done.8.near_ref, bf16[64,2048]{1,0:T(8,128)(2,1)S(1)} %collective-permute-done.9.far_ref, f32[64,2048]{1,0:T(8,128)S(1)} %shard_map.57.acc_ref, ...), custom_call_target="tpu_custom_call" | custom-call | flops 134217728 | bytes 2097152 | tf_op jit(solution)/shard_map/pallas_call | solution.py:125
  28.4 1.6 %collective-permute-start.10 = (bf16[64,2048]{1,0:T(8,128)(2,1)S(1)}, bf16[64,2048]{1,0:T(8,128)(2,1)S(1)}, u32[]{:S(2)}, u32[]{:S(2)}) collective-permute-start(bf16[64,2048]{1,0:T(8,128)(2,1)S(1)} %shard_map.58.vec_ref), channel_id=1, source_target_pairs={{0,2},{2,0},{4,6},{6,4},{8,10},{10,8},{12,14},{14,12},{16,18},{18,... | collective-permute-start | bytes 786440 | tf_op jit(solution)/shard_map/ppermute | solution.py:345
  30.0 2.5 %collective-permute-start.11 = (bf16[64,2048]{1,0:T(8,128)(2,1)S(1)}, bf16[64,2048]{1,0:T(8,128)(2,1)S(1)}, u32[]{:S(2)}, u32[]{:S(2)}) collective-permute-start(bf16[64,2048]{1,0:T(8,128)(2,1)S(1)} %shard_map.58.vec_ref), channel_id=1, source_target_pairs={{0,30},{2,4},{4,2},{6,8},{8,6},{10,12},{12,10},{14,16},{16,14},{18... | collective-permute-start | bytes 786440 | tf_op jit(solution)/shard_map/ppermute | solution.py:344
  32.5 0.0 collective-permute-done.3.far_ref
  32.5 1.1 %shard_map.53.vec_ref = bf16[64,2048]{1,0:T(8,128)(2,1)S(1)} custom-call(s32[8,6]{1,0:T(8,128)S(1)} %add_select_fusion.1.loc_ref, bf16[64,2048]{1,0:T(8,128)(2,1)S(1)} %collective-permute-done.2.near_ref, bf16[64,2048]{1,0:T(8,128)(2,1)S(1)} %collective-permute-done.3.far_ref, f32[64,2048]{1,0:T(8,128)S(1)} %shard_map.52.acc_ref, ...), custom_call_target="tpu_custom_call" | custom-call | flops 134217728 | bytes 2097152 | tf_op jit(solution)/shard_map/pallas_call | solution.py:125
  33.7 0.5 collective-permute-start.4
  34.1 3.8 %collective-permute-start.5 = (bf16[64,2048]{1,0:T(8,128)(2,1)S(1)}, bf16[64,2048]{1,0:T(8,128)(2,1)S(1)}, u32[]{:S(2)}, u32[]{:S(2)}) collective-permute-start(bf16[64,2048]{1,0:T(8,128)(2,1)S(1)} %shard_map.53.vec_ref), channel_id=1, source_target_pairs={{0,30},{2,4},{4,2},{6,8},{8,6},{10,12},{12,10},{14,16},{16,14},{18... | collective-permute-start | bytes 786440 | tf_op jit(solution)/shard_map/ppermute | solution.py:344
  37.9 1.6 %shard_map.59.acc_ref = f32[64,2048]{1,0:T(8,128)S(1)} custom-call(s32[8,6]{1,0:T(8,128)S(1)} %add_select_fusion.1.loc_ref, bf16[64,2048]{1,0:T(8,128)(2,1)S(1)} %shard_map.58.vec_ref, bf16[8,7,256,256]{3,2,1,0:T(8,128)(2,1)S(1)} %get-tuple-element.14.turned_ref), custom_call_target="tpu_custom_call" | custom-call | flops 335544320 | bytes 5242880 | tf_op jit(solution)/shard_map/pallas_call | solution.py:90
  39.6 1.7 %shard_map.54.acc_ref = f32[64,2048]{1,0:T(8,128)S(1)} custom-call(s32[8,6]{1,0:T(8,128)S(1)} %add_select_fusion.1.loc_ref, bf16[64,2048]{1,0:T(8,128)(2,1)S(1)} %shard_map.53.vec_ref, bf16[8,7,256,256]{3,2,1,0:T(8,128)(2,1)S(1)} %get-tuple-element.14.turned_ref), custom_call_target="tpu_custom_call" | custom-call | flops 335544320 | bytes 5242880 | tf_op jit(solution)/shard_map/pallas_call | solution.py:90
  41.2 0.0 collective-permute-done.10.near_ref
  41.3 1.1 %shard_map.60 = (f32[64,2048]{1,0:T(8,128)S(1)}, bf16[64,2048]{1,0:T(8,128)(2,1)S(1)}) custom-call(s32[8,6]{1,0:T(8,128)S(1)} %add_select_fusion.1.loc_ref, bf16[64,2048]{1,0:T(8,128)(2,1)S(1)} %collective-permute-done.10.near_ref, bf16[64,2048]{1,0:T(8,128)(2,1)S(1)} %collective-permute-done.11.far_ref, f32[64,2048]{1,0:T(8,128)S(1)} %shard_map.59.acc_ref, ...), custom_call_target="tpu_custom_call" | custom-call | flops 134217728 | bytes 2097152 | tf_op jit(solution)/shard_map/pallas_call | solution.py:125
  42.4 1.6 %collective-permute-start.18 = (bf16[64,2048]{1,0:T(8,128)(2,1)S(1)}, bf16[64,2048]{1,0:T(8,128)(2,1)S(1)}, u32[]{:S(2)}, u32[]{:S(2)}) collective-permute-start(bf16[64,2048]{1,0:T(8,128)(2,1)S(1)} %get-tuple-element.19.refs_3_.refs_1_), channel_id=1, source_target_pairs={{0,1},{1,0},{2,3},{3,2},{4,5},{5,4},{6,7},{7,6},{8,9},{9,8},{10,11... | collective-permute-start | bytes 786440 | tf_op jit(solution)/shard_map/ppermute | solution.py:374
  44.0 0.0 collective-permute-done.4.near_ref
  44.0 0.0 collective-permute-done.5.far_ref
  44.0 1.1 %shard_map.55 = (f32[64,2048]{1,0:T(8,128)S(1)}, bf16[64,2048]{1,0:T(8,128)(2,1)S(1)}) custom-call(s32[8,6]{1,0:T(8,128)S(1)} %add_select_fusion.1.loc_ref, bf16[64,2048]{1,0:T(8,128)(2,1)S(1)} %collective-permute-done.4.near_ref, bf16[64,2048]{1,0:T(8,128)(2,1)S(1)} %collective-permute-done.5.far_ref, f32[64,2048]{1,0:T(8,128)S(1)} %shard_map.54.acc_ref, ...), custom_call_target="tpu_custom_call" | custom-call | flops 134217728 | bytes 2097152 | tf_op jit(solution)/shard_map/pallas_call | solution.py:125
  45.1 0.6 collective-permute-start.17
  45.7 0.5 shard_map.61
  46.2 1.8 %collective-permute-start.12 = (f32[128,128]{1,0:T(8,128)S(1)}, f32[128,128]{1,0:T(8,128)S(1)}, u32[]{:S(2)}, u32[]{:S(2)}) collective-permute-start(f32[128,128]{1,0:T(8,128)S(1)} %shard_map.61), channel_id=1, source_target_pairs={{0,2},{2,0},{4,6},{6,4},{8,10},{10,8},{12,14},{14,12},{16,18},{18,... | collective-permute-start | bytes 196616 | tf_op jit(solution)/shard_map/ppermute | solution.py:367
  48.1 0.9 %collective-permute-done.12 = f32[128,128]{1,0:T(8,128)S(1)} collective-permute-done((f32[128,128]{1,0:T(8,128)S(1)}, f32[128,128]{1,0:T(8,128)S(1)}, u32[]{:S(2)}, u32[]{:S(2)}) %collective-permute-start.12) | collective-permute-done | bytes 65568 | tf_op jit(solution)/shard_map/ppermute | solution.py:367
  49.0 2.3 %collective-permute-start.13 = (f32[128,128]{1,0:T(8,128)S(1)}, f32[128,128]{1,0:T(8,128)S(1)}, u32[]{:S(2)}, u32[]{:S(2)}) collective-permute-start(f32[128,128]{1,0:T(8,128)S(1)} %add.38), channel_id=1, source_target_pairs={{0,4},{2,6},{4,0},{6,2},{8,12},{10,14},{12,8},{14,10},{16,20},{18,... | collective-permute-start | bytes 196616 | tf_op jit(solution)/shard_map/ppermute | solution.py:367
  51.3 0.3 collective-permute-done.18.refs_3_
  51.6 4.9 %collective-permute-done.17.refs_2_ = bf16[64,2048]{1,0:T(8,128)(2,1)S(1)} collective-permute-done((bf16[64,2048]{1,0:T(8,128)(2,1)S(1)}, bf16[64,2048]{1,0:T(8,128)(2,1)S(1)}, u32[]{:S(2)}, u32[]{:S(2)}) %collective-permute-start.17) | collective-permute-done | bytes 262176 | tf_op jit(solution)/shard_map/ppermute | solution.py:374
  56.6 0.3 shard_map.62
  56.9 0.1 collective-permute-start.19
  56.9 0.0 collective-permute-done.13
  57.0 0.1 collective-permute-start.14
  57.1 1.1 %collective-permute-done.19 = f32[128,128]{1,0:T(8,128)S(1)} collective-permute-done((f32[128,128]{1,0:T(8,128)S(1)}, f32[128,128]{1,0:T(8,128)S(1)}, u32[]{:S(2)}, u32[]{:S(2)}) %collective-permute-start.19) | collective-permute-done | bytes 65568 | tf_op jit(solution)/shard_map/ppermute | solution.py:367
  58.2 0.1 collective-permute-start.20
  58.3 3.2 %collective-permute-done.14 = f32[128,128]{1,0:T(8,128)S(1)} collective-permute-done((f32[128,128]{1,0:T(8,128)S(1)}, f32[128,128]{1,0:T(8,128)S(1)}, u32[]{:S(2)}, u32[]{:S(2)}) %collective-permute-start.14) | collective-permute-done | bytes 65568 | tf_op jit(solution)/shard_map/ppermute | solution.py:367
  61.5 0.1 collective-permute-start.15
  61.6 0.9 %collective-permute-done.20 = f32[128,128]{1,0:T(8,128)S(1)} collective-permute-done((f32[128,128]{1,0:T(8,128)S(1)}, f32[128,128]{1,0:T(8,128)S(1)}, u32[]{:S(2)}, u32[]{:S(2)}) %collective-permute-start.20) | collective-permute-done | bytes 65568 | tf_op jit(solution)/shard_map/ppermute | solution.py:367
  62.5 0.9 %collective-permute-start.21 = (f32[128,128]{1,0:T(8,128)S(1)}, f32[128,128]{1,0:T(8,128)S(1)}, u32[]{:S(2)}, u32[]{:S(2)}) collective-permute-start(f32[128,128]{1,0:T(8,128)S(1)} %add.43), channel_id=1, source_target_pairs={{0,8},{2,10},{4,12},{6,14},{8,0},{10,2},{12,4},{14,6},{16,24},{18,... | collective-permute-start | bytes 196616 | tf_op jit(solution)/shard_map/ppermute | solution.py:367
  63.5 4.1 %collective-permute-done.15 = f32[128,128]{1,0:T(8,128)S(1)} collective-permute-done((f32[128,128]{1,0:T(8,128)S(1)}, f32[128,128]{1,0:T(8,128)S(1)}, u32[]{:S(2)}, u32[]{:S(2)}) %collective-permute-start.15) | collective-permute-done | bytes 65568 | tf_op jit(solution)/shard_map/ppermute | solution.py:367
  67.7 1.6 %collective-permute-start.16 = (f32[128,128]{1,0:T(8,128)S(1)}, f32[128,128]{1,0:T(8,128)S(1)}, u32[]{:S(2)}, u32[]{:S(2)}) collective-permute-start(f32[128,128]{1,0:T(8,128)S(1)} %add.41.own_ref), channel_id=1, source_target_pairs={{0,1},{1,0},{2,3},{3,2},{4,5},{5,4},{6,7},{7,6},{8,9},{9,8},{10,11... | collective-permute-start | bytes 196616 | tf_op jit(solution)/shard_map/ppermute | solution.py:385
  69.2 0.1 collective-permute-start.22
  69.3 2.7 %collective-permute-done.16.other_ref = f32[128,128]{1,0:T(8,128)S(1)} collective-permute-done((f32[128,128]{1,0:T(8,128)S(1)}, f32[128,128]{1,0:T(8,128)S(1)}, u32[]{:S(2)}, u32[]{:S(2)}) %collective-permute-start.16) | collective-permute-done | bytes 65568 | tf_op jit(solution)/shard_map/ppermute | solution.py:385
  72.0 4.7 %shard_map.63 = (f32[128,128]{1,0:T(8,128)S(1)}, f32[128,128]{1,0:T(8,128)S(1)}) custom-call(s32[1]{0:T(128)} %bitcast.place_ref, f32[128,128]{1,0:T(8,128)S(1)} %add.41.own_ref, f32[128,128]{1,0:T(8,128)S(1)} %collective-permute-done.16.other_ref), custom_call_target="tpu_custom_call" | custom-call | flops 4194304 | bytes 16777216 | tf_op jit(solution)/shard_map/pallas_call | solution.py:286
  76.7 6.3 %shard_map.64 = (f32[256,256]{1,0:T(8,128)}, f32[256,256]{1,0:T(8,128)S(1)}) custom-call(s32[1]{0:T(128)} %bitcast.place_ref, f32[128,128]{1,0:T(8,128)S(1)} %add.41.own_ref, f32[128,128]{1,0:T(8,128)S(1)} %collective-permute-done.16.other_ref, f32[128,128]{1,0:T(8,128)S(1)} %add.45.cross_ref, f32[128,128]{1,0:T(8,128)S(1)} %get-tuple-element.20.first_ref, ...), custom_call_target="tpu_custom_call" | custom-call | tf_op jit(solution)/shard_map/pallas_call | solution.py:295
  83.0 1.8 %shard_map.65 = f32[128,2048]{1,0:T(8,128)} custom-call(s32[1]{0:T(128)} %bitcast.place_ref, f32[256,256]{1,0:T(8,128)S(1)} %get-tuple-element.22.inv_ref, f32[64,2048]{1,0:T(8,128)S(1)} %get-tuple-element.15.refs_0_, f32[64,2048]{1,0:T(8,128)S(1)} %get-tuple-element.17.refs_1_, bf16[64,2048]{1,0:T(8,128)(2,1)S(1)} %collective-permute-done.17.refs_2_, ...), custom_call_target="tpu_custom_call" | custom-call | tf_op jit(solution)/shard_map/pallas_call | solution.py:401
  (15 shorter events, 0.1 us)
Async XLA Ops:
  1.7 15.3 %collective-permute-start.6 = (bf16[64,2048]{1,0:T(8,128)(2,1)S(1)}, bf16[64,2048]{1,0:T(8,128)(2,1)S(1)}, u32[]{:S(2)}, u32[]{:S(2)}) collective-permute-start(bf16[64,2048]{1,0:T(8,128)(2,1)S(1)} %get-tuple-element.24.vec_ref.prior_ref), channel_id=1, source_target_pairs={{0,2},{2,0},{4,6},{6,4},{8,10},{10,8},{12,14},{14,12},{16,18},{18,... | collective-permute-start | bytes 786440 | tf_op jit(solution)/shard_map/ppermute | solution.py:351
  2.2 14.8 %collective-permute-start.7 = (bf16[64,2048]{1,0:T(8,128)(2,1)S(1)}, bf16[64,2048]{1,0:T(8,128)(2,1)S(1)}, u32[]{:S(2)}, u32[]{:S(2)}) collective-permute-start(bf16[64,2048]{1,0:T(8,128)(2,1)S(1)} %get-tuple-element.24.vec_ref.prior_ref), channel_id=1, source_target_pairs={{0,30},{2,4},{4,2},{6,8},{8,6},{10,12},{12,10},{14,16},{16,14},{18... | collective-permute-start | bytes 786440 | tf_op jit(solution)/shard_map/ppermute | solution.py:350
  7.9 14.2 %collective-permute-start = (bf16[64,2048]{1,0:T(8,128)(2,1)S(1)}, bf16[64,2048]{1,0:T(8,128)(2,1)S(1)}, u32[]{:S(2)}, u32[]{:S(2)}) collective-permute-start(bf16[64,2048]{1,0:T(8,128)(2,1)S(1)} %get-tuple-element.25.vec_ref.prior_ref), channel_id=1, source_target_pairs={{0,2},{2,0},{4,6},{6,4},{8,10},{10,8},{12,14},{14,12},{16,18},{18,... | collective-permute-start | bytes 786440 | tf_op jit(solution)/shard_map/ppermute | solution.py:351
  7.9 14.2 %collective-permute-start.1 = (bf16[64,2048]{1,0:T(8,128)(2,1)S(1)}, bf16[64,2048]{1,0:T(8,128)(2,1)S(1)}, u32[]{:S(2)}, u32[]{:S(2)}) collective-permute-start(bf16[64,2048]{1,0:T(8,128)(2,1)S(1)} %get-tuple-element.25.vec_ref.prior_ref), channel_id=1, source_target_pairs={{0,30},{2,4},{4,2},{6,8},{8,6},{10,12},{12,10},{14,16},{16,14},{18... | collective-permute-start | bytes 786440 | tf_op jit(solution)/shard_map/ppermute | solution.py:350
  10.1 3.1 %copy-start = (bf16[8,7,256,256]{3,2,1,0:T(8,128)(2,1)S(1)}, bf16[8,7,256,256]{3,2,1,0:T(8,128)(2,1)}, u32[]{:S(2)}) copy-start(bf16[8,7,256,256]{3,2,1,0:T(8,128)(2,1)} %ham_ref.1) | copy-start | bytes 22020100
  13.2 1.0 %copy-start.1 = (bf16[128,2048]{1,0:T(8,128)(2,1)S(1)}, bf16[128,2048]{1,0:T(8,128)(2,1)}, u32[]{:S(2)}) copy-start(bf16[128,2048]{1,0:T(8,128)(2,1)} %vec_ref.1) | copy-start | bytes 1572868
  18.1 9.1 %collective-permute-start.8 = (bf16[64,2048]{1,0:T(8,128)(2,1)S(1)}, bf16[64,2048]{1,0:T(8,128)(2,1)S(1)}, u32[]{:S(2)}, u32[]{:S(2)}) collective-permute-start(bf16[64,2048]{1,0:T(8,128)(2,1)S(1)} %shard_map.56.vec_ref.prior_ref), channel_id=1, source_target_pairs={{0,2},{2,0},{4,6},{6,4},{8,10},{10,8},{12,14},{14,12},{16,18},{18,... | collective-permute-start | bytes 786440 | tf_op jit(solution)/shard_map/ppermute | solution.py:345
  18.2 9.1 %collective-permute-start.9 = (bf16[64,2048]{1,0:T(8,128)(2,1)S(1)}, bf16[64,2048]{1,0:T(8,128)(2,1)S(1)}, u32[]{:S(2)}, u32[]{:S(2)}) collective-permute-start(bf16[64,2048]{1,0:T(8,128)(2,1)S(1)} %shard_map.56.vec_ref.prior_ref), channel_id=1, source_target_pairs={{0,30},{2,4},{4,2},{6,8},{8,6},{10,12},{12,10},{14,16},{16,14},{18... | collective-permute-start | bytes 786440 | tf_op jit(solution)/shard_map/ppermute | solution.py:344
  23.2 9.3 %collective-permute-start.2 = (bf16[64,2048]{1,0:T(8,128)(2,1)S(1)}, bf16[64,2048]{1,0:T(8,128)(2,1)S(1)}, u32[]{:S(2)}, u32[]{:S(2)}) collective-permute-start(bf16[64,2048]{1,0:T(8,128)(2,1)S(1)} %shard_map.51.vec_ref.prior_ref), channel_id=1, source_target_pairs={{0,2},{2,0},{4,6},{6,4},{8,10},{10,8},{12,14},{14,12},{16,18},{18,... | collective-permute-start | bytes 786440 | tf_op jit(solution)/shard_map/ppermute | solution.py:345
  23.3 9.3 %collective-permute-start.3 = (bf16[64,2048]{1,0:T(8,128)(2,1)S(1)}, bf16[64,2048]{1,0:T(8,128)(2,1)S(1)}, u32[]{:S(2)}, u32[]{:S(2)}) collective-permute-start(bf16[64,2048]{1,0:T(8,128)(2,1)S(1)} %shard_map.51.vec_ref.prior_ref), channel_id=1, source_target_pairs={{0,30},{2,4},{4,2},{6,8},{8,6},{10,12},{12,10},{14,16},{16,14},{18... | collective-permute-start | bytes 786440 | tf_op jit(solution)/shard_map/ppermute | solution.py:344
  28.4 12.8 %collective-permute-start.10 = (bf16[64,2048]{1,0:T(8,128)(2,1)S(1)}, bf16[64,2048]{1,0:T(8,128)(2,1)S(1)}, u32[]{:S(2)}, u32[]{:S(2)}) collective-permute-start(bf16[64,2048]{1,0:T(8,128)(2,1)S(1)} %shard_map.58.vec_ref), channel_id=1, source_target_pairs={{0,2},{2,0},{4,6},{6,4},{8,10},{10,8},{12,14},{14,12},{16,18},{18,... | collective-permute-start | bytes 786440 | tf_op jit(solution)/shard_map/ppermute | solution.py:345
  30.0 11.2 %collective-permute-start.11 = (bf16[64,2048]{1,0:T(8,128)(2,1)S(1)}, bf16[64,2048]{1,0:T(8,128)(2,1)S(1)}, u32[]{:S(2)}, u32[]{:S(2)}) collective-permute-start(bf16[64,2048]{1,0:T(8,128)(2,1)S(1)} %shard_map.58.vec_ref), channel_id=1, source_target_pairs={{0,30},{2,4},{4,2},{6,8},{8,6},{10,12},{12,10},{14,16},{16,14},{18... | collective-permute-start | bytes 786440 | tf_op jit(solution)/shard_map/ppermute | solution.py:344
  33.7 10.3 %collective-permute-start.4 = (bf16[64,2048]{1,0:T(8,128)(2,1)S(1)}, bf16[64,2048]{1,0:T(8,128)(2,1)S(1)}, u32[]{:S(2)}, u32[]{:S(2)}) collective-permute-start(bf16[64,2048]{1,0:T(8,128)(2,1)S(1)} %shard_map.53.vec_ref), channel_id=1, source_target_pairs={{0,2},{2,0},{4,6},{6,4},{8,10},{10,8},{12,14},{14,12},{16,18},{18,... | collective-permute-start | bytes 786440 | tf_op jit(solution)/shard_map/ppermute | solution.py:345
  34.1 9.8 %collective-permute-start.5 = (bf16[64,2048]{1,0:T(8,128)(2,1)S(1)}, bf16[64,2048]{1,0:T(8,128)(2,1)S(1)}, u32[]{:S(2)}, u32[]{:S(2)}) collective-permute-start(bf16[64,2048]{1,0:T(8,128)(2,1)S(1)} %shard_map.53.vec_ref), channel_id=1, source_target_pairs={{0,30},{2,4},{4,2},{6,8},{8,6},{10,12},{12,10},{14,16},{16,14},{18... | collective-permute-start | bytes 786440 | tf_op jit(solution)/shard_map/ppermute | solution.py:344
  42.4 9.2 %collective-permute-start.18 = (bf16[64,2048]{1,0:T(8,128)(2,1)S(1)}, bf16[64,2048]{1,0:T(8,128)(2,1)S(1)}, u32[]{:S(2)}, u32[]{:S(2)}) collective-permute-start(bf16[64,2048]{1,0:T(8,128)(2,1)S(1)} %get-tuple-element.19.refs_3_.refs_1_), channel_id=1, source_target_pairs={{0,1},{1,0},{2,3},{3,2},{4,5},{5,4},{6,7},{7,6},{8,9},{9,8},{10,11... | collective-permute-start | bytes 786440 | tf_op jit(solution)/shard_map/ppermute | solution.py:374
  45.1 11.4 %collective-permute-start.17 = (bf16[64,2048]{1,0:T(8,128)(2,1)S(1)}, bf16[64,2048]{1,0:T(8,128)(2,1)S(1)}, u32[]{:S(2)}, u32[]{:S(2)}) collective-permute-start(bf16[64,2048]{1,0:T(8,128)(2,1)S(1)} %get-tuple-element.18.refs_2_.refs_0_), channel_id=1, source_target_pairs={{0,1},{1,0},{2,3},{3,2},{4,5},{5,4},{6,7},{7,6},{8,9},{9,8},{10,11... | collective-permute-start | bytes 786440 | tf_op jit(solution)/shard_map/ppermute | solution.py:374
  46.2 2.7 %collective-permute-start.12 = (f32[128,128]{1,0:T(8,128)S(1)}, f32[128,128]{1,0:T(8,128)S(1)}, u32[]{:S(2)}, u32[]{:S(2)}) collective-permute-start(f32[128,128]{1,0:T(8,128)S(1)} %shard_map.61), channel_id=1, source_target_pairs={{0,2},{2,0},{4,6},{6,4},{8,10},{10,8},{12,14},{14,12},{16,18},{18,... | collective-permute-start | bytes 196616 | tf_op jit(solution)/shard_map/ppermute | solution.py:367
  49.0 8.0 %collective-permute-start.13 = (f32[128,128]{1,0:T(8,128)S(1)}, f32[128,128]{1,0:T(8,128)S(1)}, u32[]{:S(2)}, u32[]{:S(2)}) collective-permute-start(f32[128,128]{1,0:T(8,128)S(1)} %add.38), channel_id=1, source_target_pairs={{0,4},{2,6},{4,0},{6,2},{8,12},{10,14},{12,8},{14,10},{16,20},{18,... | collective-permute-start | bytes 196616 | tf_op jit(solution)/shard_map/ppermute | solution.py:367
  56.9 1.3 %collective-permute-start.19 = (f32[128,128]{1,0:T(8,128)S(1)}, f32[128,128]{1,0:T(8,128)S(1)}, u32[]{:S(2)}, u32[]{:S(2)}) collective-permute-start(f32[128,128]{1,0:T(8,128)S(1)} %shard_map.62), channel_id=1, source_target_pairs={{0,2},{2,0},{4,6},{6,4},{8,10},{10,8},{12,14},{14,12},{16,18},{18,... | collective-permute-start | bytes 196616 | tf_op jit(solution)/shard_map/ppermute | solution.py:367
  57.0 4.5 %collective-permute-start.14 = (f32[128,128]{1,0:T(8,128)S(1)}, f32[128,128]{1,0:T(8,128)S(1)}, u32[]{:S(2)}, u32[]{:S(2)}) collective-permute-start(f32[128,128]{1,0:T(8,128)S(1)} %add.39), channel_id=1, source_target_pairs={{0,8},{2,10},{4,12},{6,14},{8,0},{10,2},{12,4},{14,6},{16,24},{18,... | collective-permute-start | bytes 196616 | tf_op jit(solution)/shard_map/ppermute | solution.py:367
  58.2 4.3 %collective-permute-start.20 = (f32[128,128]{1,0:T(8,128)S(1)}, f32[128,128]{1,0:T(8,128)S(1)}, u32[]{:S(2)}, u32[]{:S(2)}) collective-permute-start(f32[128,128]{1,0:T(8,128)S(1)} %add.42), channel_id=1, source_target_pairs={{0,4},{2,6},{4,0},{6,2},{8,12},{10,14},{12,8},{14,10},{16,20},{18,... | collective-permute-start | bytes 196616 | tf_op jit(solution)/shard_map/ppermute | solution.py:367
  61.5 6.1 %collective-permute-start.15 = (f32[128,128]{1,0:T(8,128)S(1)}, f32[128,128]{1,0:T(8,128)S(1)}, u32[]{:S(2)}, u32[]{:S(2)}) collective-permute-start(f32[128,128]{1,0:T(8,128)S(1)} %add.40), channel_id=1, source_target_pairs={{0,16},{2,18},{4,20},{6,22},{8,24},{10,26},{12,28},{14,30},{16,0},... | collective-permute-start | bytes 196616 | tf_op jit(solution)/shard_map/ppermute | solution.py:367
  62.5 6.7 %collective-permute-start.21 = (f32[128,128]{1,0:T(8,128)S(1)}, f32[128,128]{1,0:T(8,128)S(1)}, u32[]{:S(2)}, u32[]{:S(2)}) collective-permute-start(f32[128,128]{1,0:T(8,128)S(1)} %add.43), channel_id=1, source_target_pairs={{0,8},{2,10},{4,12},{6,14},{8,0},{10,2},{12,4},{14,6},{16,24},{18,... | collective-permute-start | bytes 196616 | tf_op jit(solution)/shard_map/ppermute | solution.py:367
  67.7 4.3 %collective-permute-start.16 = (f32[128,128]{1,0:T(8,128)S(1)}, f32[128,128]{1,0:T(8,128)S(1)}, u32[]{:S(2)}, u32[]{:S(2)}) collective-permute-start(f32[128,128]{1,0:T(8,128)S(1)} %add.41.own_ref), channel_id=1, source_target_pairs={{0,1},{1,0},{2,3},{3,2},{4,5},{5,4},{6,7},{7,6},{8,9},{9,8},{10,11... | collective-permute-start | bytes 196616 | tf_op jit(solution)/shard_map/ppermute | solution.py:385
  69.2 7.5 %collective-permute-start.22 = (f32[128,128]{1,0:T(8,128)S(1)}, f32[128,128]{1,0:T(8,128)S(1)}, u32[]{:S(2)}, u32[]{:S(2)}) collective-permute-start(f32[128,128]{1,0:T(8,128)S(1)} %add.44), channel_id=1, source_target_pairs={{0,16},{2,18},{4,20},{6,22},{8,24},{10,26},{12,28},{14,30},{16,0},... | collective-permute-start | bytes 196616 | tf_op jit(solution)/shard_map/ppermute | solution.py:367

commit v8 on v6

--- a/solution.py
+++ b/solution.py
@@ -141,7 +141,9 @@
     out_ref[...] = dot_nt(high, high) + (mixed + mixed.T)
 
 
-def cross_gram_kernel(place_ref, own_ref, other_ref, out_ref):
+def cross_gram_kernel(place_ref, own_ref, other_ref, after_ref, out_ref):
+    del after_ref
+
     @pl.when(place_ref[0] == 0)
     def _():
         out_ref[...] = dot_nt(own_ref[...], other_ref[...])
@@ -232,7 +234,9 @@
     inv_ref[...] = jnp.where(col <= row, right[...], 0.0)
 
 
-def first_kernel(place_ref, own_ref, other_ref, upper_ref, inv_ref, work, right):
+def first_kernel(place_ref, own_ref, other_ref, after_ref, upper_ref, inv_ref, work, right):
+    del after_ref
+
     @pl.when(place_ref[0] == 0)
     def _():
         work[...] = own_ref[...]
@@ -268,7 +272,7 @@
     inv_ref[half:, 0:half] = -dot_full(inv_ref[half:, half:], between)
 
 
-def factorize(place, own, other, cross):
+def factorize(place, own, other, cross, after):
     half = own.shape[0]
     smem = [pl.BlockSpec(memory_space=pltpu.SMEM)]
     tile = jax.ShapeDtypeStruct((half, half), jnp.float32)
@@ -277,12 +281,12 @@
     first, first_inv = pl.pallas_call(
         first_kernel,
         out_shape=[tile] * 2,
-        in_specs=smem + vmem(2),
+        in_specs=smem + vmem(2) + [pl.BlockSpec(memory_space=pl.ANY)],
         out_specs=vmem(2),
         scratch_shapes=scratch,
         compiler_params=params,
         cost_estimate=pl.CostEstimate(flops=2 * half**3, bytes_accessed=1 << 24, transcendentals=half),
-    )(place, own, other)
+    )(place, own, other, after)
     return pl.pallas_call(
         second_kernel,
         out_shape=[jax.ShapeDtypeStruct((2 * half, 2 * half), jnp.float32)] * 2,
@@ -340,11 +344,11 @@
     side = halo(two)
     filtered, narrow = halo_part(3, *side, own_part(two, turned, loc), two, one, turned, loc)
 
-    def summed(part):
-        step = 1
-        while step < blocks:
+    steps = [1 << i for i in range((blocks - 1).bit_length())]
+
+    def summed(part, chosen):
+        for step in chosen:
             part = part + lax.ppermute(part, "space", [(i, i ^ step) for i in range(blocks)])
-            step *= 2
         return part
 
     place = lax.axis_index("orb").astype(jnp.int32).reshape(1)
@@ -360,21 +364,23 @@
             out_specs=pl.BlockSpec(memory_space=pltpu.VMEM),
             compiler_params=params,
         )(filtered, narrow)
-        near = summed(near)
-        far = lax.ppermute(near, "orb", swap)
+        near = summed(near, steps[:-1])
         cross = pl.pallas_call(
             cross_gram_kernel,
             out_shape=tile,
-            in_specs=smem + vmem(2),
+            in_specs=smem + vmem(2) + [pl.BlockSpec(memory_space=pl.ANY)],
             out_specs=pl.BlockSpec(memory_space=pltpu.VMEM),
             compiler_params=params,
-        )(place, narrow, other)
-        upper, inverse = factorize(place, near, far, summed(cross))
+        )(place, narrow, other, near)
+        near = summed(near, steps[-1:])
+        far = lax.ppermute(near, "orb", swap)
+        cross = summed(cross, steps[:-1])
+        upper, inverse = factorize(place, near, far, summed(cross, steps[-1:]), cross)
     else:
         columns = lax.all_gather(narrow, "orb", axis=0, tiled=True)
-        whole = summed(dot_nt(columns, columns))
+        whole = summed(dot_nt(columns, columns), steps)
         upper, inverse = factorize(
-            jnp.zeros_like(place), whole[:half, :half], whole[half:, half:], whole[:half, half:]
+            jnp.zeros_like(place), whole[:half, :half], whole[half:, half:], whole[:half, half:], whole
         )
     if groups == 2:
         basis = pl.pallas_call(

time: 84.2 us -> 85 us (level)
  waiting for transfers between devices: 17.4 us -> 21.8 us
  starting transfers between devices: 36.9 us -> 33.3 us
    ppermute x8, waiting for transfers between devices: 7.18 us -> 12.9 us  [summed(): lax.ppermute(part, 'space', [(i, i ^ step) for i in range(blocks)])]
    ppermute x8, starting transfers between devices: 15.8 us -> 13.1 us  [summed(): lax.ppermute(part, 'space', [(i, i ^ step) for i in range(blocks)])]
    ppermute x1, starting transfers between devices: 1.55 us -> 0.59 us  [shards(): far = lax.ppermute(near, 'orb', swap)]
  transfers between devices with their start and end apart: 16 -> 16, of which waited for: 8 -> 10; matrix products, arithmetic and copies ran while one was open for 2% -> 2% of each run, Pallas kernels for 13% -> 13%
where the time goes in v8:
time: 85 us; the launch traced here: 84.8 us
  starting transfers between devices  33.3 us (39%)
  Pallas kernels  23.1 us (27%)
  waiting for transfers between devices  21.8 us (26%)
  local copies, waits for them, and re-layouts  4.27 us (5%)
  other arithmetic  1.53 us (2%)
    ppermute x8, starting transfers between devices, summed(): lax.ppermute(part, 'space', [(i, i ^ step) for i in range(blocks)])  13.1 us
    ppermute x8, waiting for transfers between devices, summed(): lax.ppermute(part, 'space', [(i, i ^ step) for i in range(blocks)])  12.9 us
    ppermute x3, starting transfers between devices, halo(): far = lax.ppermute(vec, 'space', far_pairs)  11.9 us
    ppermute x3, waiting for transfers between devices, halo(): far = lax.ppermute(vec, 'space', far_pairs)  7.43 us
    pallas_call x1, Pallas kernels, factorize(): pl.pallas_call(second_kernel, out_shape=[jax.ShapeDtypeStruct((2 * half,...  6.53 us
    ppermute x3, starting transfers between devices, halo(): return (lax.ppermute(vec, 'space', near_pairs), far)  6.11 us
    pallas_call x1, Pallas kernels, factorize(): pl.pallas_call(first_kernel, out_shape=[tile] * 2, in_specs=smem + vmem(2...  4.68 us
    unnamed x6, local copies, waits for them, and re-layouts  4.13 us
  transfers between devices with their start and end apart: 16, of which 10 were waited for; matrix products, arithmetic and copies ran while one was open for 2% of the time, Pallas kernels for 13%

profile of v8, /device:TPU:0, one launch (start us, length us, event | category | flops | bytes accessed | tf_op | source)
XLA Modules:
  0.0 84.8 jit_solution(3557903910293983667)
XLA Ops:
  0.6 5.5 %collective-permute-start.1 = (bf16[128,2048]{1,0:T(8,128)(2,1)}, bf16[128,2048]{1,0:T(8,128)(2,1)S(1)}, u32[]{:S(2)}, u32[]{:S(2)}) collective-permute-start(bf16[128,2048]{1,0:T(8,128)(2,1)} %prior_ref.3), channel_id=1, source_target_pairs={{0,30},{2,4},{4,2},{6,8},{8,6},{10,12},{12,10},{14,16},{16,14},{18... | collective-permute-start | bytes 1572872 | tf_op jit(solution)/shard_map/ppermute | solution.py:336
  6.1 0.0 collective-permute-start
  6.1 0.7 add_select_fusion
  6.8 0.1 slice.11
  6.9 0.1 fusion.1
  7.0 0.8 add_select_fusion.1.loc_ref
  7.7 0.0 copy-start
  7.8 1.0 %copy-done = bf16[128,2048]{1,0:T(8,128)(2,1)S(1)} copy-done((bf16[128,2048]{1,0:T(8,128)(2,1)S(1)}, bf16[128,2048]{1,0:T(8,128)(2,1)}, u32[]{:S(2)}) %copy-start) | copy-done | bytes 524312
  8.8 0.0 copy-start.2
  8.8 3.1 %copy-done.2 = bf16[8,7,256,256]{3,2,1,0:T(8,128)(2,1)S(1)} copy-done((bf16[8,7,256,256]{3,2,1,0:T(8,128)(2,1)S(1)}, bf16[8,7,256,256]{3,2,1,0:T(8,128)(2,1)}, u32[]{:S(2)}) %copy-start.2) | copy-done | bytes 7340056
  11.9 0.0 copy-start.1
  11.9 2.7 %shard_map.50 = (bf16[8,7,256,256]{3,2,1,0:T(8,128)(2,1)S(1)}, f32[128,2048]{1,0:T(8,128)S(1)}) custom-call(s32[8,6]{1,0:T(8,128)S(1)} %add_select_fusion.1.loc_ref, s32[1]{0:T(128)S(6)} %select_n.21.odd_ref, bf16[128,2048]{1,0:T(8,128)(2,1)S(1)} %copy-done, bf16[8,7,256,256]{3,2,1,0:T(8,128)(2,1)S(1)} %copy-done.2), custom_call_target="tpu_custom_call" | custom-call | flops 671088640 | bytes 14680064 | tf_op jit(solution)/shard_map/pallas_call | solution.py:55
  14.6 0.0 collective-permute-done.1.far_ref
  14.6 0.0 collective-permute-done.near_ref
  14.6 0.0 copy-done.1
  14.6 1.1 %shard_map.51.vec_ref.prior_ref = bf16[128,2048]{1,0:T(8,128)(2,1)S(1)} custom-call(s32[8,6]{1,0:T(8,128)S(1)} %add_select_fusion.1.loc_ref, bf16[128,2048]{1,0:T(8,128)(2,1)S(1)} %collective-permute-done.near_ref, bf16[128,2048]{1,0:T(8,128)(2,1)S(1)} %collective-permute-done.1.far_ref, f32[128,2048]{1,0:T(8,128)S(1)} %get-tuple-element.10.acc_ref, ...), custom_call_target="tpu_custom_call" | custom-call | flops 268435456 | bytes 2097152 | tf_op jit(solution)/shard_map/pallas_call | solution.py:123
  15.8 3.2 %collective-permute-start.3 = (bf16[128,2048]{1,0:T(8,128)(2,1)S(1)}, bf16[128,2048]{1,0:T(8,128)(2,1)S(1)}, u32[]{:S(2)}, u32[]{:S(2)}) collective-permute-start(bf16[128,2048]{1,0:T(8,128)(2,1)S(1)} %shard_map.51.vec_ref.prior_ref), channel_id=1, source_target_pairs={{0,30},{2,4},{4,2},{6,8},{8,6},{10,12},{12,10},{14,16},{16,14},{18... | collective-permute-start | bytes 1572872 | tf_op jit(solution)/shard_map/ppermute | solution.py:336
  18.9 0.5 collective-permute-start.2
  19.4 1.5 %shard_map.52.acc_ref = f32[128,2048]{1,0:T(8,128)S(1)} custom-call(s32[8,6]{1,0:T(8,128)S(1)} %add_select_fusion.1.loc_ref, bf16[128,2048]{1,0:T(8,128)(2,1)S(1)} %shard_map.51.vec_ref.prior_ref, bf16[8,7,256,256]{3,2,1,0:T(8,128)(2,1)S(1)} %get-tuple-element.11.turned_ref), custom_call_target="tpu_custom_call" | custom-call | flops 671088640 | bytes 5242880 | tf_op jit(solution)/shard_map/pallas_call | solution.py:88
  20.9 6.3 %collective-permute-done.3.far_ref = bf16[128,2048]{1,0:T(8,128)(2,1)S(1)} collective-permute-done((bf16[128,2048]{1,0:T(8,128)(2,1)S(1)}, bf16[128,2048]{1,0:T(8,128)(2,1)S(1)}, u32[]{:S(2)}, u32[]{:S(2)}) %collective-permute-start.3) | collective-permute-done | bytes 524320 | tf_op jit(solution)/shard_map/ppermute | solution.py:336
  27.2 0.0 collective-permute-done.2.near_ref
  27.2 1.2 %shard_map.53.vec_ref = bf16[128,2048]{1,0:T(8,128)(2,1)S(1)} custom-call(s32[8,6]{1,0:T(8,128)S(1)} %add_select_fusion.1.loc_ref, bf16[128,2048]{1,0:T(8,128)(2,1)S(1)} %collective-permute-done.2.near_ref, bf16[128,2048]{1,0:T(8,128)(2,1)S(1)} %collective-permute-done.3.far_ref, f32[128,2048]{1,0:T(8,128)S(1)} %shard_map.52.acc_ref, ...), custom_call_target="tpu_custom_call" | custom-call | flops 268435456 | bytes 2097152 | tf_op jit(solution)/shard_map/pallas_call | solution.py:123
  28.4 3.2 %collective-permute-start.5 = (bf16[128,2048]{1,0:T(8,128)(2,1)S(1)}, bf16[128,2048]{1,0:T(8,128)(2,1)S(1)}, u32[]{:S(2)}, u32[]{:S(2)}) collective-permute-start(bf16[128,2048]{1,0:T(8,128)(2,1)S(1)} %shard_map.53.vec_ref), channel_id=1, source_target_pairs={{0,30},{2,4},{4,2},{6,8},{8,6},{10,12},{12,10},{14,16},{16,14},{18... | collective-permute-start | bytes 1572872 | tf_op jit(solution)/shard_map/ppermute | solution.py:336
  31.6 5.7 %collective-permute-start.4 = (bf16[128,2048]{1,0:T(8,128)(2,1)S(1)}, bf16[128,2048]{1,0:T(8,128)(2,1)S(1)}, u32[]{:S(2)}, u32[]{:S(2)}) collective-permute-start(bf16[128,2048]{1,0:T(8,128)(2,1)S(1)} %shard_map.53.vec_ref), channel_id=1, source_target_pairs={{0,2},{2,0},{4,6},{6,4},{8,10},{10,8},{12,14},{14,12},{16,18},{18,... | collective-permute-start | bytes 1572872 | tf_op jit(solution)/shard_map/ppermute | solution.py:337
  37.3 1.5 %shard_map.54.acc_ref = f32[128,2048]{1,0:T(8,128)S(1)} custom-call(s32[8,6]{1,0:T(8,128)S(1)} %add_select_fusion.1.loc_ref, bf16[128,2048]{1,0:T(8,128)(2,1)S(1)} %shard_map.53.vec_ref, bf16[8,7,256,256]{3,2,1,0:T(8,128)(2,1)S(1)} %get-tuple-element.11.turned_ref), custom_call_target="tpu_custom_call" | custom-call | flops 671088640 | bytes 5242880 | tf_op jit(solution)/shard_map/pallas_call | solution.py:88
  38.8 1.1 %collective-permute-done.5.far_ref = bf16[128,2048]{1,0:T(8,128)(2,1)S(1)} collective-permute-done((bf16[128,2048]{1,0:T(8,128)(2,1)S(1)}, bf16[128,2048]{1,0:T(8,128)(2,1)S(1)}, u32[]{:S(2)}, u32[]{:S(2)}) %collective-permute-start.5) | collective-permute-done | bytes 524320 | tf_op jit(solution)/shard_map/ppermute | solution.py:336
  39.9 0.0 collective-permute-done.4.near_ref
  39.9 1.2 %shard_map.55 = (f32[128,2048]{1,0:T(8,128)S(1)}, bf16[128,2048]{1,0:T(8,128)(2,1)S(1)}) custom-call(s32[8,6]{1,0:T(8,128)S(1)} %add_select_fusion.1.loc_ref, bf16[128,2048]{1,0:T(8,128)(2,1)S(1)} %collective-permute-done.4.near_ref, bf16[128,2048]{1,0:T(8,128)(2,1)S(1)} %collective-permute-done.5.far_ref, f32[128,2048]{1,0:T(8,128)S(1)} %shard_map.54.acc_ref, ...), custom_call_target="tpu_custom_call" | custom-call | flops 268435456 | bytes 2097152 | tf_op jit(solution)/shard_map/pallas_call | solution.py:123
  41.1 1.6 %collective-permute-start.11 = (bf16[128,2048]{1,0:T(8,128)(2,1)S(1)}, bf16[128,2048]{1,0:T(8,128)(2,1)S(1)}, u32[]{:S(2)}, u32[]{:S(2)}) collective-permute-start(bf16[128,2048]{1,0:T(8,128)(2,1)S(1)} %get-tuple-element.13.high_ref.own_ref), channel_id=1, source_target_pairs={{0,1},{1,0},{2,3},{3,2},{4,5},{5,4},{6,7},{7,6},{8,9},{9,8},{10,11... | collective-permute-start | bytes 1572872 | tf_op jit(solution)/shard_map/ppermute | solution.py:357
  42.7 0.5 shard_map.56
  43.2 5.4 %collective-permute-start.6 = (f32[128,128]{1,0:T(8,128)S(1)}, f32[128,128]{1,0:T(8,128)S(1)}, u32[]{:S(2)}, u32[]{:S(2)}) collective-permute-start(f32[128,128]{1,0:T(8,128)S(1)} %shard_map.56), channel_id=1, source_target_pairs={{0,2},{2,0},{4,6},{6,4},{8,10},{10,8},{12,14},{14,12},{16,18},{18,... | collective-permute-start | bytes 196616 | tf_op jit(solution)/shard_map/ppermute | solution.py:351
  48.6 0.9 %collective-permute-done.6 = f32[128,128]{1,0:T(8,128)S(1)} collective-permute-done((f32[128,128]{1,0:T(8,128)S(1)}, f32[128,128]{1,0:T(8,128)S(1)}, u32[]{:S(2)}, u32[]{:S(2)}) %collective-permute-start.6) | collective-permute-done | bytes 65568 | tf_op jit(solution)/shard_map/ppermute | solution.py:351
  49.5 0.9 %collective-permute-start.7 = (f32[128,128]{1,0:T(8,128)S(1)}, f32[128,128]{1,0:T(8,128)S(1)}, u32[]{:S(2)}, u32[]{:S(2)}) collective-permute-start(f32[128,128]{1,0:T(8,128)S(1)} %add.38), channel_id=1, source_target_pairs={{0,4},{2,6},{4,0},{6,2},{8,12},{10,14},{12,8},{14,10},{16,20},{18,... | collective-permute-start | bytes 196616 | tf_op jit(solution)/shard_map/ppermute | solution.py:351
  50.4 3.5 %collective-permute-done.7 = f32[128,128]{1,0:T(8,128)S(1)} collective-permute-done((f32[128,128]{1,0:T(8,128)S(1)}, f32[128,128]{1,0:T(8,128)S(1)}, u32[]{:S(2)}, u32[]{:S(2)}) %collective-permute-start.7) | collective-permute-done | bytes 65568 | tf_op jit(solution)/shard_map/ppermute | solution.py:351
  53.9 0.6 collective-permute-start.8
  54.5 3.7 %collective-permute-done.8 = f32[128,128]{1,0:T(8,128)S(1)} collective-permute-done((f32[128,128]{1,0:T(8,128)S(1)}, f32[128,128]{1,0:T(8,128)S(1)}, u32[]{:S(2)}, u32[]{:S(2)}) %collective-permute-start.8) | collective-permute-done | bytes 65568 | tf_op jit(solution)/shard_map/ppermute | solution.py:351
  58.3 0.0 collective-permute-done.11.other_ref
  58.3 0.3 shard_map.57
  58.6 0.1 collective-permute-start.12
  58.7 1.2 %collective-permute-done.12 = f32[128,128]{1,0:T(8,128)S(1)} collective-permute-done((f32[128,128]{1,0:T(8,128)S(1)}, f32[128,128]{1,0:T(8,128)S(1)}, u32[]{:S(2)}, u32[]{:S(2)}) %collective-permute-start.12) | collective-permute-done | bytes 65568 | tf_op jit(solution)/shard_map/ppermute | solution.py:351
  59.9 0.8 collective-permute-start.13
  60.8 2.6 %collective-permute-start.9 = (f32[128,128]{1,0:T(8,128)S(1)}, f32[128,128]{1,0:T(8,128)S(1)}, u32[]{:S(2)}, u32[]{:S(2)}) collective-permute-start(f32[128,128]{1,0:T(8,128)S(1)} %add.40.after_ref), channel_id=1, source_target_pairs={{0,16},{2,18},{4,20},{6,22},{8,24},{10,26},{12,28},{14,30},{16,0},... | collective-permute-start | bytes 196616 | tf_op jit(solution)/shard_map/ppermute | solution.py:351
  63.4 0.9 %collective-permute-done.13 = f32[128,128]{1,0:T(8,128)S(1)} collective-permute-done((f32[128,128]{1,0:T(8,128)S(1)}, f32[128,128]{1,0:T(8,128)S(1)}, u32[]{:S(2)}, u32[]{:S(2)}) %collective-permute-start.13) | collective-permute-done | bytes 65568 | tf_op jit(solution)/shard_map/ppermute | solution.py:351
  64.3 1.1 %collective-permute-start.14 = (f32[128,128]{1,0:T(8,128)S(1)}, f32[128,128]{1,0:T(8,128)S(1)}, u32[]{:S(2)}, u32[]{:S(2)}) collective-permute-start(f32[128,128]{1,0:T(8,128)S(1)} %add.43), channel_id=1, source_target_pairs={{0,8},{2,10},{4,12},{6,14},{8,0},{10,2},{12,4},{14,6},{16,24},{18,... | collective-permute-start | bytes 196616 | tf_op jit(solution)/shard_map/ppermute | solution.py:351
  65.4 2.0 %collective-permute-done.9 = f32[128,128]{1,0:T(8,128)S(1)} collective-permute-done((f32[128,128]{1,0:T(8,128)S(1)}, f32[128,128]{1,0:T(8,128)S(1)}, u32[]{:S(2)}, u32[]{:S(2)}) %collective-permute-start.9) | collective-permute-done | bytes 65568 | tf_op jit(solution)/shard_map/ppermute | solution.py:351
  67.4 0.6 collective-permute-start.10
  68.0 0.7 collective-permute-done.14
  68.6 1.6 %collective-permute-start.15 = (f32[128,128]{1,0:T(8,128)S(1)}, f32[128,128]{1,0:T(8,128)S(1)}, u32[]{:S(2)}, u32[]{:S(2)}) collective-permute-start(f32[128,128]{1,0:T(8,128)S(1)} %add.44.after_ref), channel_id=1, source_target_pairs={{0,16},{2,18},{4,20},{6,22},{8,24},{10,26},{12,28},{14,30},{16,0},... | collective-permute-start | bytes 196616 | tf_op jit(solution)/shard_map/ppermute | solution.py:351
  70.2 1.5 %collective-permute-done.10.other_ref = f32[128,128]{1,0:T(8,128)S(1)} collective-permute-done((f32[128,128]{1,0:T(8,128)S(1)}, f32[128,128]{1,0:T(8,128)S(1)}, u32[]{:S(2)}, u32[]{:S(2)}) %collective-permute-start.10) | collective-permute-done | bytes 65568 | tf_op jit(solution)/shard_map/ppermute | solution.py:376
  71.7 4.7 %shard_map.58 = (f32[128,128]{1,0:T(8,128)S(1)}, f32[128,128]{1,0:T(8,128)S(1)}) custom-call(s32[1]{0:T(128)} %bitcast.place_ref, f32[128,128]{1,0:T(8,128)S(1)} %add.41.own_ref, f32[128,128]{1,0:T(8,128)S(1)} %collective-permute-done.10.other_ref, f32[128,128]{1,0:T(8,128)S(1)} %add.44.after_ref), custom_call_target="tpu_custom_call" | custom-call | flops 4194304 | bytes 16777216 | tf_op jit(solution)/shard_map/pallas_call | solution.py:281
  76.4 0.0 collective-permute-done.15
  76.4 6.5 %shard_map.59 = (f32[256,256]{1,0:T(8,128)}, f32[256,256]{1,0:T(8,128)S(1)}) custom-call(s32[1]{0:T(128)} %bitcast.place_ref, f32[128,128]{1,0:T(8,128)S(1)} %add.41.own_ref, f32[128,128]{1,0:T(8,128)S(1)} %collective-permute-done.10.other_ref, f32[128,128]{1,0:T(8,128)S(1)} %add.45.cross_ref, f32[128,128]{1,0:T(8,128)S(1)} %get-tuple-element.14.first_ref, ...), custom_call_target="tpu_custom_call" | custom-call | tf_op jit(solution)/shard_map/pallas_call | solution.py:290
  83.0 1.8 %shard_map.60 = f32[128,2048]{1,0:T(8,128)} custom-call(s32[1]{0:T(128)} %bitcast.place_ref, f32[256,256]{1,0:T(8,128)S(1)} %get-tuple-element.16.inv_ref, f32[128,2048]{1,0:T(8,128)S(1)} %get-tuple-element.12.own_ref, bf16[128,2048]{1,0:T(8,128)(2,1)S(1)} %collective-permute-done.11.other_ref), custom_call_target="tpu_custom_call" | custom-call | tf_op jit(solution)/shard_map/pallas_call | solution.py:386
  (8 shorter events, 0.1 us)
Async XLA Ops:
  0.6 14.0 %collective-permute-start.1 = (bf16[128,2048]{1,0:T(8,128)(2,1)}, bf16[128,2048]{1,0:T(8,128)(2,1)S(1)}, u32[]{:S(2)}, u32[]{:S(2)}) collective-permute-start(bf16[128,2048]{1,0:T(8,128)(2,1)} %prior_ref.3), channel_id=1, source_target_pairs={{0,30},{2,4},{4,2},{6,8},{8,6},{10,12},{12,10},{14,16},{16,14},{18... | collective-permute-start | bytes 1572872 | tf_op jit(solution)/shard_map/ppermute | solution.py:336
  6.1 8.5 %collective-permute-start = (bf16[128,2048]{1,0:T(8,128)(2,1)}, bf16[128,2048]{1,0:T(8,128)(2,1)S(1)}, u32[]{:S(2)}, u32[]{:S(2)}) collective-permute-start(bf16[128,2048]{1,0:T(8,128)(2,1)} %prior_ref.3), channel_id=1, source_target_pairs={{0,2},{2,0},{4,6},{6,4},{8,10},{10,8},{12,14},{14,12},{16,18},{18,... | collective-permute-start | bytes 1572872 | tf_op jit(solution)/shard_map/ppermute | solution.py:337
  7.7 1.0 %copy-start = (bf16[128,2048]{1,0:T(8,128)(2,1)S(1)}, bf16[128,2048]{1,0:T(8,128)(2,1)}, u32[]{:S(2)}) copy-start(bf16[128,2048]{1,0:T(8,128)(2,1)} %prior_ref.3) | copy-start | bytes 1572868
  8.8 3.1 %copy-start.2 = (bf16[8,7,256,256]{3,2,1,0:T(8,128)(2,1)S(1)}, bf16[8,7,256,256]{3,2,1,0:T(8,128)(2,1)}, u32[]{:S(2)}) copy-start(bf16[8,7,256,256]{3,2,1,0:T(8,128)(2,1)} %ham_ref.1) | copy-start | bytes 22020100
  11.9 2.8 %copy-start.1 = (bf16[128,2048]{1,0:T(8,128)(2,1)S(1)}, bf16[128,2048]{1,0:T(8,128)(2,1)}, u32[]{:S(2)}) copy-start(bf16[128,2048]{1,0:T(8,128)(2,1)} %prior_ref.3) | copy-start | bytes 1572868
  15.8 11.5 %collective-permute-start.3 = (bf16[128,2048]{1,0:T(8,128)(2,1)S(1)}, bf16[128,2048]{1,0:T(8,128)(2,1)S(1)}, u32[]{:S(2)}, u32[]{:S(2)}) collective-permute-start(bf16[128,2048]{1,0:T(8,128)(2,1)S(1)} %shard_map.51.vec_ref.prior_ref), channel_id=1, source_target_pairs={{0,30},{2,4},{4,2},{6,8},{8,6},{10,12},{12,10},{14,16},{16,14},{18... | collective-permute-start | bytes 1572872 | tf_op jit(solution)/shard_map/ppermute | solution.py:336
  18.9 8.3 %collective-permute-start.2 = (bf16[128,2048]{1,0:T(8,128)(2,1)S(1)}, bf16[128,2048]{1,0:T(8,128)(2,1)S(1)}, u32[]{:S(2)}, u32[]{:S(2)}) collective-permute-start(bf16[128,2048]{1,0:T(8,128)(2,1)S(1)} %shard_map.51.vec_ref.prior_ref), channel_id=1, source_target_pairs={{0,2},{2,0},{4,6},{6,4},{8,10},{10,8},{12,14},{14,12},{16,18},{18,... | collective-permute-start | bytes 1572872 | tf_op jit(solution)/shard_map/ppermute | solution.py:337
  28.4 11.5 %collective-permute-start.5 = (bf16[128,2048]{1,0:T(8,128)(2,1)S(1)}, bf16[128,2048]{1,0:T(8,128)(2,1)S(1)}, u32[]{:S(2)}, u32[]{:S(2)}) collective-permute-start(bf16[128,2048]{1,0:T(8,128)(2,1)S(1)} %shard_map.53.vec_ref), channel_id=1, source_target_pairs={{0,30},{2,4},{4,2},{6,8},{8,6},{10,12},{12,10},{14,16},{16,14},{18... | collective-permute-start | bytes 1572872 | tf_op jit(solution)/shard_map/ppermute | solution.py:336
  31.6 8.3 %collective-permute-start.4 = (bf16[128,2048]{1,0:T(8,128)(2,1)S(1)}, bf16[128,2048]{1,0:T(8,128)(2,1)S(1)}, u32[]{:S(2)}, u32[]{:S(2)}) collective-permute-start(bf16[128,2048]{1,0:T(8,128)(2,1)S(1)} %shard_map.53.vec_ref), channel_id=1, source_target_pairs={{0,2},{2,0},{4,6},{6,4},{8,10},{10,8},{12,14},{14,12},{16,18},{18,... | collective-permute-start | bytes 1572872 | tf_op jit(solution)/shard_map/ppermute | solution.py:337
  41.1 17.2 %collective-permute-start.11 = (bf16[128,2048]{1,0:T(8,128)(2,1)S(1)}, bf16[128,2048]{1,0:T(8,128)(2,1)S(1)}, u32[]{:S(2)}, u32[]{:S(2)}) collective-permute-start(bf16[128,2048]{1,0:T(8,128)(2,1)S(1)} %get-tuple-element.13.high_ref.own_ref), channel_id=1, source_target_pairs={{0,1},{1,0},{2,3},{3,2},{4,5},{5,4},{6,7},{7,6},{8,9},{9,8},{10,11... | collective-permute-start | bytes 1572872 | tf_op jit(solution)/shard_map/ppermute | solution.py:357
  43.2 6.3 %collective-permute-start.6 = (f32[128,128]{1,0:T(8,128)S(1)}, f32[128,128]{1,0:T(8,128)S(1)}, u32[]{:S(2)}, u32[]{:S(2)}) collective-permute-start(f32[128,128]{1,0:T(8,128)S(1)} %shard_map.56), channel_id=1, source_target_pairs={{0,2},{2,0},{4,6},{6,4},{8,10},{10,8},{12,14},{14,12},{16,18},{18,... | collective-permute-start | bytes 196616 | tf_op jit(solution)/shard_map/ppermute | solution.py:351
  49.5 4.4 %collective-permute-start.7 = (f32[128,128]{1,0:T(8,128)S(1)}, f32[128,128]{1,0:T(8,128)S(1)}, u32[]{:S(2)}, u32[]{:S(2)}) collective-permute-start(f32[128,128]{1,0:T(8,128)S(1)} %add.38), channel_id=1, source_target_pairs={{0,4},{2,6},{4,0},{6,2},{8,12},{10,14},{12,8},{14,10},{16,20},{18,... | collective-permute-start | bytes 196616 | tf_op jit(solution)/shard_map/ppermute | solution.py:351
  53.9 4.3 %collective-permute-start.8 = (f32[128,128]{1,0:T(8,128)S(1)}, f32[128,128]{1,0:T(8,128)S(1)}, u32[]{:S(2)}, u32[]{:S(2)}) collective-permute-start(f32[128,128]{1,0:T(8,128)S(1)} %add.39), channel_id=1, source_target_pairs={{0,8},{2,10},{4,12},{6,14},{8,0},{10,2},{12,4},{14,6},{16,24},{18,... | collective-permute-start | bytes 196616 | tf_op jit(solution)/shard_map/ppermute | solution.py:351
  58.6 1.3 %collective-permute-start.12 = (f32[128,128]{1,0:T(8,128)S(1)}, f32[128,128]{1,0:T(8,128)S(1)}, u32[]{:S(2)}, u32[]{:S(2)}) collective-permute-start(f32[128,128]{1,0:T(8,128)S(1)} %shard_map.57), channel_id=1, source_target_pairs={{0,2},{2,0},{4,6},{6,4},{8,10},{10,8},{12,14},{14,12},{16,18},{18,... | collective-permute-start | bytes 196616 | tf_op jit(solution)/shard_map/ppermute | solution.py:351
  59.9 4.3 %collective-permute-start.13 = (f32[128,128]{1,0:T(8,128)S(1)}, f32[128,128]{1,0:T(8,128)S(1)}, u32[]{:S(2)}, u32[]{:S(2)}) collective-permute-start(f32[128,128]{1,0:T(8,128)S(1)} %add.42), channel_id=1, source_target_pairs={{0,4},{2,6},{4,0},{6,2},{8,12},{10,14},{12,8},{14,10},{16,20},{18,... | collective-permute-start | bytes 196616 | tf_op jit(solution)/shard_map/ppermute | solution.py:351
  60.8 6.6 %collective-permute-start.9 = (f32[128,128]{1,0:T(8,128)S(1)}, f32[128,128]{1,0:T(8,128)S(1)}, u32[]{:S(2)}, u32[]{:S(2)}) collective-permute-start(f32[128,128]{1,0:T(8,128)S(1)} %add.40.after_ref), channel_id=1, source_target_pairs={{0,16},{2,18},{4,20},{6,22},{8,24},{10,26},{12,28},{14,30},{16,0},... | collective-permute-start | bytes 196616 | tf_op jit(solution)/shard_map/ppermute | solution.py:351
  64.3 4.3 %collective-permute-start.14 = (f32[128,128]{1,0:T(8,128)S(1)}, f32[128,128]{1,0:T(8,128)S(1)}, u32[]{:S(2)}, u32[]{:S(2)}) collective-permute-start(f32[128,128]{1,0:T(8,128)S(1)} %add.43), channel_id=1, source_target_pairs={{0,8},{2,10},{4,12},{6,14},{8,0},{10,2},{12,4},{14,6},{16,24},{18,... | collective-permute-start | bytes 196616 | tf_op jit(solution)/shard_map/ppermute | solution.py:351
  67.4 4.3 %collective-permute-start.10 = (f32[128,128]{1,0:T(8,128)S(1)}, f32[128,128]{1,0:T(8,128)S(1)}, u32[]{:S(2)}, u32[]{:S(2)}) collective-permute-start(f32[128,128]{1,0:T(8,128)S(1)} %add.41.own_ref), channel_id=1, source_target_pairs={{0,1},{1,0},{2,3},{3,2},{4,5},{5,4},{6,7},{7,6},{8,9},{9,8},{10,11... | collective-permute-start | bytes 196616 | tf_op jit(solution)/shard_map/ppermute | solution.py:376
  68.6 7.8 %collective-permute-start.15 = (f32[128,128]{1,0:T(8,128)S(1)}, f32[128,128]{1,0:T(8,128)S(1)}, u32[]{:S(2)}, u32[]{:S(2)}) collective-permute-start(f32[128,128]{1,0:T(8,128)S(1)} %add.44.after_ref), channel_id=1, source_target_pairs={{0,16},{2,18},{4,20},{6,22},{8,24},{10,26},{12,28},{14,30},{16,0},... | collective-permute-start | bytes 196616 | tf_op jit(solution)/shard_map/ppermute | solution.py:351

commit v9 on v6

--- a/solution.py
+++ b/solution.py
@@ -151,68 +151,73 @@
         out_ref[...] = dot_nt(other_ref[...], own_ref[...])
 
 
+def tree(terms):
+    while len(terms) > 1:
+        terms = [terms[i] + terms[i + 1] if i + 1 < len(terms) else terms[i] for i in range(0, len(terms), 2)]
+    return terms[0]
+
+
 def factor_block(rows, right):
     strips = len(rows)
     shape = rows[0].shape
     sub = lax.broadcasted_iota(jnp.int32, shape, 0)
     upper, inverse = [], []
     for k in range(strips):
-        strip, beside = rows[k], right[k]
-        lanes = [jnp.broadcast_to(strip[:, k * SUB + j : k * SUB + j + 1], shape) for j in range(SUB)]
+        lanes = [
+            jnp.broadcast_to(rows[k][:, k * SUB + j : k * SUB + j + 1], shape) for j in range(SUB)
+        ]
         entry = [
             [jnp.broadcast_to(lanes[j][i : i + 1, :], shape) if j <= i else None for j in range(SUB)]
             for i in range(SUB)
         ]
-        low = [[None] * SUB for _ in range(SUB)]
-        root = []
-        for j in range(SUB):
-            root.append(lax.rsqrt(entry[j][j]))
-            for i in range(j + 1, SUB):
-                low[i][j] = entry[i][j] * root[j]
-            for i in range(j + 1, SUB):
-                for t in range(j + 1, i + 1):
-                    entry[i][t] = entry[i][t] - low[i][j] * low[t][j]
-        inv = [[None] * SUB for _ in range(SUB)]
-        for i in range(SUB):
-            inv[i][i] = root[i]
-            for j in range(i):
-                total = low[i][j] * inv[j][j]
-                for t in range(j + 1, i):
-                    total = total + low[i][t] * inv[t][j]
-                inv[i][j] = -root[i] * total
-
-        def solve(source):
-            wide = [jnp.broadcast_to(source[i : i + 1, :], shape) for i in range(SUB)]
-            solved = []
-            for i in range(SUB):
-                total = inv[i][0] * wide[0]
-                for j in range(1, i + 1):
-                    total = total + inv[i][j] * wide[j]
-                solved.append(total)
-            back = []
-            for i in range(SUB):
-                total = inv[i][i] * solved[i]
-                for j in range(i + 1, SUB):
-                    total = total + inv[j][i] * solved[j]
-                back.append(total)
-            packed = solved[0]
-            for i in range(1, SUB):
-                packed = jnp.where(sub == i, solved[i], packed)
-            return packed, back
-
-        row_packed, row_back = solve(strip)
-        inv_packed, inv_back = solve(beside)
-        upper.append(row_packed)
-        inverse.append(inv_packed)
+        parts = [
+            [jnp.broadcast_to(source[i : i + 1, :], shape) for i in range(SUB)]
+            for source in (rows[k], right[k])
+        ]
+        pairs = []
+        for p in range(0, SUB, 2):
+            q = p + 1
+            a, b, c = entry[p][p], entry[q][p], entry[q][q]
+            det = a * c - b * b
+            root = lax.rsqrt(det)
+            over = root * root
+            scaled = {}
+            for i in range(q + 1, SUB):
+                first = c * entry[i][p] - b * entry[i][q]
+                second = a * entry[i][q] - b * entry[i][p]
+                scaled[i] = (first * over, second * over)
+                for t in range(q + 1, i + 1):
+                    entry[i][t] = entry[i][t] - (first * entry[t][p] + second * entry[t][q]) * over
+                for part in parts:
+                    part[i] = part[i] - (scaled[i][0] * part[p] + scaled[i][1] * part[q])
+            pairs.append((p, a, b, c, root, over, scaled))
+        packed = [None, None]
+        backs = []
+        for at, part in enumerate(parts):
+            back = [None] * SUB
+            for p, a, b, c, root, over, scaled in reversed(pairs):
+                q = p + 1
+                one = (c * part[p] - b * part[q]) * over
+                two = (a * part[q] - b * part[p]) * over
+                if scaled:
+                    one = one - tree([scaled[i][0] * back[i] for i in scaled])
+                    two = two - tree([scaled[i][1] * back[i] for i in scaled])
+                back[p], back[q] = one, two
+            backs.append(back)
+            for p, a, b, c, root, over, scaled in pairs:
+                first_root = lax.rsqrt(a)
+                high = part[p] * first_root
+                low = (a * part[p + 1] - b * part[p]) * (first_root * root)
+                packed[at] = high if packed[at] is None else jnp.where(sub == p, high, packed[at])
+                packed[at] = jnp.where(sub == p + 1, low, packed[at])
+        upper.append(packed[0])
+        inverse.append(packed[1])
         for r in range(k + 1, strips):
-            for i in range(SUB):
-                column = jnp.broadcast_to(rows[r][:, k * SUB + i : k * SUB + i + 1], shape)
-                rows_r = row_back[i] * column
-                right_r = inv_back[i] * column
-                total = rows_r if i == 0 else total + rows_r
-                beyond = right_r if i == 0 else beyond + right_r
-            rows[r] = rows[r] - total
-            right[r] = right[r] - beyond
+            columns = [
+                jnp.broadcast_to(rows[r][:, k * SUB + i : k * SUB + i + 1], shape) for i in range(SUB)
+            ]
+            rows[r] = rows[r] - tree([backs[0][i] * columns[i] for i in range(SUB)])
+            right[r] = right[r] - tree([backs[1][i] * columns[i] for i in range(SUB)])
     return upper, inverse
 
 
@@ -221,6 +226,11 @@
     strips = half // SUB
     row = lax.broadcasted_iota(jnp.int32, (half, half), 0)
     col = lax.broadcasted_iota(jnp.int32, (half, half), 1)
+    whole = work[...]
+    diagonal = jnp.where(row == col, whole, 0.0)
+    across = jnp.sum(diagonal, axis=0, keepdims=True)
+    scale = lax.rsqrt(across)
+    work[...] = whole * lax.rsqrt(jnp.sum(diagonal, axis=1, keepdims=True)) * scale
     rows = [work[SUB * s : SUB * (s + 1), :] for s in range(strips)]
     eye = (row == col).astype(jnp.float32)
     beside = [eye[SUB * s : SUB * (s + 1), :] for s in range(strips)]
@@ -228,8 +238,8 @@
     for s in range(strips):
         work[SUB * s : SUB * (s + 1), :] = upper[s]
         right[SUB * s : SUB * (s + 1), :] = inverse[s]
-    upper_ref[...] = jnp.where(col >= row, work[...], 0.0)
-    inv_ref[...] = jnp.where(col <= row, right[...], 0.0)
+    upper_ref[...] = jnp.where(col >= row, work[...] * (across * scale), 0.0)
+    inv_ref[...] = jnp.where(col <= row, right[...] * scale, 0.0)
 
 
 def first_kernel(place_ref, own_ref, other_ref, upper_ref, inv_ref, work, right):
@@ -300,17 +310,17 @@
     away = pl.ds(pl.multiple_of((1 - place) * half, half), half)
     near_high, near_low = split(inv_ref[rows, rows])
     far_high, far_low = split(inv_ref[rows, away])
+    both_high = jnp.concatenate([near_high, far_high], axis=1)
+    both_low = jnp.concatenate([near_low, far_low], axis=1)
     step = 512 if total % 512 == 0 else total
     for at in range(0, total, step):
         here = slice(at, at + step)
         high, low = split(own_ref[:, here])
-        other = other_ref[:, here]
+        both = jnp.concatenate([high, other_ref[:, here]], axis=0)
         out_ref[:, here] = (
-            jnp.dot(near_high, high, preferred_element_type=jnp.float32)
+            jnp.dot(both_high, both, preferred_element_type=jnp.float32)
+            + jnp.dot(both_low, both, preferred_element_type=jnp.float32)
             + jnp.dot(near_high, low, preferred_element_type=jnp.float32)
-            + jnp.dot(near_low, high, preferred_element_type=jnp.float32)
-            + jnp.dot(far_high, other, preferred_element_type=jnp.float32)
-            + jnp.dot(far_low, other, preferred_element_type=jnp.float32)
         )
 
 

time: 84.2 us -> 83.3 us (0.989)
  Pallas kernels: 23.1 us -> 22.2 us
where the time goes in v9:
time: 83.3 us; the launch traced here: 83 us
  starting transfers between devices  37 us (44%)
  Pallas kernels  22.2 us (27%)
  waiting for transfers between devices  17.3 us (21%)
  local copies, waits for them, and re-layouts  4.27 us (5%)
  other arithmetic  1.53 us (2%)
    ppermute x8, starting transfers between devices, summed(): lax.ppermute(part, 'space', [(i, i ^ step) for i in range(blocks)])  15.8 us
    ppermute x3, starting transfers between devices, halo(): far = lax.ppermute(vec, 'space', far_pairs)  11.9 us
    ppermute x3, waiting for transfers between devices, halo(): far = lax.ppermute(vec, 'space', far_pairs)  7.42 us
    ppermute x8, waiting for transfers between devices, summed(): lax.ppermute(part, 'space', [(i, i ^ step) for i in range(blocks)])  7.16 us
    pallas_call x1, Pallas kernels, factorize(): pl.pallas_call(second_kernel, out_shape=[jax.ShapeDtypeStruct((2 * half,...  6.24 us
    ppermute x3, starting transfers between devices, halo(): return (lax.ppermute(vec, 'space', near_pairs), far)  6.11 us
    pallas_call x1, Pallas kernels, factorize(): pl.pallas_call(first_kernel, out_shape=[tile] * 2, in_specs=smem + vmem(2...  4.29 us
    unnamed x6, local copies, waits for them, and re-layouts  4.13 us
  transfers between devices with their start and end apart: 16, of which 8 were waited for; matrix products, arithmetic and copies ran while one was open for 2% of the time, Pallas kernels for 13%

profile of v9, /device:TPU:0, one launch (start us, length us, event | category | flops | bytes accessed | tf_op | source)
XLA Modules:
  0.0 83.0 jit_solution(2915380329554982603)
XLA Ops:
  0.6 5.5 %collective-permute-start.1 = (bf16[128,2048]{1,0:T(8,128)(2,1)}, bf16[128,2048]{1,0:T(8,128)(2,1)S(1)}, u32[]{:S(2)}, u32[]{:S(2)}) collective-permute-start(bf16[128,2048]{1,0:T(8,128)(2,1)} %prior_ref.3), channel_id=1, source_target_pairs={{0,30},{2,4},{4,2},{6,8},{8,6},{10,12},{12,10},{14,16},{16,14},{18... | collective-permute-start | bytes 1572872 | tf_op jit(solution)/shard_map/ppermute | solution.py:342
  6.1 0.0 collective-permute-start
  6.1 0.7 add_select_fusion
  6.8 0.1 slice.11
  6.9 0.1 fusion.1
  7.0 0.8 add_select_fusion.1.loc_ref
  7.7 0.0 copy-start
  7.8 1.0 %copy-done = bf16[128,2048]{1,0:T(8,128)(2,1)S(1)} copy-done((bf16[128,2048]{1,0:T(8,128)(2,1)S(1)}, bf16[128,2048]{1,0:T(8,128)(2,1)}, u32[]{:S(2)}) %copy-start) | copy-done | bytes 524312
  8.8 0.0 copy-start.2
  8.8 3.1 %copy-done.2 = bf16[8,7,256,256]{3,2,1,0:T(8,128)(2,1)S(1)} copy-done((bf16[8,7,256,256]{3,2,1,0:T(8,128)(2,1)S(1)}, bf16[8,7,256,256]{3,2,1,0:T(8,128)(2,1)}, u32[]{:S(2)}) %copy-start.2) | copy-done | bytes 7340056
  11.9 0.0 copy-start.1
  11.9 2.7 %shard_map.50 = (bf16[8,7,256,256]{3,2,1,0:T(8,128)(2,1)S(1)}, f32[128,2048]{1,0:T(8,128)S(1)}) custom-call(s32[8,6]{1,0:T(8,128)S(1)} %add_select_fusion.1.loc_ref, s32[1]{0:T(128)S(6)} %select_n.21.odd_ref, bf16[128,2048]{1,0:T(8,128)(2,1)S(1)} %copy-done, bf16[8,7,256,256]{3,2,1,0:T(8,128)(2,1)S(1)} %copy-done.2), custom_call_target="tpu_custom_call" | custom-call | flops 671088640 | bytes 14680064 | tf_op jit(solution)/shard_map/pallas_call | solution.py:55
  14.6 0.0 collective-permute-done.1.far_ref
  14.6 0.0 collective-permute-done.near_ref
  14.6 0.0 copy-done.1
  14.6 1.1 %shard_map.51.vec_ref.prior_ref = bf16[128,2048]{1,0:T(8,128)(2,1)S(1)} custom-call(s32[8,6]{1,0:T(8,128)S(1)} %add_select_fusion.1.loc_ref, bf16[128,2048]{1,0:T(8,128)(2,1)S(1)} %collective-permute-done.near_ref, bf16[128,2048]{1,0:T(8,128)(2,1)S(1)} %collective-permute-done.1.far_ref, f32[128,2048]{1,0:T(8,128)S(1)} %get-tuple-element.10.acc_ref, ...), custom_call_target="tpu_custom_call" | custom-call | flops 268435456 | bytes 2097152 | tf_op jit(solution)/shard_map/pallas_call | solution.py:123
  15.8 3.2 %collective-permute-start.3 = (bf16[128,2048]{1,0:T(8,128)(2,1)S(1)}, bf16[128,2048]{1,0:T(8,128)(2,1)S(1)}, u32[]{:S(2)}, u32[]{:S(2)}) collective-permute-start(bf16[128,2048]{1,0:T(8,128)(2,1)S(1)} %shard_map.51.vec_ref.prior_ref), channel_id=1, source_target_pairs={{0,30},{2,4},{4,2},{6,8},{8,6},{10,12},{12,10},{14,16},{16,14},{18... | collective-permute-start | bytes 1572872 | tf_op jit(solution)/shard_map/ppermute | solution.py:342
  19.0 0.5 collective-permute-start.2
  19.4 1.5 %shard_map.52.acc_ref = f32[128,2048]{1,0:T(8,128)S(1)} custom-call(s32[8,6]{1,0:T(8,128)S(1)} %add_select_fusion.1.loc_ref, bf16[128,2048]{1,0:T(8,128)(2,1)S(1)} %shard_map.51.vec_ref.prior_ref, bf16[8,7,256,256]{3,2,1,0:T(8,128)(2,1)S(1)} %get-tuple-element.11.turned_ref), custom_call_target="tpu_custom_call" | custom-call | flops 671088640 | bytes 5242880 | tf_op jit(solution)/shard_map/pallas_call | solution.py:88
  20.9 6.3 %collective-permute-done.3.far_ref = bf16[128,2048]{1,0:T(8,128)(2,1)S(1)} collective-permute-done((bf16[128,2048]{1,0:T(8,128)(2,1)S(1)}, bf16[128,2048]{1,0:T(8,128)(2,1)S(1)}, u32[]{:S(2)}, u32[]{:S(2)}) %collective-permute-start.3) | collective-permute-done | bytes 524320 | tf_op jit(solution)/shard_map/ppermute | solution.py:342
  27.2 0.0 collective-permute-done.2.near_ref
  27.2 1.2 %shard_map.53.vec_ref = bf16[128,2048]{1,0:T(8,128)(2,1)S(1)} custom-call(s32[8,6]{1,0:T(8,128)S(1)} %add_select_fusion.1.loc_ref, bf16[128,2048]{1,0:T(8,128)(2,1)S(1)} %collective-permute-done.2.near_ref, bf16[128,2048]{1,0:T(8,128)(2,1)S(1)} %collective-permute-done.3.far_ref, f32[128,2048]{1,0:T(8,128)S(1)} %shard_map.52.acc_ref, ...), custom_call_target="tpu_custom_call" | custom-call | flops 268435456 | bytes 2097152 | tf_op jit(solution)/shard_map/pallas_call | solution.py:123
  28.4 3.2 %collective-permute-start.5 = (bf16[128,2048]{1,0:T(8,128)(2,1)S(1)}, bf16[128,2048]{1,0:T(8,128)(2,1)S(1)}, u32[]{:S(2)}, u32[]{:S(2)}) collective-permute-start(bf16[128,2048]{1,0:T(8,128)(2,1)S(1)} %shard_map.53.vec_ref), channel_id=1, source_target_pairs={{0,30},{2,4},{4,2},{6,8},{8,6},{10,12},{12,10},{14,16},{16,14},{18... | collective-permute-start | bytes 1572872 | tf_op jit(solution)/shard_map/ppermute | solution.py:342
  31.6 5.7 %collective-permute-start.4 = (bf16[128,2048]{1,0:T(8,128)(2,1)S(1)}, bf16[128,2048]{1,0:T(8,128)(2,1)S(1)}, u32[]{:S(2)}, u32[]{:S(2)}) collective-permute-start(bf16[128,2048]{1,0:T(8,128)(2,1)S(1)} %shard_map.53.vec_ref), channel_id=1, source_target_pairs={{0,2},{2,0},{4,6},{6,4},{8,10},{10,8},{12,14},{14,12},{16,18},{18,... | collective-permute-start | bytes 1572872 | tf_op jit(solution)/shard_map/ppermute | solution.py:343
  37.3 1.5 %shard_map.54.acc_ref = f32[128,2048]{1,0:T(8,128)S(1)} custom-call(s32[8,6]{1,0:T(8,128)S(1)} %add_select_fusion.1.loc_ref, bf16[128,2048]{1,0:T(8,128)(2,1)S(1)} %shard_map.53.vec_ref, bf16[8,7,256,256]{3,2,1,0:T(8,128)(2,1)S(1)} %get-tuple-element.11.turned_ref), custom_call_target="tpu_custom_call" | custom-call | flops 671088640 | bytes 5242880 | tf_op jit(solution)/shard_map/pallas_call | solution.py:88
  38.8 1.1 %collective-permute-done.5.far_ref = bf16[128,2048]{1,0:T(8,128)(2,1)S(1)} collective-permute-done((bf16[128,2048]{1,0:T(8,128)(2,1)S(1)}, bf16[128,2048]{1,0:T(8,128)(2,1)S(1)}, u32[]{:S(2)}, u32[]{:S(2)}) %collective-permute-start.5) | collective-permute-done | bytes 524320 | tf_op jit(solution)/shard_map/ppermute | solution.py:342
  39.9 0.0 collective-permute-done.4.near_ref
  39.9 1.2 %shard_map.55 = (f32[128,2048]{1,0:T(8,128)S(1)}, bf16[128,2048]{1,0:T(8,128)(2,1)S(1)}) custom-call(s32[8,6]{1,0:T(8,128)S(1)} %add_select_fusion.1.loc_ref, bf16[128,2048]{1,0:T(8,128)(2,1)S(1)} %collective-permute-done.4.near_ref, bf16[128,2048]{1,0:T(8,128)(2,1)S(1)} %collective-permute-done.5.far_ref, f32[128,2048]{1,0:T(8,128)S(1)} %shard_map.54.acc_ref, ...), custom_call_target="tpu_custom_call" | custom-call | flops 268435456 | bytes 2097152 | tf_op jit(solution)/shard_map/pallas_call | solution.py:123
  41.1 1.6 %collective-permute-start.11 = (bf16[128,2048]{1,0:T(8,128)(2,1)S(1)}, bf16[128,2048]{1,0:T(8,128)(2,1)S(1)}, u32[]{:S(2)}, u32[]{:S(2)}) collective-permute-start(bf16[128,2048]{1,0:T(8,128)(2,1)S(1)} %get-tuple-element.13.high_ref.own_ref), channel_id=1, source_target_pairs={{0,1},{1,0},{2,3},{3,2},{4,5},{5,4},{6,7},{7,6},{8,9},{9,8},{10,11... | collective-permute-start | bytes 1572872 | tf_op jit(solution)/shard_map/ppermute | solution.py:363
  42.7 0.5 shard_map.56
  43.2 5.4 %collective-permute-start.6 = (f32[128,128]{1,0:T(8,128)S(1)}, f32[128,128]{1,0:T(8,128)S(1)}, u32[]{:S(2)}, u32[]{:S(2)}) collective-permute-start(f32[128,128]{1,0:T(8,128)S(1)} %shard_map.56), channel_id=1, source_target_pairs={{0,2},{2,0},{4,6},{6,4},{8,10},{10,8},{12,14},{14,12},{16,18},{18,... | collective-permute-start | bytes 196616 | tf_op jit(solution)/shard_map/ppermute | solution.py:356
  48.6 0.9 %collective-permute-done.6 = f32[128,128]{1,0:T(8,128)S(1)} collective-permute-done((f32[128,128]{1,0:T(8,128)S(1)}, f32[128,128]{1,0:T(8,128)S(1)}, u32[]{:S(2)}, u32[]{:S(2)}) %collective-permute-start.6) | collective-permute-done | bytes 65568 | tf_op jit(solution)/shard_map/ppermute | solution.py:356
  49.5 0.9 %collective-permute-start.7 = (f32[128,128]{1,0:T(8,128)S(1)}, f32[128,128]{1,0:T(8,128)S(1)}, u32[]{:S(2)}, u32[]{:S(2)}) collective-permute-start(f32[128,128]{1,0:T(8,128)S(1)} %add.38), channel_id=1, source_target_pairs={{0,4},{2,6},{4,0},{6,2},{8,12},{10,14},{12,8},{14,10},{16,20},{18,... | collective-permute-start | bytes 196616 | tf_op jit(solution)/shard_map/ppermute | solution.py:356
  50.5 0.8 collective-permute-done.11.other_ref
  51.2 0.3 shard_map.57
  51.6 4.6 %collective-permute-start.12 = (f32[128,128]{1,0:T(8,128)S(1)}, f32[128,128]{1,0:T(8,128)S(1)}, u32[]{:S(2)}, u32[]{:S(2)}) collective-permute-start(f32[128,128]{1,0:T(8,128)S(1)} %shard_map.57), channel_id=1, source_target_pairs={{0,2},{2,0},{4,6},{6,4},{8,10},{10,8},{12,14},{14,12},{16,18},{18,... | collective-permute-start | bytes 196616 | tf_op jit(solution)/shard_map/ppermute | solution.py:356
  56.2 0.0 collective-permute-done.7
  56.2 0.6 collective-permute-start.8
  56.8 0.3 collective-permute-done.12
  57.1 1.3 %collective-permute-start.13 = (f32[128,128]{1,0:T(8,128)S(1)}, f32[128,128]{1,0:T(8,128)S(1)}, u32[]{:S(2)}, u32[]{:S(2)}) collective-permute-start(f32[128,128]{1,0:T(8,128)S(1)} %add.42), channel_id=1, source_target_pairs={{0,4},{2,6},{4,0},{6,2},{8,12},{10,14},{12,8},{14,10},{16,20},{18,... | collective-permute-start | bytes 196616 | tf_op jit(solution)/shard_map/ppermute | solution.py:356
  58.4 2.1 %collective-permute-done.8 = f32[128,128]{1,0:T(8,128)S(1)} collective-permute-done((f32[128,128]{1,0:T(8,128)S(1)}, f32[128,128]{1,0:T(8,128)S(1)}, u32[]{:S(2)}, u32[]{:S(2)}) %collective-permute-start.8) | collective-permute-done | bytes 65568 | tf_op jit(solution)/shard_map/ppermute | solution.py:356
  60.5 1.6 %collective-permute-start.9 = (f32[128,128]{1,0:T(8,128)S(1)}, f32[128,128]{1,0:T(8,128)S(1)}, u32[]{:S(2)}, u32[]{:S(2)}) collective-permute-start(f32[128,128]{1,0:T(8,128)S(1)} %add.40), channel_id=1, source_target_pairs={{0,16},{2,18},{4,20},{6,22},{8,24},{10,26},{12,28},{14,30},{16,0},... | collective-permute-start | bytes 196616 | tf_op jit(solution)/shard_map/ppermute | solution.py:356
  62.1 0.0 collective-permute-done.13
  62.1 0.6 collective-permute-start.14
  62.7 3.8 %collective-permute-done.9 = f32[128,128]{1,0:T(8,128)S(1)} collective-permute-done((f32[128,128]{1,0:T(8,128)S(1)}, f32[128,128]{1,0:T(8,128)S(1)}, u32[]{:S(2)}, u32[]{:S(2)}) %collective-permute-start.9) | collective-permute-done | bytes 65568 | tf_op jit(solution)/shard_map/ppermute | solution.py:356
  66.5 1.6 %collective-permute-start.10 = (f32[128,128]{1,0:T(8,128)S(1)}, f32[128,128]{1,0:T(8,128)S(1)}, u32[]{:S(2)}, u32[]{:S(2)}) collective-permute-start(f32[128,128]{1,0:T(8,128)S(1)} %add.41.own_ref), channel_id=1, source_target_pairs={{0,1},{1,0},{2,3},{3,2},{4,5},{5,4},{6,7},{7,6},{8,9},{9,8},{10,11... | collective-permute-start | bytes 196616 | tf_op jit(solution)/shard_map/ppermute | solution.py:374
  68.1 0.0 collective-permute-done.14
  68.1 0.8 %collective-permute-start.15 = (f32[128,128]{1,0:T(8,128)S(1)}, f32[128,128]{1,0:T(8,128)S(1)}, u32[]{:S(2)}, u32[]{:S(2)}) collective-permute-start(f32[128,128]{1,0:T(8,128)S(1)} %add.44), channel_id=1, source_target_pairs={{0,16},{2,18},{4,20},{6,22},{8,24},{10,26},{12,28},{14,30},{16,0},... | collective-permute-start | bytes 196616 | tf_op jit(solution)/shard_map/ppermute | solution.py:356
  68.9 1.9 %collective-permute-done.10.other_ref = f32[128,128]{1,0:T(8,128)S(1)} collective-permute-done((f32[128,128]{1,0:T(8,128)S(1)}, f32[128,128]{1,0:T(8,128)S(1)}, u32[]{:S(2)}, u32[]{:S(2)}) %collective-permute-start.10) | collective-permute-done | bytes 65568 | tf_op jit(solution)/shard_map/ppermute | solution.py:374
  70.9 4.3 %shard_map.58 = (f32[128,128]{1,0:T(8,128)S(1)}, f32[128,128]{1,0:T(8,128)S(1)}) custom-call(s32[1]{0:T(128)} %bitcast.place_ref, f32[128,128]{1,0:T(8,128)S(1)} %add.41.own_ref, f32[128,128]{1,0:T(8,128)S(1)} %collective-permute-done.10.other_ref), custom_call_target="tpu_custom_call" | custom-call | flops 4194304 | bytes 16777216 | tf_op jit(solution)/shard_map/pallas_call | solution.py:287
  75.2 0.0 collective-permute-done.15
  75.2 6.2 %shard_map.59 = (f32[256,256]{1,0:T(8,128)}, f32[256,256]{1,0:T(8,128)S(1)}) custom-call(s32[1]{0:T(128)} %bitcast.place_ref, f32[128,128]{1,0:T(8,128)S(1)} %add.41.own_ref, f32[128,128]{1,0:T(8,128)S(1)} %collective-permute-done.10.other_ref, f32[128,128]{1,0:T(8,128)S(1)} %add.45.cross_ref, f32[128,128]{1,0:T(8,128)S(1)} %get-tuple-element.14.first_ref, ...), custom_call_target="tpu_custom_call" | custom-call | tf_op jit(solution)/shard_map/pallas_call | solution.py:296
  81.4 1.6 %shard_map.60 = f32[128,2048]{1,0:T(8,128)} custom-call(s32[1]{0:T(128)} %bitcast.place_ref, f32[256,256]{1,0:T(8,128)S(1)} %get-tuple-element.16.inv_ref, f32[128,2048]{1,0:T(8,128)S(1)} %get-tuple-element.12.own_ref, bf16[128,2048]{1,0:T(8,128)(2,1)S(1)} %collective-permute-done.11.other_ref), custom_call_target="tpu_custom_call" | custom-call | tf_op jit(solution)/shard_map/pallas_call | solution.py:390
  (8 shorter events, 0.1 us)
Async XLA Ops:
  0.6 14.0 %collective-permute-start.1 = (bf16[128,2048]{1,0:T(8,128)(2,1)}, bf16[128,2048]{1,0:T(8,128)(2,1)S(1)}, u32[]{:S(2)}, u32[]{:S(2)}) collective-permute-start(bf16[128,2048]{1,0:T(8,128)(2,1)} %prior_ref.3), channel_id=1, source_target_pairs={{0,30},{2,4},{4,2},{6,8},{8,6},{10,12},{12,10},{14,16},{16,14},{18... | collective-permute-start | bytes 1572872 | tf_op jit(solution)/shard_map/ppermute | solution.py:342
  6.1 8.5 %collective-permute-start = (bf16[128,2048]{1,0:T(8,128)(2,1)}, bf16[128,2048]{1,0:T(8,128)(2,1)S(1)}, u32[]{:S(2)}, u32[]{:S(2)}) collective-permute-start(bf16[128,2048]{1,0:T(8,128)(2,1)} %prior_ref.3), channel_id=1, source_target_pairs={{0,2},{2,0},{4,6},{6,4},{8,10},{10,8},{12,14},{14,12},{16,18},{18,... | collective-permute-start | bytes 1572872 | tf_op jit(solution)/shard_map/ppermute | solution.py:343
  7.7 1.0 %copy-start = (bf16[128,2048]{1,0:T(8,128)(2,1)S(1)}, bf16[128,2048]{1,0:T(8,128)(2,1)}, u32[]{:S(2)}) copy-start(bf16[128,2048]{1,0:T(8,128)(2,1)} %prior_ref.3) | copy-start | bytes 1572868
  8.8 3.1 %copy-start.2 = (bf16[8,7,256,256]{3,2,1,0:T(8,128)(2,1)S(1)}, bf16[8,7,256,256]{3,2,1,0:T(8,128)(2,1)}, u32[]{:S(2)}) copy-start(bf16[8,7,256,256]{3,2,1,0:T(8,128)(2,1)} %ham_ref.1) | copy-start | bytes 22020100
  11.9 2.8 %copy-start.1 = (bf16[128,2048]{1,0:T(8,128)(2,1)S(1)}, bf16[128,2048]{1,0:T(8,128)(2,1)}, u32[]{:S(2)}) copy-start(bf16[128,2048]{1,0:T(8,128)(2,1)} %prior_ref.3) | copy-start | bytes 1572868
  15.8 11.5 %collective-permute-start.3 = (bf16[128,2048]{1,0:T(8,128)(2,1)S(1)}, bf16[128,2048]{1,0:T(8,128)(2,1)S(1)}, u32[]{:S(2)}, u32[]{:S(2)}) collective-permute-start(bf16[128,2048]{1,0:T(8,128)(2,1)S(1)} %shard_map.51.vec_ref.prior_ref), channel_id=1, source_target_pairs={{0,30},{2,4},{4,2},{6,8},{8,6},{10,12},{12,10},{14,16},{16,14},{18... | collective-permute-start | bytes 1572872 | tf_op jit(solution)/shard_map/ppermute | solution.py:342
  19.0 8.3 %collective-permute-start.2 = (bf16[128,2048]{1,0:T(8,128)(2,1)S(1)}, bf16[128,2048]{1,0:T(8,128)(2,1)S(1)}, u32[]{:S(2)}, u32[]{:S(2)}) collective-permute-start(bf16[128,2048]{1,0:T(8,128)(2,1)S(1)} %shard_map.51.vec_ref.prior_ref), channel_id=1, source_target_pairs={{0,2},{2,0},{4,6},{6,4},{8,10},{10,8},{12,14},{14,12},{16,18},{18,... | collective-permute-start | bytes 1572872 | tf_op jit(solution)/shard_map/ppermute | solution.py:343
  28.4 11.5 %collective-permute-start.5 = (bf16[128,2048]{1,0:T(8,128)(2,1)S(1)}, bf16[128,2048]{1,0:T(8,128)(2,1)S(1)}, u32[]{:S(2)}, u32[]{:S(2)}) collective-permute-start(bf16[128,2048]{1,0:T(8,128)(2,1)S(1)} %shard_map.53.vec_ref), channel_id=1, source_target_pairs={{0,30},{2,4},{4,2},{6,8},{8,6},{10,12},{12,10},{14,16},{16,14},{18... | collective-permute-start | bytes 1572872 | tf_op jit(solution)/shard_map/ppermute | solution.py:342
  31.6 8.3 %collective-permute-start.4 = (bf16[128,2048]{1,0:T(8,128)(2,1)S(1)}, bf16[128,2048]{1,0:T(8,128)(2,1)S(1)}, u32[]{:S(2)}, u32[]{:S(2)}) collective-permute-start(bf16[128,2048]{1,0:T(8,128)(2,1)S(1)} %shard_map.53.vec_ref), channel_id=1, source_target_pairs={{0,2},{2,0},{4,6},{6,4},{8,10},{10,8},{12,14},{14,12},{16,18},{18,... | collective-permute-start | bytes 1572872 | tf_op jit(solution)/shard_map/ppermute | solution.py:343
  41.1 10.1 %collective-permute-start.11 = (bf16[128,2048]{1,0:T(8,128)(2,1)S(1)}, bf16[128,2048]{1,0:T(8,128)(2,1)S(1)}, u32[]{:S(2)}, u32[]{:S(2)}) collective-permute-start(bf16[128,2048]{1,0:T(8,128)(2,1)S(1)} %get-tuple-element.13.high_ref.own_ref), channel_id=1, source_target_pairs={{0,1},{1,0},{2,3},{3,2},{4,5},{5,4},{6,7},{7,6},{8,9},{9,8},{10,11... | collective-permute-start | bytes 1572872 | tf_op jit(solution)/shard_map/ppermute | solution.py:363
  43.2 6.3 %collective-permute-start.6 = (f32[128,128]{1,0:T(8,128)S(1)}, f32[128,128]{1,0:T(8,128)S(1)}, u32[]{:S(2)}, u32[]{:S(2)}) collective-permute-start(f32[128,128]{1,0:T(8,128)S(1)} %shard_map.56), channel_id=1, source_target_pairs={{0,2},{2,0},{4,6},{6,4},{8,10},{10,8},{12,14},{14,12},{16,18},{18,... | collective-permute-start | bytes 196616 | tf_op jit(solution)/shard_map/ppermute | solution.py:356
  49.5 6.7 %collective-permute-start.7 = (f32[128,128]{1,0:T(8,128)S(1)}, f32[128,128]{1,0:T(8,128)S(1)}, u32[]{:S(2)}, u32[]{:S(2)}) collective-permute-start(f32[128,128]{1,0:T(8,128)S(1)} %add.38), channel_id=1, source_target_pairs={{0,4},{2,6},{4,0},{6,2},{8,12},{10,14},{12,8},{14,10},{16,20},{18,... | collective-permute-start | bytes 196616 | tf_op jit(solution)/shard_map/ppermute | solution.py:356
  51.6 5.5 %collective-permute-start.12 = (f32[128,128]{1,0:T(8,128)S(1)}, f32[128,128]{1,0:T(8,128)S(1)}, u32[]{:S(2)}, u32[]{:S(2)}) collective-permute-start(f32[128,128]{1,0:T(8,128)S(1)} %shard_map.57), channel_id=1, source_target_pairs={{0,2},{2,0},{4,6},{6,4},{8,10},{10,8},{12,14},{14,12},{16,18},{18,... | collective-permute-start | bytes 196616 | tf_op jit(solution)/shard_map/ppermute | solution.py:356
  56.2 4.3 %collective-permute-start.8 = (f32[128,128]{1,0:T(8,128)S(1)}, f32[128,128]{1,0:T(8,128)S(1)}, u32[]{:S(2)}, u32[]{:S(2)}) collective-permute-start(f32[128,128]{1,0:T(8,128)S(1)} %add.39), channel_id=1, source_target_pairs={{0,8},{2,10},{4,12},{6,14},{8,0},{10,2},{12,4},{14,6},{16,24},{18,... | collective-permute-start | bytes 196616 | tf_op jit(solution)/shard_map/ppermute | solution.py:356
  57.1 5.0 %collective-permute-start.13 = (f32[128,128]{1,0:T(8,128)S(1)}, f32[128,128]{1,0:T(8,128)S(1)}, u32[]{:S(2)}, u32[]{:S(2)}) collective-permute-start(f32[128,128]{1,0:T(8,128)S(1)} %add.42), channel_id=1, source_target_pairs={{0,4},{2,6},{4,0},{6,2},{8,12},{10,14},{12,8},{14,10},{16,20},{18,... | collective-permute-start | bytes 196616 | tf_op jit(solution)/shard_map/ppermute | solution.py:356
  60.5 6.0 %collective-permute-start.9 = (f32[128,128]{1,0:T(8,128)S(1)}, f32[128,128]{1,0:T(8,128)S(1)}, u32[]{:S(2)}, u32[]{:S(2)}) collective-permute-start(f32[128,128]{1,0:T(8,128)S(1)} %add.40), channel_id=1, source_target_pairs={{0,16},{2,18},{4,20},{6,22},{8,24},{10,26},{12,28},{14,30},{16,0},... | collective-permute-start | bytes 196616 | tf_op jit(solution)/shard_map/ppermute | solution.py:356
  62.1 5.9 %collective-permute-start.14 = (f32[128,128]{1,0:T(8,128)S(1)}, f32[128,128]{1,0:T(8,128)S(1)}, u32[]{:S(2)}, u32[]{:S(2)}) collective-permute-start(f32[128,128]{1,0:T(8,128)S(1)} %add.43), channel_id=1, source_target_pairs={{0,8},{2,10},{4,12},{6,14},{8,0},{10,2},{12,4},{14,6},{16,24},{18,... | collective-permute-start | bytes 196616 | tf_op jit(solution)/shard_map/ppermute | solution.py:356
  66.5 4.3 %collective-permute-start.10 = (f32[128,128]{1,0:T(8,128)S(1)}, f32[128,128]{1,0:T(8,128)S(1)}, u32[]{:S(2)}, u32[]{:S(2)}) collective-permute-start(f32[128,128]{1,0:T(8,128)S(1)} %add.41.own_ref), channel_id=1, source_target_pairs={{0,1},{1,0},{2,3},{3,2},{4,5},{5,4},{6,7},{7,6},{8,9},{9,8},{10,11... | collective-permute-start | bytes 196616 | tf_op jit(solution)/shard_map/ppermute | solution.py:374
  68.1 7.1 %collective-permute-start.15 = (f32[128,128]{1,0:T(8,128)S(1)}, f32[128,128]{1,0:T(8,128)S(1)}, u32[]{:S(2)}, u32[]{:S(2)}) collective-permute-start(f32[128,128]{1,0:T(8,128)S(1)} %add.44), channel_id=1, source_target_pairs={{0,16},{2,18},{4,20},{6,22},{8,24},{10,26},{12,28},{14,30},{16,0},... | collective-permute-start | bytes 196616 | tf_op jit(solution)/shard_map/ppermute | solution.py:356

commit v10 on v9

--- a/solution.py
+++ b/solution.py
@@ -141,7 +141,9 @@
     out_ref[...] = dot_nt(high, high) + (mixed + mixed.T)
 
 
-def cross_gram_kernel(place_ref, own_ref, other_ref, out_ref):
+def cross_gram_kernel(place_ref, own_ref, other_ref, after_ref, out_ref):
+    del after_ref
+
     @pl.when(place_ref[0] == 0)
     def _():
         out_ref[...] = dot_nt(own_ref[...], other_ref[...])
@@ -242,7 +244,9 @@
     inv_ref[...] = jnp.where(col <= row, right[...] * scale, 0.0)
 
 
-def first_kernel(place_ref, own_ref, other_ref, upper_ref, inv_ref, work, right):
+def first_kernel(place_ref, own_ref, other_ref, after_ref, upper_ref, inv_ref, work, right):
+    del after_ref
+
     @pl.when(place_ref[0] == 0)
     def _():
         work[...] = own_ref[...]
@@ -278,7 +282,7 @@
     inv_ref[half:, 0:half] = -dot_full(inv_ref[half:, half:], between)
 
 
-def factorize(place, own, other, cross):
+def factorize(place, own, other, cross, after):
     half = own.shape[0]
     smem = [pl.BlockSpec(memory_space=pltpu.SMEM)]
     tile = jax.ShapeDtypeStruct((half, half), jnp.float32)
@@ -287,12 +291,12 @@
     first, first_inv = pl.pallas_call(
         first_kernel,
         out_shape=[tile] * 2,
-        in_specs=smem + vmem(2),
+        in_specs=smem + vmem(2) + [pl.BlockSpec(memory_space=pl.ANY)],
         out_specs=vmem(2),
         scratch_shapes=scratch,
         compiler_params=params,
         cost_estimate=pl.CostEstimate(flops=2 * half**3, bytes_accessed=1 << 24, transcendentals=half),
-    )(place, own, other)
+    )(place, own, other, after)
     return pl.pallas_call(
         second_kernel,
         out_shape=[jax.ShapeDtypeStruct((2 * half, 2 * half), jnp.float32)] * 2,
@@ -350,11 +354,19 @@
     side = halo(two)
     filtered, narrow = halo_part(3, *side, own_part(two, turned, loc), two, one, turned, loc)
 
-    def summed(part):
-        step = 1
-        while step < blocks:
-            part = part + lax.ppermute(part, "space", [(i, i ^ step) for i in range(blocks)])
-            step *= 2
+    steps = [1 << i for i in range((blocks - 1).bit_length())]
+    stages = [steps[:1]] + [steps[i : i + 2] for i in range(1, len(steps), 2)]
+
+    def summed(part, chosen):
+        def moved(step):
+            return lax.ppermute(part, "space", [(i, i ^ step) for i in range(blocks)])
+
+        for stage in chosen:
+            if len(stage) == 1:
+                part = part + moved(stage[0])
+            else:
+                one, two = stage
+                part = (part + moved(one)) + (moved(two) + moved(one ^ two))
         return part
 
     place = lax.axis_index("orb").astype(jnp.int32).reshape(1)
@@ -370,21 +382,23 @@
             out_specs=pl.BlockSpec(memory_space=pltpu.VMEM),
             compiler_params=params,
         )(filtered, narrow)
-        near = summed(near)
-        far = lax.ppermute(near, "orb", swap)
+        near = summed(near, stages[:-1])
         cross = pl.pallas_call(
             cross_gram_kernel,
             out_shape=tile,
-            in_specs=smem + vmem(2),
+            in_specs=smem + vmem(2) + [pl.BlockSpec(memory_space=pl.ANY)],
             out_specs=pl.BlockSpec(memory_space=pltpu.VMEM),
             compiler_params=params,
-        )(place, narrow, other)
-        upper, inverse = factorize(place, near, far, summed(cross))
+        )(place, narrow, other, near)
+        near = summed(near, stages[-1:])
+        far = lax.ppermute(near, "orb", swap)
+        cross = summed(cross, stages[:-1])
+        upper, inverse = factorize(place, near, far, summed(cross, stages[-1:]), cross)
     else:
         columns = lax.all_gather(narrow, "orb", axis=0, tiled=True)
-        whole = summed(dot_nt(columns, columns))
+        whole = summed(dot_nt(columns, columns), stages)
         upper, inverse = factorize(
-            jnp.zeros_like(place), whole[:half, :half], whole[half:, half:], whole[:half, half:]
+            jnp.zeros_like(place), whole[:half, :half], whole[half:, half:], whole[:half, half:], whole
         )
     if groups == 2:
         basis = pl.pallas_call(

time: 83.3 us -> 80.1 us (0.962)
  waiting for transfers between devices: 17.3 us -> 14.2 us
    ppermute x1, waiting for transfers between devices: 1.93 us -> 0.52 us  [shards(): far = lax.ppermute(near, 'orb', swap)]
    ppermute x8 -> x10, waiting for transfers between devices: 7.16 us -> 6.24 us  [moved(): return lax.ppermute(part, 'space', [(i, i ^ step) for i in range(blocks)])]
    ppermute x8 -> x10, starting transfers between devices: 15.8 us -> 16.3 us  [moved(): return lax.ppermute(part, 'space', [(i, i ^ step) for i in range(blocks)])]
  transfers between devices with their start and end apart: 16 -> 18, of which waited for: 8 -> 11; matrix products, arithmetic and copies ran while one was open for 2% -> 2% of each run, Pallas kernels for 13% -> 13%
where the time goes in v10:
time: 80.1 us; the launch traced here: 79.8 us
  starting transfers between devices  36.9 us (46%)
  Pallas kernels  22.1 us (28%)
  waiting for transfers between devices  14.2 us (18%)
  local copies, waits for them, and re-layouts  4.27 us (5%)
  other arithmetic  1.53 us (2%)
    ppermute x10, starting transfers between devices, moved(): return lax.ppermute(part, 'space', [(i, i ^ step) for i in range(blocks)])  16.3 us
    ppermute x3, starting transfers between devices, halo(): far = lax.ppermute(vec, 'space', far_pairs)  11.9 us
    ppermute x3, waiting for transfers between devices, halo(): far = lax.ppermute(vec, 'space', far_pairs)  7.41 us
    pallas_call x1, Pallas kernels, factorize(): pl.pallas_call(second_kernel, out_shape=[jax.ShapeDtypeStruct((2 * half,...  6.24 us
    ppermute x10, waiting for transfers between devices, moved(): return lax.ppermute(part, 'space', [(i, i ^ step) for i in range(blocks)])  6.24 us
    ppermute x3, starting transfers between devices, halo(): return (lax.ppermute(vec, 'space', near_pairs), far)  6.13 us
    pallas_call x1, Pallas kernels, factorize(): pl.pallas_call(first_kernel, out_shape=[tile] * 2, in_specs=smem + vmem(2...  4.29 us
    unnamed x6, local copies, waits for them, and re-layouts  4.13 us
  transfers between devices with their start and end apart: 18, of which 11 were waited for; matrix products, arithmetic and copies ran while one was open for 2% of the time, Pallas kernels for 13%

profile of v10, /device:TPU:0, one launch (start us, length us, event | category | flops | bytes accessed | tf_op | source)
XLA Modules:
  0.0 79.8 jit_solution(14975537464827080509)
XLA Ops:
  0.6 5.5 %collective-permute-start.1 = (bf16[128,2048]{1,0:T(8,128)(2,1)}, bf16[128,2048]{1,0:T(8,128)(2,1)S(1)}, u32[]{:S(2)}, u32[]{:S(2)}) collective-permute-start(bf16[128,2048]{1,0:T(8,128)(2,1)} %prior_ref.3), channel_id=1, source_target_pairs={{0,30},{2,4},{4,2},{6,8},{8,6},{10,12},{12,10},{14,16},{16,14},{18... | collective-permute-start | bytes 1572872 | tf_op jit(solution)/shard_map/ppermute | solution.py:346
  6.1 0.0 collective-permute-start
  6.1 0.7 add_select_fusion
  6.8 0.1 slice.11
  6.9 0.1 fusion.1
  7.0 0.8 add_select_fusion.1.loc_ref
  7.7 0.0 copy-start
  7.8 1.0 %copy-done = bf16[128,2048]{1,0:T(8,128)(2,1)S(1)} copy-done((bf16[128,2048]{1,0:T(8,128)(2,1)S(1)}, bf16[128,2048]{1,0:T(8,128)(2,1)}, u32[]{:S(2)}) %copy-start) | copy-done | bytes 524312
  8.8 0.0 copy-start.2
  8.8 3.1 %copy-done.2 = bf16[8,7,256,256]{3,2,1,0:T(8,128)(2,1)S(1)} copy-done((bf16[8,7,256,256]{3,2,1,0:T(8,128)(2,1)S(1)}, bf16[8,7,256,256]{3,2,1,0:T(8,128)(2,1)}, u32[]{:S(2)}) %copy-start.2) | copy-done | bytes 7340056
  11.9 0.0 copy-start.1
  11.9 2.7 %shard_map.50 = (bf16[8,7,256,256]{3,2,1,0:T(8,128)(2,1)S(1)}, f32[128,2048]{1,0:T(8,128)S(1)}) custom-call(s32[8,6]{1,0:T(8,128)S(1)} %add_select_fusion.1.loc_ref, s32[1]{0:T(128)S(6)} %select_n.21.odd_ref, bf16[128,2048]{1,0:T(8,128)(2,1)S(1)} %copy-done, bf16[8,7,256,256]{3,2,1,0:T(8,128)(2,1)S(1)} %copy-done.2), custom_call_target="tpu_custom_call" | custom-call | flops 671088640 | bytes 14680064 | tf_op jit(solution)/shard_map/pallas_call | solution.py:55
  14.6 0.0 collective-permute-done.1.far_ref
  14.6 0.0 collective-permute-done.near_ref
  14.6 0.0 copy-done.1
  14.6 1.1 %shard_map.51.vec_ref.prior_ref = bf16[128,2048]{1,0:T(8,128)(2,1)S(1)} custom-call(s32[8,6]{1,0:T(8,128)S(1)} %add_select_fusion.1.loc_ref, bf16[128,2048]{1,0:T(8,128)(2,1)S(1)} %collective-permute-done.near_ref, bf16[128,2048]{1,0:T(8,128)(2,1)S(1)} %collective-permute-done.1.far_ref, f32[128,2048]{1,0:T(8,128)S(1)} %get-tuple-element.10.acc_ref, ...), custom_call_target="tpu_custom_call" | custom-call | flops 268435456 | bytes 2097152 | tf_op jit(solution)/shard_map/pallas_call | solution.py:123
  15.8 3.2 %collective-permute-start.3 = (bf16[128,2048]{1,0:T(8,128)(2,1)S(1)}, bf16[128,2048]{1,0:T(8,128)(2,1)S(1)}, u32[]{:S(2)}, u32[]{:S(2)}) collective-permute-start(bf16[128,2048]{1,0:T(8,128)(2,1)S(1)} %shard_map.51.vec_ref.prior_ref), channel_id=1, source_target_pairs={{0,30},{2,4},{4,2},{6,8},{8,6},{10,12},{12,10},{14,16},{16,14},{18... | collective-permute-start | bytes 1572872 | tf_op jit(solution)/shard_map/ppermute | solution.py:346
  18.9 0.5 collective-permute-start.2
  19.4 1.5 %shard_map.52.acc_ref = f32[128,2048]{1,0:T(8,128)S(1)} custom-call(s32[8,6]{1,0:T(8,128)S(1)} %add_select_fusion.1.loc_ref, bf16[128,2048]{1,0:T(8,128)(2,1)S(1)} %shard_map.51.vec_ref.prior_ref, bf16[8,7,256,256]{3,2,1,0:T(8,128)(2,1)S(1)} %get-tuple-element.11.turned_ref), custom_call_target="tpu_custom_call" | custom-call | flops 671088640 | bytes 5242880 | tf_op jit(solution)/shard_map/pallas_call | solution.py:88
  20.9 6.3 %collective-permute-done.3.far_ref = bf16[128,2048]{1,0:T(8,128)(2,1)S(1)} collective-permute-done((bf16[128,2048]{1,0:T(8,128)(2,1)S(1)}, bf16[128,2048]{1,0:T(8,128)(2,1)S(1)}, u32[]{:S(2)}, u32[]{:S(2)}) %collective-permute-start.3) | collective-permute-done | bytes 524320 | tf_op jit(solution)/shard_map/ppermute | solution.py:346
  27.2 0.0 collective-permute-done.2.near_ref
  27.2 1.2 %shard_map.53.vec_ref = bf16[128,2048]{1,0:T(8,128)(2,1)S(1)} custom-call(s32[8,6]{1,0:T(8,128)S(1)} %add_select_fusion.1.loc_ref, bf16[128,2048]{1,0:T(8,128)(2,1)S(1)} %collective-permute-done.2.near_ref, bf16[128,2048]{1,0:T(8,128)(2,1)S(1)} %collective-permute-done.3.far_ref, f32[128,2048]{1,0:T(8,128)S(1)} %shard_map.52.acc_ref, ...), custom_call_target="tpu_custom_call" | custom-call | flops 268435456 | bytes 2097152 | tf_op jit(solution)/shard_map/pallas_call | solution.py:123
  28.4 3.2 %collective-permute-start.5 = (bf16[128,2048]{1,0:T(8,128)(2,1)S(1)}, bf16[128,2048]{1,0:T(8,128)(2,1)S(1)}, u32[]{:S(2)}, u32[]{:S(2)}) collective-permute-start(bf16[128,2048]{1,0:T(8,128)(2,1)S(1)} %shard_map.53.vec_ref), channel_id=1, source_target_pairs={{0,30},{2,4},{4,2},{6,8},{8,6},{10,12},{12,10},{14,16},{16,14},{18... | collective-permute-start | bytes 1572872 | tf_op jit(solution)/shard_map/ppermute | solution.py:346
  31.6 5.7 %collective-permute-start.4 = (bf16[128,2048]{1,0:T(8,128)(2,1)S(1)}, bf16[128,2048]{1,0:T(8,128)(2,1)S(1)}, u32[]{:S(2)}, u32[]{:S(2)}) collective-permute-start(bf16[128,2048]{1,0:T(8,128)(2,1)S(1)} %shard_map.53.vec_ref), channel_id=1, source_target_pairs={{0,2},{2,0},{4,6},{6,4},{8,10},{10,8},{12,14},{14,12},{16,18},{18,... | collective-permute-start | bytes 1572872 | tf_op jit(solution)/shard_map/ppermute | solution.py:347
  37.3 1.5 %shard_map.54.acc_ref = f32[128,2048]{1,0:T(8,128)S(1)} custom-call(s32[8,6]{1,0:T(8,128)S(1)} %add_select_fusion.1.loc_ref, bf16[128,2048]{1,0:T(8,128)(2,1)S(1)} %shard_map.53.vec_ref, bf16[8,7,256,256]{3,2,1,0:T(8,128)(2,1)S(1)} %get-tuple-element.11.turned_ref), custom_call_target="tpu_custom_call" | custom-call | flops 671088640 | bytes 5242880 | tf_op jit(solution)/shard_map/pallas_call | solution.py:88
  38.8 1.1 %collective-permute-done.5.far_ref = bf16[128,2048]{1,0:T(8,128)(2,1)S(1)} collective-permute-done((bf16[128,2048]{1,0:T(8,128)(2,1)S(1)}, bf16[128,2048]{1,0:T(8,128)(2,1)S(1)}, u32[]{:S(2)}, u32[]{:S(2)}) %collective-permute-start.5) | collective-permute-done | bytes 524320 | tf_op jit(solution)/shard_map/ppermute | solution.py:346
  39.9 0.0 collective-permute-done.4.near_ref
  39.9 1.2 %shard_map.55 = (f32[128,2048]{1,0:T(8,128)S(1)}, bf16[128,2048]{1,0:T(8,128)(2,1)S(1)}) custom-call(s32[8,6]{1,0:T(8,128)S(1)} %add_select_fusion.1.loc_ref, bf16[128,2048]{1,0:T(8,128)(2,1)S(1)} %collective-permute-done.4.near_ref, bf16[128,2048]{1,0:T(8,128)(2,1)S(1)} %collective-permute-done.5.far_ref, f32[128,2048]{1,0:T(8,128)S(1)} %shard_map.54.acc_ref, ...), custom_call_target="tpu_custom_call" | custom-call | flops 268435456 | bytes 2097152 | tf_op jit(solution)/shard_map/pallas_call | solution.py:123
  41.1 1.6 %collective-permute-start.12 = (bf16[128,2048]{1,0:T(8,128)(2,1)S(1)}, bf16[128,2048]{1,0:T(8,128)(2,1)S(1)}, u32[]{:S(2)}, u32[]{:S(2)}) collective-permute-start(bf16[128,2048]{1,0:T(8,128)(2,1)S(1)} %get-tuple-element.13.high_ref.own_ref), channel_id=1, source_target_pairs={{0,1},{1,0},{2,3},{3,2},{4,5},{5,4},{6,7},{7,6},{8,9},{9,8},{10,11... | collective-permute-start | bytes 1572872 | tf_op jit(solution)/shard_map/ppermute | solution.py:375
  42.7 0.5 shard_map.56
  43.2 5.4 %collective-permute-start.6 = (f32[128,128]{1,0:T(8,128)S(1)}, f32[128,128]{1,0:T(8,128)S(1)}, u32[]{:S(2)}, u32[]{:S(2)}) collective-permute-start(f32[128,128]{1,0:T(8,128)S(1)} %shard_map.56), channel_id=1, source_target_pairs={{0,2},{2,0},{4,6},{6,4},{8,10},{10,8},{12,14},{14,12},{16,18},{18,... | collective-permute-start | bytes 196616 | tf_op jit(solution)/shard_map/ppermute | solution.py:362
  48.6 0.9 %collective-permute-done.6 = f32[128,128]{1,0:T(8,128)S(1)} collective-permute-done((f32[128,128]{1,0:T(8,128)S(1)}, f32[128,128]{1,0:T(8,128)S(1)}, u32[]{:S(2)}, u32[]{:S(2)}) %collective-permute-start.6) | collective-permute-done | bytes 65568 | tf_op jit(solution)/shard_map/ppermute | solution.py:362
  49.5 1.9 %collective-permute-start.9 = (f32[128,128]{1,0:T(8,128)S(1)}, f32[128,128]{1,0:T(8,128)S(1)}, u32[]{:S(2)}, u32[]{:S(2)}) collective-permute-start(f32[128,128]{1,0:T(8,128)S(1)} %add.44), channel_id=1, source_target_pairs={{0,12},{2,14},{4,8},{6,10},{8,4},{10,6},{12,0},{14,2},{16,28},{18,... | collective-permute-start | bytes 196616 | tf_op jit(solution)/shard_map/ppermute | solution.py:362
  51.5 0.5 collective-permute-start.8
  51.9 1.1 %collective-permute-start.7 = (f32[128,128]{1,0:T(8,128)S(1)}, f32[128,128]{1,0:T(8,128)S(1)}, u32[]{:S(2)}, u32[]{:S(2)}) collective-permute-start(f32[128,128]{1,0:T(8,128)S(1)} %add.44), channel_id=1, source_target_pairs={{0,4},{2,6},{4,0},{6,2},{8,12},{10,14},{12,8},{14,10},{16,20},{18,... | collective-permute-start | bytes 196616 | tf_op jit(solution)/shard_map/ppermute | solution.py:362
  53.1 2.3 %collective-permute-done.9 = f32[128,128]{1,0:T(8,128)S(1)} collective-permute-done((f32[128,128]{1,0:T(8,128)S(1)}, f32[128,128]{1,0:T(8,128)S(1)}, u32[]{:S(2)}, u32[]{:S(2)}) %collective-permute-start.9) | collective-permute-done | bytes 65568 | tf_op jit(solution)/shard_map/ppermute | solution.py:362
  55.4 0.3 collective-permute-done.8
  55.7 0.5 collective-permute-done.7
  56.3 0.0 collective-permute-done.12.other_ref
  56.3 0.3 shard_map.57
  56.6 0.1 collective-permute-start.13
  56.7 2.6 %collective-permute-start.10 = (f32[128,128]{1,0:T(8,128)S(1)}, f32[128,128]{1,0:T(8,128)S(1)}, u32[]{:S(2)}, u32[]{:S(2)}) collective-permute-start(f32[128,128]{1,0:T(8,128)S(1)} %add_add_fusion.1.after_ref), channel_id=1, source_target_pairs={{0,16},{2,18},{4,20},{6,22},{8,24},{10,26},{12,28},{14,30},{16,0},... | collective-permute-start | bytes 196616 | tf_op jit(solution)/shard_map/ppermute | solution.py:362
  59.3 0.0 collective-permute-done.13
  59.3 2.1 %collective-permute-start.16 = (f32[128,128]{1,0:T(8,128)S(1)}, f32[128,128]{1,0:T(8,128)S(1)}, u32[]{:S(2)}, u32[]{:S(2)}) collective-permute-start(f32[128,128]{1,0:T(8,128)S(1)} %add.49), channel_id=1, source_target_pairs={{0,12},{2,14},{4,8},{6,10},{8,4},{10,6},{12,0},{14,2},{16,28},{18,... | collective-permute-start | bytes 196616 | tf_op jit(solution)/shard_map/ppermute | solution.py:362
  61.4 0.2 collective-permute-start.15
  61.6 1.2 %collective-permute-start.14 = (f32[128,128]{1,0:T(8,128)S(1)}, f32[128,128]{1,0:T(8,128)S(1)}, u32[]{:S(2)}, u32[]{:S(2)}) collective-permute-start(f32[128,128]{1,0:T(8,128)S(1)} %add.49), channel_id=1, source_target_pairs={{0,4},{2,6},{4,0},{6,2},{8,12},{10,14},{12,8},{14,10},{16,20},{18,... | collective-permute-start | bytes 196616 | tf_op jit(solution)/shard_map/ppermute | solution.py:362
  62.9 0.5 collective-permute-done.10
  63.4 1.0 %collective-permute-start.11 = (f32[128,128]{1,0:T(8,128)S(1)}, f32[128,128]{1,0:T(8,128)S(1)}, u32[]{:S(2)}, u32[]{:S(2)}) collective-permute-start(f32[128,128]{1,0:T(8,128)S(1)} %add.48.own_ref), channel_id=1, source_target_pairs={{0,1},{1,0},{2,3},{3,2},{4,5},{5,4},{6,7},{7,6},{8,9},{9,8},{10,11... | collective-permute-start | bytes 196616 | tf_op jit(solution)/shard_map/ppermute | solution.py:394
  64.4 0.9 %collective-permute-done.16 = f32[128,128]{1,0:T(8,128)S(1)} collective-permute-done((f32[128,128]{1,0:T(8,128)S(1)}, f32[128,128]{1,0:T(8,128)S(1)}, u32[]{:S(2)}, u32[]{:S(2)}) %collective-permute-start.16) | collective-permute-done | bytes 65568 | tf_op jit(solution)/shard_map/ppermute | solution.py:362
  65.3 0.4 collective-permute-done.15
  65.7 0.4 collective-permute-done.14
  66.1 1.1 %collective-permute-start.17 = (f32[128,128]{1,0:T(8,128)S(1)}, f32[128,128]{1,0:T(8,128)S(1)}, u32[]{:S(2)}, u32[]{:S(2)}) collective-permute-start(f32[128,128]{1,0:T(8,128)S(1)} %add_add_fusion.after_ref), channel_id=1, source_target_pairs={{0,16},{2,18},{4,20},{6,22},{8,24},{10,26},{12,28},{14,30},{16,0},... | collective-permute-start | bytes 196616 | tf_op jit(solution)/shard_map/ppermute | solution.py:362
  67.2 0.5 collective-permute-done.11.other_ref
  67.7 4.3 %shard_map.58 = (f32[128,128]{1,0:T(8,128)S(1)}, f32[128,128]{1,0:T(8,128)S(1)}) custom-call(s32[1]{0:T(128)} %bitcast.place_ref, f32[128,128]{1,0:T(8,128)S(1)} %add.48.own_ref, f32[128,128]{1,0:T(8,128)S(1)} %collective-permute-done.11.other_ref, f32[128,128]{1,0:T(8,128)S(1)} %add_add_fusion.after_ref), custom_call_target="tpu_custom_call" | custom-call | flops 4194304 | bytes 16777216 | tf_op jit(solution)/shard_map/pallas_call | solution.py:291
  72.0 0.0 collective-permute-done.17
  72.0 6.2 %shard_map.59 = (f32[256,256]{1,0:T(8,128)}, f32[256,256]{1,0:T(8,128)S(1)}) custom-call(s32[1]{0:T(128)} %bitcast.place_ref, f32[128,128]{1,0:T(8,128)S(1)} %add.48.own_ref, f32[128,128]{1,0:T(8,128)S(1)} %collective-permute-done.11.other_ref, f32[128,128]{1,0:T(8,128)S(1)} %add.53.cross_ref, f32[128,128]{1,0:T(8,128)S(1)} %get-tuple-element.14.first_ref, ...), custom_call_target="tpu_custom_call" | custom-call | tf_op jit(solution)/shard_map/pallas_call | solution.py:300
  78.3 1.6 %shard_map.60 = f32[128,2048]{1,0:T(8,128)} custom-call(s32[1]{0:T(128)} %bitcast.place_ref, f32[256,256]{1,0:T(8,128)S(1)} %get-tuple-element.16.inv_ref, f32[128,2048]{1,0:T(8,128)S(1)} %get-tuple-element.12.own_ref, bf16[128,2048]{1,0:T(8,128)(2,1)S(1)} %collective-permute-done.12.other_ref), custom_call_target="tpu_custom_call" | custom-call | tf_op jit(solution)/shard_map/pallas_call | solution.py:404
  (6 shorter events, 0.1 us)
Async XLA Ops:
  0.6 14.0 %collective-permute-start.1 = (bf16[128,2048]{1,0:T(8,128)(2,1)}, bf16[128,2048]{1,0:T(8,128)(2,1)S(1)}, u32[]{:S(2)}, u32[]{:S(2)}) collective-permute-start(bf16[128,2048]{1,0:T(8,128)(2,1)} %prior_ref.3), channel_id=1, source_target_pairs={{0,30},{2,4},{4,2},{6,8},{8,6},{10,12},{12,10},{14,16},{16,14},{18... | collective-permute-start | bytes 1572872 | tf_op jit(solution)/shard_map/ppermute | solution.py:346
  6.1 8.5 %collective-permute-start = (bf16[128,2048]{1,0:T(8,128)(2,1)}, bf16[128,2048]{1,0:T(8,128)(2,1)S(1)}, u32[]{:S(2)}, u32[]{:S(2)}) collective-permute-start(bf16[128,2048]{1,0:T(8,128)(2,1)} %prior_ref.3), channel_id=1, source_target_pairs={{0,2},{2,0},{4,6},{6,4},{8,10},{10,8},{12,14},{14,12},{16,18},{18,... | collective-permute-start | bytes 1572872 | tf_op jit(solution)/shard_map/ppermute | solution.py:347
  7.7 1.0 %copy-start = (bf16[128,2048]{1,0:T(8,128)(2,1)S(1)}, bf16[128,2048]{1,0:T(8,128)(2,1)}, u32[]{:S(2)}) copy-start(bf16[128,2048]{1,0:T(8,128)(2,1)} %prior_ref.3) | copy-start | bytes 1572868
  8.8 3.1 %copy-start.2 = (bf16[8,7,256,256]{3,2,1,0:T(8,128)(2,1)S(1)}, bf16[8,7,256,256]{3,2,1,0:T(8,128)(2,1)}, u32[]{:S(2)}) copy-start(bf16[8,7,256,256]{3,2,1,0:T(8,128)(2,1)} %ham_ref.1) | copy-start | bytes 22020100
  11.9 2.8 %copy-start.1 = (bf16[128,2048]{1,0:T(8,128)(2,1)S(1)}, bf16[128,2048]{1,0:T(8,128)(2,1)}, u32[]{:S(2)}) copy-start(bf16[128,2048]{1,0:T(8,128)(2,1)} %prior_ref.3) | copy-start | bytes 1572868
  15.8 11.5 %collective-permute-start.3 = (bf16[128,2048]{1,0:T(8,128)(2,1)S(1)}, bf16[128,2048]{1,0:T(8,128)(2,1)S(1)}, u32[]{:S(2)}, u32[]{:S(2)}) collective-permute-start(bf16[128,2048]{1,0:T(8,128)(2,1)S(1)} %shard_map.51.vec_ref.prior_ref), channel_id=1, source_target_pairs={{0,30},{2,4},{4,2},{6,8},{8,6},{10,12},{12,10},{14,16},{16,14},{18... | collective-permute-start | bytes 1572872 | tf_op jit(solution)/shard_map/ppermute | solution.py:346
  18.9 8.3 %collective-permute-start.2 = (bf16[128,2048]{1,0:T(8,128)(2,1)S(1)}, bf16[128,2048]{1,0:T(8,128)(2,1)S(1)}, u32[]{:S(2)}, u32[]{:S(2)}) collective-permute-start(bf16[128,2048]{1,0:T(8,128)(2,1)S(1)} %shard_map.51.vec_ref.prior_ref), channel_id=1, source_target_pairs={{0,2},{2,0},{4,6},{6,4},{8,10},{10,8},{12,14},{14,12},{16,18},{18,... | collective-permute-start | bytes 1572872 | tf_op jit(solution)/shard_map/ppermute | solution.py:347
  28.4 11.5 %collective-permute-start.5 = (bf16[128,2048]{1,0:T(8,128)(2,1)S(1)}, bf16[128,2048]{1,0:T(8,128)(2,1)S(1)}, u32[]{:S(2)}, u32[]{:S(2)}) collective-permute-start(bf16[128,2048]{1,0:T(8,128)(2,1)S(1)} %shard_map.53.vec_ref), channel_id=1, source_target_pairs={{0,30},{2,4},{4,2},{6,8},{8,6},{10,12},{12,10},{14,16},{16,14},{18... | collective-permute-start | bytes 1572872 | tf_op jit(solution)/shard_map/ppermute | solution.py:346
  31.6 8.3 %collective-permute-start.4 = (bf16[128,2048]{1,0:T(8,128)(2,1)S(1)}, bf16[128,2048]{1,0:T(8,128)(2,1)S(1)}, u32[]{:S(2)}, u32[]{:S(2)}) collective-permute-start(bf16[128,2048]{1,0:T(8,128)(2,1)S(1)} %shard_map.53.vec_ref), channel_id=1, source_target_pairs={{0,2},{2,0},{4,6},{6,4},{8,10},{10,8},{12,14},{14,12},{16,18},{18,... | collective-permute-start | bytes 1572872 | tf_op jit(solution)/shard_map/ppermute | solution.py:347
  41.1 15.2 %collective-permute-start.12 = (bf16[128,2048]{1,0:T(8,128)(2,1)S(1)}, bf16[128,2048]{1,0:T(8,128)(2,1)S(1)}, u32[]{:S(2)}, u32[]{:S(2)}) collective-permute-start(bf16[128,2048]{1,0:T(8,128)(2,1)S(1)} %get-tuple-element.13.high_ref.own_ref), channel_id=1, source_target_pairs={{0,1},{1,0},{2,3},{3,2},{4,5},{5,4},{6,7},{7,6},{8,9},{9,8},{10,11... | collective-permute-start | bytes 1572872 | tf_op jit(solution)/shard_map/ppermute | solution.py:375
  43.2 6.3 %collective-permute-start.6 = (f32[128,128]{1,0:T(8,128)S(1)}, f32[128,128]{1,0:T(8,128)S(1)}, u32[]{:S(2)}, u32[]{:S(2)}) collective-permute-start(f32[128,128]{1,0:T(8,128)S(1)} %shard_map.56), channel_id=1, source_target_pairs={{0,2},{2,0},{4,6},{6,4},{8,10},{10,8},{12,14},{14,12},{16,18},{18,... | collective-permute-start | bytes 196616 | tf_op jit(solution)/shard_map/ppermute | solution.py:362
  49.5 5.9 %collective-permute-start.9 = (f32[128,128]{1,0:T(8,128)S(1)}, f32[128,128]{1,0:T(8,128)S(1)}, u32[]{:S(2)}, u32[]{:S(2)}) collective-permute-start(f32[128,128]{1,0:T(8,128)S(1)} %add.44), channel_id=1, source_target_pairs={{0,12},{2,14},{4,8},{6,10},{8,4},{10,6},{12,0},{14,2},{16,28},{18,... | collective-permute-start | bytes 196616 | tf_op jit(solution)/shard_map/ppermute | solution.py:362
  51.5 4.3 %collective-permute-start.8 = (f32[128,128]{1,0:T(8,128)S(1)}, f32[128,128]{1,0:T(8,128)S(1)}, u32[]{:S(2)}, u32[]{:S(2)}) collective-permute-start(f32[128,128]{1,0:T(8,128)S(1)} %add.44), channel_id=1, source_target_pairs={{0,8},{2,10},{4,12},{6,14},{8,0},{10,2},{12,4},{14,6},{16,24},{18,... | collective-permute-start | bytes 196616 | tf_op jit(solution)/shard_map/ppermute | solution.py:362
  51.9 4.3 %collective-permute-start.7 = (f32[128,128]{1,0:T(8,128)S(1)}, f32[128,128]{1,0:T(8,128)S(1)}, u32[]{:S(2)}, u32[]{:S(2)}) collective-permute-start(f32[128,128]{1,0:T(8,128)S(1)} %add.44), channel_id=1, source_target_pairs={{0,4},{2,6},{4,0},{6,2},{8,12},{10,14},{12,8},{14,10},{16,20},{18,... | collective-permute-start | bytes 196616 | tf_op jit(solution)/shard_map/ppermute | solution.py:362
  56.6 2.7 %collective-permute-start.13 = (f32[128,128]{1,0:T(8,128)S(1)}, f32[128,128]{1,0:T(8,128)S(1)}, u32[]{:S(2)}, u32[]{:S(2)}) collective-permute-start(f32[128,128]{1,0:T(8,128)S(1)} %shard_map.57), channel_id=1, source_target_pairs={{0,2},{2,0},{4,6},{6,4},{8,10},{10,8},{12,14},{14,12},{16,18},{18,... | collective-permute-start | bytes 196616 | tf_op jit(solution)/shard_map/ppermute | solution.py:362
  56.7 6.7 %collective-permute-start.10 = (f32[128,128]{1,0:T(8,128)S(1)}, f32[128,128]{1,0:T(8,128)S(1)}, u32[]{:S(2)}, u32[]{:S(2)}) collective-permute-start(f32[128,128]{1,0:T(8,128)S(1)} %add_add_fusion.1.after_ref), channel_id=1, source_target_pairs={{0,16},{2,18},{4,20},{6,22},{8,24},{10,26},{12,28},{14,30},{16,0},... | collective-permute-start | bytes 196616 | tf_op jit(solution)/shard_map/ppermute | solution.py:362
  59.3 6.0 %collective-permute-start.16 = (f32[128,128]{1,0:T(8,128)S(1)}, f32[128,128]{1,0:T(8,128)S(1)}, u32[]{:S(2)}, u32[]{:S(2)}) collective-permute-start(f32[128,128]{1,0:T(8,128)S(1)} %add.49), channel_id=1, source_target_pairs={{0,12},{2,14},{4,8},{6,10},{8,4},{10,6},{12,0},{14,2},{16,28},{18,... | collective-permute-start | bytes 196616 | tf_op jit(solution)/shard_map/ppermute | solution.py:362
  61.4 4.3 %collective-permute-start.15 = (f32[128,128]{1,0:T(8,128)S(1)}, f32[128,128]{1,0:T(8,128)S(1)}, u32[]{:S(2)}, u32[]{:S(2)}) collective-permute-start(f32[128,128]{1,0:T(8,128)S(1)} %add.49), channel_id=1, source_target_pairs={{0,8},{2,10},{4,12},{6,14},{8,0},{10,2},{12,4},{14,6},{16,24},{18,... | collective-permute-start | bytes 196616 | tf_op jit(solution)/shard_map/ppermute | solution.py:362
  61.6 4.4 %collective-permute-start.14 = (f32[128,128]{1,0:T(8,128)S(1)}, f32[128,128]{1,0:T(8,128)S(1)}, u32[]{:S(2)}, u32[]{:S(2)}) collective-permute-start(f32[128,128]{1,0:T(8,128)S(1)} %add.49), channel_id=1, source_target_pairs={{0,4},{2,6},{4,0},{6,2},{8,12},{10,14},{12,8},{14,10},{16,20},{18,... | collective-permute-start | bytes 196616 | tf_op jit(solution)/shard_map/ppermute | solution.py:362
  63.4 4.3 %collective-permute-start.11 = (f32[128,128]{1,0:T(8,128)S(1)}, f32[128,128]{1,0:T(8,128)S(1)}, u32[]{:S(2)}, u32[]{:S(2)}) collective-permute-start(f32[128,128]{1,0:T(8,128)S(1)} %add.48.own_ref), channel_id=1, source_target_pairs={{0,1},{1,0},{2,3},{3,2},{4,5},{5,4},{6,7},{7,6},{8,9},{9,8},{10,11... | collective-permute-start | bytes 196616 | tf_op jit(solution)/shard_map/ppermute | solution.py:394
  66.1 5.9 %collective-permute-start.17 = (f32[128,128]{1,0:T(8,128)S(1)}, f32[128,128]{1,0:T(8,128)S(1)}, u32[]{:S(2)}, u32[]{:S(2)}) collective-permute-start(f32[128,128]{1,0:T(8,128)S(1)} %add_add_fusion.after_ref), channel_id=1, source_target_pairs={{0,16},{2,18},{4,20},{6,22},{8,24},{10,26},{12,28},{14,30},{16,0},... | collective-permute-start | bytes 196616 | tf_op jit(solution)/shard_map/ppermute | solution.py:362

commit v11 on v10

--- a/solution.py
+++ b/solution.py
@@ -146,11 +146,11 @@
 
     @pl.when(place_ref[0] == 0)
     def _():
+        out_ref[...] = dot_nt(other_ref[...], own_ref[...])
+
+    @pl.when(place_ref[0] != 0)
+    def _():
         out_ref[...] = dot_nt(own_ref[...], other_ref[...])
-
-    @pl.when(place_ref[0] != 0)
-    def _():
-        out_ref[...] = dot_nt(other_ref[...], own_ref[...])
 
 
 def tree(terms):
@@ -282,50 +282,105 @@
     inv_ref[half:, 0:half] = -dot_full(inv_ref[half:, half:], between)
 
 
-def factorize(place, own, other, cross, after):
+def factor_first(place, own, other, after):
     half = own.shape[0]
-    smem = [pl.BlockSpec(memory_space=pltpu.SMEM)]
-    tile = jax.ShapeDtypeStruct((half, half), jnp.float32)
-    scratch = [pltpu.VMEM((half, half), jnp.float32)] * 2
-    params = pltpu.CompilerParams(vmem_limit_bytes=24 << 20)
-    first, first_inv = pl.pallas_call(
+    return pl.pallas_call(
         first_kernel,
-        out_shape=[tile] * 2,
-        in_specs=smem + vmem(2) + [pl.BlockSpec(memory_space=pl.ANY)],
+        out_shape=[jax.ShapeDtypeStruct((half, half), jnp.float32)] * 2,
+        in_specs=[pl.BlockSpec(memory_space=pltpu.SMEM)]
+        + vmem(2)
+        + [pl.BlockSpec(memory_space=pl.ANY)],
         out_specs=vmem(2),
-        scratch_shapes=scratch,
-        compiler_params=params,
+        scratch_shapes=[pltpu.VMEM((half, half), jnp.float32)] * 2,
+        compiler_params=pltpu.CompilerParams(vmem_limit_bytes=24 << 20),
         cost_estimate=pl.CostEstimate(flops=2 * half**3, bytes_accessed=1 << 24, transcendentals=half),
     )(place, own, other, after)
+
+
+def factor_second(place, own, other, cross, first, first_inv):
+    half = own.shape[0]
     return pl.pallas_call(
         second_kernel,
         out_shape=[jax.ShapeDtypeStruct((2 * half, 2 * half), jnp.float32)] * 2,
-        in_specs=smem + vmem(5),
+        in_specs=[pl.BlockSpec(memory_space=pltpu.SMEM)] + vmem(5),
         out_specs=vmem(2),
-        scratch_shapes=scratch,
-        compiler_params=params,
+        scratch_shapes=[pltpu.VMEM((half, half), jnp.float32)] * 2,
+        compiler_params=pltpu.CompilerParams(vmem_limit_bytes=24 << 20),
     )(place, own, other, cross, first, first_inv)
 
 
-def basis_kernel(place_ref, inv_ref, own_ref, other_ref, out_ref):
-    half, total = out_ref.shape
-    place = place_ref[0]
-    rows = pl.ds(pl.multiple_of(place * half, half), half)
-    away = pl.ds(pl.multiple_of((1 - place) * half, half), half)
-    near_high, near_low = split(inv_ref[rows, rows])
-    far_high, far_low = split(inv_ref[rows, away])
-    both_high = jnp.concatenate([near_high, far_high], axis=1)
-    both_low = jnp.concatenate([near_low, far_low], axis=1)
-    step = 512 if total % 512 == 0 else total
-    for at in range(0, total, step):
-        here = slice(at, at + step)
-        high, low = split(own_ref[:, here])
-        both = jnp.concatenate([high, other_ref[:, here]], axis=0)
-        out_ref[:, here] = (
-            jnp.dot(both_high, both, preferred_element_type=jnp.float32)
-            + jnp.dot(both_low, both, preferred_element_type=jnp.float32)
-            + jnp.dot(near_high, low, preferred_element_type=jnp.float32)
-        )
+def finish_kernel(
+    place_ref, own_ref, other_ref, cross_ref, first_ref, first_inv_ref, wide_ref, high_ref, away_ref,
+    upper_ref, basis_ref, work, right, inverse, part, result, sems,
+):
+    half, total = wide_ref.shape
+    pieces = sems.shape[0]
+    spans = [slice(i * (total // pieces), (i + 1) * (total // pieces)) for i in range(pieces)]
+    leading = place_ref[0] == 0
+    trailing = place_ref[0] != 0
+    copies = [
+        pltpu.make_async_copy(result.at[:, here], basis_ref.at[:, here], sems.at[i])
+        for i, here in enumerate(spans)
+    ]
+
+    def dot(a, b):
+        return jnp.dot(a, b, preferred_element_type=jnp.float32)
+
+    lower = dot_full(cross_ref[...], first_inv_ref[...], ((1,), (1,)))
+    update = dot_full(lower, lower, ((1,), (1,)))
+
+    @pl.when(leading)
+    def _():
+        work[...] = other_ref[...] - update
+        high_inv, low_inv = split(first_inv_ref[...])
+        for copy, here in zip(copies, spans):
+            high = high_ref[:, here]
+            low = (wide_ref[:, here] - high.astype(jnp.float32)).astype(jnp.bfloat16)
+            result[:, here] = dot(high_inv, high) + (dot(high_inv, low) + dot(low_inv, high))
+            copy.start()
+
+    @pl.when(trailing)
+    def _():
+        work[...] = own_ref[...] - update
+        high_mix, low_mix = split(dot_full(lower, first_inv_ref[...]))
+        for here in spans:
+            away = away_ref[:, here]
+            part[:, here] = wide_ref[:, here] - (dot(high_mix, away) + dot(low_mix, away))
+
+    upper_ref[0:half, 0:half] = first_ref[...]
+    upper_ref[0:half, half:] = lower.T
+    upper_ref[half:, 0:half] = jnp.zeros((half, half), jnp.float32)
+    factor_into(work, right, upper_ref.at[half:, half:], inverse)
+
+    @pl.when(trailing)
+    def _():
+        high_inv, low_inv = split(inverse[...])
+        for copy, here in zip(copies, spans):
+            high, low = split(part[:, here])
+            result[:, here] = dot(high_inv, high) + (dot(high_inv, low) + dot(low_inv, high))
+            copy.start()
+
+    for copy in copies:
+        copy.wait()
+
+
+def finish(place, own, other, cross, first, first_inv, wide, high, away):
+    half, total = wide.shape
+    pieces = 4 if total % 512 == 0 else 1
+    tile = pltpu.VMEM((half, half), jnp.float32)
+    return pl.pallas_call(
+        finish_kernel,
+        out_shape=[
+            jax.ShapeDtypeStruct((2 * half, 2 * half), jnp.float32),
+            jax.ShapeDtypeStruct(wide.shape, jnp.float32),
+        ],
+        in_specs=[pl.BlockSpec(memory_space=pltpu.SMEM)] + vmem(8),
+        out_specs=vmem(1) + [pl.BlockSpec(memory_space=pl.ANY)],
+        scratch_shapes=[tile] * 3
+        + [pltpu.VMEM((half, total), jnp.float32)] * 2
+        + [pltpu.SemaphoreType.DMA((pieces,))],
+        compiler_params=pltpu.CompilerParams(vmem_limit_bytes=24 << 20),
+    )(place, own, other, cross, first, first_inv, wide, high, away)
 
 
 def shards(hamiltonian, orbitals, adjacency):
@@ -393,22 +448,15 @@
         near = summed(near, stages[-1:])
         far = lax.ppermute(near, "orb", swap)
         cross = summed(cross, stages[:-1])
-        upper, inverse = factorize(place, near, far, summed(cross, stages[-1:]), cross)
+        first, first_inv = factor_first(place, near, far, cross)
+        cross = summed(cross, stages[-1:])
+        upper, basis = finish(place, near, far, cross, first, first_inv, filtered, narrow, other)
     else:
         columns = lax.all_gather(narrow, "orb", axis=0, tiled=True)
         whole = summed(dot_nt(columns, columns), stages)
-        upper, inverse = factorize(
-            jnp.zeros_like(place), whole[:half, :half], whole[half:, half:], whole[:half, half:], whole
-        )
-    if groups == 2:
-        basis = pl.pallas_call(
-            basis_kernel,
-            out_shape=jax.ShapeDtypeStruct(orbitals.shape, jnp.float32),
-            in_specs=smem + vmem(3),
-            out_specs=pl.BlockSpec(memory_space=pltpu.VMEM),
-            compiler_params=pltpu.CompilerParams(vmem_limit_bytes=24 << 20),
-        )(place, inverse, filtered, other)
-    else:
+        blocks_of = (jnp.zeros_like(place), whole[:half, :half], whole[half:, half:])
+        first, first_inv = factor_first(*blocks_of, whole)
+        upper, inverse = factor_second(*blocks_of, whole[:half, half:], first, first_inv)
         mine = lax.dynamic_slice_in_dim(inverse, place[0] * owned, owned, 0)
         near = lax.dynamic_slice_in_dim(mine, place[0] * owned, owned, 1)
         rest = filtered - narrow.astype(jnp.float32)

time: 80.1 us -> 78.9 us (0.985)
  Pallas kernels: 22.1 us -> 20.8 us
    pallas_call x3 -> x2, Pallas kernels: 12.1 us -> 10.7 us  [the longest x1 6.44 us: finish(): pl.pallas_call(finish_kernel, out_shape=[jax.ShapeDtypeStruct((2 * half,...]
where the time goes in v11:
time: 78.9 us; the launch traced here: 78.6 us
  starting transfers between devices  36.9 us (47%)
  Pallas kernels  20.8 us (26%)
  waiting for transfers between devices  14.2 us (18%)
  local copies, waits for them, and re-layouts  4.27 us (5%)
  other arithmetic  1.53 us (2%)
  between operations  0.94 us (1%)
    ppermute x10, starting transfers between devices, moved(): return lax.ppermute(part, 'space', [(i, i ^ step) for i in range(blocks)])  16.3 us
    ppermute x3, starting transfers between devices, halo(): far = lax.ppermute(vec, 'space', far_pairs)  11.9 us
    ppermute x3, waiting for transfers between devices, halo(): far = lax.ppermute(vec, 'space', far_pairs)  7.45 us
    pallas_call x1, Pallas kernels, finish(): pl.pallas_call(finish_kernel, out_shape=[jax.ShapeDtypeStruct((2 * half,...  6.44 us
    ppermute x10, waiting for transfers between devices, moved(): return lax.ppermute(part, 'space', [(i, i ^ step) for i in range(blocks)])  6.22 us
    ppermute x3, starting transfers between devices, halo(): return (lax.ppermute(vec, 'space', near_pairs), far)  6.09 us
    pallas_call x1, Pallas kernels, factor_first(): pl.pallas_call(first_kernel, out_shape=[jax.ShapeDtypeStruct((half, half)...  4.29 us
    unnamed x6, local copies, waits for them, and re-layouts  4.13 us
  transfers between devices with their start and end apart: 18, of which 11 were waited for; matrix products, arithmetic and copies ran while one was open for 2% of the time, Pallas kernels for 13%

profile of v11, /device:TPU:0, one launch (start us, length us, event | category | flops | bytes accessed | tf_op | source)
XLA Modules:
  0.0 78.6 jit_solution(10640338814970823486)
XLA Ops:
  0.6 5.5 %collective-permute-start.1 = (bf16[128,2048]{1,0:T(8,128)(2,1)}, bf16[128,2048]{1,0:T(8,128)(2,1)S(1)}, u32[]{:S(2)}, u32[]{:S(2)}) collective-permute-start(bf16[128,2048]{1,0:T(8,128)(2,1)} %prior_ref.3), channel_id=1, source_target_pairs={{0,30},{2,4},{4,2},{6,8},{8,6},{10,12},{12,10},{14,16},{16,14},{18... | collective-permute-start | bytes 1572872 | tf_op jit(solution)/shard_map/ppermute | solution.py:401
  6.1 0.0 collective-permute-start
  6.1 0.7 add_select_fusion
  6.8 0.1 slice.11
  6.9 0.1 fusion.1
  7.0 0.8 add_select_fusion.1.loc_ref
  7.7 0.0 copy-start
  7.8 1.0 %copy-done = bf16[128,2048]{1,0:T(8,128)(2,1)S(1)} copy-done((bf16[128,2048]{1,0:T(8,128)(2,1)S(1)}, bf16[128,2048]{1,0:T(8,128)(2,1)}, u32[]{:S(2)}) %copy-start) | copy-done | bytes 524312
  8.8 0.0 copy-start.2
  8.8 3.1 %copy-done.2 = bf16[8,7,256,256]{3,2,1,0:T(8,128)(2,1)S(1)} copy-done((bf16[8,7,256,256]{3,2,1,0:T(8,128)(2,1)S(1)}, bf16[8,7,256,256]{3,2,1,0:T(8,128)(2,1)}, u32[]{:S(2)}) %copy-start.2) | copy-done | bytes 7340056
  11.9 0.0 copy-start.1
  11.9 2.7 %shard_map.50 = (bf16[8,7,256,256]{3,2,1,0:T(8,128)(2,1)S(1)}, f32[128,2048]{1,0:T(8,128)S(1)}) custom-call(s32[8,6]{1,0:T(8,128)S(1)} %add_select_fusion.1.loc_ref, s32[1]{0:T(128)S(6)} %select_n.21.odd_ref, bf16[128,2048]{1,0:T(8,128)(2,1)S(1)} %copy-done, bf16[8,7,256,256]{3,2,1,0:T(8,128)(2,1)S(1)} %copy-done.2), custom_call_target="tpu_custom_call" | custom-call | flops 671088640 | bytes 14680064 | tf_op jit(solution)/shard_map/pallas_call | solution.py:55
  14.6 0.0 collective-permute-done.1.far_ref
  14.6 0.0 collective-permute-done.near_ref
  14.6 0.0 copy-done.1
  14.6 1.1 %shard_map.51.vec_ref.prior_ref = bf16[128,2048]{1,0:T(8,128)(2,1)S(1)} custom-call(s32[8,6]{1,0:T(8,128)S(1)} %add_select_fusion.1.loc_ref, bf16[128,2048]{1,0:T(8,128)(2,1)S(1)} %collective-permute-done.near_ref, bf16[128,2048]{1,0:T(8,128)(2,1)S(1)} %collective-permute-done.1.far_ref, f32[128,2048]{1,0:T(8,128)S(1)} %get-tuple-element.10.acc_ref, ...), custom_call_target="tpu_custom_call" | custom-call | flops 268435456 | bytes 2097152 | tf_op jit(solution)/shard_map/pallas_call | solution.py:123
  15.7 3.2 %collective-permute-start.3 = (bf16[128,2048]{1,0:T(8,128)(2,1)S(1)}, bf16[128,2048]{1,0:T(8,128)(2,1)S(1)}, u32[]{:S(2)}, u32[]{:S(2)}) collective-permute-start(bf16[128,2048]{1,0:T(8,128)(2,1)S(1)} %shard_map.51.vec_ref.prior_ref), channel_id=1, source_target_pairs={{0,30},{2,4},{4,2},{6,8},{8,6},{10,12},{12,10},{14,16},{16,14},{18... | collective-permute-start | bytes 1572872 | tf_op jit(solution)/shard_map/ppermute | solution.py:401
  18.9 0.4 collective-permute-start.2
  19.4 1.5 %shard_map.52.acc_ref = f32[128,2048]{1,0:T(8,128)S(1)} custom-call(s32[8,6]{1,0:T(8,128)S(1)} %add_select_fusion.1.loc_ref, bf16[128,2048]{1,0:T(8,128)(2,1)S(1)} %shard_map.51.vec_ref.prior_ref, bf16[8,7,256,256]{3,2,1,0:T(8,128)(2,1)S(1)} %get-tuple-element.11.turned_ref), custom_call_target="tpu_custom_call" | custom-call | flops 671088640 | bytes 5242880 | tf_op jit(solution)/shard_map/pallas_call | solution.py:88
  20.9 6.3 %collective-permute-done.3.far_ref = bf16[128,2048]{1,0:T(8,128)(2,1)S(1)} collective-permute-done((bf16[128,2048]{1,0:T(8,128)(2,1)S(1)}, bf16[128,2048]{1,0:T(8,128)(2,1)S(1)}, u32[]{:S(2)}, u32[]{:S(2)}) %collective-permute-start.3) | collective-permute-done | bytes 524320 | tf_op jit(solution)/shard_map/ppermute | solution.py:401
  27.2 0.0 collective-permute-done.2.near_ref
  27.2 1.2 %shard_map.53.vec_ref = bf16[128,2048]{1,0:T(8,128)(2,1)S(1)} custom-call(s32[8,6]{1,0:T(8,128)S(1)} %add_select_fusion.1.loc_ref, bf16[128,2048]{1,0:T(8,128)(2,1)S(1)} %collective-permute-done.2.near_ref, bf16[128,2048]{1,0:T(8,128)(2,1)S(1)} %collective-permute-done.3.far_ref, f32[128,2048]{1,0:T(8,128)S(1)} %shard_map.52.acc_ref, ...), custom_call_target="tpu_custom_call" | custom-call | flops 268435456 | bytes 2097152 | tf_op jit(solution)/shard_map/pallas_call | solution.py:123
  28.4 3.2 %collective-permute-start.5 = (bf16[128,2048]{1,0:T(8,128)(2,1)S(1)}, bf16[128,2048]{1,0:T(8,128)(2,1)S(1)}, u32[]{:S(2)}, u32[]{:S(2)}) collective-permute-start(bf16[128,2048]{1,0:T(8,128)(2,1)S(1)} %shard_map.53.vec_ref), channel_id=1, source_target_pairs={{0,30},{2,4},{4,2},{6,8},{8,6},{10,12},{12,10},{14,16},{16,14},{18... | collective-permute-start | bytes 1572872 | tf_op jit(solution)/shard_map/ppermute | solution.py:401
  31.6 5.6 %collective-permute-start.4 = (bf16[128,2048]{1,0:T(8,128)(2,1)S(1)}, bf16[128,2048]{1,0:T(8,128)(2,1)S(1)}, u32[]{:S(2)}, u32[]{:S(2)}) collective-permute-start(bf16[128,2048]{1,0:T(8,128)(2,1)S(1)} %shard_map.53.vec_ref), channel_id=1, source_target_pairs={{0,2},{2,0},{4,6},{6,4},{8,10},{10,8},{12,14},{14,12},{16,18},{18,... | collective-permute-start | bytes 1572872 | tf_op jit(solution)/shard_map/ppermute | solution.py:402
  37.3 1.5 %shard_map.54.acc_ref = f32[128,2048]{1,0:T(8,128)S(1)} custom-call(s32[8,6]{1,0:T(8,128)S(1)} %add_select_fusion.1.loc_ref, bf16[128,2048]{1,0:T(8,128)(2,1)S(1)} %shard_map.53.vec_ref, bf16[8,7,256,256]{3,2,1,0:T(8,128)(2,1)S(1)} %get-tuple-element.11.turned_ref), custom_call_target="tpu_custom_call" | custom-call | flops 671088640 | bytes 5242880 | tf_op jit(solution)/shard_map/pallas_call | solution.py:88
  38.8 1.1 %collective-permute-done.5.far_ref = bf16[128,2048]{1,0:T(8,128)(2,1)S(1)} collective-permute-done((bf16[128,2048]{1,0:T(8,128)(2,1)S(1)}, bf16[128,2048]{1,0:T(8,128)(2,1)S(1)}, u32[]{:S(2)}, u32[]{:S(2)}) %collective-permute-start.5) | collective-permute-done | bytes 524320 | tf_op jit(solution)/shard_map/ppermute | solution.py:401
  39.9 0.0 collective-permute-done.4.near_ref
  39.9 1.2 %shard_map.55 = (f32[128,2048]{1,0:T(8,128)S(1)}, bf16[128,2048]{1,0:T(8,128)(2,1)S(1)}) custom-call(s32[8,6]{1,0:T(8,128)S(1)} %add_select_fusion.1.loc_ref, bf16[128,2048]{1,0:T(8,128)(2,1)S(1)} %collective-permute-done.4.near_ref, bf16[128,2048]{1,0:T(8,128)(2,1)S(1)} %collective-permute-done.5.far_ref, f32[128,2048]{1,0:T(8,128)S(1)} %shard_map.54.acc_ref, ...), custom_call_target="tpu_custom_call" | custom-call | flops 268435456 | bytes 2097152 | tf_op jit(solution)/shard_map/pallas_call | solution.py:123
  41.1 1.6 %collective-permute-start.12 = (bf16[128,2048]{1,0:T(8,128)(2,1)S(1)}, bf16[128,2048]{1,0:T(8,128)(2,1)S(1)}, u32[]{:S(2)}, u32[]{:S(2)}) collective-permute-start(bf16[128,2048]{1,0:T(8,128)(2,1)S(1)} %get-tuple-element.13.high_ref.own_ref), channel_id=1, source_target_pairs={{0,1},{1,0},{2,3},{3,2},{4,5},{5,4},{6,7},{7,6},{8,9},{9,8},{10,11... | collective-permute-start | bytes 1572872 | tf_op jit(solution)/shard_map/ppermute | solution.py:430
  42.7 0.5 shard_map.56
  43.2 5.4 %collective-permute-start.6 = (f32[128,128]{1,0:T(8,128)S(1)}, f32[128,128]{1,0:T(8,128)S(1)}, u32[]{:S(2)}, u32[]{:S(2)}) collective-permute-start(f32[128,128]{1,0:T(8,128)S(1)} %shard_map.56), channel_id=1, source_target_pairs={{0,2},{2,0},{4,6},{6,4},{8,10},{10,8},{12,14},{14,12},{16,18},{18,... | collective-permute-start | bytes 196616 | tf_op jit(solution)/shard_map/ppermute | solution.py:417
  48.6 0.9 %collective-permute-done.6 = f32[128,128]{1,0:T(8,128)S(1)} collective-permute-done((f32[128,128]{1,0:T(8,128)S(1)}, f32[128,128]{1,0:T(8,128)S(1)}, u32[]{:S(2)}, u32[]{:S(2)}) %collective-permute-start.6) | collective-permute-done | bytes 65568 | tf_op jit(solution)/shard_map/ppermute | solution.py:417
  49.5 2.0 %collective-permute-start.9 = (f32[128,128]{1,0:T(8,128)S(1)}, f32[128,128]{1,0:T(8,128)S(1)}, u32[]{:S(2)}, u32[]{:S(2)}) collective-permute-start(f32[128,128]{1,0:T(8,128)S(1)} %add.44), channel_id=1, source_target_pairs={{0,12},{2,14},{4,8},{6,10},{8,4},{10,6},{12,0},{14,2},{16,28},{18,... | collective-permute-start | bytes 196616 | tf_op jit(solution)/shard_map/ppermute | solution.py:417
  51.5 0.4 collective-permute-start.8
  51.9 1.2 %collective-permute-start.7 = (f32[128,128]{1,0:T(8,128)S(1)}, f32[128,128]{1,0:T(8,128)S(1)}, u32[]{:S(2)}, u32[]{:S(2)}) collective-permute-start(f32[128,128]{1,0:T(8,128)S(1)} %add.44), channel_id=1, source_target_pairs={{0,4},{2,6},{4,0},{6,2},{8,12},{10,14},{12,8},{14,10},{16,20},{18,... | collective-permute-start | bytes 196616 | tf_op jit(solution)/shard_map/ppermute | solution.py:417
  53.1 2.3 %collective-permute-done.9 = f32[128,128]{1,0:T(8,128)S(1)} collective-permute-done((f32[128,128]{1,0:T(8,128)S(1)}, f32[128,128]{1,0:T(8,128)S(1)}, u32[]{:S(2)}, u32[]{:S(2)}) %collective-permute-start.9) | collective-permute-done | bytes 65568 | tf_op jit(solution)/shard_map/ppermute | solution.py:417
  55.4 0.4 collective-permute-done.8
  55.8 0.5 collective-permute-done.7
  56.3 0.0 collective-permute-done.12.other_ref.away_ref
  56.3 0.3 shard_map.57
  56.6 0.1 collective-permute-start.13
  56.7 2.6 %collective-permute-start.10 = (f32[128,128]{1,0:T(8,128)S(1)}, f32[128,128]{1,0:T(8,128)S(1)}, u32[]{:S(2)}, u32[]{:S(2)}) collective-permute-start(f32[128,128]{1,0:T(8,128)S(1)} %add_add_fusion.1.after_ref), channel_id=1, source_target_pairs={{0,16},{2,18},{4,20},{6,22},{8,24},{10,26},{12,28},{14,30},{16,0},... | collective-permute-start | bytes 196616 | tf_op jit(solution)/shard_map/ppermute | solution.py:417
  59.3 0.0 collective-permute-done.13
  59.3 2.1 %collective-permute-start.16 = (f32[128,128]{1,0:T(8,128)S(1)}, f32[128,128]{1,0:T(8,128)S(1)}, u32[]{:S(2)}, u32[]{:S(2)}) collective-permute-start(f32[128,128]{1,0:T(8,128)S(1)} %add.49), channel_id=1, source_target_pairs={{0,12},{2,14},{4,8},{6,10},{8,4},{10,6},{12,0},{14,2},{16,28},{18,... | collective-permute-start | bytes 196616 | tf_op jit(solution)/shard_map/ppermute | solution.py:417
  61.4 0.2 collective-permute-start.15
  61.6 1.2 %collective-permute-start.14 = (f32[128,128]{1,0:T(8,128)S(1)}, f32[128,128]{1,0:T(8,128)S(1)}, u32[]{:S(2)}, u32[]{:S(2)}) collective-permute-start(f32[128,128]{1,0:T(8,128)S(1)} %add.49), channel_id=1, source_target_pairs={{0,4},{2,6},{4,0},{6,2},{8,12},{10,14},{12,8},{14,10},{16,20},{18,... | collective-permute-start | bytes 196616 | tf_op jit(solution)/shard_map/ppermute | solution.py:417
  62.8 0.5 collective-permute-done.10
  63.3 1.0 %collective-permute-start.11 = (f32[128,128]{1,0:T(8,128)S(1)}, f32[128,128]{1,0:T(8,128)S(1)}, u32[]{:S(2)}, u32[]{:S(2)}) collective-permute-start(f32[128,128]{1,0:T(8,128)S(1)} %add.48.own_ref), channel_id=1, source_target_pairs={{0,1},{1,0},{2,3},{3,2},{4,5},{5,4},{6,7},{7,6},{8,9},{9,8},{10,11... | collective-permute-start | bytes 196616 | tf_op jit(solution)/shard_map/ppermute | solution.py:449
  64.4 0.8 %collective-permute-done.16 = f32[128,128]{1,0:T(8,128)S(1)} collective-permute-done((f32[128,128]{1,0:T(8,128)S(1)}, f32[128,128]{1,0:T(8,128)S(1)}, u32[]{:S(2)}, u32[]{:S(2)}) %collective-permute-start.16) | collective-permute-done | bytes 65568 | tf_op jit(solution)/shard_map/ppermute | solution.py:417
  65.2 0.5 collective-permute-done.15
  65.7 0.4 collective-permute-done.14
  66.1 1.1 %collective-permute-start.17 = (f32[128,128]{1,0:T(8,128)S(1)}, f32[128,128]{1,0:T(8,128)S(1)}, u32[]{:S(2)}, u32[]{:S(2)}) collective-permute-start(f32[128,128]{1,0:T(8,128)S(1)} %add_add_fusion.after_ref), channel_id=1, source_target_pairs={{0,16},{2,18},{4,20},{6,22},{8,24},{10,26},{12,28},{14,30},{16,0},... | collective-permute-start | bytes 196616 | tf_op jit(solution)/shard_map/ppermute | solution.py:417
  67.2 0.5 collective-permute-done.11.other_ref
  67.7 4.3 %shard_map.58 = (f32[128,128]{1,0:T(8,128)S(1)}, f32[128,128]{1,0:T(8,128)S(1)}) custom-call(s32[1]{0:T(128)} %bitcast.place_ref, f32[128,128]{1,0:T(8,128)S(1)} %add.48.own_ref, f32[128,128]{1,0:T(8,128)S(1)} %collective-permute-done.11.other_ref, f32[128,128]{1,0:T(8,128)S(1)} %add_add_fusion.after_ref), custom_call_target="tpu_custom_call" | custom-call | flops 4194304 | bytes 16777216 | tf_op jit(solution)/shard_map/pallas_call | solution.py:287
  72.0 0.0 collective-permute-done.17
  72.0 6.4 %shard_map.59 = (f32[256,256]{1,0:T(8,128)}, f32[128,2048]{1,0:T(8,128)}) custom-call(s32[1]{0:T(128)} %bitcast.place_ref, f32[128,128]{1,0:T(8,128)S(1)} %add.48.own_ref, f32[128,128]{1,0:T(8,128)S(1)} %collective-permute-done.11.other_ref, f32[128,128]{1,0:T(8,128)S(1)} %add.53.cross_ref, f32[128,128]{1,0:T(8,128)S(1)} %get-tuple-element.14.first_ref, ...), custom_call_target="tpu_custom_call" | custom-call | tf_op jit(solution)/shard_map/pallas_call | solution.py:371
  (6 shorter events, 0.1 us)
Async XLA Ops:
  0.6 14.0 %collective-permute-start.1 = (bf16[128,2048]{1,0:T(8,128)(2,1)}, bf16[128,2048]{1,0:T(8,128)(2,1)S(1)}, u32[]{:S(2)}, u32[]{:S(2)}) collective-permute-start(bf16[128,2048]{1,0:T(8,128)(2,1)} %prior_ref.3), channel_id=1, source_target_pairs={{0,30},{2,4},{4,2},{6,8},{8,6},{10,12},{12,10},{14,16},{16,14},{18... | collective-permute-start | bytes 1572872 | tf_op jit(solution)/shard_map/ppermute | solution.py:401
  6.1 8.5 %collective-permute-start = (bf16[128,2048]{1,0:T(8,128)(2,1)}, bf16[128,2048]{1,0:T(8,128)(2,1)S(1)}, u32[]{:S(2)}, u32[]{:S(2)}) collective-permute-start(bf16[128,2048]{1,0:T(8,128)(2,1)} %prior_ref.3), channel_id=1, source_target_pairs={{0,2},{2,0},{4,6},{6,4},{8,10},{10,8},{12,14},{14,12},{16,18},{18,... | collective-permute-start | bytes 1572872 | tf_op jit(solution)/shard_map/ppermute | solution.py:402
  7.7 1.0 %copy-start = (bf16[128,2048]{1,0:T(8,128)(2,1)S(1)}, bf16[128,2048]{1,0:T(8,128)(2,1)}, u32[]{:S(2)}) copy-start(bf16[128,2048]{1,0:T(8,128)(2,1)} %prior_ref.3) | copy-start | bytes 1572868
  8.8 3.1 %copy-start.2 = (bf16[8,7,256,256]{3,2,1,0:T(8,128)(2,1)S(1)}, bf16[8,7,256,256]{3,2,1,0:T(8,128)(2,1)}, u32[]{:S(2)}) copy-start(bf16[8,7,256,256]{3,2,1,0:T(8,128)(2,1)} %ham_ref.1) | copy-start | bytes 22020100
  11.9 2.8 %copy-start.1 = (bf16[128,2048]{1,0:T(8,128)(2,1)S(1)}, bf16[128,2048]{1,0:T(8,128)(2,1)}, u32[]{:S(2)}) copy-start(bf16[128,2048]{1,0:T(8,128)(2,1)} %prior_ref.3) | copy-start | bytes 1572868
  15.7 11.5 %collective-permute-start.3 = (bf16[128,2048]{1,0:T(8,128)(2,1)S(1)}, bf16[128,2048]{1,0:T(8,128)(2,1)S(1)}, u32[]{:S(2)}, u32[]{:S(2)}) collective-permute-start(bf16[128,2048]{1,0:T(8,128)(2,1)S(1)} %shard_map.51.vec_ref.prior_ref), channel_id=1, source_target_pairs={{0,30},{2,4},{4,2},{6,8},{8,6},{10,12},{12,10},{14,16},{16,14},{18... | collective-permute-start | bytes 1572872 | tf_op jit(solution)/shard_map/ppermute | solution.py:401
  18.9 8.3 %collective-permute-start.2 = (bf16[128,2048]{1,0:T(8,128)(2,1)S(1)}, bf16[128,2048]{1,0:T(8,128)(2,1)S(1)}, u32[]{:S(2)}, u32[]{:S(2)}) collective-permute-start(bf16[128,2048]{1,0:T(8,128)(2,1)S(1)} %shard_map.51.vec_ref.prior_ref), channel_id=1, source_target_pairs={{0,2},{2,0},{4,6},{6,4},{8,10},{10,8},{12,14},{14,12},{16,18},{18,... | collective-permute-start | bytes 1572872 | tf_op jit(solution)/shard_map/ppermute | solution.py:402
  28.4 11.5 %collective-permute-start.5 = (bf16[128,2048]{1,0:T(8,128)(2,1)S(1)}, bf16[128,2048]{1,0:T(8,128)(2,1)S(1)}, u32[]{:S(2)}, u32[]{:S(2)}) collective-permute-start(bf16[128,2048]{1,0:T(8,128)(2,1)S(1)} %shard_map.53.vec_ref), channel_id=1, source_target_pairs={{0,30},{2,4},{4,2},{6,8},{8,6},{10,12},{12,10},{14,16},{16,14},{18... | collective-permute-start | bytes 1572872 | tf_op jit(solution)/shard_map/ppermute | solution.py:401
  31.6 8.3 %collective-permute-start.4 = (bf16[128,2048]{1,0:T(8,128)(2,1)S(1)}, bf16[128,2048]{1,0:T(8,128)(2,1)S(1)}, u32[]{:S(2)}, u32[]{:S(2)}) collective-permute-start(bf16[128,2048]{1,0:T(8,128)(2,1)S(1)} %shard_map.53.vec_ref), channel_id=1, source_target_pairs={{0,2},{2,0},{4,6},{6,4},{8,10},{10,8},{12,14},{14,12},{16,18},{18,... | collective-permute-start | bytes 1572872 | tf_op jit(solution)/shard_map/ppermute | solution.py:402
  41.1 15.2 %collective-permute-start.12 = (bf16[128,2048]{1,0:T(8,128)(2,1)S(1)}, bf16[128,2048]{1,0:T(8,128)(2,1)S(1)}, u32[]{:S(2)}, u32[]{:S(2)}) collective-permute-start(bf16[128,2048]{1,0:T(8,128)(2,1)S(1)} %get-tuple-element.13.high_ref.own_ref), channel_id=1, source_target_pairs={{0,1},{1,0},{2,3},{3,2},{4,5},{5,4},{6,7},{7,6},{8,9},{9,8},{10,11... | collective-permute-start | bytes 1572872 | tf_op jit(solution)/shard_map/ppermute | solution.py:430
  43.2 6.3 %collective-permute-start.6 = (f32[128,128]{1,0:T(8,128)S(1)}, f32[128,128]{1,0:T(8,128)S(1)}, u32[]{:S(2)}, u32[]{:S(2)}) collective-permute-start(f32[128,128]{1,0:T(8,128)S(1)} %shard_map.56), channel_id=1, source_target_pairs={{0,2},{2,0},{4,6},{6,4},{8,10},{10,8},{12,14},{14,12},{16,18},{18,... | collective-permute-start | bytes 196616 | tf_op jit(solution)/shard_map/ppermute | solution.py:417
  49.5 5.9 %collective-permute-start.9 = (f32[128,128]{1,0:T(8,128)S(1)}, f32[128,128]{1,0:T(8,128)S(1)}, u32[]{:S(2)}, u32[]{:S(2)}) collective-permute-start(f32[128,128]{1,0:T(8,128)S(1)} %add.44), channel_id=1, source_target_pairs={{0,12},{2,14},{4,8},{6,10},{8,4},{10,6},{12,0},{14,2},{16,28},{18,... | collective-permute-start | bytes 196616 | tf_op jit(solution)/shard_map/ppermute | solution.py:417
  51.5 4.3 %collective-permute-start.8 = (f32[128,128]{1,0:T(8,128)S(1)}, f32[128,128]{1,0:T(8,128)S(1)}, u32[]{:S(2)}, u32[]{:S(2)}) collective-permute-start(f32[128,128]{1,0:T(8,128)S(1)} %add.44), channel_id=1, source_target_pairs={{0,8},{2,10},{4,12},{6,14},{8,0},{10,2},{12,4},{14,6},{16,24},{18,... | collective-permute-start | bytes 196616 | tf_op jit(solution)/shard_map/ppermute | solution.py:417
  51.9 4.3 %collective-permute-start.7 = (f32[128,128]{1,0:T(8,128)S(1)}, f32[128,128]{1,0:T(8,128)S(1)}, u32[]{:S(2)}, u32[]{:S(2)}) collective-permute-start(f32[128,128]{1,0:T(8,128)S(1)} %add.44), channel_id=1, source_target_pairs={{0,4},{2,6},{4,0},{6,2},{8,12},{10,14},{12,8},{14,10},{16,20},{18,... | collective-permute-start | bytes 196616 | tf_op jit(solution)/shard_map/ppermute | solution.py:417
  56.6 2.7 %collective-permute-start.13 = (f32[128,128]{1,0:T(8,128)S(1)}, f32[128,128]{1,0:T(8,128)S(1)}, u32[]{:S(2)}, u32[]{:S(2)}) collective-permute-start(f32[128,128]{1,0:T(8,128)S(1)} %shard_map.57), channel_id=1, source_target_pairs={{0,2},{2,0},{4,6},{6,4},{8,10},{10,8},{12,14},{14,12},{16,18},{18,... | collective-permute-start | bytes 196616 | tf_op jit(solution)/shard_map/ppermute | solution.py:417
  56.7 6.7 %collective-permute-start.10 = (f32[128,128]{1,0:T(8,128)S(1)}, f32[128,128]{1,0:T(8,128)S(1)}, u32[]{:S(2)}, u32[]{:S(2)}) collective-permute-start(f32[128,128]{1,0:T(8,128)S(1)} %add_add_fusion.1.after_ref), channel_id=1, source_target_pairs={{0,16},{2,18},{4,20},{6,22},{8,24},{10,26},{12,28},{14,30},{16,0},... | collective-permute-start | bytes 196616 | tf_op jit(solution)/shard_map/ppermute | solution.py:417
  59.3 5.9 %collective-permute-start.16 = (f32[128,128]{1,0:T(8,128)S(1)}, f32[128,128]{1,0:T(8,128)S(1)}, u32[]{:S(2)}, u32[]{:S(2)}) collective-permute-start(f32[128,128]{1,0:T(8,128)S(1)} %add.49), channel_id=1, source_target_pairs={{0,12},{2,14},{4,8},{6,10},{8,4},{10,6},{12,0},{14,2},{16,28},{18,... | collective-permute-start | bytes 196616 | tf_op jit(solution)/shard_map/ppermute | solution.py:417
  61.4 4.3 %collective-permute-start.15 = (f32[128,128]{1,0:T(8,128)S(1)}, f32[128,128]{1,0:T(8,128)S(1)}, u32[]{:S(2)}, u32[]{:S(2)}) collective-permute-start(f32[128,128]{1,0:T(8,128)S(1)} %add.49), channel_id=1, source_target_pairs={{0,8},{2,10},{4,12},{6,14},{8,0},{10,2},{12,4},{14,6},{16,24},{18,... | collective-permute-start | bytes 196616 | tf_op jit(solution)/shard_map/ppermute | solution.py:417
  61.6 4.4 %collective-permute-start.14 = (f32[128,128]{1,0:T(8,128)S(1)}, f32[128,128]{1,0:T(8,128)S(1)}, u32[]{:S(2)}, u32[]{:S(2)}) collective-permute-start(f32[128,128]{1,0:T(8,128)S(1)} %add.49), channel_id=1, source_target_pairs={{0,4},{2,6},{4,0},{6,2},{8,12},{10,14},{12,8},{14,10},{16,20},{18,... | collective-permute-start | bytes 196616 | tf_op jit(solution)/shard_map/ppermute | solution.py:417
  63.3 4.3 %collective-permute-start.11 = (f32[128,128]{1,0:T(8,128)S(1)}, f32[128,128]{1,0:T(8,128)S(1)}, u32[]{:S(2)}, u32[]{:S(2)}) collective-permute-start(f32[128,128]{1,0:T(8,128)S(1)} %add.48.own_ref), channel_id=1, source_target_pairs={{0,1},{1,0},{2,3},{3,2},{4,5},{5,4},{6,7},{7,6},{8,9},{9,8},{10,11... | collective-permute-start | bytes 196616 | tf_op jit(solution)/shard_map/ppermute | solution.py:449
  66.1 5.9 %collective-permute-start.17 = (f32[128,128]{1,0:T(8,128)S(1)}, f32[128,128]{1,0:T(8,128)S(1)}, u32[]{:S(2)}, u32[]{:S(2)}) collective-permute-start(f32[128,128]{1,0:T(8,128)S(1)} %add_add_fusion.after_ref), channel_id=1, source_target_pairs={{0,16},{2,18},{4,20},{6,22},{8,24},{10,26},{12,28},{14,30},{16,0},... | collective-permute-start | bytes 196616 | tf_op jit(solution)/shard_map/ppermute | solution.py:417

commit v12 on v11

--- a/solution.py
+++ b/solution.py
@@ -326,27 +326,27 @@
     def dot(a, b):
         return jnp.dot(a, b, preferred_element_type=jnp.float32)
 
-    lower = dot_full(cross_ref[...], first_inv_ref[...], ((1,), (1,)))
-    update = dot_full(lower, lower, ((1,), (1,)))
+    def product(inverse, high, low):
+        high_inv, low_inv = split(inverse)
+        stacked = jnp.concatenate([high_inv, high_inv], axis=1)
+        return dot(stacked, jnp.concatenate([high, low], axis=0)) + dot(low_inv, high)
 
     @pl.when(leading)
     def _():
-        work[...] = other_ref[...] - update
-        high_inv, low_inv = split(first_inv_ref[...])
         for copy, here in zip(copies, spans):
             high = high_ref[:, here]
             low = (wide_ref[:, here] - high.astype(jnp.float32)).astype(jnp.bfloat16)
-            result[:, here] = dot(high_inv, high) + (dot(high_inv, low) + dot(low_inv, high))
+            result[:, here] = product(first_inv_ref[...], high, low)
             copy.start()
 
-    @pl.when(trailing)
-    def _():
-        work[...] = own_ref[...] - update
-        high_mix, low_mix = split(dot_full(lower, first_inv_ref[...]))
-        for here in spans:
-            away = away_ref[:, here]
-            part[:, here] = wide_ref[:, here] - (dot(high_mix, away) + dot(low_mix, away))
-
+    lower = dot_full(cross_ref[...], first_inv_ref[...], ((1,), (1,)))
+    rest = jnp.where(leading, other_ref[...], own_ref[...])
+    work[...] = rest - dot_full(lower, lower, ((1,), (1,)))
+    high_mix, low_mix = split(dot_full(lower, first_inv_ref[...]))
+    mixes = jnp.concatenate([high_mix, low_mix], axis=1)
+    for here in spans:
+        away = away_ref[:, here]
+        part[:, here] = wide_ref[:, here] - dot(mixes, jnp.concatenate([away, away], axis=0))
     upper_ref[0:half, 0:half] = first_ref[...]
     upper_ref[0:half, half:] = lower.T
     upper_ref[half:, 0:half] = jnp.zeros((half, half), jnp.float32)
@@ -354,10 +354,8 @@
 
     @pl.when(trailing)
     def _():
-        high_inv, low_inv = split(inverse[...])
         for copy, here in zip(copies, spans):
-            high, low = split(part[:, here])
-            result[:, here] = dot(high_inv, high) + (dot(high_inv, low) + dot(low_inv, high))
+            result[:, here] = product(inverse[...], *split(part[:, here]))
             copy.start()
 
     for copy in copies:
@@ -437,7 +435,7 @@
             out_specs=pl.BlockSpec(memory_space=pltpu.VMEM),
             compiler_params=params,
         )(filtered, narrow)
-        near = summed(near, stages[:-1])
+        near = summed(near, stages[:1])
         cross = pl.pallas_call(
             cross_gram_kernel,
             out_shape=tile,
@@ -445,7 +443,7 @@
             out_specs=pl.BlockSpec(memory_space=pltpu.VMEM),
             compiler_params=params,
         )(place, narrow, other, near)
-        near = summed(near, stages[-1:])
+        near = summed(near, stages[1:])
         far = lax.ppermute(near, "orb", swap)
         cross = summed(cross, stages[:-1])
         first, first_inv = factor_first(place, near, far, cross)

time: 78.9 us -> 78.7 us (level)
  waiting for transfers between devices: 14.2 us -> 10.7 us
  starting transfers between devices: 36.9 us -> 39.9 us
    ppermute x10, waiting for transfers between devices: 6.22 us -> 2.49 us  [moved(): return lax.ppermute(part, 'space', [(i, i ^ step) for i in range(blocks)])]
    ppermute x10, starting transfers between devices: 16.3 us -> 18.9 us  [moved(): return lax.ppermute(part, 'space', [(i, i ^ step) for i in range(blocks)])]
  transfers between devices with their start and end apart: 18 -> 18, of which waited for: 11 -> 8; matrix products, arithmetic and copies ran while one was open for 2% -> 2% of each run, Pallas kernels for 13% -> 14%
where the time goes in v12:
time: 78.7 us; the launch traced here: 78.4 us
  starting transfers between devices  39.9 us (51%)
  Pallas kernels  21.1 us (27%)
  waiting for transfers between devices  10.7 us (14%)
  local copies, waits for them, and re-layouts  4.27 us (5%)
  other arithmetic  1.53 us (2%)
  between operations  0.93 us (1%)
    ppermute x10, starting transfers between devices, moved(): return lax.ppermute(part, 'space', [(i, i ^ step) for i in range(blocks)])  18.9 us
    ppermute x3, starting transfers between devices, halo(): far = lax.ppermute(vec, 'space', far_pairs)  11.9 us
    ppermute x3, waiting for transfers between devices, halo(): far = lax.ppermute(vec, 'space', far_pairs)  7.41 us
    pallas_call x1, Pallas kernels, finish(): pl.pallas_call(finish_kernel, out_shape=[jax.ShapeDtypeStruct((2 * half,...  6.73 us
    ppermute x3, starting transfers between devices, halo(): return (lax.ppermute(vec, 'space', near_pairs), far)  6.12 us
    pallas_call x1, Pallas kernels, factor_first(): pl.pallas_call(first_kernel, out_shape=[jax.ShapeDtypeStruct((half, half)...  4.29 us
    unnamed x6, local copies, waits for them, and re-layouts  4.13 us
    pallas_call x3, Pallas kernels, halo_part(): pl.pallas_call(functools.partial(halo_kernel, level), out_shape=[jax.Shap...  3.5 us
  transfers between devices with their start and end apart: 18, of which 8 were waited for; matrix products, arithmetic and copies ran while one was open for 2% of the time, Pallas kernels for 14%

profile of v12, /device:TPU:0, one launch (start us, length us, event | category | flops | bytes accessed | tf_op | source)
XLA Modules:
  0.0 78.4 jit_solution(6808763489368833024)
XLA Ops:
  0.6 5.5 %collective-permute-start.1 = (bf16[128,2048]{1,0:T(8,128)(2,1)}, bf16[128,2048]{1,0:T(8,128)(2,1)S(1)}, u32[]{:S(2)}, u32[]{:S(2)}) collective-permute-start(bf16[128,2048]{1,0:T(8,128)(2,1)} %prior_ref.3), channel_id=1, source_target_pairs={{0,30},{2,4},{4,2},{6,8},{8,6},{10,12},{12,10},{14,16},{16,14},{18... | collective-permute-start | bytes 1572872 | tf_op jit(solution)/shard_map/ppermute | solution.py:399
  6.1 0.0 collective-permute-start
  6.1 0.7 add_select_fusion
  6.8 0.1 slice.11
  6.9 0.1 fusion.1
  7.0 0.8 add_select_fusion.1.loc_ref
  7.7 0.0 copy-start
  7.8 1.0 %copy-done = bf16[128,2048]{1,0:T(8,128)(2,1)S(1)} copy-done((bf16[128,2048]{1,0:T(8,128)(2,1)S(1)}, bf16[128,2048]{1,0:T(8,128)(2,1)}, u32[]{:S(2)}) %copy-start) | copy-done | bytes 524312
  8.8 0.0 copy-start.2
  8.8 3.1 %copy-done.2 = bf16[8,7,256,256]{3,2,1,0:T(8,128)(2,1)S(1)} copy-done((bf16[8,7,256,256]{3,2,1,0:T(8,128)(2,1)S(1)}, bf16[8,7,256,256]{3,2,1,0:T(8,128)(2,1)}, u32[]{:S(2)}) %copy-start.2) | copy-done | bytes 7340056
  11.9 0.0 copy-start.1
  11.9 2.7 %shard_map.50 = (bf16[8,7,256,256]{3,2,1,0:T(8,128)(2,1)S(1)}, f32[128,2048]{1,0:T(8,128)S(1)}) custom-call(s32[8,6]{1,0:T(8,128)S(1)} %add_select_fusion.1.loc_ref, s32[1]{0:T(128)S(6)} %select_n.21.odd_ref, bf16[128,2048]{1,0:T(8,128)(2,1)S(1)} %copy-done, bf16[8,7,256,256]{3,2,1,0:T(8,128)(2,1)S(1)} %copy-done.2), custom_call_target="tpu_custom_call" | custom-call | flops 671088640 | bytes 14680064 | tf_op jit(solution)/shard_map/pallas_call | solution.py:55
  14.6 0.0 collective-permute-done.1.far_ref
  14.6 0.0 collective-permute-done.near_ref
  14.6 0.0 copy-done.1
  14.6 1.1 %shard_map.51.vec_ref.prior_ref = bf16[128,2048]{1,0:T(8,128)(2,1)S(1)} custom-call(s32[8,6]{1,0:T(8,128)S(1)} %add_select_fusion.1.loc_ref, bf16[128,2048]{1,0:T(8,128)(2,1)S(1)} %collective-permute-done.near_ref, bf16[128,2048]{1,0:T(8,128)(2,1)S(1)} %collective-permute-done.1.far_ref, f32[128,2048]{1,0:T(8,128)S(1)} %get-tuple-element.10.acc_ref, ...), custom_call_target="tpu_custom_call" | custom-call | flops 268435456 | bytes 2097152 | tf_op jit(solution)/shard_map/pallas_call | solution.py:123
  15.7 3.2 %collective-permute-start.3 = (bf16[128,2048]{1,0:T(8,128)(2,1)S(1)}, bf16[128,2048]{1,0:T(8,128)(2,1)S(1)}, u32[]{:S(2)}, u32[]{:S(2)}) collective-permute-start(bf16[128,2048]{1,0:T(8,128)(2,1)S(1)} %shard_map.51.vec_ref.prior_ref), channel_id=1, source_target_pairs={{0,30},{2,4},{4,2},{6,8},{8,6},{10,12},{12,10},{14,16},{16,14},{18... | collective-permute-start | bytes 1572872 | tf_op jit(solution)/shard_map/ppermute | solution.py:399
  18.9 0.4 collective-permute-start.2
  19.4 1.5 %shard_map.52.acc_ref = f32[128,2048]{1,0:T(8,128)S(1)} custom-call(s32[8,6]{1,0:T(8,128)S(1)} %add_select_fusion.1.loc_ref, bf16[128,2048]{1,0:T(8,128)(2,1)S(1)} %shard_map.51.vec_ref.prior_ref, bf16[8,7,256,256]{3,2,1,0:T(8,128)(2,1)S(1)} %get-tuple-element.11.turned_ref), custom_call_target="tpu_custom_call" | custom-call | flops 671088640 | bytes 5242880 | tf_op jit(solution)/shard_map/pallas_call | solution.py:88
  20.9 6.3 %collective-permute-done.3.far_ref = bf16[128,2048]{1,0:T(8,128)(2,1)S(1)} collective-permute-done((bf16[128,2048]{1,0:T(8,128)(2,1)S(1)}, bf16[128,2048]{1,0:T(8,128)(2,1)S(1)}, u32[]{:S(2)}, u32[]{:S(2)}) %collective-permute-start.3) | collective-permute-done | bytes 524320 | tf_op jit(solution)/shard_map/ppermute | solution.py:399
  27.2 0.0 collective-permute-done.2.near_ref
  27.2 1.2 %shard_map.53.vec_ref = bf16[128,2048]{1,0:T(8,128)(2,1)S(1)} custom-call(s32[8,6]{1,0:T(8,128)S(1)} %add_select_fusion.1.loc_ref, bf16[128,2048]{1,0:T(8,128)(2,1)S(1)} %collective-permute-done.2.near_ref, bf16[128,2048]{1,0:T(8,128)(2,1)S(1)} %collective-permute-done.3.far_ref, f32[128,2048]{1,0:T(8,128)S(1)} %shard_map.52.acc_ref, ...), custom_call_target="tpu_custom_call" | custom-call | flops 268435456 | bytes 2097152 | tf_op jit(solution)/shard_map/pallas_call | solution.py:123
  28.4 3.2 %collective-permute-start.5 = (bf16[128,2048]{1,0:T(8,128)(2,1)S(1)}, bf16[128,2048]{1,0:T(8,128)(2,1)S(1)}, u32[]{:S(2)}, u32[]{:S(2)}) collective-permute-start(bf16[128,2048]{1,0:T(8,128)(2,1)S(1)} %shard_map.53.vec_ref), channel_id=1, source_target_pairs={{0,30},{2,4},{4,2},{6,8},{8,6},{10,12},{12,10},{14,16},{16,14},{18... | collective-permute-start | bytes 1572872 | tf_op jit(solution)/shard_map/ppermute | solution.py:399
  31.6 5.7 %collective-permute-start.4 = (bf16[128,2048]{1,0:T(8,128)(2,1)S(1)}, bf16[128,2048]{1,0:T(8,128)(2,1)S(1)}, u32[]{:S(2)}, u32[]{:S(2)}) collective-permute-start(bf16[128,2048]{1,0:T(8,128)(2,1)S(1)} %shard_map.53.vec_ref), channel_id=1, source_target_pairs={{0,2},{2,0},{4,6},{6,4},{8,10},{10,8},{12,14},{14,12},{16,18},{18,... | collective-permute-start | bytes 1572872 | tf_op jit(solution)/shard_map/ppermute | solution.py:400
  37.3 1.5 %shard_map.54.acc_ref = f32[128,2048]{1,0:T(8,128)S(1)} custom-call(s32[8,6]{1,0:T(8,128)S(1)} %add_select_fusion.1.loc_ref, bf16[128,2048]{1,0:T(8,128)(2,1)S(1)} %shard_map.53.vec_ref, bf16[8,7,256,256]{3,2,1,0:T(8,128)(2,1)S(1)} %get-tuple-element.11.turned_ref), custom_call_target="tpu_custom_call" | custom-call | flops 671088640 | bytes 5242880 | tf_op jit(solution)/shard_map/pallas_call | solution.py:88
  38.8 1.1 %collective-permute-done.5.far_ref = bf16[128,2048]{1,0:T(8,128)(2,1)S(1)} collective-permute-done((bf16[128,2048]{1,0:T(8,128)(2,1)S(1)}, bf16[128,2048]{1,0:T(8,128)(2,1)S(1)}, u32[]{:S(2)}, u32[]{:S(2)}) %collective-permute-start.5) | collective-permute-done | bytes 524320 | tf_op jit(solution)/shard_map/ppermute | solution.py:399
  39.9 0.0 collective-permute-done.4.near_ref
  39.9 1.2 %shard_map.55 = (f32[128,2048]{1,0:T(8,128)S(1)}, bf16[128,2048]{1,0:T(8,128)(2,1)S(1)}) custom-call(s32[8,6]{1,0:T(8,128)S(1)} %add_select_fusion.1.loc_ref, bf16[128,2048]{1,0:T(8,128)(2,1)S(1)} %collective-permute-done.4.near_ref, bf16[128,2048]{1,0:T(8,128)(2,1)S(1)} %collective-permute-done.5.far_ref, f32[128,2048]{1,0:T(8,128)S(1)} %shard_map.54.acc_ref, ...), custom_call_target="tpu_custom_call" | custom-call | flops 268435456 | bytes 2097152 | tf_op jit(solution)/shard_map/pallas_call | solution.py:123
  41.1 1.6 %collective-permute-start.12 = (bf16[128,2048]{1,0:T(8,128)(2,1)S(1)}, bf16[128,2048]{1,0:T(8,128)(2,1)S(1)}, u32[]{:S(2)}, u32[]{:S(2)}) collective-permute-start(bf16[128,2048]{1,0:T(8,128)(2,1)S(1)} %get-tuple-element.13.high_ref.own_ref), channel_id=1, source_target_pairs={{0,1},{1,0},{2,3},{3,2},{4,5},{5,4},{6,7},{7,6},{8,9},{9,8},{10,11... | collective-permute-start | bytes 1572872 | tf_op jit(solution)/shard_map/ppermute | solution.py:428
  42.7 0.5 shard_map.56
  43.2 5.4 %collective-permute-start.6 = (f32[128,128]{1,0:T(8,128)S(1)}, f32[128,128]{1,0:T(8,128)S(1)}, u32[]{:S(2)}, u32[]{:S(2)}) collective-permute-start(f32[128,128]{1,0:T(8,128)S(1)} %shard_map.56), channel_id=1, source_target_pairs={{0,2},{2,0},{4,6},{6,4},{8,10},{10,8},{12,14},{14,12},{16,18},{18,... | collective-permute-start | bytes 196616 | tf_op jit(solution)/shard_map/ppermute | solution.py:415
  48.6 0.9 %collective-permute-done.6 = f32[128,128]{1,0:T(8,128)S(1)} collective-permute-done((f32[128,128]{1,0:T(8,128)S(1)}, f32[128,128]{1,0:T(8,128)S(1)}, u32[]{:S(2)}, u32[]{:S(2)}) %collective-permute-start.6) | collective-permute-done | bytes 65568 | tf_op jit(solution)/shard_map/ppermute | solution.py:415
  49.5 1.9 %collective-permute-start.9 = (f32[128,128]{1,0:T(8,128)S(1)}, f32[128,128]{1,0:T(8,128)S(1)}, u32[]{:S(2)}, u32[]{:S(2)}) collective-permute-start(f32[128,128]{1,0:T(8,128)S(1)} %add.44.after_ref), channel_id=1, source_target_pairs={{0,12},{2,14},{4,8},{6,10},{8,4},{10,6},{12,0},{14,2},{16,28},{18,... | collective-permute-start | bytes 196616 | tf_op jit(solution)/shard_map/ppermute | solution.py:415
  51.5 0.5 collective-permute-start.8
  51.9 1.1 %collective-permute-start.7 = (f32[128,128]{1,0:T(8,128)S(1)}, f32[128,128]{1,0:T(8,128)S(1)}, u32[]{:S(2)}, u32[]{:S(2)}) collective-permute-start(f32[128,128]{1,0:T(8,128)S(1)} %add.44.after_ref), channel_id=1, source_target_pairs={{0,4},{2,6},{4,0},{6,2},{8,12},{10,14},{12,8},{14,10},{16,20},{18,... | collective-permute-start | bytes 196616 | tf_op jit(solution)/shard_map/ppermute | solution.py:415
  53.1 0.0 collective-permute-done.12.other_ref.away_ref
  53.1 0.3 shard_map.57
  53.4 3.1 %collective-permute-start.13 = (f32[128,128]{1,0:T(8,128)S(1)}, f32[128,128]{1,0:T(8,128)S(1)}, u32[]{:S(2)}, u32[]{:S(2)}) collective-permute-start(f32[128,128]{1,0:T(8,128)S(1)} %shard_map.57), channel_id=1, source_target_pairs={{0,2},{2,0},{4,6},{6,4},{8,10},{10,8},{12,14},{14,12},{16,18},{18,... | collective-permute-start | bytes 196616 | tf_op jit(solution)/shard_map/ppermute | solution.py:415
  56.5 0.0 collective-permute-done.9
  56.5 0.0 collective-permute-done.8
  56.5 0.0 collective-permute-done.7
  56.5 2.4 %collective-permute-start.10 = (f32[128,128]{1,0:T(8,128)S(1)}, f32[128,128]{1,0:T(8,128)S(1)}, u32[]{:S(2)}, u32[]{:S(2)}) collective-permute-start(f32[128,128]{1,0:T(8,128)S(1)} %add_add_fusion.1), channel_id=1, source_target_pairs={{0,16},{2,18},{4,20},{6,22},{8,24},{10,26},{12,28},{14,30},{16,0},... | collective-permute-start | bytes 196616 | tf_op jit(solution)/shard_map/ppermute | solution.py:415
  58.9 0.0 collective-permute-done.13
  58.9 2.1 %collective-permute-start.16 = (f32[128,128]{1,0:T(8,128)S(1)}, f32[128,128]{1,0:T(8,128)S(1)}, u32[]{:S(2)}, u32[]{:S(2)}) collective-permute-start(f32[128,128]{1,0:T(8,128)S(1)} %add.49), channel_id=1, source_target_pairs={{0,12},{2,14},{4,8},{6,10},{8,4},{10,6},{12,0},{14,2},{16,28},{18,... | collective-permute-start | bytes 196616 | tf_op jit(solution)/shard_map/ppermute | solution.py:415
  61.0 0.2 collective-permute-start.15
  61.2 1.2 %collective-permute-start.14 = (f32[128,128]{1,0:T(8,128)S(1)}, f32[128,128]{1,0:T(8,128)S(1)}, u32[]{:S(2)}, u32[]{:S(2)}) collective-permute-start(f32[128,128]{1,0:T(8,128)S(1)} %add.49), channel_id=1, source_target_pairs={{0,4},{2,6},{4,0},{6,2},{8,12},{10,14},{12,8},{14,10},{16,20},{18,... | collective-permute-start | bytes 196616 | tf_op jit(solution)/shard_map/ppermute | solution.py:415
  62.4 0.4 collective-permute-done.10
  62.8 1.4 %collective-permute-start.11 = (f32[128,128]{1,0:T(8,128)S(1)}, f32[128,128]{1,0:T(8,128)S(1)}, u32[]{:S(2)}, u32[]{:S(2)}) collective-permute-start(f32[128,128]{1,0:T(8,128)S(1)} %add.48.own_ref), channel_id=1, source_target_pairs={{0,1},{1,0},{2,3},{3,2},{4,5},{5,4},{6,7},{7,6},{8,9},{9,8},{10,11... | collective-permute-start | bytes 196616 | tf_op jit(solution)/shard_map/ppermute | solution.py:447
  64.3 0.2 collective-permute-done.16
  64.5 0.8 %collective-permute-done.15 = f32[128,128]{1,0:T(8,128)S(1)} collective-permute-done((f32[128,128]{1,0:T(8,128)S(1)}, f32[128,128]{1,0:T(8,128)S(1)}, u32[]{:S(2)}, u32[]{:S(2)}) %collective-permute-start.15) | collective-permute-done | bytes 65568 | tf_op jit(solution)/shard_map/ppermute | solution.py:415
  65.2 0.2 collective-permute-done.14
  65.5 0.9 %collective-permute-start.17 = (f32[128,128]{1,0:T(8,128)S(1)}, f32[128,128]{1,0:T(8,128)S(1)}, u32[]{:S(2)}, u32[]{:S(2)}) collective-permute-start(f32[128,128]{1,0:T(8,128)S(1)} %add_add_fusion.after_ref), channel_id=1, source_target_pairs={{0,16},{2,18},{4,20},{6,22},{8,24},{10,26},{12,28},{14,30},{16,0},... | collective-permute-start | bytes 196616 | tf_op jit(solution)/shard_map/ppermute | solution.py:415
  66.4 0.8 collective-permute-done.11.other_ref
  67.2 4.3 %shard_map.58 = (f32[128,128]{1,0:T(8,128)S(1)}, f32[128,128]{1,0:T(8,128)S(1)}) custom-call(s32[1]{0:T(128)} %bitcast.place_ref, f32[128,128]{1,0:T(8,128)S(1)} %add.48.own_ref, f32[128,128]{1,0:T(8,128)S(1)} %collective-permute-done.11.other_ref, f32[128,128]{1,0:T(8,128)S(1)} %add_add_fusion.after_ref), custom_call_target="tpu_custom_call" | custom-call | flops 4194304 | bytes 16777216 | tf_op jit(solution)/shard_map/pallas_call | solution.py:287
  71.5 0.0 collective-permute-done.17
  71.5 6.7 %shard_map.59 = (f32[256,256]{1,0:T(8,128)}, f32[128,2048]{1,0:T(8,128)}) custom-call(s32[1]{0:T(128)} %bitcast.place_ref, f32[128,128]{1,0:T(8,128)S(1)} %add.48.own_ref, f32[128,128]{1,0:T(8,128)S(1)} %collective-permute-done.11.other_ref, f32[128,128]{1,0:T(8,128)S(1)} %add.53.cross_ref, f32[128,128]{1,0:T(8,128)S(1)} %get-tuple-element.14.first_ref, ...), custom_call_target="tpu_custom_call" | custom-call | tf_op jit(solution)/shard_map/pallas_call | solution.py:369
  (6 shorter events, 0.1 us)
Async XLA Ops:
  0.6 14.0 %collective-permute-start.1 = (bf16[128,2048]{1,0:T(8,128)(2,1)}, bf16[128,2048]{1,0:T(8,128)(2,1)S(1)}, u32[]{:S(2)}, u32[]{:S(2)}) collective-permute-start(bf16[128,2048]{1,0:T(8,128)(2,1)} %prior_ref.3), channel_id=1, source_target_pairs={{0,30},{2,4},{4,2},{6,8},{8,6},{10,12},{12,10},{14,16},{16,14},{18... | collective-permute-start | bytes 1572872 | tf_op jit(solution)/shard_map/ppermute | solution.py:399
  6.1 8.5 %collective-permute-start = (bf16[128,2048]{1,0:T(8,128)(2,1)}, bf16[128,2048]{1,0:T(8,128)(2,1)S(1)}, u32[]{:S(2)}, u32[]{:S(2)}) collective-permute-start(bf16[128,2048]{1,0:T(8,128)(2,1)} %prior_ref.3), channel_id=1, source_target_pairs={{0,2},{2,0},{4,6},{6,4},{8,10},{10,8},{12,14},{14,12},{16,18},{18,... | collective-permute-start | bytes 1572872 | tf_op jit(solution)/shard_map/ppermute | solution.py:400
  7.7 1.0 %copy-start = (bf16[128,2048]{1,0:T(8,128)(2,1)S(1)}, bf16[128,2048]{1,0:T(8,128)(2,1)}, u32[]{:S(2)}) copy-start(bf16[128,2048]{1,0:T(8,128)(2,1)} %prior_ref.3) | copy-start | bytes 1572868
  8.8 3.1 %copy-start.2 = (bf16[8,7,256,256]{3,2,1,0:T(8,128)(2,1)S(1)}, bf16[8,7,256,256]{3,2,1,0:T(8,128)(2,1)}, u32[]{:S(2)}) copy-start(bf16[8,7,256,256]{3,2,1,0:T(8,128)(2,1)} %ham_ref.1) | copy-start | bytes 22020100
  11.9 2.8 %copy-start.1 = (bf16[128,2048]{1,0:T(8,128)(2,1)S(1)}, bf16[128,2048]{1,0:T(8,128)(2,1)}, u32[]{:S(2)}) copy-start(bf16[128,2048]{1,0:T(8,128)(2,1)} %prior_ref.3) | copy-start | bytes 1572868
  15.7 11.5 %collective-permute-start.3 = (bf16[128,2048]{1,0:T(8,128)(2,1)S(1)}, bf16[128,2048]{1,0:T(8,128)(2,1)S(1)}, u32[]{:S(2)}, u32[]{:S(2)}) collective-permute-start(bf16[128,2048]{1,0:T(8,128)(2,1)S(1)} %shard_map.51.vec_ref.prior_ref), channel_id=1, source_target_pairs={{0,30},{2,4},{4,2},{6,8},{8,6},{10,12},{12,10},{14,16},{16,14},{18... | collective-permute-start | bytes 1572872 | tf_op jit(solution)/shard_map/ppermute | solution.py:399
  18.9 8.3 %collective-permute-start.2 = (bf16[128,2048]{1,0:T(8,128)(2,1)S(1)}, bf16[128,2048]{1,0:T(8,128)(2,1)S(1)}, u32[]{:S(2)}, u32[]{:S(2)}) collective-permute-start(bf16[128,2048]{1,0:T(8,128)(2,1)S(1)} %shard_map.51.vec_ref.prior_ref), channel_id=1, source_target_pairs={{0,2},{2,0},{4,6},{6,4},{8,10},{10,8},{12,14},{14,12},{16,18},{18,... | collective-permute-start | bytes 1572872 | tf_op jit(solution)/shard_map/ppermute | solution.py:400
  28.4 11.5 %collective-permute-start.5 = (bf16[128,2048]{1,0:T(8,128)(2,1)S(1)}, bf16[128,2048]{1,0:T(8,128)(2,1)S(1)}, u32[]{:S(2)}, u32[]{:S(2)}) collective-permute-start(bf16[128,2048]{1,0:T(8,128)(2,1)S(1)} %shard_map.53.vec_ref), channel_id=1, source_target_pairs={{0,30},{2,4},{4,2},{6,8},{8,6},{10,12},{12,10},{14,16},{16,14},{18... | collective-permute-start | bytes 1572872 | tf_op jit(solution)/shard_map/ppermute | solution.py:399
  31.6 8.3 %collective-permute-start.4 = (bf16[128,2048]{1,0:T(8,128)(2,1)S(1)}, bf16[128,2048]{1,0:T(8,128)(2,1)S(1)}, u32[]{:S(2)}, u32[]{:S(2)}) collective-permute-start(bf16[128,2048]{1,0:T(8,128)(2,1)S(1)} %shard_map.53.vec_ref), channel_id=1, source_target_pairs={{0,2},{2,0},{4,6},{6,4},{8,10},{10,8},{12,14},{14,12},{16,18},{18,... | collective-permute-start | bytes 1572872 | tf_op jit(solution)/shard_map/ppermute | solution.py:400
  41.1 12.0 %collective-permute-start.12 = (bf16[128,2048]{1,0:T(8,128)(2,1)S(1)}, bf16[128,2048]{1,0:T(8,128)(2,1)S(1)}, u32[]{:S(2)}, u32[]{:S(2)}) collective-permute-start(bf16[128,2048]{1,0:T(8,128)(2,1)S(1)} %get-tuple-element.13.high_ref.own_ref), channel_id=1, source_target_pairs={{0,1},{1,0},{2,3},{3,2},{4,5},{5,4},{6,7},{7,6},{8,9},{9,8},{10,11... | collective-permute-start | bytes 1572872 | tf_op jit(solution)/shard_map/ppermute | solution.py:428
  43.2 6.3 %collective-permute-start.6 = (f32[128,128]{1,0:T(8,128)S(1)}, f32[128,128]{1,0:T(8,128)S(1)}, u32[]{:S(2)}, u32[]{:S(2)}) collective-permute-start(f32[128,128]{1,0:T(8,128)S(1)} %shard_map.56), channel_id=1, source_target_pairs={{0,2},{2,0},{4,6},{6,4},{8,10},{10,8},{12,14},{14,12},{16,18},{18,... | collective-permute-start | bytes 196616 | tf_op jit(solution)/shard_map/ppermute | solution.py:415
  49.5 7.0 %collective-permute-start.9 = (f32[128,128]{1,0:T(8,128)S(1)}, f32[128,128]{1,0:T(8,128)S(1)}, u32[]{:S(2)}, u32[]{:S(2)}) collective-permute-start(f32[128,128]{1,0:T(8,128)S(1)} %add.44.after_ref), channel_id=1, source_target_pairs={{0,12},{2,14},{4,8},{6,10},{8,4},{10,6},{12,0},{14,2},{16,28},{18,... | collective-permute-start | bytes 196616 | tf_op jit(solution)/shard_map/ppermute | solution.py:415
  51.5 5.0 %collective-permute-start.8 = (f32[128,128]{1,0:T(8,128)S(1)}, f32[128,128]{1,0:T(8,128)S(1)}, u32[]{:S(2)}, u32[]{:S(2)}) collective-permute-start(f32[128,128]{1,0:T(8,128)S(1)} %add.44.after_ref), channel_id=1, source_target_pairs={{0,8},{2,10},{4,12},{6,14},{8,0},{10,2},{12,4},{14,6},{16,24},{18,... | collective-permute-start | bytes 196616 | tf_op jit(solution)/shard_map/ppermute | solution.py:415
  51.9 4.5 %collective-permute-start.7 = (f32[128,128]{1,0:T(8,128)S(1)}, f32[128,128]{1,0:T(8,128)S(1)}, u32[]{:S(2)}, u32[]{:S(2)}) collective-permute-start(f32[128,128]{1,0:T(8,128)S(1)} %add.44.after_ref), channel_id=1, source_target_pairs={{0,4},{2,6},{4,0},{6,2},{8,12},{10,14},{12,8},{14,10},{16,20},{18,... | collective-permute-start | bytes 196616 | tf_op jit(solution)/shard_map/ppermute | solution.py:415
  53.4 5.5 %collective-permute-start.13 = (f32[128,128]{1,0:T(8,128)S(1)}, f32[128,128]{1,0:T(8,128)S(1)}, u32[]{:S(2)}, u32[]{:S(2)}) collective-permute-start(f32[128,128]{1,0:T(8,128)S(1)} %shard_map.57), channel_id=1, source_target_pairs={{0,2},{2,0},{4,6},{6,4},{8,10},{10,8},{12,14},{14,12},{16,18},{18,... | collective-permute-start | bytes 196616 | tf_op jit(solution)/shard_map/ppermute | solution.py:415
  56.5 6.3 %collective-permute-start.10 = (f32[128,128]{1,0:T(8,128)S(1)}, f32[128,128]{1,0:T(8,128)S(1)}, u32[]{:S(2)}, u32[]{:S(2)}) collective-permute-start(f32[128,128]{1,0:T(8,128)S(1)} %add_add_fusion.1), channel_id=1, source_target_pairs={{0,16},{2,18},{4,20},{6,22},{8,24},{10,26},{12,28},{14,30},{16,0},... | collective-permute-start | bytes 196616 | tf_op jit(solution)/shard_map/ppermute | solution.py:415
  58.9 5.6 %collective-permute-start.16 = (f32[128,128]{1,0:T(8,128)S(1)}, f32[128,128]{1,0:T(8,128)S(1)}, u32[]{:S(2)}, u32[]{:S(2)}) collective-permute-start(f32[128,128]{1,0:T(8,128)S(1)} %add.49), channel_id=1, source_target_pairs={{0,12},{2,14},{4,8},{6,10},{8,4},{10,6},{12,0},{14,2},{16,28},{18,... | collective-permute-start | bytes 196616 | tf_op jit(solution)/shard_map/ppermute | solution.py:415
  61.0 4.3 %collective-permute-start.15 = (f32[128,128]{1,0:T(8,128)S(1)}, f32[128,128]{1,0:T(8,128)S(1)}, u32[]{:S(2)}, u32[]{:S(2)}) collective-permute-start(f32[128,128]{1,0:T(8,128)S(1)} %add.49), channel_id=1, source_target_pairs={{0,8},{2,10},{4,12},{6,14},{8,0},{10,2},{12,4},{14,6},{16,24},{18,... | collective-permute-start | bytes 196616 | tf_op jit(solution)/shard_map/ppermute | solution.py:415
  61.2 4.3 %collective-permute-start.14 = (f32[128,128]{1,0:T(8,128)S(1)}, f32[128,128]{1,0:T(8,128)S(1)}, u32[]{:S(2)}, u32[]{:S(2)}) collective-permute-start(f32[128,128]{1,0:T(8,128)S(1)} %add.49), channel_id=1, source_target_pairs={{0,4},{2,6},{4,0},{6,2},{8,12},{10,14},{12,8},{14,10},{16,20},{18,... | collective-permute-start | bytes 196616 | tf_op jit(solution)/shard_map/ppermute | solution.py:415
  62.8 4.3 %collective-permute-start.11 = (f32[128,128]{1,0:T(8,128)S(1)}, f32[128,128]{1,0:T(8,128)S(1)}, u32[]{:S(2)}, u32[]{:S(2)}) collective-permute-start(f32[128,128]{1,0:T(8,128)S(1)} %add.48.own_ref), channel_id=1, source_target_pairs={{0,1},{1,0},{2,3},{3,2},{4,5},{5,4},{6,7},{7,6},{8,9},{9,8},{10,11... | collective-permute-start | bytes 196616 | tf_op jit(solution)/shard_map/ppermute | solution.py:447
  65.5 6.0 %collective-permute-start.17 = (f32[128,128]{1,0:T(8,128)S(1)}, f32[128,128]{1,0:T(8,128)S(1)}, u32[]{:S(2)}, u32[]{:S(2)}) collective-permute-start(f32[128,128]{1,0:T(8,128)S(1)} %add_add_fusion.after_ref), channel_id=1, source_target_pairs={{0,16},{2,18},{4,20},{6,22},{8,24},{10,26},{12,28},{14,30},{16,0},... | collective-permute-start | bytes 196616 | tf_op jit(solution)/shard_map/ppermute | solution.py:415

commit v13 on v12

--- a/solution.py
+++ b/solution.py
@@ -435,7 +435,7 @@
             out_specs=pl.BlockSpec(memory_space=pltpu.VMEM),
             compiler_params=params,
         )(filtered, narrow)
-        near = summed(near, stages[:1])
+        near = summed(near, stages[:-1])
         cross = pl.pallas_call(
             cross_gram_kernel,
             out_shape=tile,
@@ -443,8 +443,18 @@
             out_specs=pl.BlockSpec(memory_space=pltpu.VMEM),
             compiler_params=params,
         )(place, narrow, other, near)
-        near = summed(near, stages[1:])
-        far = lax.ppermute(near, "orb", swap)
+        last = stages[-1]
+
+        def away(step):
+            pairs = [(2 * i + j, 2 * (i ^ step) + 1 - j) for i in range(blocks) for j in range(2)]
+            return lax.ppermute(near, ("space", "orb"), pairs)
+
+        if len(last) == 1:
+            far = away(0) + away(last[0])
+            near = summed(near, [last])
+        else:
+            near = summed(near, [last])
+            far = away(0)
         cross = summed(cross, stages[:-1])
         first, first_inv = factor_first(place, near, far, cross)
         cross = summed(cross, stages[-1:])

time: 78.7 us -> 83.6 us (1.062)
  waiting for transfers between devices: 10.7 us -> 16.3 us
    ppermute x10, waiting for transfers between devices: 2.49 us -> 8.88 us  [moved(): return lax.ppermute(part, 'space', [(i, i ^ step) for i in range(blocks)])]
    ppermute x10, starting transfers between devices: 18.9 us -> 15.6 us  [moved(): return lax.ppermute(part, 'space', [(i, i ^ step) for i in range(blocks)])]
    ppermute x1 -> x2, starting transfers between devices: 1.43 us -> 4.02 us  [away(): return lax.ppermute(near, ('space', 'orb'), pairs)]
  transfers between devices with their start and end apart: 18 -> 19, of which waited for: 8 -> 8; matrix products, arithmetic and copies ran while one was open for 2% -> 2% of each run, Pallas kernels for 14% -> 13%
where the time goes in v13:
time: 83.6 us; the launch traced here: 83.4 us
  starting transfers between devices  39.2 us (47%)
  Pallas kernels  21.1 us (25%)
  waiting for transfers between devices  16.3 us (19%)
  local copies, waits for them, and re-layouts  4.27 us (5%)
  other arithmetic  1.54 us (2%)
  between operations  0.97 us (1%)
    ppermute x10, starting transfers between devices, moved(): return lax.ppermute(part, 'space', [(i, i ^ step) for i in range(blocks)])  15.6 us
    ppermute x3, starting transfers between devices, halo(): far = lax.ppermute(vec, 'space', far_pairs)  11.9 us
    ppermute x10, waiting for transfers between devices, moved(): return lax.ppermute(part, 'space', [(i, i ^ step) for i in range(blocks)])  8.88 us
    ppermute x3, waiting for transfers between devices, halo(): far = lax.ppermute(vec, 'space', far_pairs)  7.43 us
    pallas_call x1, Pallas kernels, finish(): pl.pallas_call(finish_kernel, out_shape=[jax.ShapeDtypeStruct((2 * half,...  6.73 us
    ppermute x3, starting transfers between devices, halo(): return (lax.ppermute(vec, 'space', near_pairs), far)  6.14 us
    pallas_call x1, Pallas kernels, factor_first(): pl.pallas_call(first_kernel, out_shape=[jax.ShapeDtypeStruct((half, half)...  4.31 us
    unnamed x6, local copies, waits for them, and re-layouts  4.13 us
  transfers between devices with their start and end apart: 19, of which 8 were waited for; matrix products, arithmetic and copies ran while one was open for 2% of the time, Pallas kernels for 13%

profile of v13, /device:TPU:0, one launch (start us, length us, event | category | flops | bytes accessed | tf_op | source)
XLA Modules:
  0.0 83.4 jit_solution(16567637409656213750)
XLA Ops:
  0.6 5.5 %collective-permute-start.1 = (bf16[128,2048]{1,0:T(8,128)(2,1)}, bf16[128,2048]{1,0:T(8,128)(2,1)S(1)}, u32[]{:S(2)}, u32[]{:S(2)}) collective-permute-start(bf16[128,2048]{1,0:T(8,128)(2,1)} %prior_ref.3), channel_id=1, source_target_pairs={{0,30},{2,4},{4,2},{6,8},{8,6},{10,12},{12,10},{14,16},{16,14},{18... | collective-permute-start | bytes 1572872 | tf_op jit(solution)/shard_map/ppermute | solution.py:399
  6.1 0.0 collective-permute-start
  6.1 0.7 add_select_fusion
  6.8 0.1 slice.11
  6.9 0.1 fusion.1
  7.0 0.8 add_select_fusion.1.loc_ref
  7.7 0.0 copy-start
  7.8 1.0 %copy-done = bf16[128,2048]{1,0:T(8,128)(2,1)S(1)} copy-done((bf16[128,2048]{1,0:T(8,128)(2,1)S(1)}, bf16[128,2048]{1,0:T(8,128)(2,1)}, u32[]{:S(2)}) %copy-start) | copy-done | bytes 524312
  8.8 0.0 copy-start.2
  8.8 3.1 %copy-done.2 = bf16[8,7,256,256]{3,2,1,0:T(8,128)(2,1)S(1)} copy-done((bf16[8,7,256,256]{3,2,1,0:T(8,128)(2,1)S(1)}, bf16[8,7,256,256]{3,2,1,0:T(8,128)(2,1)}, u32[]{:S(2)}) %copy-start.2) | copy-done | bytes 7340056
  11.9 0.0 copy-start.1
  11.9 2.7 %shard_map.50 = (bf16[8,7,256,256]{3,2,1,0:T(8,128)(2,1)S(1)}, f32[128,2048]{1,0:T(8,128)S(1)}) custom-call(s32[8,6]{1,0:T(8,128)S(1)} %add_select_fusion.1.loc_ref, s32[1]{0:T(128)S(6)} %select_n.21.odd_ref, bf16[128,2048]{1,0:T(8,128)(2,1)S(1)} %copy-done, bf16[8,7,256,256]{3,2,1,0:T(8,128)(2,1)S(1)} %copy-done.2), custom_call_target="tpu_custom_call" | custom-call | flops 671088640 | bytes 14680064 | tf_op jit(solution)/shard_map/pallas_call | solution.py:55
  14.6 0.0 collective-permute-done.1.far_ref
  14.6 0.0 collective-permute-done.near_ref
  14.6 0.0 copy-done.1
  14.6 1.1 %shard_map.51.vec_ref.prior_ref = bf16[128,2048]{1,0:T(8,128)(2,1)S(1)} custom-call(s32[8,6]{1,0:T(8,128)S(1)} %add_select_fusion.1.loc_ref, bf16[128,2048]{1,0:T(8,128)(2,1)S(1)} %collective-permute-done.near_ref, bf16[128,2048]{1,0:T(8,128)(2,1)S(1)} %collective-permute-done.1.far_ref, f32[128,2048]{1,0:T(8,128)S(1)} %get-tuple-element.10.acc_ref, ...), custom_call_target="tpu_custom_call" | custom-call | flops 268435456 | bytes 2097152 | tf_op jit(solution)/shard_map/pallas_call | solution.py:123
  15.8 3.2 %collective-permute-start.3 = (bf16[128,2048]{1,0:T(8,128)(2,1)S(1)}, bf16[128,2048]{1,0:T(8,128)(2,1)S(1)}, u32[]{:S(2)}, u32[]{:S(2)}) collective-permute-start(bf16[128,2048]{1,0:T(8,128)(2,1)S(1)} %shard_map.51.vec_ref.prior_ref), channel_id=1, source_target_pairs={{0,30},{2,4},{4,2},{6,8},{8,6},{10,12},{12,10},{14,16},{16,14},{18... | collective-permute-start | bytes 1572872 | tf_op jit(solution)/shard_map/ppermute | solution.py:399
  18.9 0.5 collective-permute-start.2
  19.4 1.5 %shard_map.52.acc_ref = f32[128,2048]{1,0:T(8,128)S(1)} custom-call(s32[8,6]{1,0:T(8,128)S(1)} %add_select_fusion.1.loc_ref, bf16[128,2048]{1,0:T(8,128)(2,1)S(1)} %shard_map.51.vec_ref.prior_ref, bf16[8,7,256,256]{3,2,1,0:T(8,128)(2,1)S(1)} %get-tuple-element.11.turned_ref), custom_call_target="tpu_custom_call" | custom-call | flops 671088640 | bytes 5242880 | tf_op jit(solution)/shard_map/pallas_call | solution.py:88
  20.9 6.3 %collective-permute-done.3.far_ref = bf16[128,2048]{1,0:T(8,128)(2,1)S(1)} collective-permute-done((bf16[128,2048]{1,0:T(8,128)(2,1)S(1)}, bf16[128,2048]{1,0:T(8,128)(2,1)S(1)}, u32[]{:S(2)}, u32[]{:S(2)}) %collective-permute-start.3) | collective-permute-done | bytes 524320 | tf_op jit(solution)/shard_map/ppermute | solution.py:399
  27.2 0.0 collective-permute-done.2.near_ref
  27.2 1.2 %shard_map.53.vec_ref = bf16[128,2048]{1,0:T(8,128)(2,1)S(1)} custom-call(s32[8,6]{1,0:T(8,128)S(1)} %add_select_fusion.1.loc_ref, bf16[128,2048]{1,0:T(8,128)(2,1)S(1)} %collective-permute-done.2.near_ref, bf16[128,2048]{1,0:T(8,128)(2,1)S(1)} %collective-permute-done.3.far_ref, f32[128,2048]{1,0:T(8,128)S(1)} %shard_map.52.acc_ref, ...), custom_call_target="tpu_custom_call" | custom-call | flops 268435456 | bytes 2097152 | tf_op jit(solution)/shard_map/pallas_call | solution.py:123
  28.4 3.2 %collective-permute-start.5 = (bf16[128,2048]{1,0:T(8,128)(2,1)S(1)}, bf16[128,2048]{1,0:T(8,128)(2,1)S(1)}, u32[]{:S(2)}, u32[]{:S(2)}) collective-permute-start(bf16[128,2048]{1,0:T(8,128)(2,1)S(1)} %shard_map.53.vec_ref), channel_id=1, source_target_pairs={{0,30},{2,4},{4,2},{6,8},{8,6},{10,12},{12,10},{14,16},{16,14},{18... | collective-permute-start | bytes 1572872 | tf_op jit(solution)/shard_map/ppermute | solution.py:399
  31.6 5.7 %collective-permute-start.4 = (bf16[128,2048]{1,0:T(8,128)(2,1)S(1)}, bf16[128,2048]{1,0:T(8,128)(2,1)S(1)}, u32[]{:S(2)}, u32[]{:S(2)}) collective-permute-start(bf16[128,2048]{1,0:T(8,128)(2,1)S(1)} %shard_map.53.vec_ref), channel_id=1, source_target_pairs={{0,2},{2,0},{4,6},{6,4},{8,10},{10,8},{12,14},{14,12},{16,18},{18,... | collective-permute-start | bytes 1572872 | tf_op jit(solution)/shard_map/ppermute | solution.py:400
  37.3 1.5 %shard_map.54.acc_ref = f32[128,2048]{1,0:T(8,128)S(1)} custom-call(s32[8,6]{1,0:T(8,128)S(1)} %add_select_fusion.1.loc_ref, bf16[128,2048]{1,0:T(8,128)(2,1)S(1)} %shard_map.53.vec_ref, bf16[8,7,256,256]{3,2,1,0:T(8,128)(2,1)S(1)} %get-tuple-element.11.turned_ref), custom_call_target="tpu_custom_call" | custom-call | flops 671088640 | bytes 5242880 | tf_op jit(solution)/shard_map/pallas_call | solution.py:88
  38.8 1.1 %collective-permute-done.5.far_ref = bf16[128,2048]{1,0:T(8,128)(2,1)S(1)} collective-permute-done((bf16[128,2048]{1,0:T(8,128)(2,1)S(1)}, bf16[128,2048]{1,0:T(8,128)(2,1)S(1)}, u32[]{:S(2)}, u32[]{:S(2)}) %collective-permute-start.5) | collective-permute-done | bytes 524320 | tf_op jit(solution)/shard_map/ppermute | solution.py:399
  39.9 0.0 collective-permute-done.4.near_ref
  39.9 1.2 %shard_map.55 = (f32[128,2048]{1,0:T(8,128)S(1)}, bf16[128,2048]{1,0:T(8,128)(2,1)S(1)}) custom-call(s32[8,6]{1,0:T(8,128)S(1)} %add_select_fusion.1.loc_ref, bf16[128,2048]{1,0:T(8,128)(2,1)S(1)} %collective-permute-done.4.near_ref, bf16[128,2048]{1,0:T(8,128)(2,1)S(1)} %collective-permute-done.5.far_ref, f32[128,2048]{1,0:T(8,128)S(1)} %shard_map.54.acc_ref, ...), custom_call_target="tpu_custom_call" | custom-call | flops 268435456 | bytes 2097152 | tf_op jit(solution)/shard_map/pallas_call | solution.py:123
  41.1 1.6 %collective-permute-start.13 = (bf16[128,2048]{1,0:T(8,128)(2,1)S(1)}, bf16[128,2048]{1,0:T(8,128)(2,1)S(1)}, u32[]{:S(2)}, u32[]{:S(2)}) collective-permute-start(bf16[128,2048]{1,0:T(8,128)(2,1)S(1)} %get-tuple-element.13.high_ref.own_ref), channel_id=1, source_target_pairs={{0,1},{1,0},{2,3},{3,2},{4,5},{5,4},{6,7},{7,6},{8,9},{9,8},{10,11... | collective-permute-start | bytes 1572872 | tf_op jit(solution)/shard_map/ppermute | solution.py:428
  42.7 0.5 shard_map.56
  43.2 5.4 %collective-permute-start.6 = (f32[128,128]{1,0:T(8,128)S(1)}, f32[128,128]{1,0:T(8,128)S(1)}, u32[]{:S(2)}, u32[]{:S(2)}) collective-permute-start(f32[128,128]{1,0:T(8,128)S(1)} %shard_map.56), channel_id=1, source_target_pairs={{0,2},{2,0},{4,6},{6,4},{8,10},{10,8},{12,14},{14,12},{16,18},{18,... | collective-permute-start | bytes 196616 | tf_op jit(solution)/shard_map/ppermute | solution.py:415
  48.6 0.9 %collective-permute-done.6 = f32[128,128]{1,0:T(8,128)S(1)} collective-permute-done((f32[128,128]{1,0:T(8,128)S(1)}, f32[128,128]{1,0:T(8,128)S(1)}, u32[]{:S(2)}, u32[]{:S(2)}) %collective-permute-start.6) | collective-permute-done | bytes 65568 | tf_op jit(solution)/shard_map/ppermute | solution.py:415
  49.5 1.9 %collective-permute-start.9 = (f32[128,128]{1,0:T(8,128)S(1)}, f32[128,128]{1,0:T(8,128)S(1)}, u32[]{:S(2)}, u32[]{:S(2)}) collective-permute-start(f32[128,128]{1,0:T(8,128)S(1)} %add.47), channel_id=1, source_target_pairs={{0,12},{2,14},{4,8},{6,10},{8,4},{10,6},{12,0},{14,2},{16,28},{18,... | collective-permute-start | bytes 196616 | tf_op jit(solution)/shard_map/ppermute | solution.py:415
  51.5 0.5 collective-permute-start.8
  51.9 1.2 %collective-permute-start.7 = (f32[128,128]{1,0:T(8,128)S(1)}, f32[128,128]{1,0:T(8,128)S(1)}, u32[]{:S(2)}, u32[]{:S(2)}) collective-permute-start(f32[128,128]{1,0:T(8,128)S(1)} %add.47), channel_id=1, source_target_pairs={{0,4},{2,6},{4,0},{6,2},{8,12},{10,14},{12,8},{14,10},{16,20},{18,... | collective-permute-start | bytes 196616 | tf_op jit(solution)/shard_map/ppermute | solution.py:415
  53.1 2.3 %collective-permute-done.9 = f32[128,128]{1,0:T(8,128)S(1)} collective-permute-done((f32[128,128]{1,0:T(8,128)S(1)}, f32[128,128]{1,0:T(8,128)S(1)}, u32[]{:S(2)}, u32[]{:S(2)}) %collective-permute-start.9) | collective-permute-done | bytes 65568 | tf_op jit(solution)/shard_map/ppermute | solution.py:415
  55.4 0.3 collective-permute-done.8
  55.7 0.5 collective-permute-done.7
  56.3 0.0 collective-permute-done.13.other_ref.away_ref
  56.3 0.3 shard_map.57
  56.6 0.1 collective-permute-start.14
  56.7 1.2 %collective-permute-done.14 = f32[128,128]{1,0:T(8,128)S(1)} collective-permute-done((f32[128,128]{1,0:T(8,128)S(1)}, f32[128,128]{1,0:T(8,128)S(1)}, u32[]{:S(2)}, u32[]{:S(2)}) %collective-permute-start.14) | collective-permute-done | bytes 65568 | tf_op jit(solution)/shard_map/ppermute | solution.py:415
  57.9 1.7 %collective-permute-start.17 = (f32[128,128]{1,0:T(8,128)S(1)}, f32[128,128]{1,0:T(8,128)S(1)}, u32[]{:S(2)}, u32[]{:S(2)}) collective-permute-start(f32[128,128]{1,0:T(8,128)S(1)} %add.53), channel_id=1, source_target_pairs={{0,12},{2,14},{4,8},{6,10},{8,4},{10,6},{12,0},{14,2},{16,28},{18,... | collective-permute-start | bytes 196616 | tf_op jit(solution)/shard_map/ppermute | solution.py:415
  59.7 0.9 %collective-permute-start.16 = (f32[128,128]{1,0:T(8,128)S(1)}, f32[128,128]{1,0:T(8,128)S(1)}, u32[]{:S(2)}, u32[]{:S(2)}) collective-permute-start(f32[128,128]{1,0:T(8,128)S(1)} %add.53), channel_id=1, source_target_pairs={{0,8},{2,10},{4,12},{6,14},{8,0},{10,2},{12,4},{14,6},{16,24},{18,... | collective-permute-start | bytes 196616 | tf_op jit(solution)/shard_map/ppermute | solution.py:415
  60.6 0.9 %collective-permute-start.15 = (f32[128,128]{1,0:T(8,128)S(1)}, f32[128,128]{1,0:T(8,128)S(1)}, u32[]{:S(2)}, u32[]{:S(2)}) collective-permute-start(f32[128,128]{1,0:T(8,128)S(1)} %add.53), channel_id=1, source_target_pairs={{0,4},{2,6},{4,0},{6,2},{8,12},{10,14},{12,8},{14,10},{16,20},{18,... | collective-permute-start | bytes 196616 | tf_op jit(solution)/shard_map/ppermute | solution.py:415
  61.5 2.5 %collective-permute-start.12 = (f32[128,128]{1,0:T(8,128)S(1)}, f32[128,128]{1,0:T(8,128)S(1)}, u32[]{:S(2)}, u32[]{:S(2)}) collective-permute-start(f32[128,128]{1,0:T(8,128)S(1)} %add_add_fusion.1.after_ref), channel_id=1, source_target_pairs={{0,17},{1,16},{2,19},{3,18},{4,21},{5,20},{6,23},{7,22},{8,25},{9,... | collective-permute-start | bytes 196616 | tf_op jit(solution)/shard_map/ppermute | solution.py:450
  64.0 1.5 %collective-permute-start.11 = (f32[128,128]{1,0:T(8,128)S(1)}, f32[128,128]{1,0:T(8,128)S(1)}, u32[]{:S(2)}, u32[]{:S(2)}) collective-permute-start(f32[128,128]{1,0:T(8,128)S(1)} %add_add_fusion.1.after_ref), channel_id=1, source_target_pairs={{0,1},{1,0},{2,3},{3,2},{4,5},{5,4},{6,7},{7,6},{8,9},{9,8},{10,11... | collective-permute-start | bytes 196616 | tf_op jit(solution)/shard_map/ppermute | solution.py:450
  65.5 0.0 collective-permute-done.17
  65.5 0.4 collective-permute-start.10
  65.9 0.0 collective-permute-done.16
  65.9 0.0 collective-permute-done.15
  65.9 2.6 %collective-permute-start.18 = (f32[128,128]{1,0:T(8,128)S(1)}, f32[128,128]{1,0:T(8,128)S(1)}, u32[]{:S(2)}, u32[]{:S(2)}) collective-permute-start(f32[128,128]{1,0:T(8,128)S(1)} %add_add_fusion.after_ref), channel_id=1, source_target_pairs={{0,16},{2,18},{4,20},{6,22},{8,24},{10,26},{12,28},{14,30},{16,0},... | collective-permute-start | bytes 196616 | tf_op jit(solution)/shard_map/ppermute | solution.py:415
  68.5 3.6 %collective-permute-done.10 = f32[128,128]{1,0:T(8,128)S(1)} collective-permute-done((f32[128,128]{1,0:T(8,128)S(1)}, f32[128,128]{1,0:T(8,128)S(1)}, u32[]{:S(2)}, u32[]{:S(2)}) %collective-permute-start.10) | collective-permute-done | bytes 65568 | tf_op jit(solution)/shard_map/ppermute | solution.py:415
  72.1 0.0 collective-permute-done.12
  72.1 0.0 collective-permute-done.11
  72.1 4.3 %shard_map.58 = (f32[128,128]{1,0:T(8,128)S(1)}, f32[128,128]{1,0:T(8,128)S(1)}) custom-call(s32[1]{0:T(128)} %bitcast.place_ref, f32[128,128]{1,0:T(8,128)S(1)} %add.51.own_ref, f32[128,128]{1,0:T(8,128)S(1)} %add.52.other_ref, f32[128,128]{1,0:T(8,128)S(1)} %add_add_fusion.after_ref), custom_call_target="tpu_custom_call" | custom-call | flops 4194304 | bytes 16777216 | tf_op jit(solution)/shard_map/pallas_call | solution.py:287
  76.4 0.0 collective-permute-done.18
  76.5 6.7 %shard_map.59 = (f32[256,256]{1,0:T(8,128)}, f32[128,2048]{1,0:T(8,128)}) custom-call(s32[1]{0:T(128)} %bitcast.place_ref, f32[128,128]{1,0:T(8,128)S(1)} %add.51.own_ref, f32[128,128]{1,0:T(8,128)S(1)} %add.52.other_ref, f32[128,128]{1,0:T(8,128)S(1)} %add.57.cross_ref, f32[128,128]{1,0:T(8,128)S(1)} %get-tuple-element.14.first_ref, ...), custom_call_target="tpu_custom_call" | custom-call | tf_op jit(solution)/shard_map/pallas_call | solution.py:369
  (7 shorter events, 0.1 us)
Async XLA Ops:
  0.6 14.0 %collective-permute-start.1 = (bf16[128,2048]{1,0:T(8,128)(2,1)}, bf16[128,2048]{1,0:T(8,128)(2,1)S(1)}, u32[]{:S(2)}, u32[]{:S(2)}) collective-permute-start(bf16[128,2048]{1,0:T(8,128)(2,1)} %prior_ref.3), channel_id=1, source_target_pairs={{0,30},{2,4},{4,2},{6,8},{8,6},{10,12},{12,10},{14,16},{16,14},{18... | collective-permute-start | bytes 1572872 | tf_op jit(solution)/shard_map/ppermute | solution.py:399
  6.1 8.5 %collective-permute-start = (bf16[128,2048]{1,0:T(8,128)(2,1)}, bf16[128,2048]{1,0:T(8,128)(2,1)S(1)}, u32[]{:S(2)}, u32[]{:S(2)}) collective-permute-start(bf16[128,2048]{1,0:T(8,128)(2,1)} %prior_ref.3), channel_id=1, source_target_pairs={{0,2},{2,0},{4,6},{6,4},{8,10},{10,8},{12,14},{14,12},{16,18},{18,... | collective-permute-start | bytes 1572872 | tf_op jit(solution)/shard_map/ppermute | solution.py:400
  7.7 1.0 %copy-start = (bf16[128,2048]{1,0:T(8,128)(2,1)S(1)}, bf16[128,2048]{1,0:T(8,128)(2,1)}, u32[]{:S(2)}) copy-start(bf16[128,2048]{1,0:T(8,128)(2,1)} %prior_ref.3) | copy-start | bytes 1572868
  8.8 3.1 %copy-start.2 = (bf16[8,7,256,256]{3,2,1,0:T(8,128)(2,1)S(1)}, bf16[8,7,256,256]{3,2,1,0:T(8,128)(2,1)}, u32[]{:S(2)}) copy-start(bf16[8,7,256,256]{3,2,1,0:T(8,128)(2,1)} %ham_ref.1) | copy-start | bytes 22020100
  11.9 2.8 %copy-start.1 = (bf16[128,2048]{1,0:T(8,128)(2,1)S(1)}, bf16[128,2048]{1,0:T(8,128)(2,1)}, u32[]{:S(2)}) copy-start(bf16[128,2048]{1,0:T(8,128)(2,1)} %prior_ref.3) | copy-start | bytes 1572868
  15.8 11.5 %collective-permute-start.3 = (bf16[128,2048]{1,0:T(8,128)(2,1)S(1)}, bf16[128,2048]{1,0:T(8,128)(2,1)S(1)}, u32[]{:S(2)}, u32[]{:S(2)}) collective-permute-start(bf16[128,2048]{1,0:T(8,128)(2,1)S(1)} %shard_map.51.vec_ref.prior_ref), channel_id=1, source_target_pairs={{0,30},{2,4},{4,2},{6,8},{8,6},{10,12},{12,10},{14,16},{16,14},{18... | collective-permute-start | bytes 1572872 | tf_op jit(solution)/shard_map/ppermute | solution.py:399
  18.9 8.3 %collective-permute-start.2 = (bf16[128,2048]{1,0:T(8,128)(2,1)S(1)}, bf16[128,2048]{1,0:T(8,128)(2,1)S(1)}, u32[]{:S(2)}, u32[]{:S(2)}) collective-permute-start(bf16[128,2048]{1,0:T(8,128)(2,1)S(1)} %shard_map.51.vec_ref.prior_ref), channel_id=1, source_target_pairs={{0,2},{2,0},{4,6},{6,4},{8,10},{10,8},{12,14},{14,12},{16,18},{18,... | collective-permute-start | bytes 1572872 | tf_op jit(solution)/shard_map/ppermute | solution.py:400
  28.4 11.5 %collective-permute-start.5 = (bf16[128,2048]{1,0:T(8,128)(2,1)S(1)}, bf16[128,2048]{1,0:T(8,128)(2,1)S(1)}, u32[]{:S(2)}, u32[]{:S(2)}) collective-permute-start(bf16[128,2048]{1,0:T(8,128)(2,1)S(1)} %shard_map.53.vec_ref), channel_id=1, source_target_pairs={{0,30},{2,4},{4,2},{6,8},{8,6},{10,12},{12,10},{14,16},{16,14},{18... | collective-permute-start | bytes 1572872 | tf_op jit(solution)/shard_map/ppermute | solution.py:399
  31.6 8.3 %collective-permute-start.4 = (bf16[128,2048]{1,0:T(8,128)(2,1)S(1)}, bf16[128,2048]{1,0:T(8,128)(2,1)S(1)}, u32[]{:S(2)}, u32[]{:S(2)}) collective-permute-start(bf16[128,2048]{1,0:T(8,128)(2,1)S(1)} %shard_map.53.vec_ref), channel_id=1, source_target_pairs={{0,2},{2,0},{4,6},{6,4},{8,10},{10,8},{12,14},{14,12},{16,18},{18,... | collective-permute-start | bytes 1572872 | tf_op jit(solution)/shard_map/ppermute | solution.py:400
  41.1 15.1 %collective-permute-start.13 = (bf16[128,2048]{1,0:T(8,128)(2,1)S(1)}, bf16[128,2048]{1,0:T(8,128)(2,1)S(1)}, u32[]{:S(2)}, u32[]{:S(2)}) collective-permute-start(bf16[128,2048]{1,0:T(8,128)(2,1)S(1)} %get-tuple-element.13.high_ref.own_ref), channel_id=1, source_target_pairs={{0,1},{1,0},{2,3},{3,2},{4,5},{5,4},{6,7},{7,6},{8,9},{9,8},{10,11... | collective-permute-start | bytes 1572872 | tf_op jit(solution)/shard_map/ppermute | solution.py:428
  43.2 6.3 %collective-permute-start.6 = (f32[128,128]{1,0:T(8,128)S(1)}, f32[128,128]{1,0:T(8,128)S(1)}, u32[]{:S(2)}, u32[]{:S(2)}) collective-permute-start(f32[128,128]{1,0:T(8,128)S(1)} %shard_map.56), channel_id=1, source_target_pairs={{0,2},{2,0},{4,6},{6,4},{8,10},{10,8},{12,14},{14,12},{16,18},{18,... | collective-permute-start | bytes 196616 | tf_op jit(solution)/shard_map/ppermute | solution.py:415
  49.5 5.9 %collective-permute-start.9 = (f32[128,128]{1,0:T(8,128)S(1)}, f32[128,128]{1,0:T(8,128)S(1)}, u32[]{:S(2)}, u32[]{:S(2)}) collective-permute-start(f32[128,128]{1,0:T(8,128)S(1)} %add.47), channel_id=1, source_target_pairs={{0,12},{2,14},{4,8},{6,10},{8,4},{10,6},{12,0},{14,2},{16,28},{18,... | collective-permute-start | bytes 196616 | tf_op jit(solution)/shard_map/ppermute | solution.py:415
  51.5 4.3 %collective-permute-start.8 = (f32[128,128]{1,0:T(8,128)S(1)}, f32[128,128]{1,0:T(8,128)S(1)}, u32[]{:S(2)}, u32[]{:S(2)}) collective-permute-start(f32[128,128]{1,0:T(8,128)S(1)} %add.47), channel_id=1, source_target_pairs={{0,8},{2,10},{4,12},{6,14},{8,0},{10,2},{12,4},{14,6},{16,24},{18,... | collective-permute-start | bytes 196616 | tf_op jit(solution)/shard_map/ppermute | solution.py:415
  51.9 4.3 %collective-permute-start.7 = (f32[128,128]{1,0:T(8,128)S(1)}, f32[128,128]{1,0:T(8,128)S(1)}, u32[]{:S(2)}, u32[]{:S(2)}) collective-permute-start(f32[128,128]{1,0:T(8,128)S(1)} %add.47), channel_id=1, source_target_pairs={{0,4},{2,6},{4,0},{6,2},{8,12},{10,14},{12,8},{14,10},{16,20},{18,... | collective-permute-start | bytes 196616 | tf_op jit(solution)/shard_map/ppermute | solution.py:415
  56.6 1.3 %collective-permute-start.14 = (f32[128,128]{1,0:T(8,128)S(1)}, f32[128,128]{1,0:T(8,128)S(1)}, u32[]{:S(2)}, u32[]{:S(2)}) collective-permute-start(f32[128,128]{1,0:T(8,128)S(1)} %shard_map.57), channel_id=1, source_target_pairs={{0,2},{2,0},{4,6},{6,4},{8,10},{10,8},{12,14},{14,12},{16,18},{18,... | collective-permute-start | bytes 196616 | tf_op jit(solution)/shard_map/ppermute | solution.py:415
  57.9 7.6 %collective-permute-start.17 = (f32[128,128]{1,0:T(8,128)S(1)}, f32[128,128]{1,0:T(8,128)S(1)}, u32[]{:S(2)}, u32[]{:S(2)}) collective-permute-start(f32[128,128]{1,0:T(8,128)S(1)} %add.53), channel_id=1, source_target_pairs={{0,12},{2,14},{4,8},{6,10},{8,4},{10,6},{12,0},{14,2},{16,28},{18,... | collective-permute-start | bytes 196616 | tf_op jit(solution)/shard_map/ppermute | solution.py:415
  59.7 6.2 %collective-permute-start.16 = (f32[128,128]{1,0:T(8,128)S(1)}, f32[128,128]{1,0:T(8,128)S(1)}, u32[]{:S(2)}, u32[]{:S(2)}) collective-permute-start(f32[128,128]{1,0:T(8,128)S(1)} %add.53), channel_id=1, source_target_pairs={{0,8},{2,10},{4,12},{6,14},{8,0},{10,2},{12,4},{14,6},{16,24},{18,... | collective-permute-start | bytes 196616 | tf_op jit(solution)/shard_map/ppermute | solution.py:415
  60.6 5.3 %collective-permute-start.15 = (f32[128,128]{1,0:T(8,128)S(1)}, f32[128,128]{1,0:T(8,128)S(1)}, u32[]{:S(2)}, u32[]{:S(2)}) collective-permute-start(f32[128,128]{1,0:T(8,128)S(1)} %add.53), channel_id=1, source_target_pairs={{0,4},{2,6},{4,0},{6,2},{8,12},{10,14},{12,8},{14,10},{16,20},{18,... | collective-permute-start | bytes 196616 | tf_op jit(solution)/shard_map/ppermute | solution.py:415
  61.5 10.6 %collective-permute-start.12 = (f32[128,128]{1,0:T(8,128)S(1)}, f32[128,128]{1,0:T(8,128)S(1)}, u32[]{:S(2)}, u32[]{:S(2)}) collective-permute-start(f32[128,128]{1,0:T(8,128)S(1)} %add_add_fusion.1.after_ref), channel_id=1, source_target_pairs={{0,17},{1,16},{2,19},{3,18},{4,21},{5,20},{6,23},{7,22},{8,25},{9,... | collective-permute-start | bytes 196616 | tf_op jit(solution)/shard_map/ppermute | solution.py:450
  64.0 8.1 %collective-permute-start.11 = (f32[128,128]{1,0:T(8,128)S(1)}, f32[128,128]{1,0:T(8,128)S(1)}, u32[]{:S(2)}, u32[]{:S(2)}) collective-permute-start(f32[128,128]{1,0:T(8,128)S(1)} %add_add_fusion.1.after_ref), channel_id=1, source_target_pairs={{0,1},{1,0},{2,3},{3,2},{4,5},{5,4},{6,7},{7,6},{8,9},{9,8},{10,11... | collective-permute-start | bytes 196616 | tf_op jit(solution)/shard_map/ppermute | solution.py:450
  65.5 6.6 %collective-permute-start.10 = (f32[128,128]{1,0:T(8,128)S(1)}, f32[128,128]{1,0:T(8,128)S(1)}, u32[]{:S(2)}, u32[]{:S(2)}) collective-permute-start(f32[128,128]{1,0:T(8,128)S(1)} %add_add_fusion.1.after_ref), channel_id=1, source_target_pairs={{0,16},{2,18},{4,20},{6,22},{8,24},{10,26},{12,28},{14,30},{16,0},... | collective-permute-start | bytes 196616 | tf_op jit(solution)/shard_map/ppermute | solution.py:415
  65.9 10.5 %collective-permute-start.18 = (f32[128,128]{1,0:T(8,128)S(1)}, f32[128,128]{1,0:T(8,128)S(1)}, u32[]{:S(2)}, u32[]{:S(2)}) collective-permute-start(f32[128,128]{1,0:T(8,128)S(1)} %add_add_fusion.after_ref), channel_id=1, source_target_pairs={{0,16},{2,18},{4,20},{6,22},{8,24},{10,26},{12,28},{14,30},{16,0},... | collective-permute-start | bytes 196616 | tf_op jit(solution)/shard_map/ppermute | solution.py:415

commit v14 on v12

--- a/solution.py
+++ b/solution.py
@@ -31,42 +31,58 @@
     return high, (a - high.astype(jnp.float32)).astype(jnp.bfloat16)
 
 
-def turn_kernel(loc_ref, odd_ref, vec_ref, ham_ref, turned_ref, out_ref):
+def stacked(refs, here=slice(None)):
+    return jnp.concatenate([ref[:, here] for ref in refs], axis=0)
+
+
+def turn_kernel(chunks, loc_ref, odd_ref, *refs):
+    vec_refs, ham_ref, turned_ref, outs = refs[:chunks], refs[chunks], refs[chunks + 1], refs[chunks + 2 : -2]
+    buf, sems = refs[-2:]
     count, faces, width, _ = ham_ref.shape
+    share = outs[0].shape[0]
     odd = odd_ref[0]
+    copies = [pltpu.make_async_copy(ham_ref.at[e], buf.at[e], sems.at[e]) for e in range(count)]
+    for copy in copies:
+        copy.start()
     for e in range(count):
+        copies[e].wait()
         here = slice(e * width, (e + 1) * width)
         total = None
         for face in range(faces):
             source = 2 - odd if face == 1 else 1 + odd if face == 2 else face
-            turned = ham_ref[e, source].T
+            turned = buf[e, source].T
             turned_ref[e, face] = turned
             if face == 1 or face == 2:
                 continue
             at = here if face == 0 else pl.ds(pl.multiple_of(loc_ref[e, face - 1] * width, width), width)
-            part = jnp.dot(vec_ref[:, at], turned, preferred_element_type=jnp.float32)
+            part = jnp.dot(stacked(vec_refs, at), turned, preferred_element_type=jnp.float32)
             total = part if total is None else total + part
-        out_ref[:, here] = total
-
-
-def turn_part(vec, hamiltonian, loc, odd):
+        for piece, out in enumerate(outs):
+            out[:, here] = total[piece * share : (piece + 1) * share]
+
+
+def turn_part(vecs, hamiltonian, loc, odd):
     count, faces, width, _ = hamiltonian.shape
-    owned = vec.shape[0]
-    return pl.pallas_call(
-        turn_kernel,
-        out_shape=[
-            jax.ShapeDtypeStruct(hamiltonian.shape, hamiltonian.dtype),
-            jax.ShapeDtypeStruct(vec.shape, jnp.float32),
+    chunks = len(vecs)
+    return pl.pallas_call(
+        functools.partial(turn_kernel, chunks),
+        out_shape=[jax.ShapeDtypeStruct(hamiltonian.shape, hamiltonian.dtype)]
+        + [jax.ShapeDtypeStruct(vec.shape, jnp.float32) for vec in vecs],
+        in_specs=[pl.BlockSpec(memory_space=pltpu.SMEM)] * 2
+        + vmem(chunks)
+        + [pl.BlockSpec(memory_space=pl.ANY)],
+        out_specs=vmem(1 + chunks),
+        scratch_shapes=[
+            pltpu.VMEM(hamiltonian.shape, hamiltonian.dtype),
+            pltpu.SemaphoreType.DMA((count,)),
         ],
-        in_specs=[pl.BlockSpec(memory_space=pltpu.SMEM)] * 2 + vmem(2),
-        out_specs=vmem(2),
-        compiler_params=pltpu.CompilerParams(vmem_limit_bytes=32 << 20),
+        compiler_params=pltpu.CompilerParams(vmem_limit_bytes=43 << 20),
         cost_estimate=pl.CostEstimate(
-            flops=2 * owned * count * width * width * 5,
+            flops=10 * chunks * vecs[0].shape[0] * count * width * width,
             bytes_accessed=count * faces * width * width * 4,
             transcendentals=0,
         ),
-    )(loc, odd, vec, hamiltonian)
+    )(loc, odd, *vecs, hamiltonian)
 
 
 def own_kernel(loc_ref, vec_ref, turned_ref, out_ref):
@@ -134,23 +150,24 @@
     )(loc, near, far, acc, vec, prior, turned)
 
 
-def own_gram_kernel(own_ref, high_ref, out_ref):
-    high = high_ref[...]
-    low = (own_ref[...] - high.astype(jnp.float32)).astype(jnp.bfloat16)
+def own_gram_kernel(chunks, *refs):
+    own_refs, high_refs, out_ref = refs[:chunks], refs[chunks:-1], refs[-1]
+    high = stacked(high_refs)
+    low = (stacked(own_refs) - high.astype(jnp.float32)).astype(jnp.bfloat16)
     mixed = dot_nt(high, low)
     out_ref[...] = dot_nt(high, high) + (mixed + mixed.T)
 
 
-def cross_gram_kernel(place_ref, own_ref, other_ref, after_ref, out_ref):
-    del after_ref
+def cross_gram_kernel(chunks, place_ref, *refs):
+    own_refs, other_refs, out_ref = refs[:chunks], refs[chunks:-2], refs[-1]
 
     @pl.when(place_ref[0] == 0)
     def _():
-        out_ref[...] = dot_nt(other_ref[...], own_ref[...])
+        out_ref[...] = dot_nt(stacked(other_refs), stacked(own_refs))
 
     @pl.when(place_ref[0] != 0)
     def _():
-        out_ref[...] = dot_nt(own_ref[...], other_ref[...])
+        out_ref[...] = dot_nt(stacked(own_refs), stacked(other_refs))
 
 
 def tree(terms):
@@ -309,11 +326,10 @@
     )(place, own, other, cross, first, first_inv)
 
 
-def finish_kernel(
-    place_ref, own_ref, other_ref, cross_ref, first_ref, first_inv_ref, wide_ref, high_ref, away_ref,
-    upper_ref, basis_ref, work, right, inverse, part, result, sems,
-):
-    half, total = wide_ref.shape
+def finish_kernel(chunks, place_ref, own_ref, other_ref, cross_ref, first_ref, first_inv_ref, *refs):
+    wides, highs, aways = refs[:chunks], refs[chunks : 2 * chunks], refs[2 * chunks : 3 * chunks]
+    upper_ref, basis_ref, work, right, inverse, part, result, sems = refs[3 * chunks :]
+    half, total = result.shape
     pieces = sems.shape[0]
     spans = [slice(i * (total // pieces), (i + 1) * (total // pieces)) for i in range(pieces)]
     leading = place_ref[0] == 0
@@ -334,8 +350,8 @@
     @pl.when(leading)
     def _():
         for copy, here in zip(copies, spans):
-            high = high_ref[:, here]
-            low = (wide_ref[:, here] - high.astype(jnp.float32)).astype(jnp.bfloat16)
+            high = stacked(highs, here)
+            low = (stacked(wides, here) - high.astype(jnp.float32)).astype(jnp.bfloat16)
             result[:, here] = product(first_inv_ref[...], high, low)
             copy.start()
 
@@ -345,8 +361,8 @@
     high_mix, low_mix = split(dot_full(lower, first_inv_ref[...]))
     mixes = jnp.concatenate([high_mix, low_mix], axis=1)
     for here in spans:
-        away = away_ref[:, here]
-        part[:, here] = wide_ref[:, here] - dot(mixes, jnp.concatenate([away, away], axis=0))
+        away = stacked(aways, here)
+        part[:, here] = stacked(wides, here) - dot(mixes, jnp.concatenate([away, away], axis=0))
     upper_ref[0:half, 0:half] = first_ref[...]
     upper_ref[0:half, half:] = lower.T
     upper_ref[half:, 0:half] = jnp.zeros((half, half), jnp.float32)
@@ -363,22 +379,22 @@
 
 
 def finish(place, own, other, cross, first, first_inv, wide, high, away):
-    half, total = wide.shape
+    half, total = own.shape[0], wide[0].shape[1]
     pieces = 4 if total % 512 == 0 else 1
     tile = pltpu.VMEM((half, half), jnp.float32)
     return pl.pallas_call(
-        finish_kernel,
+        functools.partial(finish_kernel, len(wide)),
         out_shape=[
             jax.ShapeDtypeStruct((2 * half, 2 * half), jnp.float32),
-            jax.ShapeDtypeStruct(wide.shape, jnp.float32),
+            jax.ShapeDtypeStruct((half, total), jnp.float32),
         ],
-        in_specs=[pl.BlockSpec(memory_space=pltpu.SMEM)] + vmem(8),
+        in_specs=[pl.BlockSpec(memory_space=pltpu.SMEM)] + vmem(5 + 3 * len(wide)),
         out_specs=vmem(1) + [pl.BlockSpec(memory_space=pl.ANY)],
         scratch_shapes=[tile] * 3
         + [pltpu.VMEM((half, total), jnp.float32)] * 2
         + [pltpu.SemaphoreType.DMA((pieces,))],
         compiler_params=pltpu.CompilerParams(vmem_limit_bytes=24 << 20),
-    )(place, own, other, cross, first, first_inv, wide, high, away)
+    )(place, own, other, cross, first, first_inv, *wide, *high, *away)
 
 
 def shards(hamiltonian, orbitals, adjacency):
@@ -387,6 +403,8 @@
     blocks = lax.axis_size("space")
     groups = lax.axis_size("orb")
     half = owned * groups // 2
+    chunks = 2
+    share = owned // chunks
     odd = lax.axis_index("space").astype(jnp.int32).reshape(1) % 2
     loc = adjacency % count
     swapped = jnp.concatenate([loc[:, 1:2], loc[:, 0:1], loc[:, 2:]], axis=1)
@@ -395,17 +413,25 @@
     far_pairs = [(i, (i + 1 if i % 2 else i - 1) % blocks) for i in range(blocks)]
     smem = [pl.BlockSpec(memory_space=pltpu.SMEM)]
 
-    def halo(vec):
+    def level(number, vec, prior, turned):
         far = lax.ppermute(vec, "space", far_pairs)
-        return lax.ppermute(vec, "space", near_pairs), far
-
-    side = halo(orbitals)
-    turned, acc = turn_part(orbitals, hamiltonian, loc, odd)
-    (one,) = halo_part(1, *side, acc, orbitals, orbitals, turned, loc)
-    side = halo(one)
-    (two,) = halo_part(2, *side, own_part(one, turned, loc), one, orbitals, turned, loc)
-    side = halo(two)
-    filtered, narrow = halo_part(3, *side, own_part(two, turned, loc), two, one, turned, loc)
+        near = lax.ppermute(vec, "space", near_pairs)
+        acc = own_part(vec, turned, loc)
+        return halo_part(number, near, far, acc, vec, prior, turned, loc)
+
+    zero = [orbitals[piece * share : (piece + 1) * share] for piece in range(chunks)]
+    fars = [lax.ppermute(vec, "space", far_pairs) for vec in zero]
+    nears = [lax.ppermute(vec, "space", near_pairs) for vec in zero]
+    turned, *accs = turn_part(zero, hamiltonian, loc, odd)
+    one, two, filtered, narrow = [], [], [], []
+    for base, near, far, acc in zip(zero, nears, fars, accs):
+        one += halo_part(1, near, far, acc, base, base, turned, loc)
+    for vec, prior in zip(one, zero):
+        two += level(2, vec, prior, turned)
+    for vec, prior in zip(two, one):
+        wide, short = level(3, vec, prior, turned)
+        filtered.append(wide)
+        narrow.append(short)
 
     steps = [1 << i for i in range((blocks - 1).bit_length())]
     stages = [steps[:1]] + [steps[i : i + 2] for i in range(1, len(steps), 2)]
@@ -425,24 +451,24 @@
     place = lax.axis_index("orb").astype(jnp.int32).reshape(1)
     if groups == 2:
         swap = [(0, 1), (1, 0)]
-        other = lax.ppermute(narrow, "orb", swap)
+        other = [lax.ppermute(piece, "orb", swap) for piece in narrow]
         tile = jax.ShapeDtypeStruct((half, half), jnp.float32)
         params = pltpu.CompilerParams(vmem_limit_bytes=24 << 20)
         near = pl.pallas_call(
-            own_gram_kernel,
+            functools.partial(own_gram_kernel, chunks),
             out_shape=tile,
-            in_specs=vmem(2),
+            in_specs=vmem(2 * chunks),
             out_specs=pl.BlockSpec(memory_space=pltpu.VMEM),
             compiler_params=params,
-        )(filtered, narrow)
+        )(*filtered, *narrow)
         near = summed(near, stages[:1])
         cross = pl.pallas_call(
-            cross_gram_kernel,
+            functools.partial(cross_gram_kernel, chunks),
             out_shape=tile,
-            in_specs=smem + vmem(2) + [pl.BlockSpec(memory_space=pl.ANY)],
+            in_specs=smem + vmem(2 * chunks) + [pl.BlockSpec(memory_space=pl.ANY)],
             out_specs=pl.BlockSpec(memory_space=pltpu.VMEM),
             compiler_params=params,
-        )(place, narrow, other, near)
+        )(place, *narrow, *other, near)
         near = summed(near, stages[1:])
         far = lax.ppermute(near, "orb", swap)
         cross = summed(cross, stages[:-1])
@@ -450,14 +476,14 @@
         cross = summed(cross, stages[-1:])
         upper, basis = finish(place, near, far, cross, first, first_inv, filtered, narrow, other)
     else:
-        columns = lax.all_gather(narrow, "orb", axis=0, tiled=True)
+        columns = lax.all_gather(jnp.concatenate(narrow), "orb", axis=0, tiled=True)
         whole = summed(dot_nt(columns, columns), stages)
         blocks_of = (jnp.zeros_like(place), whole[:half, :half], whole[half:, half:])
         first, first_inv = factor_first(*blocks_of, whole)
         upper, inverse = factor_second(*blocks_of, whole[:half, half:], first, first_inv)
         mine = lax.dynamic_slice_in_dim(inverse, place[0] * owned, owned, 0)
         near = lax.dynamic_slice_in_dim(mine, place[0] * owned, owned, 1)
-        rest = filtered - narrow.astype(jnp.float32)
+        rest = jnp.concatenate(filtered) - jnp.concatenate(narrow).astype(jnp.float32)
         basis = dot_full(mine, columns.astype(jnp.float32)) + dot_full(near, rest)
     return (basis, upper)
 

time: 78.7 us -> 77.3 us (0.982)
  Pallas kernels: 21.1 us -> 29.8 us
  starting transfers between devices: 39.9 us -> 35.8 us
  local copies, waits for them, and re-layouts: 4.27 us -> 1.21 us
  waiting for transfers between devices: 10.7 us -> 7.71 us
    ppermute x10, starting transfers between devices: 18.9 us -> 12 us  [moved(): return lax.ppermute(part, 'space', [(i, i ^ step) for i in range(blocks)])]
    unnamed x6 -> x0, local copies, waits for them, and re-layouts: 4.13 us -> none
    ppermute x7 -> x14, waiting for transfers between devices: 7.42 us -> 3.82 us  [the longest x2 3.79 us: shards(): other = [lax.ppermute(piece, 'orb', swap) for piece in narrow]]
    pallas_call x2 -> x4, Pallas kernels: 3.01 us -> 6.54 us  [own_part(): pl.pallas_call(own_kernel, out_shape=jax.ShapeDtypeStruct(vec.shape, jnp....]
    ppermute x7 -> x14, starting transfers between devices: 19.6 us -> 22.8 us  [the longest x4 12.8 us: level(): far = lax.ppermute(vec, 'space', far_pairs)]
    pallas_call x3 -> x6, Pallas kernels: 3.5 us -> 6.75 us  [halo_part(): pl.pallas_call(functools.partial(halo_kernel, level), out_shape=[jax.Shap...]
    pallas_call x4, Pallas kernels: 10.3 us -> 12.2 us  [the longest x1 6.56 us: finish(): pl.pallas_call(functools.partial(finish_kernel, len(wide)), out_shape=[ja...]
    slice x0 -> x1, local copies, waits for them, and re-layouts: none -> 1.07 us  [shards(): orbitals[piece * share:(piece + 1) * share]]
  transfers between devices with their start and end apart: 18 -> 25, of which waited for: 8 -> 7; matrix products, arithmetic and copies ran while one was open for 2% -> 2% of each run, Pallas kernels for 14% -> 30%
where the time goes in v14:
time: 77.3 us; the launch traced here: 77.1 us
  starting transfers between devices  35.8 us (46%)
  Pallas kernels  29.8 us (39%)
  waiting for transfers between devices  7.71 us (10%)
  other arithmetic  1.53 us (2%)
  local copies, waits for them, and re-layouts  1.21 us (2%)
  between operations  1.05 us (1%)
    ppermute x4, starting transfers between devices, level(): far = lax.ppermute(vec, 'space', far_pairs)  12.8 us
    ppermute x10, starting transfers between devices, moved(): return lax.ppermute(part, 'space', [(i, i ^ step) for i in range(blocks)])  12 us
    pallas_call x6, Pallas kernels, halo_part(): pl.pallas_call(functools.partial(halo_kernel, level), out_shape=[jax.Shap...  6.75 us
    pallas_call x1, Pallas kernels, finish(): pl.pallas_call(functools.partial(finish_kernel, len(wide)), out_shape=[ja...  6.56 us
    pallas_call x4, Pallas kernels, own_part(): pl.pallas_call(own_kernel, out_shape=jax.ShapeDtypeStruct(vec.shape, jnp....  6.54 us
    ppermute x2, starting transfers between devices, shards(): fars = [lax.ppermute(vec, 'space', far_pairs) for vec in zero]  6.29 us
    pallas_call x1, Pallas kernels, turn_part(): pl.pallas_call(functools.partial(turn_kernel, chunks), out_shape=[jax.Sha...  4.85 us
    pallas_call x1, Pallas kernels, factor_first(): pl.pallas_call(first_kernel, out_shape=[jax.ShapeDtypeStruct((half, half)...  4.29 us
  transfers between devices with their start and end apart: 25, of which 7 were waited for; matrix products, arithmetic and copies ran while one was open for 2% of the time, Pallas kernels for 30%

profile of v14, /device:TPU:0, one launch (start us, length us, event | category | flops | bytes accessed | tf_op | source)
XLA Modules:
  0.0 77.1 jit_solution(16786302310108333719)
XLA Ops:
  0.6 1.1 %fusion.1 = (bf16[64,2048]{1,0:T(8,128)(2,1)S(1)}, bf16[64,2048]{1,0:T(8,128)(2,1)S(1)}) fusion(bf16[128,2048]{1,0:T(8,128)(2,1)} %param.4), kind=kLoop, calls=%fused_computation.7 | loop fusion | bytes 1048576 | tf_op jit(solution)/shard_map/slice | solution.py:422
  1.7 0.5 collective-permute-start
  2.2 5.7 %collective-permute-start.1 = (bf16[64,2048]{1,0:T(8,128)(2,1)S(1)}, bf16[64,2048]{1,0:T(8,128)(2,1)S(1)}, u32[]{:S(2)}, u32[]{:S(2)}) collective-permute-start(bf16[64,2048]{1,0:T(8,128)(2,1)S(1)} %get-tuple-element.25.refs_0_.vec_ref.prior_ref), channel_id=1, source_target_pairs={{0,30},{2,4},{4,2},{6,8},{8,6},{10,12},{12,10},{14,16},{16,14},{18... | collective-permute-start | bytes 786440 | tf_op jit(solution)/shard_map/ppermute | solution.py:423
  7.9 0.0 collective-permute-start.6
  7.9 0.6 collective-permute-start.7
  8.5 0.7 add_select_fusion
  9.2 0.1 slice.17
  9.3 0.1 fusion.2
  9.3 0.8 add_select_fusion.1.loc_ref
  10.1 4.9 %shard_map.50 = (bf16[8,7,256,256]{3,2,1,0:T(8,128)(2,1)S(1)}, f32[64,2048]{1,0:T(8,128)S(1)}, f32[64,2048]{1,0:T(8,128)S(1)}) custom-call(s32[8,6]{1,0:T(8,128)S(1)} %add_select_fusion.1.loc_ref, s32[1]{0:T(128)S(6)} %select_n.21.odd_ref, bf16[64,2048]{1,0:T(8,128)(2,1)S(1)} %get-tuple-element.25.refs_0_.vec_ref.prior_ref, ...), custom_call_target="tpu_custom_call" | custom-call | flops 671088640 | bytes 14680064 | tf_op jit(solution)/shard_map/pallas_call | solution.py:67
  15.0 0.0 collective-permute-done.near_ref
  15.0 0.0 collective-permute-done.1.far_ref
  15.0 1.1 %shard_map.51.vec_ref.prior_ref = bf16[64,2048]{1,0:T(8,128)(2,1)S(1)} custom-call(s32[8,6]{1,0:T(8,128)S(1)} %add_select_fusion.1.loc_ref, bf16[64,2048]{1,0:T(8,128)(2,1)S(1)} %collective-permute-done.near_ref, bf16[64,2048]{1,0:T(8,128)(2,1)S(1)} %collective-permute-done.1.far_ref, f32[64,2048]{1,0:T(8,128)S(1)} %get-tuple-element.13.acc_ref, ...), custom_call_target="tpu_custom_call" | custom-call | flops 134217728 | bytes 2097152 | tf_op jit(solution)/shard_map/pallas_call | solution.py:139
  16.1 0.1 collective-permute-start.2
  16.2 3.9 %collective-permute-start.3 = (bf16[64,2048]{1,0:T(8,128)(2,1)S(1)}, bf16[64,2048]{1,0:T(8,128)(2,1)S(1)}, u32[]{:S(2)}, u32[]{:S(2)}) collective-permute-start(bf16[64,2048]{1,0:T(8,128)(2,1)S(1)} %shard_map.51.vec_ref.prior_ref), channel_id=1, source_target_pairs={{0,30},{2,4},{4,2},{6,8},{8,6},{10,12},{12,10},{14,16},{16,14},{18... | collective-permute-start | bytes 786440 | tf_op jit(solution)/shard_map/ppermute | solution.py:417
  20.1 0.0 collective-permute-done.6.near_ref
  20.1 0.0 collective-permute-done.7.far_ref
  20.1 1.1 %shard_map.56.vec_ref.prior_ref = bf16[64,2048]{1,0:T(8,128)(2,1)S(1)} custom-call(s32[8,6]{1,0:T(8,128)S(1)} %add_select_fusion.1.loc_ref, bf16[64,2048]{1,0:T(8,128)(2,1)S(1)} %collective-permute-done.6.near_ref, bf16[64,2048]{1,0:T(8,128)(2,1)S(1)} %collective-permute-done.7.far_ref, f32[64,2048]{1,0:T(8,128)S(1)} %get-tuple-element.16.acc_ref, ...), custom_call_target="tpu_custom_call" | custom-call | flops 134217728 | bytes 2097152 | tf_op jit(solution)/shard_map/pallas_call | solution.py:139
  21.2 0.1 collective-permute-start.8
  21.3 2.1 %collective-permute-start.9 = (bf16[64,2048]{1,0:T(8,128)(2,1)S(1)}, bf16[64,2048]{1,0:T(8,128)(2,1)S(1)}, u32[]{:S(2)}, u32[]{:S(2)}) collective-permute-start(bf16[64,2048]{1,0:T(8,128)(2,1)S(1)} %shard_map.56.vec_ref.prior_ref), channel_id=1, source_target_pairs={{0,30},{2,4},{4,2},{6,8},{8,6},{10,12},{12,10},{14,16},{16,14},{18... | collective-permute-start | bytes 786440 | tf_op jit(solution)/shard_map/ppermute | solution.py:417
  23.4 1.6 %shard_map.52.acc_ref = f32[64,2048]{1,0:T(8,128)S(1)} custom-call(s32[8,6]{1,0:T(8,128)S(1)} %add_select_fusion.1.loc_ref, bf16[64,2048]{1,0:T(8,128)(2,1)S(1)} %shard_map.51.vec_ref.prior_ref, bf16[8,7,256,256]{3,2,1,0:T(8,128)(2,1)S(1)} %get-tuple-element.14.turned_ref), custom_call_target="tpu_custom_call" | custom-call | flops 335544320 | bytes 5242880 | tf_op jit(solution)/shard_map/pallas_call | solution.py:104
  25.0 1.6 %shard_map.57.acc_ref = f32[64,2048]{1,0:T(8,128)S(1)} custom-call(s32[8,6]{1,0:T(8,128)S(1)} %add_select_fusion.1.loc_ref, bf16[64,2048]{1,0:T(8,128)(2,1)S(1)} %shard_map.56.vec_ref.prior_ref, bf16[8,7,256,256]{3,2,1,0:T(8,128)(2,1)S(1)} %get-tuple-element.14.turned_ref), custom_call_target="tpu_custom_call" | custom-call | flops 335544320 | bytes 5242880 | tf_op jit(solution)/shard_map/pallas_call | solution.py:104
  26.6 0.0 collective-permute-done.2.near_ref
  26.7 1.1 %shard_map.53.vec_ref = bf16[64,2048]{1,0:T(8,128)(2,1)S(1)} custom-call(s32[8,6]{1,0:T(8,128)S(1)} %add_select_fusion.1.loc_ref, bf16[64,2048]{1,0:T(8,128)(2,1)S(1)} %collective-permute-done.2.near_ref, bf16[64,2048]{1,0:T(8,128)(2,1)S(1)} %collective-permute-done.3.far_ref, f32[64,2048]{1,0:T(8,128)S(1)} %shard_map.52.acc_ref, ...), custom_call_target="tpu_custom_call" | custom-call | flops 134217728 | bytes 2097152 | tf_op jit(solution)/shard_map/pallas_call | solution.py:139
  27.8 0.2 collective-permute-start.4
  28.0 3.9 %collective-permute-start.5 = (bf16[64,2048]{1,0:T(8,128)(2,1)S(1)}, bf16[64,2048]{1,0:T(8,128)(2,1)S(1)}, u32[]{:S(2)}, u32[]{:S(2)}) collective-permute-start(bf16[64,2048]{1,0:T(8,128)(2,1)S(1)} %shard_map.53.vec_ref), channel_id=1, source_target_pairs={{0,30},{2,4},{4,2},{6,8},{8,6},{10,12},{12,10},{14,16},{16,14},{18... | collective-permute-start | bytes 786440 | tf_op jit(solution)/shard_map/ppermute | solution.py:417
  31.9 1.1 %shard_map.58.vec_ref = bf16[64,2048]{1,0:T(8,128)(2,1)S(1)} custom-call(s32[8,6]{1,0:T(8,128)S(1)} %add_select_fusion.1.loc_ref, bf16[64,2048]{1,0:T(8,128)(2,1)S(1)} %collective-permute-done.8.near_ref, bf16[64,2048]{1,0:T(8,128)(2,1)S(1)} %collective-permute-done.9.far_ref, f32[64,2048]{1,0:T(8,128)S(1)} %shard_map.57.acc_ref, ...), custom_call_target="tpu_custom_call" | custom-call | flops 134217728 | bytes 2097152 | tf_op jit(solution)/shard_map/pallas_call | solution.py:139
  33.0 0.1 collective-permute-start.10
  33.1 2.9 %collective-permute-start.11 = (bf16[64,2048]{1,0:T(8,128)(2,1)S(1)}, bf16[64,2048]{1,0:T(8,128)(2,1)S(1)}, u32[]{:S(2)}, u32[]{:S(2)}) collective-permute-start(bf16[64,2048]{1,0:T(8,128)(2,1)S(1)} %shard_map.58.vec_ref), channel_id=1, source_target_pairs={{0,30},{2,4},{4,2},{6,8},{8,6},{10,12},{12,10},{14,16},{16,14},{18... | collective-permute-start | bytes 786440 | tf_op jit(solution)/shard_map/ppermute | solution.py:417
  36.1 1.6 %shard_map.54.acc_ref = f32[64,2048]{1,0:T(8,128)S(1)} custom-call(s32[8,6]{1,0:T(8,128)S(1)} %add_select_fusion.1.loc_ref, bf16[64,2048]{1,0:T(8,128)(2,1)S(1)} %shard_map.53.vec_ref, bf16[8,7,256,256]{3,2,1,0:T(8,128)(2,1)S(1)} %get-tuple-element.14.turned_ref), custom_call_target="tpu_custom_call" | custom-call | flops 335544320 | bytes 5242880 | tf_op jit(solution)/shard_map/pallas_call | solution.py:104
  37.7 1.6 %shard_map.59.acc_ref = f32[64,2048]{1,0:T(8,128)S(1)} custom-call(s32[8,6]{1,0:T(8,128)S(1)} %add_select_fusion.1.loc_ref, bf16[64,2048]{1,0:T(8,128)(2,1)S(1)} %shard_map.58.vec_ref, bf16[8,7,256,256]{3,2,1,0:T(8,128)(2,1)S(1)} %get-tuple-element.14.turned_ref), custom_call_target="tpu_custom_call" | custom-call | flops 335544320 | bytes 5242880 | tf_op jit(solution)/shard_map/pallas_call | solution.py:104
  39.4 1.1 %shard_map.55 = (f32[64,2048]{1,0:T(8,128)S(1)}, bf16[64,2048]{1,0:T(8,128)(2,1)S(1)}) custom-call(s32[8,6]{1,0:T(8,128)S(1)} %add_select_fusion.1.loc_ref, bf16[64,2048]{1,0:T(8,128)(2,1)S(1)} %collective-permute-done.4.near_ref, bf16[64,2048]{1,0:T(8,128)(2,1)S(1)} %collective-permute-done.5.far_ref, f32[64,2048]{1,0:T(8,128)S(1)} %shard_map.54.acc_ref, ...), custom_call_target="tpu_custom_call" | custom-call | flops 134217728 | bytes 2097152 | tf_op jit(solution)/shard_map/pallas_call | solution.py:139
  40.5 1.6 %collective-permute-start.18 = (bf16[64,2048]{1,0:T(8,128)(2,1)S(1)}, bf16[64,2048]{1,0:T(8,128)(2,1)S(1)}, u32[]{:S(2)}, u32[]{:S(2)}) collective-permute-start(bf16[64,2048]{1,0:T(8,128)(2,1)S(1)} %get-tuple-element.18.refs_2_.refs_0_), channel_id=1, source_target_pairs={{0,1},{1,0},{2,3},{3,2},{4,5},{5,4},{6,7},{7,6},{8,9},{9,8},{10,11... | collective-permute-start | bytes 786440 | tf_op jit(solution)/shard_map/ppermute | solution.py:454
  42.1 0.0 collective-permute-done.10.near_ref
  42.1 0.0 collective-permute-done.11.far_ref
  42.1 1.1 %shard_map.60 = (f32[64,2048]{1,0:T(8,128)S(1)}, bf16[64,2048]{1,0:T(8,128)(2,1)S(1)}) custom-call(s32[8,6]{1,0:T(8,128)S(1)} %add_select_fusion.1.loc_ref, bf16[64,2048]{1,0:T(8,128)(2,1)S(1)} %collective-permute-done.10.near_ref, bf16[64,2048]{1,0:T(8,128)(2,1)S(1)} %collective-permute-done.11.far_ref, f32[64,2048]{1,0:T(8,128)S(1)} %shard_map.59.acc_ref, ...), custom_call_target="tpu_custom_call" | custom-call | flops 134217728 | bytes 2097152 | tf_op jit(solution)/shard_map/pallas_call | solution.py:139
  43.2 1.3 %collective-permute-start.19 = (bf16[64,2048]{1,0:T(8,128)(2,1)S(1)}, bf16[64,2048]{1,0:T(8,128)(2,1)S(1)}, u32[]{:S(2)}, u32[]{:S(2)}) collective-permute-start(bf16[64,2048]{1,0:T(8,128)(2,1)S(1)} %get-tuple-element.19.refs_3_.refs_1_), channel_id=1, source_target_pairs={{0,1},{1,0},{2,3},{3,2},{4,5},{5,4},{6,7},{7,6},{8,9},{9,8},{10,11... | collective-permute-start | bytes 786440 | tf_op jit(solution)/shard_map/ppermute | solution.py:454
  44.5 0.5 shard_map.61
  45.0 1.1 %collective-permute-start.12 = (f32[128,128]{1,0:T(8,128)S(1)}, f32[128,128]{1,0:T(8,128)S(1)}, u32[]{:S(2)}, u32[]{:S(2)}) collective-permute-start(f32[128,128]{1,0:T(8,128)S(1)} %shard_map.61), channel_id=1, source_target_pairs={{0,2},{2,0},{4,6},{6,4},{8,10},{10,8},{12,14},{14,12},{16,18},{18,... | collective-permute-start | bytes 196616 | tf_op jit(solution)/shard_map/ppermute | solution.py:441
  46.1 0.9 %collective-permute-done.12 = f32[128,128]{1,0:T(8,128)S(1)} collective-permute-done((f32[128,128]{1,0:T(8,128)S(1)}, f32[128,128]{1,0:T(8,128)S(1)}, u32[]{:S(2)}, u32[]{:S(2)}) %collective-permute-start.12) | collective-permute-done | bytes 65568 | tf_op jit(solution)/shard_map/ppermute | solution.py:441
  47.0 2.2 %collective-permute-start.14 = (f32[128,128]{1,0:T(8,128)S(1)}, f32[128,128]{1,0:T(8,128)S(1)}, u32[]{:S(2)}, u32[]{:S(2)}) collective-permute-start(f32[128,128]{1,0:T(8,128)S(1)} %add.44.refs_4_), channel_id=1, source_target_pairs={{0,8},{2,10},{4,12},{6,14},{8,0},{10,2},{12,4},{14,6},{16,24},{18,... | collective-permute-start | bytes 196616 | tf_op jit(solution)/shard_map/ppermute | solution.py:441
  49.2 1.6 %collective-permute-start.15 = (f32[128,128]{1,0:T(8,128)S(1)}, f32[128,128]{1,0:T(8,128)S(1)}, u32[]{:S(2)}, u32[]{:S(2)}) collective-permute-start(f32[128,128]{1,0:T(8,128)S(1)} %add.44.refs_4_), channel_id=1, source_target_pairs={{0,12},{2,14},{4,8},{6,10},{8,4},{10,6},{12,0},{14,2},{16,28},{18,... | collective-permute-start | bytes 196616 | tf_op jit(solution)/shard_map/ppermute | solution.py:441
  50.8 0.0 collective-permute-start.13
  50.8 0.0 collective-permute-done.18.refs_2_.refs_4_
  50.8 3.8 %collective-permute-done.19.refs_3_.refs_5_ = bf16[64,2048]{1,0:T(8,128)(2,1)S(1)} collective-permute-done((bf16[64,2048]{1,0:T(8,128)(2,1)S(1)}, bf16[64,2048]{1,0:T(8,128)(2,1)S(1)}, u32[]{:S(2)}, u32[]{:S(2)}) %collective-permute-start.19) | collective-permute-done | bytes 262176 | tf_op jit(solution)/shard_map/ppermute | solution.py:454
  54.5 0.3 shard_map.62
  54.9 0.1 collective-permute-start.20
  54.9 0.0 collective-permute-done.14
  55.0 0.6 collective-permute-done.13
  55.6 2.5 %collective-permute-start.16 = (f32[128,128]{1,0:T(8,128)S(1)}, f32[128,128]{1,0:T(8,128)S(1)}, u32[]{:S(2)}, u32[]{:S(2)}) collective-permute-start(f32[128,128]{1,0:T(8,128)S(1)} %add_add_fusion.1), channel_id=1, source_target_pairs={{0,16},{2,18},{4,20},{6,22},{8,24},{10,26},{12,28},{14,30},{16,0},... | collective-permute-start | bytes 196616 | tf_op jit(solution)/shard_map/ppermute | solution.py:441
  58.2 0.0 collective-permute-done.20
  58.2 0.6 collective-permute-start.22
  58.8 1.5 %collective-permute-start.23 = (f32[128,128]{1,0:T(8,128)S(1)}, f32[128,128]{1,0:T(8,128)S(1)}, u32[]{:S(2)}, u32[]{:S(2)}) collective-permute-start(f32[128,128]{1,0:T(8,128)S(1)} %add.49), channel_id=1, source_target_pairs={{0,12},{2,14},{4,8},{6,10},{8,4},{10,6},{12,0},{14,2},{16,28},{18,... | collective-permute-start | bytes 196616 | tf_op jit(solution)/shard_map/ppermute | solution.py:441
  60.3 1.5 %collective-permute-start.21 = (f32[128,128]{1,0:T(8,128)S(1)}, f32[128,128]{1,0:T(8,128)S(1)}, u32[]{:S(2)}, u32[]{:S(2)}) collective-permute-start(f32[128,128]{1,0:T(8,128)S(1)} %add.49), channel_id=1, source_target_pairs={{0,4},{2,6},{4,0},{6,2},{8,12},{10,14},{12,8},{14,10},{16,20},{18,... | collective-permute-start | bytes 196616 | tf_op jit(solution)/shard_map/ppermute | solution.py:441
  61.7 0.0 collective-permute-done.16
  61.7 1.0 %collective-permute-start.17 = (f32[128,128]{1,0:T(8,128)S(1)}, f32[128,128]{1,0:T(8,128)S(1)}, u32[]{:S(2)}, u32[]{:S(2)}) collective-permute-start(f32[128,128]{1,0:T(8,128)S(1)} %add.48.own_ref), channel_id=1, source_target_pairs={{0,1},{1,0},{2,3},{3,2},{4,5},{5,4},{6,7},{7,6},{8,9},{9,8},{10,11... | collective-permute-start | bytes 196616 | tf_op jit(solution)/shard_map/ppermute | solution.py:473
  62.8 0.5 collective-permute-done.22
  63.2 0.7 collective-permute-done.23
  64.0 0.7 collective-permute-done.21
  64.7 1.0 %collective-permute-start.24 = (f32[128,128]{1,0:T(8,128)S(1)}, f32[128,128]{1,0:T(8,128)S(1)}, u32[]{:S(2)}, u32[]{:S(2)}) collective-permute-start(f32[128,128]{1,0:T(8,128)S(1)} %add_add_fusion.after_ref), channel_id=1, source_target_pairs={{0,16},{2,18},{4,20},{6,22},{8,24},{10,26},{12,28},{14,30},{16,0},... | collective-permute-start | bytes 196616 | tf_op jit(solution)/shard_map/ppermute | solution.py:441
  65.7 0.4 collective-permute-done.17.other_ref
  66.1 4.3 %shard_map.63 = (f32[128,128]{1,0:T(8,128)S(1)}, f32[128,128]{1,0:T(8,128)S(1)}) custom-call(s32[1]{0:T(128)} %bitcast.place_ref, f32[128,128]{1,0:T(8,128)S(1)} %add.48.own_ref, f32[128,128]{1,0:T(8,128)S(1)} %collective-permute-done.17.other_ref, f32[128,128]{1,0:T(8,128)S(1)} %add_add_fusion.after_ref), custom_call_target="tpu_custom_call" | custom-call | flops 4194304 | bytes 16777216 | tf_op jit(solution)/shard_map/pallas_call | solution.py:304
  70.4 0.0 collective-permute-done.24
  70.4 6.6 %shard_map.64 = (f32[256,256]{1,0:T(8,128)}, f32[128,2048]{1,0:T(8,128)}) custom-call(s32[1]{0:T(128)} %bitcast.place_ref, f32[128,128]{1,0:T(8,128)S(1)} %add.48.own_ref, f32[128,128]{1,0:T(8,128)S(1)} %collective-permute-done.17.other_ref, f32[128,128]{1,0:T(8,128)S(1)} %add.53.cross_ref, f32[128,128]{1,0:T(8,128)S(1)} %get-tuple-element.20.first_ref, ...), custom_call_target="tpu_custom_call" | custom-call | tf_op jit(solution)/shard_map/pallas_call | solution.py:385
  (12 shorter events, 0.1 us)
Async XLA Ops:
  1.7 13.3 %collective-permute-start = (bf16[64,2048]{1,0:T(8,128)(2,1)S(1)}, bf16[64,2048]{1,0:T(8,128)(2,1)S(1)}, u32[]{:S(2)}, u32[]{:S(2)}) collective-permute-start(bf16[64,2048]{1,0:T(8,128)(2,1)S(1)} %get-tuple-element.25.refs_0_.vec_ref.prior_ref), channel_id=1, source_target_pairs={{0,2},{2,0},{4,6},{6,4},{8,10},{10,8},{12,14},{14,12},{16,18},{18,... | collective-permute-start | bytes 786440 | tf_op jit(solution)/shard_map/ppermute | solution.py:424
  2.2 12.8 %collective-permute-start.1 = (bf16[64,2048]{1,0:T(8,128)(2,1)S(1)}, bf16[64,2048]{1,0:T(8,128)(2,1)S(1)}, u32[]{:S(2)}, u32[]{:S(2)}) collective-permute-start(bf16[64,2048]{1,0:T(8,128)(2,1)S(1)} %get-tuple-element.25.refs_0_.vec_ref.prior_ref), channel_id=1, source_target_pairs={{0,30},{2,4},{4,2},{6,8},{8,6},{10,12},{12,10},{14,16},{16,14},{18... | collective-permute-start | bytes 786440 | tf_op jit(solution)/shard_map/ppermute | solution.py:423
  7.9 12.2 %collective-permute-start.6 = (bf16[64,2048]{1,0:T(8,128)(2,1)S(1)}, bf16[64,2048]{1,0:T(8,128)(2,1)S(1)}, u32[]{:S(2)}, u32[]{:S(2)}) collective-permute-start(bf16[64,2048]{1,0:T(8,128)(2,1)S(1)} %get-tuple-element.24.refs_1_.vec_ref.prior_ref), channel_id=1, source_target_pairs={{0,2},{2,0},{4,6},{6,4},{8,10},{10,8},{12,14},{14,12},{16,18},{18,... | collective-permute-start | bytes 786440 | tf_op jit(solution)/shard_map/ppermute | solution.py:424
  7.9 12.2 %collective-permute-start.7 = (bf16[64,2048]{1,0:T(8,128)(2,1)S(1)}, bf16[64,2048]{1,0:T(8,128)(2,1)S(1)}, u32[]{:S(2)}, u32[]{:S(2)}) collective-permute-start(bf16[64,2048]{1,0:T(8,128)(2,1)S(1)} %get-tuple-element.24.refs_1_.vec_ref.prior_ref), channel_id=1, source_target_pairs={{0,30},{2,4},{4,2},{6,8},{8,6},{10,12},{12,10},{14,16},{16,14},{18... | collective-permute-start | bytes 786440 | tf_op jit(solution)/shard_map/ppermute | solution.py:423
  16.1 10.6 %collective-permute-start.2 = (bf16[64,2048]{1,0:T(8,128)(2,1)S(1)}, bf16[64,2048]{1,0:T(8,128)(2,1)S(1)}, u32[]{:S(2)}, u32[]{:S(2)}) collective-permute-start(bf16[64,2048]{1,0:T(8,128)(2,1)S(1)} %shard_map.51.vec_ref.prior_ref), channel_id=1, source_target_pairs={{0,2},{2,0},{4,6},{6,4},{8,10},{10,8},{12,14},{14,12},{16,18},{18,... | collective-permute-start | bytes 786440 | tf_op jit(solution)/shard_map/ppermute | solution.py:418
  16.2 10.5 %collective-permute-start.3 = (bf16[64,2048]{1,0:T(8,128)(2,1)S(1)}, bf16[64,2048]{1,0:T(8,128)(2,1)S(1)}, u32[]{:S(2)}, u32[]{:S(2)}) collective-permute-start(bf16[64,2048]{1,0:T(8,128)(2,1)S(1)} %shard_map.51.vec_ref.prior_ref), channel_id=1, source_target_pairs={{0,30},{2,4},{4,2},{6,8},{8,6},{10,12},{12,10},{14,16},{16,14},{18... | collective-permute-start | bytes 786440 | tf_op jit(solution)/shard_map/ppermute | solution.py:417
  21.2 10.7 %collective-permute-start.8 = (bf16[64,2048]{1,0:T(8,128)(2,1)S(1)}, bf16[64,2048]{1,0:T(8,128)(2,1)S(1)}, u32[]{:S(2)}, u32[]{:S(2)}) collective-permute-start(bf16[64,2048]{1,0:T(8,128)(2,1)S(1)} %shard_map.56.vec_ref.prior_ref), channel_id=1, source_target_pairs={{0,2},{2,0},{4,6},{6,4},{8,10},{10,8},{12,14},{14,12},{16,18},{18,... | collective-permute-start | bytes 786440 | tf_op jit(solution)/shard_map/ppermute | solution.py:418
  21.3 10.6 %collective-permute-start.9 = (bf16[64,2048]{1,0:T(8,128)(2,1)S(1)}, bf16[64,2048]{1,0:T(8,128)(2,1)S(1)}, u32[]{:S(2)}, u32[]{:S(2)}) collective-permute-start(bf16[64,2048]{1,0:T(8,128)(2,1)S(1)} %shard_map.56.vec_ref.prior_ref), channel_id=1, source_target_pairs={{0,30},{2,4},{4,2},{6,8},{8,6},{10,12},{12,10},{14,16},{16,14},{18... | collective-permute-start | bytes 786440 | tf_op jit(solution)/shard_map/ppermute | solution.py:417
  27.8 11.5 %collective-permute-start.4 = (bf16[64,2048]{1,0:T(8,128)(2,1)S(1)}, bf16[64,2048]{1,0:T(8,128)(2,1)S(1)}, u32[]{:S(2)}, u32[]{:S(2)}) collective-permute-start(bf16[64,2048]{1,0:T(8,128)(2,1)S(1)} %shard_map.53.vec_ref), channel_id=1, source_target_pairs={{0,2},{2,0},{4,6},{6,4},{8,10},{10,8},{12,14},{14,12},{16,18},{18,... | collective-permute-start | bytes 786440 | tf_op jit(solution)/shard_map/ppermute | solution.py:418
  28.0 11.3 %collective-permute-start.5 = (bf16[64,2048]{1,0:T(8,128)(2,1)S(1)}, bf16[64,2048]{1,0:T(8,128)(2,1)S(1)}, u32[]{:S(2)}, u32[]{:S(2)}) collective-permute-start(bf16[64,2048]{1,0:T(8,128)(2,1)S(1)} %shard_map.53.vec_ref), channel_id=1, source_target_pairs={{0,30},{2,4},{4,2},{6,8},{8,6},{10,12},{12,10},{14,16},{16,14},{18... | collective-permute-start | bytes 786440 | tf_op jit(solution)/shard_map/ppermute | solution.py:417
  33.0 9.0 %collective-permute-start.10 = (bf16[64,2048]{1,0:T(8,128)(2,1)S(1)}, bf16[64,2048]{1,0:T(8,128)(2,1)S(1)}, u32[]{:S(2)}, u32[]{:S(2)}) collective-permute-start(bf16[64,2048]{1,0:T(8,128)(2,1)S(1)} %shard_map.58.vec_ref), channel_id=1, source_target_pairs={{0,2},{2,0},{4,6},{6,4},{8,10},{10,8},{12,14},{14,12},{16,18},{18,... | collective-permute-start | bytes 786440 | tf_op jit(solution)/shard_map/ppermute | solution.py:418
  33.1 9.0 %collective-permute-start.11 = (bf16[64,2048]{1,0:T(8,128)(2,1)S(1)}, bf16[64,2048]{1,0:T(8,128)(2,1)S(1)}, u32[]{:S(2)}, u32[]{:S(2)}) collective-permute-start(bf16[64,2048]{1,0:T(8,128)(2,1)S(1)} %shard_map.58.vec_ref), channel_id=1, source_target_pairs={{0,30},{2,4},{4,2},{6,8},{8,6},{10,12},{12,10},{14,16},{16,14},{18... | collective-permute-start | bytes 786440 | tf_op jit(solution)/shard_map/ppermute | solution.py:417
  40.5 10.3 %collective-permute-start.18 = (bf16[64,2048]{1,0:T(8,128)(2,1)S(1)}, bf16[64,2048]{1,0:T(8,128)(2,1)S(1)}, u32[]{:S(2)}, u32[]{:S(2)}) collective-permute-start(bf16[64,2048]{1,0:T(8,128)(2,1)S(1)} %get-tuple-element.18.refs_2_.refs_0_), channel_id=1, source_target_pairs={{0,1},{1,0},{2,3},{3,2},{4,5},{5,4},{6,7},{7,6},{8,9},{9,8},{10,11... | collective-permute-start | bytes 786440 | tf_op jit(solution)/shard_map/ppermute | solution.py:454
  43.2 11.3 %collective-permute-start.19 = (bf16[64,2048]{1,0:T(8,128)(2,1)S(1)}, bf16[64,2048]{1,0:T(8,128)(2,1)S(1)}, u32[]{:S(2)}, u32[]{:S(2)}) collective-permute-start(bf16[64,2048]{1,0:T(8,128)(2,1)S(1)} %get-tuple-element.19.refs_3_.refs_1_), channel_id=1, source_target_pairs={{0,1},{1,0},{2,3},{3,2},{4,5},{5,4},{6,7},{7,6},{8,9},{9,8},{10,11... | collective-permute-start | bytes 786440 | tf_op jit(solution)/shard_map/ppermute | solution.py:454
  45.0 2.0 %collective-permute-start.12 = (f32[128,128]{1,0:T(8,128)S(1)}, f32[128,128]{1,0:T(8,128)S(1)}, u32[]{:S(2)}, u32[]{:S(2)}) collective-permute-start(f32[128,128]{1,0:T(8,128)S(1)} %shard_map.61), channel_id=1, source_target_pairs={{0,2},{2,0},{4,6},{6,4},{8,10},{10,8},{12,14},{14,12},{16,18},{18,... | collective-permute-start | bytes 196616 | tf_op jit(solution)/shard_map/ppermute | solution.py:441
  47.0 8.0 %collective-permute-start.14 = (f32[128,128]{1,0:T(8,128)S(1)}, f32[128,128]{1,0:T(8,128)S(1)}, u32[]{:S(2)}, u32[]{:S(2)}) collective-permute-start(f32[128,128]{1,0:T(8,128)S(1)} %add.44.refs_4_), channel_id=1, source_target_pairs={{0,8},{2,10},{4,12},{6,14},{8,0},{10,2},{12,4},{14,6},{16,24},{18,... | collective-permute-start | bytes 196616 | tf_op jit(solution)/shard_map/ppermute | solution.py:441
  49.2 5.8 %collective-permute-start.15 = (f32[128,128]{1,0:T(8,128)S(1)}, f32[128,128]{1,0:T(8,128)S(1)}, u32[]{:S(2)}, u32[]{:S(2)}) collective-permute-start(f32[128,128]{1,0:T(8,128)S(1)} %add.44.refs_4_), channel_id=1, source_target_pairs={{0,12},{2,14},{4,8},{6,10},{8,4},{10,6},{12,0},{14,2},{16,28},{18,... | collective-permute-start | bytes 196616 | tf_op jit(solution)/shard_map/ppermute | solution.py:441
  50.8 4.8 %collective-permute-start.13 = (f32[128,128]{1,0:T(8,128)S(1)}, f32[128,128]{1,0:T(8,128)S(1)}, u32[]{:S(2)}, u32[]{:S(2)}) collective-permute-start(f32[128,128]{1,0:T(8,128)S(1)} %add.44.refs_4_), channel_id=1, source_target_pairs={{0,4},{2,6},{4,0},{6,2},{8,12},{10,14},{12,8},{14,10},{16,20},{18,... | collective-permute-start | bytes 196616 | tf_op jit(solution)/shard_map/ppermute | solution.py:441
  54.9 3.3 %collective-permute-start.20 = (f32[128,128]{1,0:T(8,128)S(1)}, f32[128,128]{1,0:T(8,128)S(1)}, u32[]{:S(2)}, u32[]{:S(2)}) collective-permute-start(f32[128,128]{1,0:T(8,128)S(1)} %shard_map.62), channel_id=1, source_target_pairs={{0,2},{2,0},{4,6},{6,4},{8,10},{10,8},{12,14},{14,12},{16,18},{18,... | collective-permute-start | bytes 196616 | tf_op jit(solution)/shard_map/ppermute | solution.py:441
  55.6 6.1 %collective-permute-start.16 = (f32[128,128]{1,0:T(8,128)S(1)}, f32[128,128]{1,0:T(8,128)S(1)}, u32[]{:S(2)}, u32[]{:S(2)}) collective-permute-start(f32[128,128]{1,0:T(8,128)S(1)} %add_add_fusion.1), channel_id=1, source_target_pairs={{0,16},{2,18},{4,20},{6,22},{8,24},{10,26},{12,28},{14,30},{16,0},... | collective-permute-start | bytes 196616 | tf_op jit(solution)/shard_map/ppermute | solution.py:441
  58.2 5.1 %collective-permute-start.22 = (f32[128,128]{1,0:T(8,128)S(1)}, f32[128,128]{1,0:T(8,128)S(1)}, u32[]{:S(2)}, u32[]{:S(2)}) collective-permute-start(f32[128,128]{1,0:T(8,128)S(1)} %add.49), channel_id=1, source_target_pairs={{0,8},{2,10},{4,12},{6,14},{8,0},{10,2},{12,4},{14,6},{16,24},{18,... | collective-permute-start | bytes 196616 | tf_op jit(solution)/shard_map/ppermute | solution.py:441
  58.8 5.2 %collective-permute-start.23 = (f32[128,128]{1,0:T(8,128)S(1)}, f32[128,128]{1,0:T(8,128)S(1)}, u32[]{:S(2)}, u32[]{:S(2)}) collective-permute-start(f32[128,128]{1,0:T(8,128)S(1)} %add.49), channel_id=1, source_target_pairs={{0,12},{2,14},{4,8},{6,10},{8,4},{10,6},{12,0},{14,2},{16,28},{18,... | collective-permute-start | bytes 196616 | tf_op jit(solution)/shard_map/ppermute | solution.py:441
  60.3 4.4 %collective-permute-start.21 = (f32[128,128]{1,0:T(8,128)S(1)}, f32[128,128]{1,0:T(8,128)S(1)}, u32[]{:S(2)}, u32[]{:S(2)}) collective-permute-start(f32[128,128]{1,0:T(8,128)S(1)} %add.49), channel_id=1, source_target_pairs={{0,4},{2,6},{4,0},{6,2},{8,12},{10,14},{12,8},{14,10},{16,20},{18,... | collective-permute-start | bytes 196616 | tf_op jit(solution)/shard_map/ppermute | solution.py:441
  61.7 4.3 %collective-permute-start.17 = (f32[128,128]{1,0:T(8,128)S(1)}, f32[128,128]{1,0:T(8,128)S(1)}, u32[]{:S(2)}, u32[]{:S(2)}) collective-permute-start(f32[128,128]{1,0:T(8,128)S(1)} %add.48.own_ref), channel_id=1, source_target_pairs={{0,1},{1,0},{2,3},{3,2},{4,5},{5,4},{6,7},{7,6},{8,9},{9,8},{10,11... | collective-permute-start | bytes 196616 | tf_op jit(solution)/shard_map/ppermute | solution.py:473
  64.7 5.7 %collective-permute-start.24 = (f32[128,128]{1,0:T(8,128)S(1)}, f32[128,128]{1,0:T(8,128)S(1)}, u32[]{:S(2)}, u32[]{:S(2)}) collective-permute-start(f32[128,128]{1,0:T(8,128)S(1)} %add_add_fusion.after_ref), channel_id=1, source_target_pairs={{0,16},{2,18},{4,20},{6,22},{8,24},{10,26},{12,28},{14,30},{16,0},... | collective-permute-start | bytes 196616 | tf_op jit(solution)/shard_map/ppermute | solution.py:441

commit v15 on v14

--- a/solution.py
+++ b/solution.py
@@ -347,26 +347,26 @@
         stacked = jnp.concatenate([high_inv, high_inv], axis=1)
         return dot(stacked, jnp.concatenate([high, low], axis=0)) + dot(low_inv, high)
 
-    @pl.when(leading)
-    def _():
-        for copy, here in zip(copies, spans):
-            high = stacked(highs, here)
-            low = (stacked(wides, here) - high.astype(jnp.float32)).astype(jnp.bfloat16)
-            result[:, here] = product(first_inv_ref[...], high, low)
-            copy.start()
-
     lower = dot_full(cross_ref[...], first_inv_ref[...], ((1,), (1,)))
     rest = jnp.where(leading, other_ref[...], own_ref[...])
     work[...] = rest - dot_full(lower, lower, ((1,), (1,)))
     high_mix, low_mix = split(dot_full(lower, first_inv_ref[...]))
     mixes = jnp.concatenate([high_mix, low_mix], axis=1)
     for here in spans:
+        high = stacked(highs, here)
+        low = (stacked(wides, here) - high.astype(jnp.float32)).astype(jnp.bfloat16)
+        result[:, here] = product(first_inv_ref[...], high, low)
         away = stacked(aways, here)
         part[:, here] = stacked(wides, here) - dot(mixes, jnp.concatenate([away, away], axis=0))
     upper_ref[0:half, 0:half] = first_ref[...]
     upper_ref[0:half, half:] = lower.T
     upper_ref[half:, 0:half] = jnp.zeros((half, half), jnp.float32)
     factor_into(work, right, upper_ref.at[half:, half:], inverse)
+
+    @pl.when(leading)
+    def _():
+        for copy in copies:
+            copy.start()
 
     @pl.when(trailing)
     def _():

time: 77.3 us -> 77.7 us (level)
  no operation moved by 1% of the time
where the time goes in v15:
time: 77.7 us; the launch traced here: 77.5 us
  starting transfers between devices  35.8 us (46%)
  Pallas kernels  30.2 us (39%)
  waiting for transfers between devices  7.68 us (10%)
  other arithmetic  1.53 us (2%)
  local copies, waits for them, and re-layouts  1.21 us (2%)
  between operations  1.05 us (1%)
    ppermute x4, starting transfers between devices, level(): far = lax.ppermute(vec, 'space', far_pairs)  12.8 us
    ppermute x10, starting transfers between devices, moved(): return lax.ppermute(part, 'space', [(i, i ^ step) for i in range(blocks)])  12 us
    pallas_call x1, Pallas kernels, finish(): pl.pallas_call(functools.partial(finish_kernel, len(wide)), out_shape=[ja...  6.98 us
    pallas_call x6, Pallas kernels, halo_part(): pl.pallas_call(functools.partial(halo_kernel, level), out_shape=[jax.Shap...  6.76 us
    pallas_call x4, Pallas kernels, own_part(): pl.pallas_call(own_kernel, out_shape=jax.ShapeDtypeStruct(vec.shape, jnp....  6.55 us
    ppermute x2, starting transfers between devices, shards(): fars = [lax.ppermute(vec, 'space', far_pairs) for vec in zero]  6.29 us
    pallas_call x1, Pallas kernels, turn_part(): pl.pallas_call(functools.partial(turn_kernel, chunks), out_shape=[jax.Sha...  4.85 us
    pallas_call x1, Pallas kernels, factor_first(): pl.pallas_call(first_kernel, out_shape=[jax.ShapeDtypeStruct((half, half)...  4.29 us
  transfers between devices with their start and end apart: 25, of which 7 were waited for; matrix products, arithmetic and copies ran while one was open for 2% of the time, Pallas kernels for 30%

profile of v15, /device:TPU:0, one launch (start us, length us, event | category | flops | bytes accessed | tf_op | source)
XLA Modules:
  0.0 77.5 jit_solution(14528552886281996540)
XLA Ops:
  0.6 1.1 %fusion.1 = (bf16[64,2048]{1,0:T(8,128)(2,1)S(1)}, bf16[64,2048]{1,0:T(8,128)(2,1)S(1)}) fusion(bf16[128,2048]{1,0:T(8,128)(2,1)} %param.4), kind=kLoop, calls=%fused_computation.7 | loop fusion | bytes 1048576 | tf_op jit(solution)/shard_map/slice | solution.py:422
  1.7 0.5 collective-permute-start
  2.2 5.7 %collective-permute-start.1 = (bf16[64,2048]{1,0:T(8,128)(2,1)S(1)}, bf16[64,2048]{1,0:T(8,128)(2,1)S(1)}, u32[]{:S(2)}, u32[]{:S(2)}) collective-permute-start(bf16[64,2048]{1,0:T(8,128)(2,1)S(1)} %get-tuple-element.25.refs_0_.vec_ref.prior_ref), channel_id=1, source_target_pairs={{0,30},{2,4},{4,2},{6,8},{8,6},{10,12},{12,10},{14,16},{16,14},{18... | collective-permute-start | bytes 786440 | tf_op jit(solution)/shard_map/ppermute | solution.py:423
  7.9 0.0 collective-permute-start.6
  7.9 0.6 collective-permute-start.7
  8.5 0.7 add_select_fusion
  9.2 0.1 slice.17
  9.3 0.1 fusion.2
  9.3 0.8 add_select_fusion.1.loc_ref
  10.1 4.9 %shard_map.50 = (bf16[8,7,256,256]{3,2,1,0:T(8,128)(2,1)S(1)}, f32[64,2048]{1,0:T(8,128)S(1)}, f32[64,2048]{1,0:T(8,128)S(1)}) custom-call(s32[8,6]{1,0:T(8,128)S(1)} %add_select_fusion.1.loc_ref, s32[1]{0:T(128)S(6)} %select_n.21.odd_ref, bf16[64,2048]{1,0:T(8,128)(2,1)S(1)} %get-tuple-element.25.refs_0_.vec_ref.prior_ref, ...), custom_call_target="tpu_custom_call" | custom-call | flops 671088640 | bytes 14680064 | tf_op jit(solution)/shard_map/pallas_call | solution.py:67
  15.0 0.0 collective-permute-done.near_ref
  15.0 0.0 collective-permute-done.1.far_ref
  15.0 1.1 %shard_map.51.vec_ref.prior_ref = bf16[64,2048]{1,0:T(8,128)(2,1)S(1)} custom-call(s32[8,6]{1,0:T(8,128)S(1)} %add_select_fusion.1.loc_ref, bf16[64,2048]{1,0:T(8,128)(2,1)S(1)} %collective-permute-done.near_ref, bf16[64,2048]{1,0:T(8,128)(2,1)S(1)} %collective-permute-done.1.far_ref, f32[64,2048]{1,0:T(8,128)S(1)} %get-tuple-element.13.acc_ref, ...), custom_call_target="tpu_custom_call" | custom-call | flops 134217728 | bytes 2097152 | tf_op jit(solution)/shard_map/pallas_call | solution.py:139
  16.1 0.1 collective-permute-start.2
  16.2 3.9 %collective-permute-start.3 = (bf16[64,2048]{1,0:T(8,128)(2,1)S(1)}, bf16[64,2048]{1,0:T(8,128)(2,1)S(1)}, u32[]{:S(2)}, u32[]{:S(2)}) collective-permute-start(bf16[64,2048]{1,0:T(8,128)(2,1)S(1)} %shard_map.51.vec_ref.prior_ref), channel_id=1, source_target_pairs={{0,30},{2,4},{4,2},{6,8},{8,6},{10,12},{12,10},{14,16},{16,14},{18... | collective-permute-start | bytes 786440 | tf_op jit(solution)/shard_map/ppermute | solution.py:417
  20.1 0.0 collective-permute-done.6.near_ref
  20.1 0.0 collective-permute-done.7.far_ref
  20.1 1.1 %shard_map.56.vec_ref.prior_ref = bf16[64,2048]{1,0:T(8,128)(2,1)S(1)} custom-call(s32[8,6]{1,0:T(8,128)S(1)} %add_select_fusion.1.loc_ref, bf16[64,2048]{1,0:T(8,128)(2,1)S(1)} %collective-permute-done.6.near_ref, bf16[64,2048]{1,0:T(8,128)(2,1)S(1)} %collective-permute-done.7.far_ref, f32[64,2048]{1,0:T(8,128)S(1)} %get-tuple-element.16.acc_ref, ...), custom_call_target="tpu_custom_call" | custom-call | flops 134217728 | bytes 2097152 | tf_op jit(solution)/shard_map/pallas_call | solution.py:139
  21.2 0.1 collective-permute-start.8
  21.3 2.1 %collective-permute-start.9 = (bf16[64,2048]{1,0:T(8,128)(2,1)S(1)}, bf16[64,2048]{1,0:T(8,128)(2,1)S(1)}, u32[]{:S(2)}, u32[]{:S(2)}) collective-permute-start(bf16[64,2048]{1,0:T(8,128)(2,1)S(1)} %shard_map.56.vec_ref.prior_ref), channel_id=1, source_target_pairs={{0,30},{2,4},{4,2},{6,8},{8,6},{10,12},{12,10},{14,16},{16,14},{18... | collective-permute-start | bytes 786440 | tf_op jit(solution)/shard_map/ppermute | solution.py:417
  23.4 1.6 %shard_map.52.acc_ref = f32[64,2048]{1,0:T(8,128)S(1)} custom-call(s32[8,6]{1,0:T(8,128)S(1)} %add_select_fusion.1.loc_ref, bf16[64,2048]{1,0:T(8,128)(2,1)S(1)} %shard_map.51.vec_ref.prior_ref, bf16[8,7,256,256]{3,2,1,0:T(8,128)(2,1)S(1)} %get-tuple-element.14.turned_ref), custom_call_target="tpu_custom_call" | custom-call | flops 335544320 | bytes 5242880 | tf_op jit(solution)/shard_map/pallas_call | solution.py:104
  25.0 1.6 %shard_map.57.acc_ref = f32[64,2048]{1,0:T(8,128)S(1)} custom-call(s32[8,6]{1,0:T(8,128)S(1)} %add_select_fusion.1.loc_ref, bf16[64,2048]{1,0:T(8,128)(2,1)S(1)} %shard_map.56.vec_ref.prior_ref, bf16[8,7,256,256]{3,2,1,0:T(8,128)(2,1)S(1)} %get-tuple-element.14.turned_ref), custom_call_target="tpu_custom_call" | custom-call | flops 335544320 | bytes 5242880 | tf_op jit(solution)/shard_map/pallas_call | solution.py:104
  26.6 0.0 collective-permute-done.2.near_ref
  26.7 0.0 collective-permute-done.3.far_ref
  26.7 1.1 %shard_map.53.vec_ref = bf16[64,2048]{1,0:T(8,128)(2,1)S(1)} custom-call(s32[8,6]{1,0:T(8,128)S(1)} %add_select_fusion.1.loc_ref, bf16[64,2048]{1,0:T(8,128)(2,1)S(1)} %collective-permute-done.2.near_ref, bf16[64,2048]{1,0:T(8,128)(2,1)S(1)} %collective-permute-done.3.far_ref, f32[64,2048]{1,0:T(8,128)S(1)} %shard_map.52.acc_ref, ...), custom_call_target="tpu_custom_call" | custom-call | flops 134217728 | bytes 2097152 | tf_op jit(solution)/shard_map/pallas_call | solution.py:139
  27.8 0.2 collective-permute-start.4
  28.0 3.9 %collective-permute-start.5 = (bf16[64,2048]{1,0:T(8,128)(2,1)S(1)}, bf16[64,2048]{1,0:T(8,128)(2,1)S(1)}, u32[]{:S(2)}, u32[]{:S(2)}) collective-permute-start(bf16[64,2048]{1,0:T(8,128)(2,1)S(1)} %shard_map.53.vec_ref), channel_id=1, source_target_pairs={{0,30},{2,4},{4,2},{6,8},{8,6},{10,12},{12,10},{14,16},{16,14},{18... | collective-permute-start | bytes 786440 | tf_op jit(solution)/shard_map/ppermute | solution.py:417
  31.9 0.0 collective-permute-done.8.near_ref
  31.9 0.0 collective-permute-done.9.far_ref
  31.9 1.1 %shard_map.58.vec_ref = bf16[64,2048]{1,0:T(8,128)(2,1)S(1)} custom-call(s32[8,6]{1,0:T(8,128)S(1)} %add_select_fusion.1.loc_ref, bf16[64,2048]{1,0:T(8,128)(2,1)S(1)} %collective-permute-done.8.near_ref, bf16[64,2048]{1,0:T(8,128)(2,1)S(1)} %collective-permute-done.9.far_ref, f32[64,2048]{1,0:T(8,128)S(1)} %shard_map.57.acc_ref, ...), custom_call_target="tpu_custom_call" | custom-call | flops 134217728 | bytes 2097152 | tf_op jit(solution)/shard_map/pallas_call | solution.py:139
  33.0 0.1 collective-permute-start.10
  33.1 2.9 %collective-permute-start.11 = (bf16[64,2048]{1,0:T(8,128)(2,1)S(1)}, bf16[64,2048]{1,0:T(8,128)(2,1)S(1)}, u32[]{:S(2)}, u32[]{:S(2)}) collective-permute-start(bf16[64,2048]{1,0:T(8,128)(2,1)S(1)} %shard_map.58.vec_ref), channel_id=1, source_target_pairs={{0,30},{2,4},{4,2},{6,8},{8,6},{10,12},{12,10},{14,16},{16,14},{18... | collective-permute-start | bytes 786440 | tf_op jit(solution)/shard_map/ppermute | solution.py:417
  36.1 1.6 %shard_map.54.acc_ref = f32[64,2048]{1,0:T(8,128)S(1)} custom-call(s32[8,6]{1,0:T(8,128)S(1)} %add_select_fusion.1.loc_ref, bf16[64,2048]{1,0:T(8,128)(2,1)S(1)} %shard_map.53.vec_ref, bf16[8,7,256,256]{3,2,1,0:T(8,128)(2,1)S(1)} %get-tuple-element.14.turned_ref), custom_call_target="tpu_custom_call" | custom-call | flops 335544320 | bytes 5242880 | tf_op jit(solution)/shard_map/pallas_call | solution.py:104
  37.7 1.6 %shard_map.59.acc_ref = f32[64,2048]{1,0:T(8,128)S(1)} custom-call(s32[8,6]{1,0:T(8,128)S(1)} %add_select_fusion.1.loc_ref, bf16[64,2048]{1,0:T(8,128)(2,1)S(1)} %shard_map.58.vec_ref, bf16[8,7,256,256]{3,2,1,0:T(8,128)(2,1)S(1)} %get-tuple-element.14.turned_ref), custom_call_target="tpu_custom_call" | custom-call | flops 335544320 | bytes 5242880 | tf_op jit(solution)/shard_map/pallas_call | solution.py:104
  39.3 0.0 collective-permute-done.4.near_ref
  39.4 0.0 collective-permute-done.5.far_ref
  39.4 1.1 %shard_map.55 = (f32[64,2048]{1,0:T(8,128)S(1)}, bf16[64,2048]{1,0:T(8,128)(2,1)S(1)}) custom-call(s32[8,6]{1,0:T(8,128)S(1)} %add_select_fusion.1.loc_ref, bf16[64,2048]{1,0:T(8,128)(2,1)S(1)} %collective-permute-done.4.near_ref, bf16[64,2048]{1,0:T(8,128)(2,1)S(1)} %collective-permute-done.5.far_ref, f32[64,2048]{1,0:T(8,128)S(1)} %shard_map.54.acc_ref, ...), custom_call_target="tpu_custom_call" | custom-call | flops 134217728 | bytes 2097152 | tf_op jit(solution)/shard_map/pallas_call | solution.py:139
  40.5 1.6 %collective-permute-start.18 = (bf16[64,2048]{1,0:T(8,128)(2,1)S(1)}, bf16[64,2048]{1,0:T(8,128)(2,1)S(1)}, u32[]{:S(2)}, u32[]{:S(2)}) collective-permute-start(bf16[64,2048]{1,0:T(8,128)(2,1)S(1)} %get-tuple-element.18.refs_2_.refs_0_), channel_id=1, source_target_pairs={{0,1},{1,0},{2,3},{3,2},{4,5},{5,4},{6,7},{7,6},{8,9},{9,8},{10,11... | collective-permute-start | bytes 786440 | tf_op jit(solution)/shard_map/ppermute | solution.py:454
  42.1 1.1 %shard_map.60 = (f32[64,2048]{1,0:T(8,128)S(1)}, bf16[64,2048]{1,0:T(8,128)(2,1)S(1)}) custom-call(s32[8,6]{1,0:T(8,128)S(1)} %add_select_fusion.1.loc_ref, bf16[64,2048]{1,0:T(8,128)(2,1)S(1)} %collective-permute-done.10.near_ref, bf16[64,2048]{1,0:T(8,128)(2,1)S(1)} %collective-permute-done.11.far_ref, f32[64,2048]{1,0:T(8,128)S(1)} %shard_map.59.acc_ref, ...), custom_call_target="tpu_custom_call" | custom-call | flops 134217728 | bytes 2097152 | tf_op jit(solution)/shard_map/pallas_call | solution.py:139
  43.2 1.3 %collective-permute-start.19 = (bf16[64,2048]{1,0:T(8,128)(2,1)S(1)}, bf16[64,2048]{1,0:T(8,128)(2,1)S(1)}, u32[]{:S(2)}, u32[]{:S(2)}) collective-permute-start(bf16[64,2048]{1,0:T(8,128)(2,1)S(1)} %get-tuple-element.19.refs_3_.refs_1_), channel_id=1, source_target_pairs={{0,1},{1,0},{2,3},{3,2},{4,5},{5,4},{6,7},{7,6},{8,9},{9,8},{10,11... | collective-permute-start | bytes 786440 | tf_op jit(solution)/shard_map/ppermute | solution.py:454
  44.5 0.5 shard_map.61
  45.0 1.1 %collective-permute-start.12 = (f32[128,128]{1,0:T(8,128)S(1)}, f32[128,128]{1,0:T(8,128)S(1)}, u32[]{:S(2)}, u32[]{:S(2)}) collective-permute-start(f32[128,128]{1,0:T(8,128)S(1)} %shard_map.61), channel_id=1, source_target_pairs={{0,2},{2,0},{4,6},{6,4},{8,10},{10,8},{12,14},{14,12},{16,18},{18,... | collective-permute-start | bytes 196616 | tf_op jit(solution)/shard_map/ppermute | solution.py:441
  46.1 0.9 %collective-permute-done.12 = f32[128,128]{1,0:T(8,128)S(1)} collective-permute-done((f32[128,128]{1,0:T(8,128)S(1)}, f32[128,128]{1,0:T(8,128)S(1)}, u32[]{:S(2)}, u32[]{:S(2)}) %collective-permute-start.12) | collective-permute-done | bytes 65568 | tf_op jit(solution)/shard_map/ppermute | solution.py:441
  47.0 2.2 %collective-permute-start.14 = (f32[128,128]{1,0:T(8,128)S(1)}, f32[128,128]{1,0:T(8,128)S(1)}, u32[]{:S(2)}, u32[]{:S(2)}) collective-permute-start(f32[128,128]{1,0:T(8,128)S(1)} %add.44.refs_4_), channel_id=1, source_target_pairs={{0,8},{2,10},{4,12},{6,14},{8,0},{10,2},{12,4},{14,6},{16,24},{18,... | collective-permute-start | bytes 196616 | tf_op jit(solution)/shard_map/ppermute | solution.py:441
  49.2 1.6 %collective-permute-start.15 = (f32[128,128]{1,0:T(8,128)S(1)}, f32[128,128]{1,0:T(8,128)S(1)}, u32[]{:S(2)}, u32[]{:S(2)}) collective-permute-start(f32[128,128]{1,0:T(8,128)S(1)} %add.44.refs_4_), channel_id=1, source_target_pairs={{0,12},{2,14},{4,8},{6,10},{8,4},{10,6},{12,0},{14,2},{16,28},{18,... | collective-permute-start | bytes 196616 | tf_op jit(solution)/shard_map/ppermute | solution.py:441
  50.8 0.0 collective-permute-start.13
  50.8 0.0 collective-permute-done.18.refs_2_.refs_4_
  50.8 3.8 %collective-permute-done.19.refs_3_.refs_5_ = bf16[64,2048]{1,0:T(8,128)(2,1)S(1)} collective-permute-done((bf16[64,2048]{1,0:T(8,128)(2,1)S(1)}, bf16[64,2048]{1,0:T(8,128)(2,1)S(1)}, u32[]{:S(2)}, u32[]{:S(2)}) %collective-permute-start.19) | collective-permute-done | bytes 262176 | tf_op jit(solution)/shard_map/ppermute | solution.py:454
  54.5 0.3 shard_map.62
  54.9 0.1 collective-permute-start.20
  54.9 0.0 collective-permute-done.14
  55.0 0.6 collective-permute-done.13
  55.6 2.5 %collective-permute-start.16 = (f32[128,128]{1,0:T(8,128)S(1)}, f32[128,128]{1,0:T(8,128)S(1)}, u32[]{:S(2)}, u32[]{:S(2)}) collective-permute-start(f32[128,128]{1,0:T(8,128)S(1)} %add_add_fusion.1), channel_id=1, source_target_pairs={{0,16},{2,18},{4,20},{6,22},{8,24},{10,26},{12,28},{14,30},{16,0},... | collective-permute-start | bytes 196616 | tf_op jit(solution)/shard_map/ppermute | solution.py:441
  58.2 0.6 collective-permute-start.22
  58.8 1.5 %collective-permute-start.23 = (f32[128,128]{1,0:T(8,128)S(1)}, f32[128,128]{1,0:T(8,128)S(1)}, u32[]{:S(2)}, u32[]{:S(2)}) collective-permute-start(f32[128,128]{1,0:T(8,128)S(1)} %add.49), channel_id=1, source_target_pairs={{0,12},{2,14},{4,8},{6,10},{8,4},{10,6},{12,0},{14,2},{16,28},{18,... | collective-permute-start | bytes 196616 | tf_op jit(solution)/shard_map/ppermute | solution.py:441
  60.3 1.5 %collective-permute-start.21 = (f32[128,128]{1,0:T(8,128)S(1)}, f32[128,128]{1,0:T(8,128)S(1)}, u32[]{:S(2)}, u32[]{:S(2)}) collective-permute-start(f32[128,128]{1,0:T(8,128)S(1)} %add.49), channel_id=1, source_target_pairs={{0,4},{2,6},{4,0},{6,2},{8,12},{10,14},{12,8},{14,10},{16,20},{18,... | collective-permute-start | bytes 196616 | tf_op jit(solution)/shard_map/ppermute | solution.py:441
  61.7 1.0 %collective-permute-start.17 = (f32[128,128]{1,0:T(8,128)S(1)}, f32[128,128]{1,0:T(8,128)S(1)}, u32[]{:S(2)}, u32[]{:S(2)}) collective-permute-start(f32[128,128]{1,0:T(8,128)S(1)} %add.48.own_ref), channel_id=1, source_target_pairs={{0,1},{1,0},{2,3},{3,2},{4,5},{5,4},{6,7},{7,6},{8,9},{9,8},{10,11... | collective-permute-start | bytes 196616 | tf_op jit(solution)/shard_map/ppermute | solution.py:473
  62.8 0.5 collective-permute-done.22
  63.2 0.7 collective-permute-done.23
  64.0 0.7 collective-permute-done.21
  64.7 1.0 %collective-permute-start.24 = (f32[128,128]{1,0:T(8,128)S(1)}, f32[128,128]{1,0:T(8,128)S(1)}, u32[]{:S(2)}, u32[]{:S(2)}) collective-permute-start(f32[128,128]{1,0:T(8,128)S(1)} %add_add_fusion.after_ref), channel_id=1, source_target_pairs={{0,16},{2,18},{4,20},{6,22},{8,24},{10,26},{12,28},{14,30},{16,0},... | collective-permute-start | bytes 196616 | tf_op jit(solution)/shard_map/ppermute | solution.py:441
  65.7 0.4 collective-permute-done.17.other_ref
  66.1 4.3 %shard_map.63 = (f32[128,128]{1,0:T(8,128)S(1)}, f32[128,128]{1,0:T(8,128)S(1)}) custom-call(s32[1]{0:T(128)} %bitcast.place_ref, f32[128,128]{1,0:T(8,128)S(1)} %add.48.own_ref, f32[128,128]{1,0:T(8,128)S(1)} %collective-permute-done.17.other_ref, f32[128,128]{1,0:T(8,128)S(1)} %add_add_fusion.after_ref), custom_call_target="tpu_custom_call" | custom-call | flops 4194304 | bytes 16777216 | tf_op jit(solution)/shard_map/pallas_call | solution.py:304
  70.4 7.0 %shard_map.64 = (f32[256,256]{1,0:T(8,128)}, f32[128,2048]{1,0:T(8,128)}) custom-call(s32[1]{0:T(128)} %bitcast.place_ref, f32[128,128]{1,0:T(8,128)S(1)} %add.48.own_ref, f32[128,128]{1,0:T(8,128)S(1)} %collective-permute-done.17.other_ref, f32[128,128]{1,0:T(8,128)S(1)} %add.53.cross_ref, f32[128,128]{1,0:T(8,128)S(1)} %get-tuple-element.20.first_ref, ...), custom_call_target="tpu_custom_call" | custom-call | tf_op jit(solution)/shard_map/pallas_call | solution.py:385
  (12 shorter events, 0.1 us)
Async XLA Ops:
  1.7 13.3 %collective-permute-start = (bf16[64,2048]{1,0:T(8,128)(2,1)S(1)}, bf16[64,2048]{1,0:T(8,128)(2,1)S(1)}, u32[]{:S(2)}, u32[]{:S(2)}) collective-permute-start(bf16[64,2048]{1,0:T(8,128)(2,1)S(1)} %get-tuple-element.25.refs_0_.vec_ref.prior_ref), channel_id=1, source_target_pairs={{0,2},{2,0},{4,6},{6,4},{8,10},{10,8},{12,14},{14,12},{16,18},{18,... | collective-permute-start | bytes 786440 | tf_op jit(solution)/shard_map/ppermute | solution.py:424
  2.2 12.8 %collective-permute-start.1 = (bf16[64,2048]{1,0:T(8,128)(2,1)S(1)}, bf16[64,2048]{1,0:T(8,128)(2,1)S(1)}, u32[]{:S(2)}, u32[]{:S(2)}) collective-permute-start(bf16[64,2048]{1,0:T(8,128)(2,1)S(1)} %get-tuple-element.25.refs_0_.vec_ref.prior_ref), channel_id=1, source_target_pairs={{0,30},{2,4},{4,2},{6,8},{8,6},{10,12},{12,10},{14,16},{16,14},{18... | collective-permute-start | bytes 786440 | tf_op jit(solution)/shard_map/ppermute | solution.py:423
  7.9 12.2 %collective-permute-start.6 = (bf16[64,2048]{1,0:T(8,128)(2,1)S(1)}, bf16[64,2048]{1,0:T(8,128)(2,1)S(1)}, u32[]{:S(2)}, u32[]{:S(2)}) collective-permute-start(bf16[64,2048]{1,0:T(8,128)(2,1)S(1)} %get-tuple-element.24.refs_1_.vec_ref.prior_ref), channel_id=1, source_target_pairs={{0,2},{2,0},{4,6},{6,4},{8,10},{10,8},{12,14},{14,12},{16,18},{18,... | collective-permute-start | bytes 786440 | tf_op jit(solution)/shard_map/ppermute | solution.py:424
  7.9 12.2 %collective-permute-start.7 = (bf16[64,2048]{1,0:T(8,128)(2,1)S(1)}, bf16[64,2048]{1,0:T(8,128)(2,1)S(1)}, u32[]{:S(2)}, u32[]{:S(2)}) collective-permute-start(bf16[64,2048]{1,0:T(8,128)(2,1)S(1)} %get-tuple-element.24.refs_1_.vec_ref.prior_ref), channel_id=1, source_target_pairs={{0,30},{2,4},{4,2},{6,8},{8,6},{10,12},{12,10},{14,16},{16,14},{18... | collective-permute-start | bytes 786440 | tf_op jit(solution)/shard_map/ppermute | solution.py:423
  16.1 10.6 %collective-permute-start.2 = (bf16[64,2048]{1,0:T(8,128)(2,1)S(1)}, bf16[64,2048]{1,0:T(8,128)(2,1)S(1)}, u32[]{:S(2)}, u32[]{:S(2)}) collective-permute-start(bf16[64,2048]{1,0:T(8,128)(2,1)S(1)} %shard_map.51.vec_ref.prior_ref), channel_id=1, source_target_pairs={{0,2},{2,0},{4,6},{6,4},{8,10},{10,8},{12,14},{14,12},{16,18},{18,... | collective-permute-start | bytes 786440 | tf_op jit(solution)/shard_map/ppermute | solution.py:418
  16.2 10.5 %collective-permute-start.3 = (bf16[64,2048]{1,0:T(8,128)(2,1)S(1)}, bf16[64,2048]{1,0:T(8,128)(2,1)S(1)}, u32[]{:S(2)}, u32[]{:S(2)}) collective-permute-start(bf16[64,2048]{1,0:T(8,128)(2,1)S(1)} %shard_map.51.vec_ref.prior_ref), channel_id=1, source_target_pairs={{0,30},{2,4},{4,2},{6,8},{8,6},{10,12},{12,10},{14,16},{16,14},{18... | collective-permute-start | bytes 786440 | tf_op jit(solution)/shard_map/ppermute | solution.py:417
  21.2 10.7 %collective-permute-start.8 = (bf16[64,2048]{1,0:T(8,128)(2,1)S(1)}, bf16[64,2048]{1,0:T(8,128)(2,1)S(1)}, u32[]{:S(2)}, u32[]{:S(2)}) collective-permute-start(bf16[64,2048]{1,0:T(8,128)(2,1)S(1)} %shard_map.56.vec_ref.prior_ref), channel_id=1, source_target_pairs={{0,2},{2,0},{4,6},{6,4},{8,10},{10,8},{12,14},{14,12},{16,18},{18,... | collective-permute-start | bytes 786440 | tf_op jit(solution)/shard_map/ppermute | solution.py:418
  21.3 10.6 %collective-permute-start.9 = (bf16[64,2048]{1,0:T(8,128)(2,1)S(1)}, bf16[64,2048]{1,0:T(8,128)(2,1)S(1)}, u32[]{:S(2)}, u32[]{:S(2)}) collective-permute-start(bf16[64,2048]{1,0:T(8,128)(2,1)S(1)} %shard_map.56.vec_ref.prior_ref), channel_id=1, source_target_pairs={{0,30},{2,4},{4,2},{6,8},{8,6},{10,12},{12,10},{14,16},{16,14},{18... | collective-permute-start | bytes 786440 | tf_op jit(solution)/shard_map/ppermute | solution.py:417
  27.8 11.5 %collective-permute-start.4 = (bf16[64,2048]{1,0:T(8,128)(2,1)S(1)}, bf16[64,2048]{1,0:T(8,128)(2,1)S(1)}, u32[]{:S(2)}, u32[]{:S(2)}) collective-permute-start(bf16[64,2048]{1,0:T(8,128)(2,1)S(1)} %shard_map.53.vec_ref), channel_id=1, source_target_pairs={{0,2},{2,0},{4,6},{6,4},{8,10},{10,8},{12,14},{14,12},{16,18},{18,... | collective-permute-start | bytes 786440 | tf_op jit(solution)/shard_map/ppermute | solution.py:418
  28.0 11.3 %collective-permute-start.5 = (bf16[64,2048]{1,0:T(8,128)(2,1)S(1)}, bf16[64,2048]{1,0:T(8,128)(2,1)S(1)}, u32[]{:S(2)}, u32[]{:S(2)}) collective-permute-start(bf16[64,2048]{1,0:T(8,128)(2,1)S(1)} %shard_map.53.vec_ref), channel_id=1, source_target_pairs={{0,30},{2,4},{4,2},{6,8},{8,6},{10,12},{12,10},{14,16},{16,14},{18... | collective-permute-start | bytes 786440 | tf_op jit(solution)/shard_map/ppermute | solution.py:417
  33.0 9.0 %collective-permute-start.10 = (bf16[64,2048]{1,0:T(8,128)(2,1)S(1)}, bf16[64,2048]{1,0:T(8,128)(2,1)S(1)}, u32[]{:S(2)}, u32[]{:S(2)}) collective-permute-start(bf16[64,2048]{1,0:T(8,128)(2,1)S(1)} %shard_map.58.vec_ref), channel_id=1, source_target_pairs={{0,2},{2,0},{4,6},{6,4},{8,10},{10,8},{12,14},{14,12},{16,18},{18,... | collective-permute-start | bytes 786440 | tf_op jit(solution)/shard_map/ppermute | solution.py:418
  33.1 9.0 %collective-permute-start.11 = (bf16[64,2048]{1,0:T(8,128)(2,1)S(1)}, bf16[64,2048]{1,0:T(8,128)(2,1)S(1)}, u32[]{:S(2)}, u32[]{:S(2)}) collective-permute-start(bf16[64,2048]{1,0:T(8,128)(2,1)S(1)} %shard_map.58.vec_ref), channel_id=1, source_target_pairs={{0,30},{2,4},{4,2},{6,8},{8,6},{10,12},{12,10},{14,16},{16,14},{18... | collective-permute-start | bytes 786440 | tf_op jit(solution)/shard_map/ppermute | solution.py:417
  40.5 10.3 %collective-permute-start.18 = (bf16[64,2048]{1,0:T(8,128)(2,1)S(1)}, bf16[64,2048]{1,0:T(8,128)(2,1)S(1)}, u32[]{:S(2)}, u32[]{:S(2)}) collective-permute-start(bf16[64,2048]{1,0:T(8,128)(2,1)S(1)} %get-tuple-element.18.refs_2_.refs_0_), channel_id=1, source_target_pairs={{0,1},{1,0},{2,3},{3,2},{4,5},{5,4},{6,7},{7,6},{8,9},{9,8},{10,11... | collective-permute-start | bytes 786440 | tf_op jit(solution)/shard_map/ppermute | solution.py:454
  43.2 11.3 %collective-permute-start.19 = (bf16[64,2048]{1,0:T(8,128)(2,1)S(1)}, bf16[64,2048]{1,0:T(8,128)(2,1)S(1)}, u32[]{:S(2)}, u32[]{:S(2)}) collective-permute-start(bf16[64,2048]{1,0:T(8,128)(2,1)S(1)} %get-tuple-element.19.refs_3_.refs_1_), channel_id=1, source_target_pairs={{0,1},{1,0},{2,3},{3,2},{4,5},{5,4},{6,7},{7,6},{8,9},{9,8},{10,11... | collective-permute-start | bytes 786440 | tf_op jit(solution)/shard_map/ppermute | solution.py:454
  45.0 2.0 %collective-permute-start.12 = (f32[128,128]{1,0:T(8,128)S(1)}, f32[128,128]{1,0:T(8,128)S(1)}, u32[]{:S(2)}, u32[]{:S(2)}) collective-permute-start(f32[128,128]{1,0:T(8,128)S(1)} %shard_map.61), channel_id=1, source_target_pairs={{0,2},{2,0},{4,6},{6,4},{8,10},{10,8},{12,14},{14,12},{16,18},{18,... | collective-permute-start | bytes 196616 | tf_op jit(solution)/shard_map/ppermute | solution.py:441
  47.0 8.0 %collective-permute-start.14 = (f32[128,128]{1,0:T(8,128)S(1)}, f32[128,128]{1,0:T(8,128)S(1)}, u32[]{:S(2)}, u32[]{:S(2)}) collective-permute-start(f32[128,128]{1,0:T(8,128)S(1)} %add.44.refs_4_), channel_id=1, source_target_pairs={{0,8},{2,10},{4,12},{6,14},{8,0},{10,2},{12,4},{14,6},{16,24},{18,... | collective-permute-start | bytes 196616 | tf_op jit(solution)/shard_map/ppermute | solution.py:441
  49.2 5.8 %collective-permute-start.15 = (f32[128,128]{1,0:T(8,128)S(1)}, f32[128,128]{1,0:T(8,128)S(1)}, u32[]{:S(2)}, u32[]{:S(2)}) collective-permute-start(f32[128,128]{1,0:T(8,128)S(1)} %add.44.refs_4_), channel_id=1, source_target_pairs={{0,12},{2,14},{4,8},{6,10},{8,4},{10,6},{12,0},{14,2},{16,28},{18,... | collective-permute-start | bytes 196616 | tf_op jit(solution)/shard_map/ppermute | solution.py:441
  50.8 4.8 %collective-permute-start.13 = (f32[128,128]{1,0:T(8,128)S(1)}, f32[128,128]{1,0:T(8,128)S(1)}, u32[]{:S(2)}, u32[]{:S(2)}) collective-permute-start(f32[128,128]{1,0:T(8,128)S(1)} %add.44.refs_4_), channel_id=1, source_target_pairs={{0,4},{2,6},{4,0},{6,2},{8,12},{10,14},{12,8},{14,10},{16,20},{18,... | collective-permute-start | bytes 196616 | tf_op jit(solution)/shard_map/ppermute | solution.py:441
  54.9 3.3 %collective-permute-start.20 = (f32[128,128]{1,0:T(8,128)S(1)}, f32[128,128]{1,0:T(8,128)S(1)}, u32[]{:S(2)}, u32[]{:S(2)}) collective-permute-start(f32[128,128]{1,0:T(8,128)S(1)} %shard_map.62), channel_id=1, source_target_pairs={{0,2},{2,0},{4,6},{6,4},{8,10},{10,8},{12,14},{14,12},{16,18},{18,... | collective-permute-start | bytes 196616 | tf_op jit(solution)/shard_map/ppermute | solution.py:441
  55.6 6.1 %collective-permute-start.16 = (f32[128,128]{1,0:T(8,128)S(1)}, f32[128,128]{1,0:T(8,128)S(1)}, u32[]{:S(2)}, u32[]{:S(2)}) collective-permute-start(f32[128,128]{1,0:T(8,128)S(1)} %add_add_fusion.1), channel_id=1, source_target_pairs={{0,16},{2,18},{4,20},{6,22},{8,24},{10,26},{12,28},{14,30},{16,0},... | collective-permute-start | bytes 196616 | tf_op jit(solution)/shard_map/ppermute | solution.py:441
  58.2 5.1 %collective-permute-start.22 = (f32[128,128]{1,0:T(8,128)S(1)}, f32[128,128]{1,0:T(8,128)S(1)}, u32[]{:S(2)}, u32[]{:S(2)}) collective-permute-start(f32[128,128]{1,0:T(8,128)S(1)} %add.49), channel_id=1, source_target_pairs={{0,8},{2,10},{4,12},{6,14},{8,0},{10,2},{12,4},{14,6},{16,24},{18,... | collective-permute-start | bytes 196616 | tf_op jit(solution)/shard_map/ppermute | solution.py:441
  58.8 5.2 %collective-permute-start.23 = (f32[128,128]{1,0:T(8,128)S(1)}, f32[128,128]{1,0:T(8,128)S(1)}, u32[]{:S(2)}, u32[]{:S(2)}) collective-permute-start(f32[128,128]{1,0:T(8,128)S(1)} %add.49), channel_id=1, source_target_pairs={{0,12},{2,14},{4,8},{6,10},{8,4},{10,6},{12,0},{14,2},{16,28},{18,... | collective-permute-start | bytes 196616 | tf_op jit(solution)/shard_map/ppermute | solution.py:441
  60.3 4.4 %collective-permute-start.21 = (f32[128,128]{1,0:T(8,128)S(1)}, f32[128,128]{1,0:T(8,128)S(1)}, u32[]{:S(2)}, u32[]{:S(2)}) collective-permute-start(f32[128,128]{1,0:T(8,128)S(1)} %add.49), channel_id=1, source_target_pairs={{0,4},{2,6},{4,0},{6,2},{8,12},{10,14},{12,8},{14,10},{16,20},{18,... | collective-permute-start | bytes 196616 | tf_op jit(solution)/shard_map/ppermute | solution.py:441
  61.7 4.3 %collective-permute-start.17 = (f32[128,128]{1,0:T(8,128)S(1)}, f32[128,128]{1,0:T(8,128)S(1)}, u32[]{:S(2)}, u32[]{:S(2)}) collective-permute-start(f32[128,128]{1,0:T(8,128)S(1)} %add.48.own_ref), channel_id=1, source_target_pairs={{0,1},{1,0},{2,3},{3,2},{4,5},{5,4},{6,7},{7,6},{8,9},{9,8},{10,11... | collective-permute-start | bytes 196616 | tf_op jit(solution)/shard_map/ppermute | solution.py:473
  64.7 5.7 %collective-permute-start.24 = (f32[128,128]{1,0:T(8,128)S(1)}, f32[128,128]{1,0:T(8,128)S(1)}, u32[]{:S(2)}, u32[]{:S(2)}) collective-permute-start(f32[128,128]{1,0:T(8,128)S(1)} %add_add_fusion.after_ref), channel_id=1, source_target_pairs={{0,16},{2,18},{4,20},{6,22},{8,24},{10,26},{12,28},{14,30},{16,0},... | collective-permute-start | bytes 196616 | tf_op jit(solution)/shard_map/ppermute | solution.py:441

commit v16 on v14

--- a/solution.py
+++ b/solution.py
@@ -468,7 +468,7 @@
             in_specs=smem + vmem(2 * chunks) + [pl.BlockSpec(memory_space=pl.ANY)],
             out_specs=pl.BlockSpec(memory_space=pltpu.VMEM),
             compiler_params=params,
-        )(place, *narrow, *other, near)
+        )(place, *narrow, *other, narrow[0])
         near = summed(near, stages[1:])
         far = lax.ppermute(near, "orb", swap)
         cross = summed(cross, stages[:-1])

time: 77.3 us -> 77.3 us (level)
  no operation moved by 1% of the time
where the time goes in v16:
time: 77.3 us; the launch traced here: 77.1 us
  starting transfers between devices  35.8 us (46%)
  Pallas kernels  29.8 us (39%)
  waiting for transfers between devices  7.67 us (10%)
  other arithmetic  1.53 us (2%)
  local copies, waits for them, and re-layouts  1.21 us (2%)
  between operations  1.04 us (1%)
    ppermute x4, starting transfers between devices, level(): far = lax.ppermute(vec, 'space', far_pairs)  12.8 us
    ppermute x10, starting transfers between devices, moved(): return lax.ppermute(part, 'space', [(i, i ^ step) for i in range(blocks)])  12 us
    pallas_call x6, Pallas kernels, halo_part(): pl.pallas_call(functools.partial(halo_kernel, level), out_shape=[jax.Shap...  6.75 us
    pallas_call x1, Pallas kernels, finish(): pl.pallas_call(functools.partial(finish_kernel, len(wide)), out_shape=[ja...  6.55 us
    pallas_call x4, Pallas kernels, own_part(): pl.pallas_call(own_kernel, out_shape=jax.ShapeDtypeStruct(vec.shape, jnp....  6.54 us
    ppermute x2, starting transfers between devices, shards(): fars = [lax.ppermute(vec, 'space', far_pairs) for vec in zero]  6.29 us
    pallas_call x1, Pallas kernels, turn_part(): pl.pallas_call(functools.partial(turn_kernel, chunks), out_shape=[jax.Sha...  4.85 us
    pallas_call x1, Pallas kernels, factor_first(): pl.pallas_call(first_kernel, out_shape=[jax.ShapeDtypeStruct((half, half)...  4.29 us
  transfers between devices with their start and end apart: 25, of which 7 were waited for; matrix products, arithmetic and copies ran while one was open for 2% of the time, Pallas kernels for 30%

profile of v16, /device:TPU:0, one launch (start us, length us, event | category | flops | bytes accessed | tf_op | source)
XLA Modules:
  0.0 77.1 jit_solution(6726400118203567580)
XLA Ops:
  0.6 1.1 %fusion.1 = (bf16[64,2048]{1,0:T(8,128)(2,1)S(1)}, bf16[64,2048]{1,0:T(8,128)(2,1)S(1)}) fusion(bf16[128,2048]{1,0:T(8,128)(2,1)} %param.4), kind=kLoop, calls=%fused_computation.7 | loop fusion | bytes 1048576 | tf_op jit(solution)/shard_map/slice | solution.py:422
  1.7 0.5 collective-permute-start
  2.2 5.7 %collective-permute-start.1 = (bf16[64,2048]{1,0:T(8,128)(2,1)S(1)}, bf16[64,2048]{1,0:T(8,128)(2,1)S(1)}, u32[]{:S(2)}, u32[]{:S(2)}) collective-permute-start(bf16[64,2048]{1,0:T(8,128)(2,1)S(1)} %get-tuple-element.25.refs_0_.vec_ref.prior_ref), channel_id=1, source_target_pairs={{0,30},{2,4},{4,2},{6,8},{8,6},{10,12},{12,10},{14,16},{16,14},{18... | collective-permute-start | bytes 786440 | tf_op jit(solution)/shard_map/ppermute | solution.py:423
  7.9 0.0 collective-permute-start.6
  7.9 0.6 collective-permute-start.7
  8.5 0.7 add_select_fusion
  9.2 0.1 slice.17
  9.3 0.1 fusion.2
  9.3 0.8 add_select_fusion.1.loc_ref
  10.1 4.9 %shard_map.50 = (bf16[8,7,256,256]{3,2,1,0:T(8,128)(2,1)S(1)}, f32[64,2048]{1,0:T(8,128)S(1)}, f32[64,2048]{1,0:T(8,128)S(1)}) custom-call(s32[8,6]{1,0:T(8,128)S(1)} %add_select_fusion.1.loc_ref, s32[1]{0:T(128)S(6)} %select_n.21.odd_ref, bf16[64,2048]{1,0:T(8,128)(2,1)S(1)} %get-tuple-element.25.refs_0_.vec_ref.prior_ref, ...), custom_call_target="tpu_custom_call" | custom-call | flops 671088640 | bytes 14680064 | tf_op jit(solution)/shard_map/pallas_call | solution.py:67
  15.0 0.0 collective-permute-done.1.far_ref
  15.0 1.1 %shard_map.51.vec_ref.prior_ref = bf16[64,2048]{1,0:T(8,128)(2,1)S(1)} custom-call(s32[8,6]{1,0:T(8,128)S(1)} %add_select_fusion.1.loc_ref, bf16[64,2048]{1,0:T(8,128)(2,1)S(1)} %collective-permute-done.near_ref, bf16[64,2048]{1,0:T(8,128)(2,1)S(1)} %collective-permute-done.1.far_ref, f32[64,2048]{1,0:T(8,128)S(1)} %get-tuple-element.13.acc_ref, ...), custom_call_target="tpu_custom_call" | custom-call | flops 134217728 | bytes 2097152 | tf_op jit(solution)/shard_map/pallas_call | solution.py:139
  16.1 0.1 collective-permute-start.2
  16.2 3.9 %collective-permute-start.3 = (bf16[64,2048]{1,0:T(8,128)(2,1)S(1)}, bf16[64,2048]{1,0:T(8,128)(2,1)S(1)}, u32[]{:S(2)}, u32[]{:S(2)}) collective-permute-start(bf16[64,2048]{1,0:T(8,128)(2,1)S(1)} %shard_map.51.vec_ref.prior_ref), channel_id=1, source_target_pairs={{0,30},{2,4},{4,2},{6,8},{8,6},{10,12},{12,10},{14,16},{16,14},{18... | collective-permute-start | bytes 786440 | tf_op jit(solution)/shard_map/ppermute | solution.py:417
  20.1 0.0 collective-permute-done.6.near_ref
  20.1 1.1 %shard_map.56.vec_ref.prior_ref = bf16[64,2048]{1,0:T(8,128)(2,1)S(1)} custom-call(s32[8,6]{1,0:T(8,128)S(1)} %add_select_fusion.1.loc_ref, bf16[64,2048]{1,0:T(8,128)(2,1)S(1)} %collective-permute-done.6.near_ref, bf16[64,2048]{1,0:T(8,128)(2,1)S(1)} %collective-permute-done.7.far_ref, f32[64,2048]{1,0:T(8,128)S(1)} %get-tuple-element.16.acc_ref, ...), custom_call_target="tpu_custom_call" | custom-call | flops 134217728 | bytes 2097152 | tf_op jit(solution)/shard_map/pallas_call | solution.py:139
  21.2 0.1 collective-permute-start.8
  21.3 2.1 %collective-permute-start.9 = (bf16[64,2048]{1,0:T(8,128)(2,1)S(1)}, bf16[64,2048]{1,0:T(8,128)(2,1)S(1)}, u32[]{:S(2)}, u32[]{:S(2)}) collective-permute-start(bf16[64,2048]{1,0:T(8,128)(2,1)S(1)} %shard_map.56.vec_ref.prior_ref), channel_id=1, source_target_pairs={{0,30},{2,4},{4,2},{6,8},{8,6},{10,12},{12,10},{14,16},{16,14},{18... | collective-permute-start | bytes 786440 | tf_op jit(solution)/shard_map/ppermute | solution.py:417
  23.3 1.6 %shard_map.52.acc_ref = f32[64,2048]{1,0:T(8,128)S(1)} custom-call(s32[8,6]{1,0:T(8,128)S(1)} %add_select_fusion.1.loc_ref, bf16[64,2048]{1,0:T(8,128)(2,1)S(1)} %shard_map.51.vec_ref.prior_ref, bf16[8,7,256,256]{3,2,1,0:T(8,128)(2,1)S(1)} %get-tuple-element.14.turned_ref), custom_call_target="tpu_custom_call" | custom-call | flops 335544320 | bytes 5242880 | tf_op jit(solution)/shard_map/pallas_call | solution.py:104
  25.0 1.6 %shard_map.57.acc_ref = f32[64,2048]{1,0:T(8,128)S(1)} custom-call(s32[8,6]{1,0:T(8,128)S(1)} %add_select_fusion.1.loc_ref, bf16[64,2048]{1,0:T(8,128)(2,1)S(1)} %shard_map.56.vec_ref.prior_ref, bf16[8,7,256,256]{3,2,1,0:T(8,128)(2,1)S(1)} %get-tuple-element.14.turned_ref), custom_call_target="tpu_custom_call" | custom-call | flops 335544320 | bytes 5242880 | tf_op jit(solution)/shard_map/pallas_call | solution.py:104
  26.6 0.0 collective-permute-done.2.near_ref
  26.6 0.0 collective-permute-done.3.far_ref
  26.7 1.1 %shard_map.53.vec_ref = bf16[64,2048]{1,0:T(8,128)(2,1)S(1)} custom-call(s32[8,6]{1,0:T(8,128)S(1)} %add_select_fusion.1.loc_ref, bf16[64,2048]{1,0:T(8,128)(2,1)S(1)} %collective-permute-done.2.near_ref, bf16[64,2048]{1,0:T(8,128)(2,1)S(1)} %collective-permute-done.3.far_ref, f32[64,2048]{1,0:T(8,128)S(1)} %shard_map.52.acc_ref, ...), custom_call_target="tpu_custom_call" | custom-call | flops 134217728 | bytes 2097152 | tf_op jit(solution)/shard_map/pallas_call | solution.py:139
  27.8 0.2 collective-permute-start.4
  28.0 3.9 %collective-permute-start.5 = (bf16[64,2048]{1,0:T(8,128)(2,1)S(1)}, bf16[64,2048]{1,0:T(8,128)(2,1)S(1)}, u32[]{:S(2)}, u32[]{:S(2)}) collective-permute-start(bf16[64,2048]{1,0:T(8,128)(2,1)S(1)} %shard_map.53.vec_ref), channel_id=1, source_target_pairs={{0,30},{2,4},{4,2},{6,8},{8,6},{10,12},{12,10},{14,16},{16,14},{18... | collective-permute-start | bytes 786440 | tf_op jit(solution)/shard_map/ppermute | solution.py:417
  31.9 0.0 collective-permute-done.8.near_ref
  31.9 1.1 %shard_map.58.vec_ref = bf16[64,2048]{1,0:T(8,128)(2,1)S(1)} custom-call(s32[8,6]{1,0:T(8,128)S(1)} %add_select_fusion.1.loc_ref, bf16[64,2048]{1,0:T(8,128)(2,1)S(1)} %collective-permute-done.8.near_ref, bf16[64,2048]{1,0:T(8,128)(2,1)S(1)} %collective-permute-done.9.far_ref, f32[64,2048]{1,0:T(8,128)S(1)} %shard_map.57.acc_ref, ...), custom_call_target="tpu_custom_call" | custom-call | flops 134217728 | bytes 2097152 | tf_op jit(solution)/shard_map/pallas_call | solution.py:139
  33.0 0.1 collective-permute-start.10
  33.1 2.9 %collective-permute-start.11 = (bf16[64,2048]{1,0:T(8,128)(2,1)S(1)}, bf16[64,2048]{1,0:T(8,128)(2,1)S(1)}, u32[]{:S(2)}, u32[]{:S(2)}) collective-permute-start(bf16[64,2048]{1,0:T(8,128)(2,1)S(1)} %shard_map.58.vec_ref), channel_id=1, source_target_pairs={{0,30},{2,4},{4,2},{6,8},{8,6},{10,12},{12,10},{14,16},{16,14},{18... | collective-permute-start | bytes 786440 | tf_op jit(solution)/shard_map/ppermute | solution.py:417
  36.1 1.6 %shard_map.54.acc_ref = f32[64,2048]{1,0:T(8,128)S(1)} custom-call(s32[8,6]{1,0:T(8,128)S(1)} %add_select_fusion.1.loc_ref, bf16[64,2048]{1,0:T(8,128)(2,1)S(1)} %shard_map.53.vec_ref, bf16[8,7,256,256]{3,2,1,0:T(8,128)(2,1)S(1)} %get-tuple-element.14.turned_ref), custom_call_target="tpu_custom_call" | custom-call | flops 335544320 | bytes 5242880 | tf_op jit(solution)/shard_map/pallas_call | solution.py:104
  37.7 1.6 %shard_map.59.acc_ref = f32[64,2048]{1,0:T(8,128)S(1)} custom-call(s32[8,6]{1,0:T(8,128)S(1)} %add_select_fusion.1.loc_ref, bf16[64,2048]{1,0:T(8,128)(2,1)S(1)} %shard_map.58.vec_ref, bf16[8,7,256,256]{3,2,1,0:T(8,128)(2,1)S(1)} %get-tuple-element.14.turned_ref), custom_call_target="tpu_custom_call" | custom-call | flops 335544320 | bytes 5242880 | tf_op jit(solution)/shard_map/pallas_call | solution.py:104
  39.3 0.0 collective-permute-done.4.near_ref
  39.4 0.0 collective-permute-done.5.far_ref
  39.4 1.1 %shard_map.55 = (f32[64,2048]{1,0:T(8,128)S(1)}, bf16[64,2048]{1,0:T(8,128)(2,1)S(1)}) custom-call(s32[8,6]{1,0:T(8,128)S(1)} %add_select_fusion.1.loc_ref, bf16[64,2048]{1,0:T(8,128)(2,1)S(1)} %collective-permute-done.4.near_ref, bf16[64,2048]{1,0:T(8,128)(2,1)S(1)} %collective-permute-done.5.far_ref, f32[64,2048]{1,0:T(8,128)S(1)} %shard_map.54.acc_ref, ...), custom_call_target="tpu_custom_call" | custom-call | flops 134217728 | bytes 2097152 | tf_op jit(solution)/shard_map/pallas_call | solution.py:139
  40.5 1.6 %collective-permute-start.18 = (bf16[64,2048]{1,0:T(8,128)(2,1)S(1)}, bf16[64,2048]{1,0:T(8,128)(2,1)S(1)}, u32[]{:S(2)}, u32[]{:S(2)}) collective-permute-start(bf16[64,2048]{1,0:T(8,128)(2,1)S(1)} %get-tuple-element.18.refs_2_.refs_0_.refs_4_), channel_id=1, source_target_pairs={{0,1},{1,0},{2,3},{3,2},{4,5},{5,4},{6,7},{7,6},{8,9},{9,8},{10,11... | collective-permute-start | bytes 786440 | tf_op jit(solution)/shard_map/ppermute | solution.py:454
  42.1 0.0 collective-permute-done.10.near_ref
  42.1 0.0 collective-permute-done.11.far_ref
  42.1 1.1 %shard_map.60 = (f32[64,2048]{1,0:T(8,128)S(1)}, bf16[64,2048]{1,0:T(8,128)(2,1)S(1)}) custom-call(s32[8,6]{1,0:T(8,128)S(1)} %add_select_fusion.1.loc_ref, bf16[64,2048]{1,0:T(8,128)(2,1)S(1)} %collective-permute-done.10.near_ref, bf16[64,2048]{1,0:T(8,128)(2,1)S(1)} %collective-permute-done.11.far_ref, f32[64,2048]{1,0:T(8,128)S(1)} %shard_map.59.acc_ref, ...), custom_call_target="tpu_custom_call" | custom-call | flops 134217728 | bytes 2097152 | tf_op jit(solution)/shard_map/pallas_call | solution.py:139
  43.2 1.3 %collective-permute-start.19 = (bf16[64,2048]{1,0:T(8,128)(2,1)S(1)}, bf16[64,2048]{1,0:T(8,128)(2,1)S(1)}, u32[]{:S(2)}, u32[]{:S(2)}) collective-permute-start(bf16[64,2048]{1,0:T(8,128)(2,1)S(1)} %get-tuple-element.19.refs_3_.refs_1_), channel_id=1, source_target_pairs={{0,1},{1,0},{2,3},{3,2},{4,5},{5,4},{6,7},{7,6},{8,9},{9,8},{10,11... | collective-permute-start | bytes 786440 | tf_op jit(solution)/shard_map/ppermute | solution.py:454
  44.5 0.5 shard_map.61
  45.0 1.1 %collective-permute-start.12 = (f32[128,128]{1,0:T(8,128)S(1)}, f32[128,128]{1,0:T(8,128)S(1)}, u32[]{:S(2)}, u32[]{:S(2)}) collective-permute-start(f32[128,128]{1,0:T(8,128)S(1)} %shard_map.61), channel_id=1, source_target_pairs={{0,2},{2,0},{4,6},{6,4},{8,10},{10,8},{12,14},{14,12},{16,18},{18,... | collective-permute-start | bytes 196616 | tf_op jit(solution)/shard_map/ppermute | solution.py:441
  46.1 0.9 %collective-permute-done.12 = f32[128,128]{1,0:T(8,128)S(1)} collective-permute-done((f32[128,128]{1,0:T(8,128)S(1)}, f32[128,128]{1,0:T(8,128)S(1)}, u32[]{:S(2)}, u32[]{:S(2)}) %collective-permute-start.12) | collective-permute-done | bytes 65568 | tf_op jit(solution)/shard_map/ppermute | solution.py:441
  47.0 2.2 %collective-permute-start.14 = (f32[128,128]{1,0:T(8,128)S(1)}, f32[128,128]{1,0:T(8,128)S(1)}, u32[]{:S(2)}, u32[]{:S(2)}) collective-permute-start(f32[128,128]{1,0:T(8,128)S(1)} %add.44), channel_id=1, source_target_pairs={{0,8},{2,10},{4,12},{6,14},{8,0},{10,2},{12,4},{14,6},{16,24},{18,... | collective-permute-start | bytes 196616 | tf_op jit(solution)/shard_map/ppermute | solution.py:441
  49.2 1.6 %collective-permute-start.15 = (f32[128,128]{1,0:T(8,128)S(1)}, f32[128,128]{1,0:T(8,128)S(1)}, u32[]{:S(2)}, u32[]{:S(2)}) collective-permute-start(f32[128,128]{1,0:T(8,128)S(1)} %add.44), channel_id=1, source_target_pairs={{0,12},{2,14},{4,8},{6,10},{8,4},{10,6},{12,0},{14,2},{16,28},{18,... | collective-permute-start | bytes 196616 | tf_op jit(solution)/shard_map/ppermute | solution.py:441
  50.8 0.0 collective-permute-start.13
  50.8 0.0 collective-permute-done.18.refs_2_.refs_4_
  50.8 3.8 %collective-permute-done.19.refs_3_.refs_5_ = bf16[64,2048]{1,0:T(8,128)(2,1)S(1)} collective-permute-done((bf16[64,2048]{1,0:T(8,128)(2,1)S(1)}, bf16[64,2048]{1,0:T(8,128)(2,1)S(1)}, u32[]{:S(2)}, u32[]{:S(2)}) %collective-permute-start.19) | collective-permute-done | bytes 262176 | tf_op jit(solution)/shard_map/ppermute | solution.py:454
  54.6 0.3 shard_map.62
  54.9 0.1 collective-permute-start.20
  55.0 0.0 collective-permute-done.14
  55.0 0.6 collective-permute-done.13
  55.6 2.5 %collective-permute-start.16 = (f32[128,128]{1,0:T(8,128)S(1)}, f32[128,128]{1,0:T(8,128)S(1)}, u32[]{:S(2)}, u32[]{:S(2)}) collective-permute-start(f32[128,128]{1,0:T(8,128)S(1)} %add_add_fusion.1), channel_id=1, source_target_pairs={{0,16},{2,18},{4,20},{6,22},{8,24},{10,26},{12,28},{14,30},{16,0},... | collective-permute-start | bytes 196616 | tf_op jit(solution)/shard_map/ppermute | solution.py:441
  58.1 0.7 collective-permute-start.22
  58.8 1.5 %collective-permute-start.23 = (f32[128,128]{1,0:T(8,128)S(1)}, f32[128,128]{1,0:T(8,128)S(1)}, u32[]{:S(2)}, u32[]{:S(2)}) collective-permute-start(f32[128,128]{1,0:T(8,128)S(1)} %add.49), channel_id=1, source_target_pairs={{0,12},{2,14},{4,8},{6,10},{8,4},{10,6},{12,0},{14,2},{16,28},{18,... | collective-permute-start | bytes 196616 | tf_op jit(solution)/shard_map/ppermute | solution.py:441
  60.3 1.4 %collective-permute-start.21 = (f32[128,128]{1,0:T(8,128)S(1)}, f32[128,128]{1,0:T(8,128)S(1)}, u32[]{:S(2)}, u32[]{:S(2)}) collective-permute-start(f32[128,128]{1,0:T(8,128)S(1)} %add.49), channel_id=1, source_target_pairs={{0,4},{2,6},{4,0},{6,2},{8,12},{10,14},{12,8},{14,10},{16,20},{18,... | collective-permute-start | bytes 196616 | tf_op jit(solution)/shard_map/ppermute | solution.py:441
  61.7 0.0 collective-permute-done.16
  61.7 1.0 %collective-permute-start.17 = (f32[128,128]{1,0:T(8,128)S(1)}, f32[128,128]{1,0:T(8,128)S(1)}, u32[]{:S(2)}, u32[]{:S(2)}) collective-permute-start(f32[128,128]{1,0:T(8,128)S(1)} %add.48.own_ref), channel_id=1, source_target_pairs={{0,1},{1,0},{2,3},{3,2},{4,5},{5,4},{6,7},{7,6},{8,9},{9,8},{10,11... | collective-permute-start | bytes 196616 | tf_op jit(solution)/shard_map/ppermute | solution.py:473
  62.8 0.5 collective-permute-done.22
  63.2 0.7 collective-permute-done.23
  64.0 0.7 collective-permute-done.21
  64.7 1.0 %collective-permute-start.24 = (f32[128,128]{1,0:T(8,128)S(1)}, f32[128,128]{1,0:T(8,128)S(1)}, u32[]{:S(2)}, u32[]{:S(2)}) collective-permute-start(f32[128,128]{1,0:T(8,128)S(1)} %add_add_fusion.after_ref), channel_id=1, source_target_pairs={{0,16},{2,18},{4,20},{6,22},{8,24},{10,26},{12,28},{14,30},{16,0},... | collective-permute-start | bytes 196616 | tf_op jit(solution)/shard_map/ppermute | solution.py:441
  65.7 0.4 collective-permute-done.17.other_ref
  66.1 4.3 %shard_map.63 = (f32[128,128]{1,0:T(8,128)S(1)}, f32[128,128]{1,0:T(8,128)S(1)}) custom-call(s32[1]{0:T(128)} %bitcast.place_ref, f32[128,128]{1,0:T(8,128)S(1)} %add.48.own_ref, f32[128,128]{1,0:T(8,128)S(1)} %collective-permute-done.17.other_ref, f32[128,128]{1,0:T(8,128)S(1)} %add_add_fusion.after_ref), custom_call_target="tpu_custom_call" | custom-call | flops 4194304 | bytes 16777216 | tf_op jit(solution)/shard_map/pallas_call | solution.py:304
  70.4 6.6 %shard_map.64 = (f32[256,256]{1,0:T(8,128)}, f32[128,2048]{1,0:T(8,128)}) custom-call(s32[1]{0:T(128)} %bitcast.place_ref, f32[128,128]{1,0:T(8,128)S(1)} %add.48.own_ref, f32[128,128]{1,0:T(8,128)S(1)} %collective-permute-done.17.other_ref, f32[128,128]{1,0:T(8,128)S(1)} %add.53.cross_ref, f32[128,128]{1,0:T(8,128)S(1)} %get-tuple-element.20.first_ref, ...), custom_call_target="tpu_custom_call" | custom-call | tf_op jit(solution)/shard_map/pallas_call | solution.py:385
  (12 shorter events, 0.1 us)
Async XLA Ops:
  1.7 13.3 %collective-permute-start = (bf16[64,2048]{1,0:T(8,128)(2,1)S(1)}, bf16[64,2048]{1,0:T(8,128)(2,1)S(1)}, u32[]{:S(2)}, u32[]{:S(2)}) collective-permute-start(bf16[64,2048]{1,0:T(8,128)(2,1)S(1)} %get-tuple-element.25.refs_0_.vec_ref.prior_ref), channel_id=1, source_target_pairs={{0,2},{2,0},{4,6},{6,4},{8,10},{10,8},{12,14},{14,12},{16,18},{18,... | collective-permute-start | bytes 786440 | tf_op jit(solution)/shard_map/ppermute | solution.py:424
  2.2 12.8 %collective-permute-start.1 = (bf16[64,2048]{1,0:T(8,128)(2,1)S(1)}, bf16[64,2048]{1,0:T(8,128)(2,1)S(1)}, u32[]{:S(2)}, u32[]{:S(2)}) collective-permute-start(bf16[64,2048]{1,0:T(8,128)(2,1)S(1)} %get-tuple-element.25.refs_0_.vec_ref.prior_ref), channel_id=1, source_target_pairs={{0,30},{2,4},{4,2},{6,8},{8,6},{10,12},{12,10},{14,16},{16,14},{18... | collective-permute-start | bytes 786440 | tf_op jit(solution)/shard_map/ppermute | solution.py:423
  7.9 12.2 %collective-permute-start.6 = (bf16[64,2048]{1,0:T(8,128)(2,1)S(1)}, bf16[64,2048]{1,0:T(8,128)(2,1)S(1)}, u32[]{:S(2)}, u32[]{:S(2)}) collective-permute-start(bf16[64,2048]{1,0:T(8,128)(2,1)S(1)} %get-tuple-element.24.refs_1_.vec_ref.prior_ref), channel_id=1, source_target_pairs={{0,2},{2,0},{4,6},{6,4},{8,10},{10,8},{12,14},{14,12},{16,18},{18,... | collective-permute-start | bytes 786440 | tf_op jit(solution)/shard_map/ppermute | solution.py:424
  7.9 12.2 %collective-permute-start.7 = (bf16[64,2048]{1,0:T(8,128)(2,1)S(1)}, bf16[64,2048]{1,0:T(8,128)(2,1)S(1)}, u32[]{:S(2)}, u32[]{:S(2)}) collective-permute-start(bf16[64,2048]{1,0:T(8,128)(2,1)S(1)} %get-tuple-element.24.refs_1_.vec_ref.prior_ref), channel_id=1, source_target_pairs={{0,30},{2,4},{4,2},{6,8},{8,6},{10,12},{12,10},{14,16},{16,14},{18... | collective-permute-start | bytes 786440 | tf_op jit(solution)/shard_map/ppermute | solution.py:423
  16.1 10.5 %collective-permute-start.2 = (bf16[64,2048]{1,0:T(8,128)(2,1)S(1)}, bf16[64,2048]{1,0:T(8,128)(2,1)S(1)}, u32[]{:S(2)}, u32[]{:S(2)}) collective-permute-start(bf16[64,2048]{1,0:T(8,128)(2,1)S(1)} %shard_map.51.vec_ref.prior_ref), channel_id=1, source_target_pairs={{0,2},{2,0},{4,6},{6,4},{8,10},{10,8},{12,14},{14,12},{16,18},{18,... | collective-permute-start | bytes 786440 | tf_op jit(solution)/shard_map/ppermute | solution.py:418
  16.2 10.5 %collective-permute-start.3 = (bf16[64,2048]{1,0:T(8,128)(2,1)S(1)}, bf16[64,2048]{1,0:T(8,128)(2,1)S(1)}, u32[]{:S(2)}, u32[]{:S(2)}) collective-permute-start(bf16[64,2048]{1,0:T(8,128)(2,1)S(1)} %shard_map.51.vec_ref.prior_ref), channel_id=1, source_target_pairs={{0,30},{2,4},{4,2},{6,8},{8,6},{10,12},{12,10},{14,16},{16,14},{18... | collective-permute-start | bytes 786440 | tf_op jit(solution)/shard_map/ppermute | solution.py:417
  21.2 10.7 %collective-permute-start.8 = (bf16[64,2048]{1,0:T(8,128)(2,1)S(1)}, bf16[64,2048]{1,0:T(8,128)(2,1)S(1)}, u32[]{:S(2)}, u32[]{:S(2)}) collective-permute-start(bf16[64,2048]{1,0:T(8,128)(2,1)S(1)} %shard_map.56.vec_ref.prior_ref), channel_id=1, source_target_pairs={{0,2},{2,0},{4,6},{6,4},{8,10},{10,8},{12,14},{14,12},{16,18},{18,... | collective-permute-start | bytes 786440 | tf_op jit(solution)/shard_map/ppermute | solution.py:418
  21.3 10.6 %collective-permute-start.9 = (bf16[64,2048]{1,0:T(8,128)(2,1)S(1)}, bf16[64,2048]{1,0:T(8,128)(2,1)S(1)}, u32[]{:S(2)}, u32[]{:S(2)}) collective-permute-start(bf16[64,2048]{1,0:T(8,128)(2,1)S(1)} %shard_map.56.vec_ref.prior_ref), channel_id=1, source_target_pairs={{0,30},{2,4},{4,2},{6,8},{8,6},{10,12},{12,10},{14,16},{16,14},{18... | collective-permute-start | bytes 786440 | tf_op jit(solution)/shard_map/ppermute | solution.py:417
  27.8 11.5 %collective-permute-start.4 = (bf16[64,2048]{1,0:T(8,128)(2,1)S(1)}, bf16[64,2048]{1,0:T(8,128)(2,1)S(1)}, u32[]{:S(2)}, u32[]{:S(2)}) collective-permute-start(bf16[64,2048]{1,0:T(8,128)(2,1)S(1)} %shard_map.53.vec_ref), channel_id=1, source_target_pairs={{0,2},{2,0},{4,6},{6,4},{8,10},{10,8},{12,14},{14,12},{16,18},{18,... | collective-permute-start | bytes 786440 | tf_op jit(solution)/shard_map/ppermute | solution.py:418
  28.0 11.3 %collective-permute-start.5 = (bf16[64,2048]{1,0:T(8,128)(2,1)S(1)}, bf16[64,2048]{1,0:T(8,128)(2,1)S(1)}, u32[]{:S(2)}, u32[]{:S(2)}) collective-permute-start(bf16[64,2048]{1,0:T(8,128)(2,1)S(1)} %shard_map.53.vec_ref), channel_id=1, source_target_pairs={{0,30},{2,4},{4,2},{6,8},{8,6},{10,12},{12,10},{14,16},{16,14},{18... | collective-permute-start | bytes 786440 | tf_op jit(solution)/shard_map/ppermute | solution.py:417
  33.0 9.0 %collective-permute-start.10 = (bf16[64,2048]{1,0:T(8,128)(2,1)S(1)}, bf16[64,2048]{1,0:T(8,128)(2,1)S(1)}, u32[]{:S(2)}, u32[]{:S(2)}) collective-permute-start(bf16[64,2048]{1,0:T(8,128)(2,1)S(1)} %shard_map.58.vec_ref), channel_id=1, source_target_pairs={{0,2},{2,0},{4,6},{6,4},{8,10},{10,8},{12,14},{14,12},{16,18},{18,... | collective-permute-start | bytes 786440 | tf_op jit(solution)/shard_map/ppermute | solution.py:418
  33.1 9.0 %collective-permute-start.11 = (bf16[64,2048]{1,0:T(8,128)(2,1)S(1)}, bf16[64,2048]{1,0:T(8,128)(2,1)S(1)}, u32[]{:S(2)}, u32[]{:S(2)}) collective-permute-start(bf16[64,2048]{1,0:T(8,128)(2,1)S(1)} %shard_map.58.vec_ref), channel_id=1, source_target_pairs={{0,30},{2,4},{4,2},{6,8},{8,6},{10,12},{12,10},{14,16},{16,14},{18... | collective-permute-start | bytes 786440 | tf_op jit(solution)/shard_map/ppermute | solution.py:417
  40.5 10.3 %collective-permute-start.18 = (bf16[64,2048]{1,0:T(8,128)(2,1)S(1)}, bf16[64,2048]{1,0:T(8,128)(2,1)S(1)}, u32[]{:S(2)}, u32[]{:S(2)}) collective-permute-start(bf16[64,2048]{1,0:T(8,128)(2,1)S(1)} %get-tuple-element.18.refs_2_.refs_0_.refs_4_), channel_id=1, source_target_pairs={{0,1},{1,0},{2,3},{3,2},{4,5},{5,4},{6,7},{7,6},{8,9},{9,8},{10,11... | collective-permute-start | bytes 786440 | tf_op jit(solution)/shard_map/ppermute | solution.py:454
  43.2 11.3 %collective-permute-start.19 = (bf16[64,2048]{1,0:T(8,128)(2,1)S(1)}, bf16[64,2048]{1,0:T(8,128)(2,1)S(1)}, u32[]{:S(2)}, u32[]{:S(2)}) collective-permute-start(bf16[64,2048]{1,0:T(8,128)(2,1)S(1)} %get-tuple-element.19.refs_3_.refs_1_), channel_id=1, source_target_pairs={{0,1},{1,0},{2,3},{3,2},{4,5},{5,4},{6,7},{7,6},{8,9},{9,8},{10,11... | collective-permute-start | bytes 786440 | tf_op jit(solution)/shard_map/ppermute | solution.py:454
  45.0 2.0 %collective-permute-start.12 = (f32[128,128]{1,0:T(8,128)S(1)}, f32[128,128]{1,0:T(8,128)S(1)}, u32[]{:S(2)}, u32[]{:S(2)}) collective-permute-start(f32[128,128]{1,0:T(8,128)S(1)} %shard_map.61), channel_id=1, source_target_pairs={{0,2},{2,0},{4,6},{6,4},{8,10},{10,8},{12,14},{14,12},{16,18},{18,... | collective-permute-start | bytes 196616 | tf_op jit(solution)/shard_map/ppermute | solution.py:441
  47.0 8.0 %collective-permute-start.14 = (f32[128,128]{1,0:T(8,128)S(1)}, f32[128,128]{1,0:T(8,128)S(1)}, u32[]{:S(2)}, u32[]{:S(2)}) collective-permute-start(f32[128,128]{1,0:T(8,128)S(1)} %add.44), channel_id=1, source_target_pairs={{0,8},{2,10},{4,12},{6,14},{8,0},{10,2},{12,4},{14,6},{16,24},{18,... | collective-permute-start | bytes 196616 | tf_op jit(solution)/shard_map/ppermute | solution.py:441
  49.2 5.8 %collective-permute-start.15 = (f32[128,128]{1,0:T(8,128)S(1)}, f32[128,128]{1,0:T(8,128)S(1)}, u32[]{:S(2)}, u32[]{:S(2)}) collective-permute-start(f32[128,128]{1,0:T(8,128)S(1)} %add.44), channel_id=1, source_target_pairs={{0,12},{2,14},{4,8},{6,10},{8,4},{10,6},{12,0},{14,2},{16,28},{18,... | collective-permute-start | bytes 196616 | tf_op jit(solution)/shard_map/ppermute | solution.py:441
  50.8 4.8 %collective-permute-start.13 = (f32[128,128]{1,0:T(8,128)S(1)}, f32[128,128]{1,0:T(8,128)S(1)}, u32[]{:S(2)}, u32[]{:S(2)}) collective-permute-start(f32[128,128]{1,0:T(8,128)S(1)} %add.44), channel_id=1, source_target_pairs={{0,4},{2,6},{4,0},{6,2},{8,12},{10,14},{12,8},{14,10},{16,20},{18,... | collective-permute-start | bytes 196616 | tf_op jit(solution)/shard_map/ppermute | solution.py:441
  54.9 3.3 %collective-permute-start.20 = (f32[128,128]{1,0:T(8,128)S(1)}, f32[128,128]{1,0:T(8,128)S(1)}, u32[]{:S(2)}, u32[]{:S(2)}) collective-permute-start(f32[128,128]{1,0:T(8,128)S(1)} %shard_map.62), channel_id=1, source_target_pairs={{0,2},{2,0},{4,6},{6,4},{8,10},{10,8},{12,14},{14,12},{16,18},{18,... | collective-permute-start | bytes 196616 | tf_op jit(solution)/shard_map/ppermute | solution.py:441
  55.6 6.1 %collective-permute-start.16 = (f32[128,128]{1,0:T(8,128)S(1)}, f32[128,128]{1,0:T(8,128)S(1)}, u32[]{:S(2)}, u32[]{:S(2)}) collective-permute-start(f32[128,128]{1,0:T(8,128)S(1)} %add_add_fusion.1), channel_id=1, source_target_pairs={{0,16},{2,18},{4,20},{6,22},{8,24},{10,26},{12,28},{14,30},{16,0},... | collective-permute-start | bytes 196616 | tf_op jit(solution)/shard_map/ppermute | solution.py:441
  58.1 5.1 %collective-permute-start.22 = (f32[128,128]{1,0:T(8,128)S(1)}, f32[128,128]{1,0:T(8,128)S(1)}, u32[]{:S(2)}, u32[]{:S(2)}) collective-permute-start(f32[128,128]{1,0:T(8,128)S(1)} %add.49), channel_id=1, source_target_pairs={{0,8},{2,10},{4,12},{6,14},{8,0},{10,2},{12,4},{14,6},{16,24},{18,... | collective-permute-start | bytes 196616 | tf_op jit(solution)/shard_map/ppermute | solution.py:441
  58.8 5.2 %collective-permute-start.23 = (f32[128,128]{1,0:T(8,128)S(1)}, f32[128,128]{1,0:T(8,128)S(1)}, u32[]{:S(2)}, u32[]{:S(2)}) collective-permute-start(f32[128,128]{1,0:T(8,128)S(1)} %add.49), channel_id=1, source_target_pairs={{0,12},{2,14},{4,8},{6,10},{8,4},{10,6},{12,0},{14,2},{16,28},{18,... | collective-permute-start | bytes 196616 | tf_op jit(solution)/shard_map/ppermute | solution.py:441
  60.3 4.4 %collective-permute-start.21 = (f32[128,128]{1,0:T(8,128)S(1)}, f32[128,128]{1,0:T(8,128)S(1)}, u32[]{:S(2)}, u32[]{:S(2)}) collective-permute-start(f32[128,128]{1,0:T(8,128)S(1)} %add.49), channel_id=1, source_target_pairs={{0,4},{2,6},{4,0},{6,2},{8,12},{10,14},{12,8},{14,10},{16,20},{18,... | collective-permute-start | bytes 196616 | tf_op jit(solution)/shard_map/ppermute | solution.py:441
  61.7 4.3 %collective-permute-start.17 = (f32[128,128]{1,0:T(8,128)S(1)}, f32[128,128]{1,0:T(8,128)S(1)}, u32[]{:S(2)}, u32[]{:S(2)}) collective-permute-start(f32[128,128]{1,0:T(8,128)S(1)} %add.48.own_ref), channel_id=1, source_target_pairs={{0,1},{1,0},{2,3},{3,2},{4,5},{5,4},{6,7},{7,6},{8,9},{9,8},{10,11... | collective-permute-start | bytes 196616 | tf_op jit(solution)/shard_map/ppermute | solution.py:473
  64.7 5.7 %collective-permute-start.24 = (f32[128,128]{1,0:T(8,128)S(1)}, f32[128,128]{1,0:T(8,128)S(1)}, u32[]{:S(2)}, u32[]{:S(2)}) collective-permute-start(f32[128,128]{1,0:T(8,128)S(1)} %add_add_fusion.after_ref), channel_id=1, source_target_pairs={{0,16},{2,18},{4,20},{6,22},{8,24},{10,26},{12,28},{14,30},{16,0},... | collective-permute-start | bytes 196616 | tf_op jit(solution)/shard_map/ppermute | solution.py:441
